TPU v7x, 128 devices: a whole 4x4x4 slice. The times are simulated.
128 devices in a mesh: dp: 16 (over y_lo, x, core), tensor: 8 (over y_hi, z).
Axes of the slice: x: 4, y: 4 (y_hi: 2, y_lo: 2; y = y_hi * 2 + y_lo), z: 4, core: 2. Of those that a mesh axis runs over, the one named last changes fastest.
Arguments:
- hidden: bfloat16 [16, 128, 8192], P('dp', 'tensor'), may hold values from -6 to 6
- query_weight: bfloat16 [8192, 4096], P(None, 'tensor'), may hold values from -0.0625 to 0.0625
- key_value_weight: bfloat16 [2, 8192, 1024], P(None, None, 'tensor'), may hold values from -0.0625 to 0.0625
- output_weight: bfloat16 [4096, 8192], P('tensor'), may hold values from -0.09375 to 0.09375
- head: bfloat16 [8192, 5], replicated, may hold values from -0.5 to 0.5
- lens: int32 [16], P('dp'), may hold values from 32 to 128
- partner: int32 [16], replicated, may hold values from 0 to 15, as said below
- adapter_down_qkv: bfloat16 [3, 8192, 16], replicated, may hold values from -0.0625 to 0.0625
- adapter_up_query: bfloat16 [16, 4096], P(None, 'tensor'), may hold values from -2 to 2
- adapter_up_key_value: bfloat16 [2, 16, 1024], P(None, None, 'tensor'), may hold values from -2 to 2
- adapter_down_output: bfloat16 [4096, 16], P('tensor'), may hold values from -0.09375 to 0.09375
- adapter_up_output: bfloat16 [16, 8192], replicated, may hold values from -2 to 2
- initial_down_qkv: float32 [3, 8192, 16], replicated, may hold values from -6 to 6
- initial_up_query: float32 [16, 4096], replicated, may hold values from -6 to 6
- initial_up_key_value: float32 [2, 16, 1024], replicated, may hold values from -6 to 6
- initial_down_output: float32 [4096, 16], replicated, may hold values from -6 to 6
- initial_up_output: float32 [16, 8192], replicated, may hold values from -6 to 6
Outputs:
- next_a: float32 [3, 8192, 16], replicated
- next_bq: float32 [16, 4096], replicated
- next_bkv: float32 [2, 16, 1024], replicated
- next_ao: float32 [4096, 16], replicated
- next_bo: float32 [16, 8192], replicated
Inputs may be any that keep to these rules, and one draw needn't show every extreme that they name: partner pairs the sequences: partner[partner[i]] = i and partner[i] differs from i.
All inputs are finite; a program needn't handle non-finite values.
Results may differ from a plain program's by a relative error of at most 0.013.
Values may be sent and summed in bfloat16 or wider, within the bound.
No kernel may reach another device: no remote copies, remote signals or barrier semaphores. Data moves between devices by JAX's collectives and lax.ppermute only.
A program may use at most 128 MiB of HBM per device.

v0:
```python
import math

import jax
import jax.numpy as jnp
from jax import lax
from jax.sharding import PartitionSpec as P

HEAD_SIZE = 128
NPARAM = 688128


ADAPTER_SCALE = 2.0
NORM_EPS = 1e-05
LANCZOS_EPS = 1e-06
SCORE_CAP = 30.0
PRECISE = lax.Precision.HIGHEST


def contract_halved(left_side, right_side, left_dim, right_dim):
    return lax.dot_general(
        left_side,
        right_side,
        (((left_dim,), (right_dim,)), ((), ())),
        preferred_element_type=jnp.float32,
    )


def contract_entire(left_side, right_side, left_dim, right_dim):
    return lax.dot_general(
        left_side,
        right_side,
        (((left_dim,), (right_dim,)), ((), ())),
        precision=PRECISE,
        preferred_element_type=jnp.float32,
    )


def attend(query_matrix_rows, key_matrix_rows, value_matrix_rows):
    seq_count, length, query_cols = query_matrix_rows.shape
    kv_heads = key_matrix_rows.shape[2] // HEAD_SIZE
    groups = query_cols // HEAD_SIZE // kv_heads
    query_split = query_matrix_rows.reshape(seq_count, length, kv_heads, groups, HEAD_SIZE)
    key_split = key_matrix_rows.reshape(seq_count, length, kv_heads, HEAD_SIZE)
    value_split = value_matrix_rows.reshape(seq_count, length, kv_heads, HEAD_SIZE)
    scores = jnp.einsum("sqgjd,skgd->sgjqk", query_split, key_split, precision=PRECISE) / math.sqrt(
        HEAD_SIZE
    )
    scores = SCORE_CAP * jnp.tanh(scores / SCORE_CAP)
    causal = jnp.arange(length)[:, None] >= jnp.arange(length)[None, :]
    weights = jnp.where(causal, jnp.exp(scores), 0.0)
    probabilities = weights / jnp.sum(weights, axis=-1, keepdims=True)
    mixed_rows = jnp.einsum("sgjqk,skgd->sqgjd", probabilities, value_split, precision=PRECISE)
    return mixed_rows.reshape(seq_count, length, query_cols)


def rms_norm(resid_rows):
    return resid_rows * lax.rsqrt(
        jnp.mean(resid_rows * resid_rows, axis=-1, keepdims=True) + NORM_EPS
    )


def adapter_projection(halved_tokens, entire_tokens, weight_matrix, adapter_down, adapter_up):
    reduced_rank = contract_entire(entire_tokens, adapter_down, 1, 0)
    return (
        contract_halved(halved_tokens, weight_matrix, 1, 0)
        + ADAPTER_SCALE * contract_entire(reduced_rank, adapter_up, 1, 0),
        reduced_rank,
    )


def full_rows(rows_half):
    return lax.all_gather(rows_half, "tensor", axis=1, tiled=True)


def head_sum(terms, seq_count):
    return lax.psum_scatter(
        terms.reshape(seq_count, -1, terms.shape[1]), "tensor", scatter_dimension=1, tiled=True
    )


def pooled(normed, head_full, share):
    seq_count, part_length, width = normed.shape
    logits = contract_entire(normed.reshape(-1, width), head_full, 1, 0).reshape(
        seq_count, part_length, -1
    )
    partial_value = jnp.sum(logits * share[:, :, None], axis=1)
    gathered = lax.all_gather(partial_value[None], ("dp", "tensor"), axis=0, tiled=True)
    summed = jnp.sum(
        gathered.reshape(
            lax.axis_size("dp"), lax.axis_size("tensor"), seq_count, partial_value.shape[1]
        ),
        axis=1,
    )
    return summed.reshape(-1, partial_value.shape[1])


def lanczos_inner(first_set, second_set):
    return (
        sum((jnp.sum(part_one * part_two) for part_one, part_two in zip(first_set, second_set)))
        / NPARAM
    )


def local(
    hidden,
    query_weight,
    key_value_weight,
    output_weight,
    head,
    lens,
    partner,
    adapter_down_qkv,
    adapter_up_query,
    adapter_up_key_value,
    adapter_down_output,
    adapter_up_output,
    initial_down_qkv,
    initial_up_query,
    initial_up_key_value,
    initial_down_output,
    initial_up_output,
):
    seq_count, part_length, width = hidden.shape
    shards = lax.axis_size("tensor")
    tensor_rank = lax.axis_index("tensor")
    group_rank = lax.axis_index("dp")
    query_cols = query_weight.shape[1]
    kv_cols = key_value_weight.shape[2]
    halved_tokens = full_rows(hidden).reshape(-1, width)
    entire_tokens = halved_tokens.astype(jnp.float32)
    length = halved_tokens.shape[0] // seq_count
    down_every_factor = adapter_down_qkv.astype(jnp.float32)
    up_query_factor = adapter_up_query.astype(jnp.float32)
    up_key_value = adapter_up_key_value.astype(jnp.float32)
    down_output = adapter_down_output.astype(jnp.float32)
    up_output = adapter_up_output.astype(jnp.float32)
    head_full = head.astype(jnp.float32)
    query_matrix_rows, reduced_query = adapter_projection(
        halved_tokens, entire_tokens, query_weight, down_every_factor[0], up_query_factor
    )
    key_matrix_rows, reduced_key = adapter_projection(
        halved_tokens, entire_tokens, key_value_weight[0], down_every_factor[1], up_key_value[0]
    )
    value_matrix_rows, reduced_value = adapter_projection(
        halved_tokens, entire_tokens, key_value_weight[1], down_every_factor[2], up_key_value[1]
    )
    shaped = (
        query_matrix_rows.reshape(seq_count, length, query_cols),
        key_matrix_rows.reshape(seq_count, length, kv_cols),
        value_matrix_rows.reshape(seq_count, length, kv_cols),
    )
    context = attend(*shaped).reshape(-1, query_cols)
    context_low = contract_entire(context, down_output, 1, 0)
    out_terms = contract_halved(
        context.astype(jnp.bfloat16), output_weight, 1, 0
    ) + ADAPTER_SCALE * contract_entire(context_low, up_output, 1, 0)
    out_rows = head_sum(out_terms, seq_count)
    resid = hidden.astype(jnp.float32) + out_rows
    normed = rms_norm(resid)
    positions = tensor_rank * part_length + jnp.arange(part_length, dtype=jnp.int32)
    share = (positions[None, :] < lens[:, None]).astype(jnp.float32) / lens.astype(jnp.float32)[
        :, None
    ]
    rewards = pooled(normed, head_full, share)
    squashed = jax.nn.sigmoid(rewards - jnp.take(rewards, partner, axis=0))
    curvature = squashed * (1.0 - squashed) / (rewards.shape[0] // 2)
    own_start = group_rank * seq_count
    query_start = tensor_rank * query_cols
    kv_start = tensor_rank * kv_cols

    def product(vector):
        vec_a, vec_bq, vec_bkv, vec_ao, vec_bo = vector
        own_bq = lax.dynamic_slice_in_dim(vec_bq, query_start, query_cols, 1)
        own_bkv = lax.dynamic_slice_in_dim(vec_bkv, kv_start, kv_cols, 2)
        own_ao = lax.dynamic_slice_in_dim(vec_ao, query_start, query_cols, 0)
        tangent_query = ADAPTER_SCALE * (
            contract_entire(contract_entire(entire_tokens, vec_a[0], 1, 0), up_query_factor, 1, 0)
            + contract_entire(reduced_query, own_bq, 1, 0)
        )
        tangent_key = ADAPTER_SCALE * (
            contract_entire(contract_entire(entire_tokens, vec_a[1], 1, 0), up_key_value[0], 1, 0)
            + contract_entire(reduced_key, own_bkv[0], 1, 0)
        )
        tangent_value = ADAPTER_SCALE * (
            contract_entire(contract_entire(entire_tokens, vec_a[2], 1, 0), up_key_value[1], 1, 0)
            + contract_entire(reduced_value, own_bkv[1], 1, 0)
        )
        tangents = (
            tangent_query.reshape(seq_count, length, query_cols),
            tangent_key.reshape(seq_count, length, kv_cols),
            tangent_value.reshape(seq_count, length, kv_cols),
        )
        tangent_context = jax.jvp(attend, shaped, tangents)[1].reshape(-1, query_cols)
        tangent_terms = contract_halved(
            tangent_context.astype(jnp.bfloat16), output_weight, 1, 0
        ) + ADAPTER_SCALE * (
            contract_entire(contract_entire(tangent_context, down_output, 1, 0), up_output, 1, 0)
            + contract_entire(contract_entire(context, own_ao, 1, 0), up_output, 1, 0)
            + contract_entire(context_low, vec_bo, 1, 0)
        )
        tangent_rows = head_sum(tangent_terms, seq_count)
        tangent_normed = jax.jvp(rms_norm, (resid,), (tangent_rows,))[1]
        tangent_rewards = pooled(tangent_normed, head_full, share)
        pull_all = curvature * (tangent_rewards - jnp.take(tangent_rewards, partner, axis=0))
        pull_own = lax.dynamic_slice_in_dim(pull_all, own_start, seq_count, 0)
        cot_normed = contract_entire(
            (pull_own[:, None, :] * share[:, :, None]).reshape(-1, pull_own.shape[1]),
            head_full,
            1,
            1,
        ).reshape(resid.shape)
        cot_resid = jax.vjp(rms_norm, resid)[1](cot_normed)[0]
        cot_half = full_rows(cot_resid.astype(jnp.bfloat16)).reshape(-1, width)
        cot_full = cot_half.astype(jnp.float32)
        cot_low = contract_entire(cot_full, up_output, 1, 1)
        cot_context = contract_halved(
            cot_half, output_weight, 1, 1
        ) + ADAPTER_SCALE * contract_entire(cot_low, down_output, 1, 1)
        grad_ao = ADAPTER_SCALE * contract_entire(context, cot_low, 0, 0)
        cot_query, cot_key, cot_value = jax.vjp(attend, *shaped)[1](
            cot_context.reshape(seq_count, length, query_cols)
        )
        cot_query = cot_query.reshape(-1, query_cols)
        cot_key = cot_key.reshape(-1, kv_cols)
        cot_value = cot_value.reshape(-1, kv_cols)
        grad_bq = ADAPTER_SCALE * contract_entire(reduced_query, cot_query, 0, 0)
        grad_bkv = ADAPTER_SCALE * jnp.stack(
            [
                contract_entire(reduced_key, cot_key, 0, 0),
                contract_entire(reduced_value, cot_value, 0, 0),
            ]
        )
        factors = (
            contract_entire(cot_query, up_query_factor, 1, 1),
            contract_entire(cot_key, up_key_value[0], 1, 1),
            contract_entire(cot_value, up_key_value[1], 1, 1),
        )
        grad_a = ADAPTER_SCALE * jnp.stack(
            [contract_entire(entire_tokens, factor, 0, 0) for factor in factors]
        )
        grad_bo = ADAPTER_SCALE * contract_entire(context_low, cot_full, 0, 0)
        wide_bq = lax.dynamic_update_slice_in_dim(
            jnp.zeros((grad_bq.shape[0], query_cols * shards), jnp.float32), grad_bq, query_start, 1
        )
        wide_bkv = lax.dynamic_update_slice_in_dim(
            jnp.zeros((2, grad_bkv.shape[1], kv_cols * shards), jnp.float32), grad_bkv, kv_start, 2
        )
        wide_ao = lax.dynamic_update_slice_in_dim(
            jnp.zeros((query_cols * shards, grad_ao.shape[1]), jnp.float32), grad_ao, query_start, 0
        )
        return lax.psum((grad_a, wide_bq, wide_bkv, wide_ao, grad_bo), ("dp", "tensor"))

    start_set = (
        initial_down_qkv,
        initial_up_query,
        initial_up_key_value,
        initial_down_output,
        initial_up_output,
    )
    start_scale = lax.rsqrt(lanczos_inner(start_set, start_set) + LANCZOS_EPS)
    first_set = tuple((block_part * start_scale for block_part in start_set))
    image_one = product(first_set)
    alpha_one = lanczos_inner(image_one, first_set)
    resid_one = tuple(
        (image_part - alpha_one * base_part for image_part, base_part in zip(image_one, first_set))
    )
    beta_one = jnp.sqrt(lanczos_inner(resid_one, resid_one) + LANCZOS_EPS)
    second_set = tuple((block_part / beta_one for block_part in resid_one))
    image_two = tuple(
        (
            image_part - beta_one * base_part
            for image_part, base_part in zip(product(second_set), first_set)
        )
    )
    alpha_two = lanczos_inner(image_two, second_set)
    resid_two = tuple(
        (image_part - alpha_two * base_part for image_part, base_part in zip(image_two, second_set))
    )
    beta_two = jnp.sqrt(lanczos_inner(resid_two, resid_two) + LANCZOS_EPS)
    return tuple((block_part / beta_two for block_part in resid_two))


def solution(mesh):
    in_specs = (
        P("dp", "tensor", None),
        P(None, "tensor"),
        P(None, None, "tensor"),
        P("tensor", None),
        P(),
        P("dp"),
        P(),
        P(),
        P(None, "tensor"),
        P(None, None, "tensor"),
        P("tensor", None),
        P(),
        P(),
        P(),
        P(),
        P(),
        P(),
    )
    out_specs = (P(), P(), P(), P(), P())
    return jax.shard_map(local, mesh=mesh, in_specs=in_specs, out_specs=out_specs, check_vma=False)
```

profile of v0, /device:TPU:1, one launch (start us, length us, event | category | flops | bytes accessed | tf_op | source)
XLA Modules:
  0.0 1068.7 jit_solution(1258972299361210290)
XLA Ops:
  8.1 1.7 multiply_reduce_fusion.22
  9.8 2.4 multiply_reduce_fusion.4
  19.6 47.8 %all-gather.7.cloned.1.call-done = bf16[1,128,8192]{2,1,0:T(8,128)(2,1)} async-done(((bf16[1,16,8192]{2,1,0:T(8,128)(2,1)}), bf16[1,128,8192]{2,1,0:T(8,128)(2,1)}) %all-gather.7.cloned.1.call-update) | async-done | bytes 2097168 | tf_op jit(solution)/shard_map/all_gather | solution.py:72
  67.4 3.6 fusion.36
  73.3 1.7 fusion.34
  76.0 4.8 fusion.42
  84.1 1.7 fusion.38
  93.4 1.8 fusion.280
  95.1 1.9 convolution_add_fusion.3
  97.0 5.4 fusion.5
  102.5 4.8 fusion.190
  107.3 4.1 fusion.7
  113.5 71.1 %reduce-scatter.6.cloned.1.call-done = f32[1,16,8192]{2,1,0:T(8,128)} async-done(((f32[1,128,8192]{2,1,0:T(8,128)}), f32[1,16,8192]{2,1,0:T(8,128)}) %reduce-scatter.6.cloned.1.call-update) | async-done | bytes 524304 | tf_op jit(solution)/shard_map/reduce_scatter | solution.py:76
  184.6 87.7 %reduce-scatter.4.cloned.1.call-done = f32[1,16,8192]{2,1,0:T(8,128)} async-done(((f32[1,128,8192]{2,1,0:T(8,128)}), f32[1,16,8192]{2,1,0:T(8,128)}) %reduce-scatter.4.cloned.1.call-update) | async-done | bytes 524304 | tf_op jit(solution)/shard_map/reduce_scatter | solution.py:76
  274.3 2.0 fusion.105
  277.2 2.2 fusion.106
  280.2 65.8 %all-reduce.3 = (f32[640]{0:T(1024)}, f32[640]{0:T(1024)}) all-reduce(f32[640]{0:T(1024)S(1)} %dynamic-update-slice.1, f32[640]{0:T(1024)S(1)} %dynamic-update-slice), channel_id=3, replica_groups=mesh['dp'=16,'tensor'=8] {'dp','tensor'}, use_global_device_ids=true, to_apply=%add.1 | all-reduce | flops 1280 | bytes 10240
  358.5 50.3 %all-gather.9.cloned.1.call-done = bf16[1,128,8192]{2,1,0:T(8,128)(2,1)} async-done(((bf16[1,16,8192]{2,1,0:T(8,128)(2,1)}), bf16[1,128,8192]{2,1,0:T(8,128)(2,1)}) %all-gather.9.cloned.1.call-update) | async-done | bytes 2097168 | tf_op jit(solution)/shard_map/all_gather | solution.py:72
  408.8 7.1 fusion.16
  418.2 1.8 copy.85
  433.2 1.7 convolution_multiply_fusion.2
  435.2 150.8 %all-reduce.11.cloned.1.call-done = (f32[3,8192,16]{1,2,0:T(8,128)}, f32[16,4096]{1,0:T(8,128)}, f32[2,16,1024]{2,1,0:T(8,128)}, f32[4096,16]{0,1:T(8,128)}, f32[16,8192]{1,0:T(8,128)}) async-done(((f32[3,8192,16]{1,2,0:T(8,128)}, f32[16,4096]{1,0:T(8,128)}, f32[2,16,1024]{2,1,0:T(8,128)}, f32[4096,16]{0,1:T(8,128)}, f32[16,8192]{1,0:T(8,128)}), (f32[3,8192,16]{1,2,0:T(8,128)}, f32[16,4096]{1,0:T(8,128)}, ...) | async-done | bytes 2752528 | tf_op jit(solution)/shard_map/psum | solution.py:251
  586.0 1.9 multiply_reduce_fusion.10
  592.8 2.4 multiply_reduce_fusion.3
  598.5 1.9 multiply_reduce_fusion.9
  605.4 2.4 multiply_reduce_fusion.2
  615.9 1.7 fusion.25
  618.0 1.7 fusion.27
  621.8 1.7 fusion.29
  627.4 2.0 fusion.285
  629.4 1.9 convolution_add_fusion.1
  631.3 5.4 fusion.2
  636.8 82.5 %reduce-scatter.8.cloned.1.call-done = f32[1,16,8192]{2,1,0:T(8,128)} async-done(((f32[1,128,8192]{2,1,0:T(8,128)}), f32[1,16,8192]{2,1,0:T(8,128)}) %reduce-scatter.8.cloned.1.call-update) | async-done | bytes 524304 | tf_op jit(solution)/shard_map/reduce_scatter | solution.py:76
  721.1 2.2 fusion.107
  725.3 65.3 %all-reduce.2 = f32[640]{0:T(1024)} all-reduce(f32[640]{0:T(1024)} %dynamic-update-slice.2), channel_id=4, replica_groups=mesh['dp'=16,'tensor'=8] {'dp','tensor'}, use_global_device_ids=true, to_apply=%add.2 | all-reduce | flops 640 | bytes 5120
  793.6 2.0 gather_fusion.2
  800.6 50.3 %all-gather.11.cloned.1.call-done = bf16[1,128,8192]{2,1,0:T(8,128)(2,1)} async-done(((bf16[1,16,8192]{2,1,0:T(8,128)(2,1)}), bf16[1,128,8192]{2,1,0:T(8,128)(2,1)}) %all-gather.11.cloned.1.call-update) | async-done | bytes 2097168 | tf_op jit(solution)/shard_map/all_gather | solution.py:72
  850.9 7.1 fusion.11
  860.3 1.8 copy.89
  876.5 1.7 convolution_multiply_fusion.1
  878.2 151.1 %all-reduce.9.cloned.1.call-done = (f32[3,8192,16]{1,2,0:T(8,128)}, f32[16,4096]{1,0:T(8,128)}, f32[2,16,1024]{2,1,0:T(8,128)}, f32[4096,16]{0,1:T(8,128)}, f32[16,8192]{1,0:T(8,128)}) async-done(((f32[3,8192,16]{1,2,0:T(8,128)}, f32[16,4096]{1,0:T(8,128)}, f32[2,16,1024]{2,1,0:T(8,128)}, f32[4096,16]{0,1:T(8,128)}, f32[16,8192]{1,0:T(8,128)}), (f32[3,8192,16]{1,2,0:T(8,128)}, f32[16,4096]{1,0:T(8,128)}, ...) | async-done | bytes 2752528 | tf_op jit(solution)/shard_map/psum | solution.py:251
  1029.3 2.7 multiply_reduce_fusion.8
  1035.3 1.7 multiply_reduce_fusion.16
  1037.0 2.5 multiply_reduce_fusion.1
  1042.7 2.4 multiply_reduce_fusion.13
  1045.1 2.3 multiply_reduce_fusion.23
  1047.4 2.3 multiply_reduce_fusion.14
  1049.8 3.6 multiply_reduce_fusion
  (372 shorter events, 108.7 us)
Async XLA Ops:
  7.2 86.2 %copy-start = (bf16[16,8192]{1,0:T(8,128)(2,1)S(1)}, bf16[16,8192]{1,0:T(8,128)(2,1)}, u32[]{:S(2)}) copy-start(bf16[16,8192]{1,0:T(8,128)(2,1)} %param.30) | copy-start | bytes 786436
  7.2 10.4 copy-start.19
  7.2 5.6 copy-start.17
  7.2 6.3 copy-start.9
  7.2 60.2 %all-gather.7.cloned.1.call-start = ((), (), s32[]{:S(2)}) async-start(), calls=%async_computation.3 | async-start | bytes 2359296 | tf_op jit(solution)/shard_map/all_gather | solution.py:72
  8.0 10.4 copy-start.2
  8.0 176.6 %reduce-scatter.6.cloned.1.call-start = ((), (), s32[]{:S(2)}) async-start(), calls=%async_computation.5 | async-start | bytes 4718592 | tf_op jit(solution)/shard_map/reduce_scatter | solution.py:76
  8.0 81.2 %copy-start.53 = (pred[128,128]{0,1:T(8,128)(4,1)}, pred[128,128]{0,1:T(8,128)(4,1)S(1)}, u32[]{:S(2)}) copy-start(pred[128,128]{0,1:T(8,128)(4,1)S(1)} %iota_compare_fusion) | copy-start | bytes 49156
  19.6 51.5 %copy-start.83 = (bf16[2,16,128]{2,1,0:T(8,128)(2,1)S(1)}, bf16[2,16,128]{2,1,0:T(8,128)(2,1)}, u32[]{:S(2)}) copy-start(bf16[2,16,128]{2,1,0:T(8,128)(2,1)} %param.28) | copy-start | bytes 24580
  67.4 5.9 copy-start.34
  73.0 8.2 copy-start.69
  76.0 7.1 copy-start.65
  76.0 5.8 copy-start.99
  83.1 6.2 copy-start.21
  83.1 6.2 copy-start.92
  83.6 8.4 slice-start
  89.3 13.3 %copy-start.25 = (f32[128,4,128]{2,0,1:T(8,128)}, f32[128,4,128]{2,0,1:T(8,128)S(1)}, u32[]{:S(2)}) copy-start(f32[128,4,128]{2,0,1:T(8,128)S(1)} %fusion.153) | copy-start | bytes 786436
  90.6 16.7 %copy-start.77 = (f32[128,16]{0,1:T(8,128)}, f32[128,16]{0,1:T(8,128)S(1)}, u32[]{:S(2)}) copy-start(f32[128,16]{0,1:T(8,128)S(1)} %fusion.277) | copy-start | bytes 24580
  102.5 169.8 %reduce-scatter.4.cloned.1.call-start = ((), (), s32[]{:S(2)}) async-start(), calls=%async_computation.4 | async-start | bytes 4718592 | tf_op jit(solution)/shard_map/reduce_scatter | solution.py:76
  111.5 297.4 %all-gather.9.cloned.1.call-start = ((), (), s32[]{:S(2)}) async-start(), calls=%async_computation.6 | async-start | bytes 2359296 | tf_op jit(solution)/shard_map/all_gather | solution.py:72
  112.9 233.2 %copy-start.91 = (f32[16]{0:T(128)}, f32[16]{0:T(128)S(1)}, u32[]{:S(2)}) copy-start(f32[16]{0:T(128)S(1)} %compare_select_fusion.1) | copy-start | bytes 196
  274.3 71.7 %copy-start.97 = (f32[16]{0:T(128)}, f32[16]{0:T(128)S(1)}, u32[]{:S(2)}) copy-start(f32[16]{0:T(128)S(1)} %get-tuple-element.33) | copy-start | bytes 196
  358.5 227.5 %all-reduce.11.cloned.1.call-start = ((), (), s32[]{:S(2)}) async-start(), calls=%async_computation.10 | async-start | bytes 5505024 | tf_op jit(solution)/shard_map/psum | solution.py:251
  408.8 7.1 copy-start.12
  434.9 284.3 %reduce-scatter.8.cloned.1.call-start = ((), (), s32[]{:S(2)}) async-start(), calls=%async_computation.7 | async-start | bytes 4718592 | tf_op jit(solution)/shard_map/reduce_scatter | solution.py:76
  586.0 6.9 copy-start.3
  598.5 6.9 copy-start.4
  612.4 18.9 %copy-start.15 = (f32[16,8192]{1,0:T(8,128)}, f32[16,8192]{1,0:T(8,128)S(1)}, u32[]{:S(2)}) copy-start(f32[16,8192]{1,0:T(8,128)S(1)} %broadcast_divide_fusion.3) | copy-start | bytes 1572868
  613.6 13.1 %copy-start.40 = (f32[4096,16]{0,1:T(8,128)}, f32[4096,16]{0,1:T(8,128)S(1)}, u32[]{:S(2)}) copy-start(f32[4096,16]{0,1:T(8,128)S(1)} %broadcast_divide_fusion.6) | copy-start | bytes 786436
  614.8 5.9 copy-start.38
  614.9 10.5 slice-start.2
  615.9 5.9 copy-start.7
  615.9 7.9 copy-start.42
  618.0 7.4 slice-start.3
  636.7 214.1 %all-gather.11.cloned.1.call-start = ((), (), s32[]{:S(2)}) async-start(), calls=%async_computation.8 | async-start | bytes 2359296 | tf_op jit(solution)/shard_map/all_gather | solution.py:72
  800.5 228.8 %all-reduce.9.cloned.1.call-start = ((), (), s32[]{:S(2)}) async-start(), calls=%async_computation.9 | async-start | bytes 5505024 | tf_op jit(solution)/shard_map/psum | solution.py:251
  850.9 7.1 copy-start.10
  859.3 5.7 copy-start.32
  876.5 152.8 %copy-start.16 = (f32[16,8192]{1,0:T(8,128)S(1)}, f32[16,8192]{1,0:T(8,128)}, u32[]{:S(2)}) copy-start(f32[16,8192]{1,0:T(8,128)} %copy-done.15) | copy-start | bytes 1572868
  878.2 153.8 %copy-start.18 = (f32[4096,16]{0,1:T(8,128)S(1)}, f32[4096,16]{0,1:T(8,128)}, u32[]{:S(2)}) copy-start(f32[4096,16]{0,1:T(8,128)} %param.34) | copy-start | bytes 786436
  878.2 157.1 %copy-start.20 = (f32[16,4096]{1,0:T(8,128)S(1)}, f32[16,4096]{1,0:T(8,128)}, u32[]{:S(2)}) copy-start(f32[16,4096]{1,0:T(8,128)} %param.32) | copy-start | bytes 786436
  878.2 158.8 %copy-start.6 = (f32[3,8192,16]{1,2,0:T(8,128)S(1)}, f32[3,8192,16]{1,2,0:T(8,128)}, u32[]{:S(2)}) copy-start(f32[3,8192,16]{1,2,0:T(8,128)} %param.31) | copy-start | bytes 4718596
  1029.3 7.7 copy-start.8
  1037.0 5.7 copy-start.41
  1037.0 10.4 copy-start.39
  1042.7 7.1 copy-start.35
  1053.4 6.1 copy-start.49
  1053.4 6.9 copy-start.36
  (65 other events, 191.0 us)
Sparse Core Ops, SparseCore 0:
  10.4 56.9 all-gather.6
  102.6 81.9 reduce-scatter.5
  188.9 83.3 reduce-scatter.3
  358.6 50.1 all-gather.8
  435.1 150.8 all-reduce.10
  636.9 82.3 reduce-scatter.7
  800.7 50.1 all-gather.10
  878.3 150.9 all-reduce.8
where the time goes:
time: 1080 us; the launch traced here: 1070 us
  waiting for transfers between devices  692 us (64%)
  blocking collectives  131 us (12%)
  matrix products  112 us (10%)
  other arithmetic  76.9 us (7%)
  between operations  32.9 us (3%)
  local copies, waits for them, and re-layouts  22.5 us (2%)
    psum x2, waiting for transfers between devices, product(): lax.psum((grad_a, wide_bq, wide_bkv, wide_ao, grad_bo), ('dp', 'tensor'))  302 us
    reduce_scatter x3, waiting for transfers between devices, head_sum(): lax.psum_scatter(terms.reshape(seq_count, -1, terms.shape[1]), 'tensor',...  241 us
    all_gather x3, waiting for transfers between devices, full_rows(): return lax.all_gather(rows_half, 'tensor', axis=1, tiled=True)  148 us
    unnamed x2, blocking collectives  131 us
    dot_general x67, matrix products, contract_entire(): lax.dot_general(left_side, right_side, (((left_dim,), (right_dim,)), ((),...  71.7 us
    reduce_sum x25, other arithmetic, lanczos_inner(): jnp.sum(part_one * part_two)  46.4 us
    dot_general x8, matrix products, contract_halved(): lax.dot_general(left_side, right_side, (((left_dim,), (right_dim,)), ((),...  27.9 us
  transfers between devices with their start and end apart: 8, of which 8 were waited for; matrix products, arithmetic and copies ran while one was open for 2% of the time, Pallas kernels for 0%

commit v1 on v0

v1 whole, which is shorter than its diff:
```python
import math

import jax
import jax.numpy as jnp
from jax import lax
from jax.sharding import PartitionSpec as P

HEAD_SIZE = 128
NPARAM = 688128
ADAPTER_SCALE = 2.0
NORM_EPS = 1e-05
LANCZOS_EPS = 1e-06
SCORE_CAP = 30.0
PRECISE = lax.Precision.HIGHEST
OBJ = 5
PIECES = 11
PIECE_ROWS = 56
LANES = 512


def dot_halved(left_side, right_side, left_dim, right_dim):
    return lax.dot_general(
        left_side,
        right_side,
        (((left_dim,), (right_dim,)), ((), ())),
        preferred_element_type=jnp.float32,
    )


def dot_entire(left_side, right_side, left_dim, right_dim):
    return lax.dot_general(
        left_side,
        right_side,
        (((left_dim,), (right_dim,)), ((), ())),
        precision=PRECISE,
        preferred_element_type=jnp.float32,
    )


def two_halves(entire):
    upper = lax.reduce_precision(entire, 8, 7)
    return upper.astype(jnp.bfloat16), (entire - upper).astype(jnp.bfloat16)


def three_halves(entire):
    upper = lax.reduce_precision(entire, 8, 7)
    rest = entire - upper
    middle = lax.reduce_precision(rest, 8, 7)
    return (
        upper.astype(jnp.bfloat16),
        middle.astype(jnp.bfloat16),
        (rest - middle).astype(jnp.bfloat16),
    )


def gather_by_exchange(block, axis):
    count = lax.axis_size(axis)
    copies = jnp.broadcast_to(block[None], (count,) + block.shape)
    return lax.all_to_all(copies, axis, 0, 0)


def local(
    hidden,
    query_weight,
    key_value_weight,
    output_weight,
    head,
    lens,
    partner,
    adapter_down_qkv,
    adapter_up_query,
    adapter_up_key_value,
    adapter_down_output,
    adapter_up_output,
    initial_down_qkv,
    initial_up_query,
    initial_up_key_value,
    initial_down_output,
    initial_up_output,
):
    _, part_length, width = hidden.shape
    shards = lax.axis_size("tensor")
    groups = lax.axis_size("dp")
    tensor_rank = lax.axis_index("tensor")
    group_rank = lax.axis_index("dp")
    query_cols = query_weight.shape[1]
    heads = query_cols // HEAD_SIZE
    length = part_length * shards
    root = 1.0 / math.sqrt(HEAD_SIZE)

    down_qkv = jnp.transpose(adapter_down_qkv, (0, 2, 1))
    down_output = adapter_down_output.T.astype(jnp.float32)
    up_query = adapter_up_query.astype(jnp.float32)
    up_key_value = adapter_up_key_value.astype(jnp.float32)
    head_rows = head.T

    tokens = gather_by_exchange(hidden[0], "tensor").reshape(length, width)

    low = dot_halved(tokens, down_qkv.reshape(48, width), 1, 1)
    low_q, low_k, low_v = low[:, :16], low[:, 16:32], low[:, 32:]
    query = dot_halved(tokens, query_weight, 1, 0) + ADAPTER_SCALE * dot_entire(
        low_q, up_query, 1, 0
    )
    keys = dot_halved(tokens, key_value_weight[0], 1, 0) + ADAPTER_SCALE * dot_entire(
        low_k, up_key_value[0], 1, 0
    )
    values = dot_halved(tokens, key_value_weight[1], 1, 0) + ADAPTER_SCALE * dot_entire(
        low_v, up_key_value[1], 1, 0
    )
    query_split = query.reshape(length, heads, HEAD_SIZE)
    capped = jnp.tanh(
        jnp.einsum("qjd,kd->jqk", query_split, keys, precision=PRECISE) * (root / SCORE_CAP)
    )
    causal = jnp.arange(length)[:, None] >= jnp.arange(length)[None, :]
    weights = jnp.where(causal, jnp.exp(SCORE_CAP * capped), 0.0)
    probabilities = weights / jnp.sum(weights, axis=-1, keepdims=True)
    context_split = jnp.einsum("jqk,kd->qjd", probabilities, values, precision=PRECISE)
    context = context_split.reshape(length, query_cols)
    context_low = dot_entire(down_output, context, 1, 1)
    low_upper, low_lower = two_halves(ADAPTER_SCALE * context_low)
    out_terms = dot_halved(context.astype(jnp.bfloat16), output_weight, 1, 0) + dot_halved(
        jnp.concatenate([low_upper, low_lower], 0),
        jnp.concatenate([adapter_up_output, adapter_up_output], 0),
        0,
        0,
    )
    out_pieces = lax.all_to_all(
        out_terms.astype(jnp.bfloat16).reshape(shards, part_length, width), "tensor", 0, 0
    )
    resid_own = hidden[0].astype(jnp.float32) + jnp.sum(out_pieces.astype(jnp.float32), 0)
    resid = gather_by_exchange(resid_own.astype(jnp.bfloat16), "tensor").reshape(length, width)

    resid_entire = resid.astype(jnp.float32)
    inverse = lax.rsqrt(jnp.mean(resid_entire * resid_entire, axis=1, keepdims=True) + NORM_EPS)
    length_own = lens[0]
    share = jnp.where(
        jnp.arange(length)[:, None] < length_own, 1.0 / length_own.astype(jnp.float32), 0.0
    )
    stacked = jnp.concatenate([resid, head_rows], 0)
    logits = inverse * dot_halved(resid, head_rows, 1, 1)
    rewards = jnp.sum(logits * share, 0)
    through = dot_halved(stacked, output_weight, 1, 1)
    through_low = dot_halved(stacked, adapter_up_output, 1, 1)
    through = through + ADAPTER_SCALE * dot_entire(through_low, down_output, 1, 0)
    lead = share * inverse
    pulled = (lead * inverse * logits / width).T
    cot_context = (
        lead[None] * through[length:][:, None, :] - pulled[:, :, None] * through[None, :length]
    )
    cot_low = (
        lead[None] * through_low[length:][:, None, :]
        - pulled[:, :, None] * through_low[None, :length]
    )
    cot_split = cot_context.reshape(OBJ, length, heads, HEAD_SIZE)
    cot_prob = jnp.einsum("oqjd,kd->ojqk", cot_split, values, precision=PRECISE)
    inner = jnp.einsum("oqjd,qjd->ojq", cot_split, context_split)
    cot_score = (
        probabilities[None]
        * (cot_prob - inner[..., None])
        * ((1.0 - capped * capped) * root)[None]
    )
    cot_query = jnp.einsum("ojqk,kd->oqjd", cot_score, keys, precision=PRECISE).reshape(
        OBJ, length, query_cols
    )
    cot_keys = jnp.einsum("ojqk,qjd->okd", cot_score, query_split, precision=PRECISE)
    cot_values = jnp.einsum("jqk,oqjd->okd", probabilities, cot_split, precision=PRECISE)

    factor_q = jnp.einsum("rc,otc->rot", up_query, cot_query, precision=PRECISE)
    factor_k = jnp.einsum("rc,otc->rot", up_key_value[0], cot_keys, precision=PRECISE)
    factor_v = jnp.einsum("rc,otc->rot", up_key_value[1], cot_values, precision=PRECISE)
    factors = jnp.concatenate(
        [factor_q, factor_k, factor_v, context_low[:, None, :]], 1
    ) * ADAPTER_SCALE
    factors = jnp.sum(
        lax.all_to_all(factors.reshape(shards, 2, 3 * OBJ + 1, length), "tensor", 0, 0), 0
    )
    context_lead = factors[:, 3 * OBJ] * lead.T
    rows_a = factors[:, : 3 * OBJ].reshape(2 * 3 * OBJ, length)
    rows_bo = (factors[:, 3 * OBJ][:, None, :] * pulled[None]).reshape(2 * OBJ, length)

    def split_dot(rows, right_side):
        upper, lower = two_halves(rows)
        both = dot_halved(jnp.concatenate([upper, lower], 0), right_side, 1, 0)
        return both[: rows.shape[0]] + both[rows.shape[0] :]

    jac_a = split_dot(rows_a, tokens).reshape(2, 3, OBJ, groups, LANES)
    jac_bo = (
        jnp.sum(context_lead, 1)[:, None, None] * head_rows.astype(jnp.float32)[None]
        - split_dot(rows_bo, resid).reshape(2, OBJ, width)
    ).reshape(2, 1, OBJ, groups, LANES)
    wide = jnp.concatenate([jac_a, jac_bo], 1).reshape(8 * OBJ, groups, LANES)
    wide = jnp.transpose(wide, (1, 0, 2)).astype(jnp.bfloat16)
    jac_bq = ADAPTER_SCALE * jnp.einsum("tr,otc->roc", low_q, cot_query, precision=PRECISE)
    jac_bk = ADAPTER_SCALE * jnp.einsum("tr,otc->roc", low_k, cot_keys, precision=PRECISE)
    jac_bv = ADAPTER_SCALE * jnp.einsum("tr,otc->roc", low_v, cot_values, precision=PRECISE)
    jac_ao = ADAPTER_SCALE * jnp.einsum("otr,tc->roc", cot_low, context, precision=PRECISE)
    spare = jnp.zeros((16, OBJ, LANES - 2 * HEAD_SIZE), jnp.float32)
    narrow = jnp.concatenate(
        [jac_bq, jac_ao, jnp.concatenate([jac_bk, jac_bv, spare], 2)], 1
    ).astype(jnp.bfloat16)
    payload = jnp.concatenate(
        [wide, narrow, jnp.zeros((16, PIECE_ROWS - PIECES * OBJ, LANES), jnp.bfloat16)], 1
    )
    spread = lax.all_to_all(payload, "dp", 0, 0)
    jac = (
        spread[:, : PIECES * OBJ]
        .reshape(groups, PIECES, OBJ, LANES)
        .transpose(0, 2, 1, 3)
        .reshape(groups * OBJ, PIECES * LANES)
    )

    own_a = lax.dynamic_slice(
        jnp.transpose(initial_down_qkv, (0, 2, 1)),
        (0, 2 * tensor_rank, group_rank * LANES),
        (3, 2, LANES),
    )
    own_bo = lax.dynamic_slice(
        initial_up_output, (2 * tensor_rank, group_rank * LANES), (2, LANES)
    )
    own_bq = lax.dynamic_slice(
        initial_up_query, (group_rank, tensor_rank * query_cols), (1, query_cols)
    )
    own_ao = lax.dynamic_slice(
        initial_down_output.T, (group_rank, tensor_rank * query_cols), (1, query_cols)
    )
    own_bkv = lax.dynamic_slice(
        initial_up_key_value, (0, group_rank, tensor_rank * HEAD_SIZE), (2, 1, HEAD_SIZE)
    )
    own_start = jnp.concatenate(
        [
            jnp.concatenate([own_a.transpose(1, 0, 2), own_bo[:, None]], 1).reshape(8, LANES),
            own_bq,
            own_ao,
            jnp.concatenate(
                [own_bkv.reshape(1, 2 * HEAD_SIZE), jnp.zeros((1, LANES - 2 * HEAD_SIZE))], 1
            ),
        ],
        0,
    ).reshape(1, PIECES * LANES)
    start_rows = jnp.concatenate(three_halves(own_start), 0)
    rows = groups * OBJ
    gram = dot_halved(jac, jac, 1, 1)
    along = jnp.sum(dot_halved(jac, start_rows, 1, 1), 1, keepdims=True)
    start_square = jnp.sum(own_start * own_start)
    own_rewards = jnp.where(
        (jnp.arange(groups)[:, None] == group_rank) & (tensor_rank == 0), rewards[None], 0.0
    ).reshape(rows, 1)
    message = jnp.concatenate(
        [
            gram,
            along,
            own_rewards,
            jnp.full((rows, 1), start_square),
            jnp.zeros((rows, 128 - rows - 3), jnp.float32),
        ],
        1,
    )
    message = jnp.sum(gather_by_exchange(message, "dp"), 0)
    message = jnp.sum(gather_by_exchange(message, "tensor"), 0)
    gram = message[:, :rows]
    along = message[:, rows]
    all_rewards = message[:, rows + 1].reshape(groups, OBJ)
    start_square = message[0, rows + 2] / NPARAM

    def against(per_row):
        shaped = per_row.reshape(groups, OBJ)
        return shaped - jnp.take(shaped, partner, axis=0)

    def gram_times(vector):
        return jnp.sum(gram * vector[None, :], 1)

    squashed = jax.nn.sigmoid(against(all_rewards))
    curvature = squashed * (1.0 - squashed) / (groups // 2)
    start_scale = lax.rsqrt(start_square + LANCZOS_EPS)
    first_square = start_square * start_scale * start_scale
    along_one = along * start_scale
    pull_one = (curvature * against(along_one)).reshape(rows)
    alpha_one = jnp.sum(pull_one * along_one) / NPARAM
    gram_pull = gram_times(pull_one)
    beta_one = jnp.sqrt(
        jnp.sum(pull_one * gram_pull) / NPARAM
        - alpha_one * alpha_one * (2.0 - first_square)
        + LANCZOS_EPS
    )
    along_two = (gram_pull - alpha_one * along_one) / beta_one
    pull_two = (curvature * against(along_two)).reshape(rows)
    first_second = alpha_one * (1.0 - first_square) / beta_one
    alpha_two = jnp.sum(pull_two * along_two) / NPARAM - beta_one * first_second
    mixed = pull_two - (alpha_two / beta_one) * pull_one
    first_part = alpha_two * alpha_one / beta_one - beta_one
    beta_two = jnp.sqrt(
        jnp.sum(mixed * gram_times(mixed)) / NPARAM
        + 2.0 * first_part * jnp.sum(mixed * along_one) / NPARAM
        + first_part * first_part * first_square
        + LANCZOS_EPS
    )
    mixed = mixed / beta_two
    start_part = first_part * start_scale / beta_two
    own_result = jnp.sum(
        dot_halved(jnp.stack(three_halves(mixed), 0), jac, 1, 0), 0
    ).astype(jnp.bfloat16)
    own_result = own_result.reshape(PIECES * LANES // 128, 128)[:42]
    own_result = jnp.concatenate([own_result, jnp.zeros((6, 128), jnp.bfloat16)], 0)
    every = lax.all_to_all(
        jnp.broadcast_to(own_result[None], (groups * shards,) + own_result.shape),
        ("dp", "tensor"),
        0,
        0,
    ).reshape(groups, shards, 48 * 128)
    wide = every[:, :, : 8 * LANES].reshape(groups, shards, 2, 4, LANES)
    wide = wide.transpose(3, 1, 2, 0, 4).reshape(4, 16, width).astype(jnp.float32)
    narrow = every[:, :, 8 * LANES : 10 * LANES].reshape(groups, shards, 2, LANES)
    narrow = narrow.transpose(2, 0, 1, 3).reshape(2, 16, shards * LANES).astype(jnp.float32)
    small = every[:, :, 10 * LANES : 10 * LANES + 256].reshape(groups, shards, 2, HEAD_SIZE)
    small = small.transpose(2, 0, 1, 3).reshape(2, 16, shards * HEAD_SIZE).astype(jnp.float32)
    return (
        jnp.transpose(wide[:3], (0, 2, 1)) + start_part * initial_down_qkv,
        narrow[0] + start_part * initial_up_query,
        small + start_part * initial_up_key_value,
        narrow[1].T + start_part * initial_down_output,
        wide[3] + start_part * initial_up_output,
    )


def solution(mesh):
    in_specs = (
        P("dp", "tensor", None),
        P(None, "tensor"),
        P(None, None, "tensor"),
        P("tensor", None),
        P(),
        P("dp"),
        P(),
        P(),
        P(None, "tensor"),
        P(None, None, "tensor"),
        P("tensor", None),
        P(),
        P(),
        P(),
        P(),
        P(),
        P(),
    )
    out_specs = (P(), P(), P(), P(), P())
    return jax.shard_map(local, mesh=mesh, in_specs=in_specs, out_specs=out_specs, check_vma=False)
```

time: 1080 us -> 288 us (0.27)
  waiting for transfers between devices: 692 us -> 134 us
  blocking collectives: 131 us -> 0 us
  matrix products: 112 us -> 39.5 us
  other arithmetic: 76.9 us -> 24 us
  starting transfers between devices: 0.5 us -> 44 us
  between operations: 32.9 us -> 7.84 us
  local copies, waits for them, and re-layouts: 22.5 us -> 37.3 us
    psum x2 -> x0, waiting for transfers between devices: 302 us -> none  [product(): lax.psum((grad_a, wide_bq, wide_bkv, wide_ao, grad_bo), ('dp', 'tensor'))]
    reduce_scatter x3 -> x0, waiting for transfers between devices: 241 us -> none  [head_sum(): lax.psum_scatter(terms.reshape(seq_count, -1, terms.shape[1]), 'tensor',...]
    all_gather x3 -> x0, waiting for transfers between devices: 148 us -> none  [full_rows(): return lax.all_gather(rows_half, 'tensor', axis=1, tiled=True)]
    all_to_all x0 -> x8, waiting for transfers between devices: none -> 134 us  [the longest x4 64.1 us: gather_by_exchange(): return lax.all_to_all(copies, axis, 0, 0)]
    unnamed x2 -> x0, blocking collectives: 131 us -> none
    dot_general x93 -> x31, matrix products: 112 us -> 39 us  [the longest x14 25.4 us: dot_halved(): lax.dot_general(left_side, right_side, (((left_dim,), (right_dim,)), ((),...]
    reduce_sum x30 -> x12, other arithmetic: 52.3 us -> 7.1 us  [the longest x1 2.12 us: local(): jnp.mean(resid_entire * resid_entire, axis=1, keepdims=True) + NORM_EPS]
    all_to_all x0 -> x8, starting transfers between devices: none -> 44 us  [the longest x4 21.4 us: gather_by_exchange(): return lax.all_to_all(copies, axis, 0, 0)]
  transfers between devices with their start and end apart: 8 -> 8, of which waited for: 8 -> 8; matrix products, arithmetic and copies ran while one was open for 2% -> 3% of each run, Pallas kernels for 0% -> 0%
where the time goes in v1:
time: 288 us; the launch traced here: 286 us
  waiting for transfers between devices  134 us (47%)
  starting transfers between devices  44 us (15%)
  matrix products  39.5 us (14%)
  local copies, waits for them, and re-layouts  37.3 us (13%)
  other arithmetic  24 us (8%)
  between operations  7.84 us (3%)
    all_to_all x4, waiting for transfers between devices, gather_by_exchange(): return lax.all_to_all(copies, axis, 0, 0)  64.1 us
    all_to_all x1, waiting for transfers between devices, local(): lax.all_to_all(out_terms.astype(jnp.bfloat16).reshape(shards, part_length...  25.6 us
    dot_general x14, matrix products, dot_halved(): lax.dot_general(left_side, right_side, (((left_dim,), (right_dim,)), ((),...  25.4 us
    all_to_all x1, waiting for transfers between devices, local(): lax.all_to_all(jnp.broadcast_to(own_result[None], (groups * shards,) + ow...  23.3 us
    all_to_all x4, starting transfers between devices, gather_by_exchange(): return lax.all_to_all(copies, axis, 0, 0)  21.4 us
    all_to_all x1, waiting for transfers between devices, local(): spread = lax.all_to_all(payload, 'dp', 0, 0)  14.2 us
    all_to_all x1, waiting for transfers between devices, local(): lax.all_to_all(factors.reshape(shards, 2, 3 * OBJ + 1, length), 'tensor',...  6.64 us
    all_to_all x1, starting transfers between devices, local(): spread = lax.all_to_all(payload, 'dp', 0, 0)  6.35 us
  transfers between devices with their start and end apart: 8, of which 8 were waited for; matrix products, arithmetic and copies ran while one was open for 3% of the time, Pallas kernels for 0%

profile of v1, /device:TPU:1, one launch (start us, length us, event | category | flops | bytes accessed | tf_op | source)
XLA Modules:
  0.0 286.4 jit_solution(12560459758492440793)
XLA Ops:
  0.6 2.6 broadcast_in_dim.69
  3.2 8.5 %all-to-all-start = ((bf16[8,16,8192]{2,1,0:T(8,128)(2,1)}), bf16[8,16,8192]{2,1,0:T(8,128)(2,1)S(1)}, u32[]{:S(2)}, u32[]{:S(2)}) async-start(bf16[8,16,8192]{2,1,0:T(8,128)(2,1)} %broadcast_in_dim.69), calls=%async_computation | async-start | bytes 4194304 | tf_op jit(solution)/shard_map/all_to_all | solution.py:59
  11.7 26.1 %all-to-all-done = bf16[8,16,8192]{2,1,0:T(8,128)(2,1)S(1)} async-done(((bf16[8,16,8192]{2,1,0:T(8,128)(2,1)}), bf16[8,16,8192]{2,1,0:T(8,128)(2,1)S(1)}, u32[]{:S(2)}, u32[]{:S(2)}) %all-to-all-start) | async-done | bytes 2097184 | tf_op jit(solution)/shard_map/all_to_all | solution.py:59
  39.3 4.8 %fusion.126 = f32[128,512]{1,0:T(8,128)S(1)} fusion(bf16[128,8192]{1,0:T(8,128)(2,1)S(1)} %bitcast.259, bf16[8192,512]{1,0:T(8,128)(2,1)} %param.20), kind=kOutput, calls=%fused_computation.224 | convolution fusion | flops 1073741824 | bytes 10747904 | tf_op jit(solution)/shard_map/dot_general | solution.py:22
  47.9 1.3 fusion.49
  49.3 2.0 fusion
  51.3 5.2 %all-to-all-start.1 = ((bf16[8,16,8192]{2,1,0:T(8,128)(2,1)}), bf16[8,16,8192]{2,1,0:T(8,128)(2,1)}, u32[]{:S(2)}, u32[]{:S(2)}) async-start(bf16[8,16,8192]{2,1,0:T(8,128)(2,1)} %bitcast.272), calls=%async_computation.1 | async-start | bytes 4194304 | tf_op jit(solution)/shard_map/all_to_all | solution.py:127
  57.2 25.6 %all-to-all-done.1 = bf16[8,16,8192]{2,1,0:T(8,128)(2,1)} async-done(((bf16[8,16,8192]{2,1,0:T(8,128)(2,1)}), bf16[8,16,8192]{2,1,0:T(8,128)(2,1)}, u32[]{:S(2)}, u32[]{:S(2)}) %all-to-all-start.1) | async-done | bytes 2097184 | tf_op jit(solution)/shard_map/all_to_all | solution.py:127
  82.8 1.9 convert_reduce_fusion
  84.8 1.5 broadcast_in_dim.128
  86.3 5.3 %all-to-all-start.2 = ((bf16[8,16,8192]{2,1,0:T(8,128)(2,1)}), bf16[8,16,8192]{2,1,0:T(8,128)(2,1)}, u32[]{:S(2)}, u32[]{:S(2)}) async-start(bf16[8,16,8192]{2,1,0:T(8,128)(2,1)} %broadcast_in_dim.128), calls=%async_computation.2 | async-start | bytes 4194304 | tf_op jit(solution)/shard_map/all_to_all | solution.py:59
  99.2 18.7 %all-to-all-done.2 = bf16[8,16,8192]{2,1,0:T(8,128)(2,1)} async-done(((bf16[8,16,8192]{2,1,0:T(8,128)(2,1)}), bf16[8,16,8192]{2,1,0:T(8,128)(2,1)}, u32[]{:S(2)}, u32[]{:S(2)}) %all-to-all-start.2) | async-done | bytes 2097184 | tf_op jit(solution)/shard_map/all_to_all | solution.py:59
  117.9 2.3 fusion.7
  120.2 7.0 %fusion.8 = f32[133,512]{1,0:T(8,128)S(1)} fusion(bf16[512,8192]{1,0:T(8,128)(2,1)} %param.22, bf16[5,8192]{1,0:T(8,128)(2,1)S(1)} %bitcast.302, bf16[128,8192]{1,0:T(8,128)(2,1)} %bitcast.24), kind=kOutput, calls=%fused_computation.16 | convolution fusion | flops 1120043008 | bytes 10840064 | tf_op jit(solution)/shard_map/dot_general | solution.py:22
  128.2 2.1 multiply_reduce_fusion
  132.4 2.4 multiply_reduce_fusion.10
  134.8 1.3 fusion.13
  136.5 1.8 fusion.11
  138.3 1.2 convolution_bitcast_fusion.1
  139.6 2.3 fusion.57
  143.4 1.9 fusion.72
  146.0 5.2 %all-to-all-start.3 = ((f32[8,2,16,128]{3,1,2,0:T(2,128)}), f32[8,2,16,128]{3,1,2,0:T(2,128)S(1)}, u32[]{:S(2)}, u32[]{:S(2)}) async-start(f32[8,2,16,128]{3,1,2,0:T(2,128)} %maximum_multiply_fusion), calls=%async_computation.3 | async-start | bytes 262144 | tf_op jit(solution)/shard_map/all_to_all | solution.py:175
  151.5 6.6 %all-to-all-done.3 = f32[8,2,16,128]{3,1,2,0:T(2,128)S(1)} async-done(((f32[8,2,16,128]{3,1,2,0:T(2,128)}), f32[8,2,16,128]{3,1,2,0:T(2,128)S(1)}, u32[]{:S(2)}, u32[]{:S(2)}) %all-to-all-start.3) | async-done | bytes 131104 | tf_op jit(solution)/shard_map/all_to_all | solution.py:175
  159.2 2.0 fusion.96
  162.9 1.2 fusion.19
  164.2 1.4 copy.171
  165.6 6.4 %all-to-all-start.4 = ((bf16[16,56,512]{2,1,0:T(8,128)(2,1)}), bf16[16,56,512]{2,1,0:T(8,128)(2,1)S(1)}, u32[]{:S(2)}, u32[]{:S(2)}) async-start(bf16[16,56,512]{2,1,0:T(8,128)(2,1)} %copy.171), calls=%async_computation.4 | async-start | bytes 1835008 | tf_op jit(solution)/shard_map/all_to_all | solution.py:204
  172.2 14.2 %all-to-all-done.4 = bf16[16,56,512]{2,1,0:T(8,128)(2,1)S(1)} async-done(((bf16[16,56,512]{2,1,0:T(8,128)(2,1)}), bf16[16,56,512]{2,1,0:T(8,128)(2,1)S(1)}, u32[]{:S(2)}, u32[]{:S(2)}) %all-to-all-start.4) | async-done | bytes 917536 | tf_op jit(solution)/shard_map/all_to_all | solution.py:204
  189.4 0.9 broadcast_in_dim.138
  190.3 4.1 %all-to-all-start.5 = ((f32[16,80,128]{2,1,0:T(8,128)}), f32[16,80,128]{2,1,0:T(8,128)S(1)}, u32[]{:S(2)}, u32[]{:S(2)}) async-start(f32[16,80,128]{2,1,0:T(8,128)} %broadcast_in_dim.138), calls=%async_computation.5 | async-start | bytes 1310720 | tf_op jit(solution)/shard_map/all_to_all | solution.py:59
  194.4 11.5 %all-to-all-done.5 = f32[16,80,128]{2,1,0:T(8,128)S(1)} async-done(((f32[16,80,128]{2,1,0:T(8,128)}), f32[16,80,128]{2,1,0:T(8,128)S(1)}, u32[]{:S(2)}, u32[]{:S(2)}) %all-to-all-start.5) | async-done | bytes 655392 | tf_op jit(solution)/shard_map/all_to_all | solution.py:59
  206.7 3.4 %all-to-all-start.6 = ((f32[8,80,128]{2,1,0:T(8,128)}), f32[8,80,128]{2,1,0:T(8,128)S(1)}, u32[]{:S(2)}, u32[]{:S(2)}) async-start(f32[8,80,128]{2,1,0:T(8,128)} %broadcast_in_dim.139), calls=%async_computation.6 | async-start | bytes 655360 | tf_op jit(solution)/shard_map/all_to_all | solution.py:59
  210.2 7.7 %all-to-all-done.6 = f32[8,80,128]{2,1,0:T(8,128)S(1)} async-done(((f32[8,80,128]{2,1,0:T(8,128)}), f32[8,80,128]{2,1,0:T(8,128)S(1)}, u32[]{:S(2)}, u32[]{:S(2)}) %all-to-all-start.6) | async-done | bytes 327712 | tf_op jit(solution)/shard_map/all_to_all | solution.py:59
  229.1 1.3 broadcast_in_dim.140
  230.5 5.9 %all-to-all-start.7 = ((bf16[128,48,128]{2,1,0:T(8,128)(2,1)}), bf16[128,48,128]{2,1,0:T(8,128)(2,1)S(1)}, u32[]{:S(2)}, u32[]{:S(2)}) async-start(bf16[128,48,128]{2,1,0:T(8,128)(2,1)} %broadcast_in_dim.140), calls=%async_computation.7 | async-start | bytes 3145728 | tf_op jit(solution)/shard_map/all_to_all | solution.py:304
  236.4 23.3 %all-to-all-done.7 = bf16[128,48,128]{2,1,0:T(8,128)(2,1)S(1)} async-done(((bf16[128,48,128]{2,1,0:T(8,128)(2,1)}), bf16[128,48,128]{2,1,0:T(8,128)(2,1)S(1)}, u32[]{:S(2)}, u32[]{:S(2)}) %all-to-all-start.7) | async-done | bytes 1572896 | tf_op jit(solution)/shard_map/all_to_all | solution.py:304
  259.7 1.6 reshape.404
  261.3 2.8 slice_convert_fusion
  264.1 1.0 slice_convert_fusion.1
  265.9 2.7 reshape.407
  269.8 1.2 reshape.408
  271.0 2.7 slice_reduce_fusion
  273.9 1.9 multiply_add_fusion
  276.6 1.6 copy_add_fusion
  278.3 1.7 multiply_add_fusion.1
  280.0 2.1 copy.177
  282.1 1.6 slice.130
  283.7 2.7 bitcast_add_fusion
  (184 shorter events, 34.1 us)
Async XLA Ops:
  0.6 37.2 %copy-start = (bf16[3,8192,16]{1,2,0:T(8,128)(2,1)S(1)}, bf16[3,8192,16]{1,2,0:T(8,128)(2,1)}, u32[]{:S(2)}) copy-start(bf16[3,8192,16]{1,2,0:T(8,128)(2,1)} %param.26) | copy-start | bytes 2359300
  3.2 34.6 %all-to-all-start = ((bf16[8,16,8192]{2,1,0:T(8,128)(2,1)}), bf16[8,16,8192]{2,1,0:T(8,128)(2,1)S(1)}, u32[]{:S(2)}, u32[]{:S(2)}) async-start(bf16[8,16,8192]{2,1,0:T(8,128)(2,1)} %broadcast_in_dim.69), calls=%async_computation | async-start | bytes 4194304 | tf_op jit(solution)/shard_map/all_to_all | solution.py:59
  11.7 27.0 %copy-start.22 = (bf16[2,16,128]{2,1,0:T(8,128)(2,1)S(1)}, bf16[2,16,128]{2,1,0:T(8,128)(2,1)}, u32[]{:S(2)}) copy-start(bf16[2,16,128]{2,1,0:T(8,128)(2,1)} %param.28) | copy-start | bytes 24580
  38.7 6.9 %copy-start.12 = (f32[128,48]{0,1:T(8,128)}, f32[128,48]{0,1:T(8,128)S(1)}, u32[]{:S(2)}) copy-start(f32[128,48]{0,1:T(8,128)S(1)} %fusion.125) | copy-start | bytes 73732
  39.0 8.9 %slice-start = ((s8[8388608]{0:T(1024)(128)(4,1)}), s8[4194304]{0:T(1024)(128)(4,1)S(1)}, s32[]{:S(2)}) async-start(s8[8388608]{0:T(1024)(128)(4,1)} %bitcast.270), calls=%async_computation.8 | async-start | bytes 8388608
  39.3 4.8 %copy-start.26 = (bf16[2,8192,128]{2,1,0:T(8,128)(2,1)S(1)}, bf16[2,8192,128]{2,1,0:T(8,128)(2,1)}, u32[]{:S(2)}) copy-start(bf16[2,8192,128]{2,1,0:T(8,128)(2,1)} %param.21) | copy-start | bytes 12582916
  39.3 8.7 %slice-start.1 = ((s8[8388608]{0:T(1024)(128)(4,1)}), s8[4194304]{0:T(1024)(128)(4,1)S(1)}, s32[]{:S(2)}) async-start(s8[8388608]{0:T(1024)(128)(4,1)} %bitcast.270), calls=%async_computation.9 | async-start | bytes 8388608
  44.8 1.3 copy-start.10
  44.9 1.0 copy-start.15
  45.8 1.3 copy-start.17
  45.8 1.3 copy-start.19
  47.9 1.3 copy-start.8
  51.3 31.5 %all-to-all-start.1 = ((bf16[8,16,8192]{2,1,0:T(8,128)(2,1)}), bf16[8,16,8192]{2,1,0:T(8,128)(2,1)}, u32[]{:S(2)}, u32[]{:S(2)}) async-start(bf16[8,16,8192]{2,1,0:T(8,128)(2,1)} %bitcast.272), calls=%async_computation.1 | async-start | bytes 4194304 | tf_op jit(solution)/shard_map/all_to_all | solution.py:127
  56.5 28.2 %copy-start.3 = (bf16[1,16,8192]{2,1,0:T(8,128)(2,1)S(1)}, bf16[1,16,8192]{2,1,0:T(8,128)(2,1)}, u32[]{:S(2)}) copy-start(bf16[1,16,8192]{2,1,0:T(8,128)(2,1)} %param.19) | copy-start | bytes 786436
  86.3 5.3 %copy-start.6 = (bf16[8192,5]{0,1:T(8,128)(2,1)S(1)}, bf16[8192,5]{0,1:T(8,128)(2,1)}, u32[]{:S(2)}) copy-start(bf16[8192,5]{0,1:T(8,128)(2,1)} %param.23) | copy-start | bytes 245764
  86.3 31.6 %all-to-all-start.2 = ((bf16[8,16,8192]{2,1,0:T(8,128)(2,1)}), bf16[8,16,8192]{2,1,0:T(8,128)(2,1)}, u32[]{:S(2)}, u32[]{:S(2)}) async-start(bf16[8,16,8192]{2,1,0:T(8,128)(2,1)} %broadcast_in_dim.128), calls=%async_computation.2 | async-start | bytes 4194304 | tf_op jit(solution)/shard_map/all_to_all | solution.py:59
  120.2 7.0 %copy-start.20 = (f32[133,16]{0,1:T(8,128)}, f32[133,16]{0,1:T(8,128)S(1)}, u32[]{:S(2)}) copy-start(f32[133,16]{0,1:T(8,128)S(1)} %fusion.7) | copy-start | bytes 25540
  128.2 2.8 copy-start.4
  131.1 5.4 %copy-start.9 = (f32[4,128,128]{1,2,0:T(8,128)S(1)}, f32[4,128,128]{1,2,0:T(8,128)}, u32[]{:S(2)}) copy-start(f32[4,128,128]{1,2,0:T(8,128)} %multiply_bitcast_fusion) | copy-start | bytes 786436
  131.8 3.0 %copy-start.21 = (f32[5,4,128]{2,1,0:T(4,128)S(1)}, f32[5,4,128]{2,1,0:T(4,128)}, u32[]{:S(2)}) copy-start(f32[5,4,128]{2,1,0:T(4,128)} %mul.455) | copy-start | bytes 30724
  131.8 4.7 %copy-start.18 = (f32[128,128]{1,0:T(8,128)S(1)}, f32[128,128]{1,0:T(8,128)}, u32[]{:S(2)}) copy-start(f32[128,128]{1,0:T(8,128)} %copy-done.17) | copy-start | bytes 196612
  136.5 3.0 %copy-start.11 = (f32[128,128]{1,0:T(8,128)S(1)}, f32[128,128]{1,0:T(8,128)}, u32[]{:S(2)}) copy-start(f32[128,128]{1,0:T(8,128)} %copy-done.10) | copy-start | bytes 196612
  138.3 3.6 %copy-start.23 = (bf16[2,16,128]{2,1,0:T(8,128)(2,1)S(1)}, bf16[2,16,128]{2,1,0:T(8,128)(2,1)}, u32[]{:S(2)}) copy-start(bf16[2,16,128]{2,1,0:T(8,128)(2,1)} %param.28) | copy-start | bytes 24580
  138.3 3.8 %copy-start.13 = (f32[128,48]{0,1:T(8,128)S(1)}, f32[128,48]{0,1:T(8,128)}, u32[]{:S(2)}) copy-start(f32[128,48]{0,1:T(8,128)} %copy-done.12) | copy-start | bytes 73732
  139.5 3.0 %slice-start.2 = ((f32[133,16]{0,1:T(8,128)}), f32[5,16]{0,1:T(8,128)S(1)}, s32[]{:S(2)}) async-start(f32[133,16]{0,1:T(8,128)} %copy-done.20), calls=%async_computation.10 | async-start | bytes 16384 | tf_op jit(solution)/shard_map/slice | solution.py:151
  139.5 3.1 %slice-start.3 = ((f32[133,16]{0,1:T(8,128)}), f32[128,16]{0,1:T(8,128)S(1)}, s32[]{:S(2)}) async-start(f32[133,16]{0,1:T(8,128)} %copy-done.20), calls=%async_computation.11 | async-start | bytes 16384 | tf_op jit(solution)/shard_map/slice | solution.py:152
  139.6 3.9 %copy-start.16 = (bf16[16,512]{1,0:T(8,128)(2,1)S(1)}, bf16[16,512]{1,0:T(8,128)(2,1)}, u32[]{:S(2)}) copy-start(bf16[16,512]{1,0:T(8,128)(2,1)} %param.27) | copy-start | bytes 49156
  141.9 3.4 %copy-start.24 = (f32[128,16]{0,1:T(8,128)S(1)}, f32[128,16]{0,1:T(8,128)}, u32[]{:S(2)}) copy-start(f32[128,16]{0,1:T(8,128)} %get-tuple-element.38) | copy-start | bytes 24580
  146.0 12.1 %all-to-all-start.3 = ((f32[8,2,16,128]{3,1,2,0:T(2,128)}), f32[8,2,16,128]{3,1,2,0:T(2,128)S(1)}, u32[]{:S(2)}, u32[]{:S(2)}) async-start(f32[8,2,16,128]{3,1,2,0:T(2,128)} %maximum_multiply_fusion), calls=%async_computation.3 | async-start | bytes 262144 | tf_op jit(solution)/shard_map/all_to_all | solution.py:175
  161.2 0.9 copy-start.5
  161.6 1.3 copy-start.2
  162.2 1.9 copy-start.25
  164.1 7.9 %copy-start.14 = (f32[1,1,11,512]{3,1,2,0:T(1,128)S(1)}, f32[1,1,11,512]{3,1,2,0:T(1,128)}, u32[]{:S(2)}) copy-start(f32[1,1,11,512]{3,1,2,0:T(1,128)} %copy.215) | copy-start | bytes 67588
  165.6 20.8 %all-to-all-start.4 = ((bf16[16,56,512]{2,1,0:T(8,128)(2,1)}), bf16[16,56,512]{2,1,0:T(8,128)(2,1)S(1)}, u32[]{:S(2)}, u32[]{:S(2)}) async-start(bf16[16,56,512]{2,1,0:T(8,128)(2,1)} %copy.171), calls=%async_computation.4 | async-start | bytes 1835008 | tf_op jit(solution)/shard_map/all_to_all | solution.py:204
  188.2 6.2 %copy-start.27 = (s32[16]{0:T(128)S(1)}, s32[16]{0:T(128)}, u32[]{:S(2)}) copy-start(s32[16]{0:T(128)} %param.25) | copy-start | bytes 196
  190.3 15.7 %all-to-all-start.5 = ((f32[16,80,128]{2,1,0:T(8,128)}), f32[16,80,128]{2,1,0:T(8,128)S(1)}, u32[]{:S(2)}, u32[]{:S(2)}) async-start(f32[16,80,128]{2,1,0:T(8,128)} %broadcast_in_dim.138), calls=%async_computation.5 | async-start | bytes 1310720 | tf_op jit(solution)/shard_map/all_to_all | solution.py:59
  206.7 11.2 %all-to-all-start.6 = ((f32[8,80,128]{2,1,0:T(8,128)}), f32[8,80,128]{2,1,0:T(8,128)S(1)}, u32[]{:S(2)}, u32[]{:S(2)}) async-start(f32[8,80,128]{2,1,0:T(8,128)} %broadcast_in_dim.139), calls=%async_computation.6 | async-start | bytes 655360 | tf_op jit(solution)/shard_map/all_to_all | solution.py:59
  230.5 29.2 %all-to-all-start.7 = ((bf16[128,48,128]{2,1,0:T(8,128)(2,1)}), bf16[128,48,128]{2,1,0:T(8,128)(2,1)S(1)}, u32[]{:S(2)}, u32[]{:S(2)}) async-start(bf16[128,48,128]{2,1,0:T(8,128)(2,1)} %broadcast_in_dim.140), calls=%async_computation.7 | async-start | bytes 3145728 | tf_op jit(solution)/shard_map/all_to_all | solution.py:304
  271.0 4.7 %copy-start.7 = (f32[4096,16]{0,1:T(8,128)S(1)}, f32[4096,16]{0,1:T(8,128)}, u32[]{:S(2)}) copy-start(f32[4096,16]{0,1:T(8,128)} %param.34) | copy-start | bytes 786436
  282.1 4.3 %copy-start.1 = (bf16[3,8192,16]{1,2,0:T(8,128)(2,1)S(1)}, bf16[3,8192,16]{1,2,0:T(8,128)(2,1)}, u32[]{:S(2)}) copy-start(bf16[3,8192,16]{1,2,0:T(8,128)(2,1)} %param.26) | copy-start | bytes 2359300

commit v2 on v1

v2 whole, which is shorter than its diff:
```python
import math

import jax
import jax.numpy as jnp
from jax import lax
from jax.experimental import pallas as pl
from jax.experimental.pallas import tpu as pltpu
from jax.sharding import PartitionSpec as P

HEAD_SIZE = 128
NPARAM = 688128
ADAPTER_SCALE = 2.0
NORM_EPS = 1e-05
LANCZOS_EPS = 1e-06
SCORE_CAP = 30.0
PRECISE = lax.Precision.HIGHEST
OBJ = 5
PIECES = 11
PIECE_ROWS = 56
LANES = 512


def dot_halved(left_side, right_side, left_dim, right_dim):
    return lax.dot_general(
        left_side,
        right_side,
        (((left_dim,), (right_dim,)), ((), ())),
        preferred_element_type=jnp.float32,
    )


def dot_entire(left_side, right_side, left_dim, right_dim):
    return lax.dot_general(
        left_side,
        right_side,
        (((left_dim,), (right_dim,)), ((), ())),
        precision=PRECISE,
        preferred_element_type=jnp.float32,
    )


def two_halves(entire):
    upper = lax.reduce_precision(entire, 8, 7)
    return upper.astype(jnp.bfloat16), (entire - upper).astype(jnp.bfloat16)


def three_halves(entire):
    upper = lax.reduce_precision(entire, 8, 7)
    rest = entire - upper
    middle = lax.reduce_precision(rest, 8, 7)
    return (
        upper.astype(jnp.bfloat16),
        middle.astype(jnp.bfloat16),
        (rest - middle).astype(jnp.bfloat16),
    )


def gather_by_exchange(block, axis):
    count = lax.axis_size(axis)
    copies = jnp.broadcast_to(block[None], (count,) + block.shape)
    return lax.all_to_all(copies, axis, 0, 0)


PAIR_ROWS = 40
PACK_ROWS = 48
PACK_LANES = 42
RESULT_LANES = 768


def rounded_parts(entire, count):
    parts = []
    for _ in range(count):
        part = entire.astype(jnp.bfloat16)
        parts.append(part)
        entire = entire - part.astype(jnp.float32)
    return parts


def lane_sum(values):
    return jnp.sum(values, axis=1, keepdims=True)


def row_sum(values):
    return jnp.sum(values, axis=0, keepdims=True)


def gram_body(rank_ref, jac_ref, start_ref, pairs_ref, rewards_ref, packed_ref):
    jac = jac_ref[...]
    start = start_ref[...]
    pairs = pairs_ref[...]
    rows = jac.shape[0]
    gram = dot_halved(jac, jac, 1, 1)
    starts = jnp.concatenate(rounded_parts(start, 3), 0)
    along = lane_sum(dot_halved(jac, starts, 1, 1))
    own_pairs = pairs[:, :rows]
    gram = dot_entire(dot_entire(own_pairs, gram, 1, 0), own_pairs, 1, 1)
    along = dot_entire(own_pairs, jnp.broadcast_to(along, (rows, 128)), 1, 0)
    rewards = pltpu.roll(rewards_ref[...], OBJ * rank_ref[0], axis=1)[:1]
    rewards = jnp.where(rank_ref[1] == 0, rewards, 0.0)
    apart = lane_sum(pairs * rewards)
    square = jnp.sum(start * start)
    lane = lax.broadcasted_iota(jnp.int32, (PACK_ROWS, 128), 1)
    row = lax.broadcasted_iota(jnp.int32, (PACK_ROWS, 128), 0)
    wide = jnp.concatenate([gram, jnp.zeros((PACK_ROWS, 128 - PACK_ROWS), jnp.float32)], 1)
    wide = jnp.where(lane < PAIR_ROWS, wide, 0.0)
    wide = jnp.where(lane == PAIR_ROWS, along, wide)
    wide = jnp.where(lane == PAIR_ROWS + 1, apart, wide)
    wide = jnp.where((row == PAIR_ROWS) & (lane == 0), square, wide)
    packed_ref[...] = (
        wide[:16]
        + pltpu.roll(wide[16:32], PACK_LANES, axis=1)
        + pltpu.roll(wide[32:], 2 * PACK_LANES, axis=1)
    )


def lanczos_body(packed_ref, pairs_ref, jac_ref, result_ref, part_ref):
    packed = jnp.sum(packed_ref[...], axis=0)
    wide = jnp.concatenate(
        [
            packed,
            pltpu.roll(packed, 128 - PACK_LANES, axis=1),
            pltpu.roll(packed, 128 - 2 * PACK_LANES, axis=1),
        ],
        0,
    )
    lane = lax.broadcasted_iota(jnp.int32, (PACK_ROWS, 128), 1)
    row = lax.broadcasted_iota(jnp.int32, (PACK_ROWS, 128), 0)
    inside = row < PAIR_ROWS
    gram = jnp.where(inside & (lane < PAIR_ROWS), wide, 0.0)
    along = lane_sum(jnp.where(inside & (lane == PAIR_ROWS), wide, 0.0))
    apart = lane_sum(jnp.where(inside & (lane == PAIR_ROWS + 1), wide, 0.0))
    picked = jnp.where((row == PAIR_ROWS) & (lane == 0), wide, 0.0)
    start_square = lane_sum(row_sum(picked)) / NPARAM
    diagonal = row == lane

    def gram_times(column):
        across = row_sum(jnp.where(diagonal, column, 0.0))
        return lane_sum(gram * across)

    def inner(left_side, right_side):
        return row_sum(left_side * right_side) / NPARAM

    decayed = jnp.exp(-jnp.abs(apart))
    curvature = decayed / ((1.0 + decayed) * (1.0 + decayed)) / (16 // 2)
    start_scale = lax.rsqrt(start_square + LANCZOS_EPS)
    first_square = start_square * start_scale * start_scale
    along_one = along * start_scale
    pull_one = curvature * along_one
    alpha_one = inner(pull_one, along_one)
    gram_pull = gram_times(pull_one)
    beta_one = jnp.sqrt(
        inner(pull_one, gram_pull) - alpha_one * alpha_one * (2.0 - first_square) + LANCZOS_EPS
    )
    along_two = (gram_pull - alpha_one * along_one) / beta_one
    pull_two = curvature * along_two
    first_second = alpha_one * (1.0 - first_square) / beta_one
    alpha_two = inner(pull_two, along_two) - beta_one * first_second
    mixed = pull_two - (alpha_two / beta_one) * pull_one
    first_part = alpha_two * alpha_one / beta_one - beta_one
    beta_two = jnp.sqrt(
        inner(mixed, gram_times(mixed))
        + 2.0 * first_part * inner(mixed, along_one)
        + first_part * first_part * first_square
        + LANCZOS_EPS
    )
    part_ref[...] = jnp.broadcast_to(first_part * start_scale / beta_two, part_ref.shape)
    across = row_sum(pairs_ref[...] * (mixed / beta_two))
    jac = jac_ref[...]
    rows = jac.shape[0]
    parts = rounded_parts(jnp.broadcast_to(across[:, :rows], (8, rows)), 3)
    result = sum(dot_halved(part, jac, 1, 0) for part in parts)[:1]
    spare = jnp.zeros((6, 128), jnp.float32)

    def chunks(start, count, size):
        return [result[:, start + size * step : start + size * (step + 1)] for step in range(count)]

    main = jnp.concatenate(chunks(0, 8, LANES), 0)
    middle = jnp.concatenate(chunks(8 * LANES, 8, 128), 0)
    last = jnp.concatenate(chunks(10 * LANES, 2, 128) + [spare], 0)
    result_ref[...] = jnp.concatenate([main, middle, last], 1).astype(jnp.bfloat16)


def assemble_body(
    part_ref,
    every_ref,
    a_ref,
    bq_ref,
    bkv_ref,
    ao_ref,
    bo_ref,
    out_a_ref,
    out_bq_ref,
    out_bkv_ref,
    out_ao_ref,
    out_bo_ref,
):
    step = pl.program_id(0)
    part = part_ref[0, 0]

    def one_hot(size, first, second):
        row = lax.broadcasted_iota(jnp.int32, (size, size), 0)
        lane = lax.broadcasted_iota(jnp.int32, (size, size), 1)
        wanted = (row % second) * first + row // second
        return jnp.where(lane == wanted, 1.0, 0.0).astype(jnp.bfloat16)

    row = lax.broadcasted_iota(jnp.int32, (64, 64), 0)
    lane = lax.broadcasted_iota(jnp.int32, (64, 64), 1)
    wanted = (row % 8) * 8 + ((row % 16) // 8) * 4 + row // 16
    moved = jnp.where(lane == wanted, 1.0, 0.0).astype(jnp.bfloat16)
    for half in range(2):
        group = 2 * step + half
        block = every_ref[pl.ds(8 * group, 8), :, :LANES].reshape(64, LANES)
        placed = dot_halved(moved, block, 1, 0).reshape(4, 16, LANES)
        lanes = slice(half * LANES, (half + 1) * LANES)
        out_a_ref[:, :, lanes] = placed[:3] + part * a_ref[:, :, lanes]
        out_bo_ref[:, lanes] = placed[3] + part * bo_ref[:, lanes]
    block = jnp.concatenate(
        [every_ref[8 * group + step, :, LANES:] for group in range(16)], 0
    )
    placed = dot_halved(one_hot(128, 8, 16), block, 1, 0)
    for chunk in range(4):
        lanes = slice(chunk * 128, (chunk + 1) * 128)
        out_bq_ref[:, lanes] = placed[16 * chunk : 16 * chunk + 16, :128] + part * bq_ref[:, lanes]
        out_ao_ref[:, lanes] = (
            placed[64 + 16 * chunk : 80 + 16 * chunk, :128] + part * ao_ref[:, lanes]
        )
    out_bkv_ref[0] = placed[:16, 128:] + part * bkv_ref[0]
    out_bkv_ref[1] = placed[16:32, 128:] + part * bkv_ref[1]


def whole(count):
    return [pl.BlockSpec(memory_space=pltpu.VMEM)] * count


def dot_parts(left_parts, right_parts, left_dim, right_dim):
    total = None
    for left_at, left_part in enumerate(left_parts):
        for right_at, right_part in enumerate(right_parts):
            if left_at + right_at < 2:
                term = dot_halved(left_part, right_part, left_dim, right_dim)
                total = term if total is None else total + term
    return total


COT_CHUNK = 2048


def cotangents_body(
    lens_ref,
    resid_ref,
    weight_ref,
    side_ref,
    query_ref,
    keys_ref,
    values_ref,
    prob_ref,
    capped_ref,
    context_ref,
    low_ref,
    context_low_ref,
    down_ref,
    up_query_ref,
    up_kv_ref,
    factors_ref,
    narrow_ref,
    rewards_ref,
    repeated_ref,
    through_ref,
    slow_ref,
    square_ref,
):
    step = pl.program_id(0)
    chunk = resid_ref[...]
    side = side_ref[...]
    left = jnp.concatenate([chunk, side[16:]], 0)
    through = dot_halved(left, weight_ref[...], 1, 1)
    slow = dot_halved(left, side, 1, 1)
    wide = chunk.astype(jnp.float32)
    square = jnp.zeros((128, 128), jnp.float32)
    for at in range(0, chunk.shape[1], 128):
        square = square + wide[:, at : at + 128] * wide[:, at : at + 128]

    @pl.when(step == 0)
    def _():
        slow_ref[...] = jnp.zeros(slow_ref.shape, jnp.float32)
        through_ref[...] = through
        slow_ref[:144, :32] = slow
        square_ref[...] = square

    @pl.when(step > 0)
    def _():
        through_ref[...] += through
        slow_ref[:144, :32] += slow
        square_ref[...] += square

    @pl.when(step == pl.num_programs(0) - 1)
    def _():
        width = chunk.shape[1] * pl.num_programs(0)
        length_own = lens_ref[0]
        root = 1.0 / math.sqrt(HEAD_SIZE)
        slow = slow_ref[...]
        slow_turned = slow.T
        square = square_ref[...]
        inverse = lax.rsqrt(lane_sum(square) / width + NORM_EPS)
        inverse_turned = lax.rsqrt(row_sum(square.T) / width + NORM_EPS)
        each = 1.0 / jnp.broadcast_to(length_own, (1, 1)).astype(jnp.float32)
        share = jnp.where(
            lax.broadcasted_iota(jnp.int32, (128, 1), 0) < length_own, each, 0.0
        )
        share_turned = jnp.where(
            lax.broadcasted_iota(jnp.int32, (1, 128), 1) < length_own, each, 0.0
        )
        logits = inverse * slow[:128, 16:32]
        lead = share * inverse
        pulled = lead * inverse * logits / width
        lead_turned = share_turned * inverse_turned
        pulled_turned = (
            lead_turned * inverse_turned * inverse_turned * slow_turned[16:32, :128] / width
        )
        low_turned = slow_turned[:16, :128]
        rewards_ref[...] = jnp.zeros(rewards_ref.shape, jnp.float32)
        rewards_ref[:1, :16] = row_sum(share * logits)
        through = through_ref[...] + ADAPTER_SCALE * dot_entire(
            slow[:144, :16], down_ref[...], 1, 0
        )

        def stack(rows):
            return jnp.concatenate([rows[:, at : at + 128] for at in range(0, 512, 128)], 0)

        narrow_ref[...] = jnp.zeros(narrow_ref.shape, jnp.float32)
        context = context_ref[...]
        context_rows = stack(context)
        probs = prob_ref[...].reshape(512, 128)
        capped = capped_ref[...].reshape(512, 128)
        slope = probs * (1.0 - capped * capped) * root
        probs_turned = rounded_parts(probs.T, 2)
        query_turned = rounded_parts(stack(query_ref[...]).T, 2)
        keys = rounded_parts(keys_ref[...], 2)
        values = rounded_parts(values_ref[...], 2)
        low = [rounded_parts(low_ref[16 * piece : 16 * piece + 16], 2) for piece in range(3)]
        up_query = up_query_ref[...]
        context_low = context_low_ref[...]
        cot_low = []
        for obj in range(OBJ):
            lead_row = through[128 + obj : 129 + obj]
            cot = stack(lead * lead_row - pulled[:, obj : obj + 1] * through[:128])
            cot_parts = rounded_parts(cot, 2)
            cot_prob = dot_parts(cot_parts, values, 1, 1)
            cot_score = slope * (cot_prob - lane_sum(cot * context_rows))
            score_parts = rounded_parts(cot_score, 2)
            cot_query = dot_parts(score_parts, keys, 1, 0)
            query_parts = rounded_parts(cot_query, 2)
            keys_parts = rounded_parts(dot_parts(query_turned, score_parts, 1, 0), 2)
            values_parts = rounded_parts(dot_parts(probs_turned, cot_parts, 1, 0), 2)
            factor_query = 0.0
            jac_query = []
            for at in range(0, 512, 128):
                block = [part[at : at + 128] for part in query_parts]
                factor_query += dot_parts([up_query[:, at : at + 128]], block, 1, 1)
                jac_query.append(dot_parts(low[0], block, 1, 0))
            rows = [
                ADAPTER_SCALE * factor_query,
                ADAPTER_SCALE * dot_parts([up_kv_ref[0]], keys_parts, 1, 0),
                ADAPTER_SCALE * dot_parts([up_kv_ref[1]], values_parts, 1, 1),
                context_low,
            ]
            for piece in range(4):
                for half in range(2):
                    factors_ref[pl.ds(20 * half + 5 * piece + obj, 8, stride=40), :] = rows[
                        piece
                    ][8 * half : 8 * half + 8]
            blocks = jac_query + [
                dot_parts(low[1], keys_parts, 1, 1),
                dot_parts(low[2], values_parts, 1, 0),
            ]
            spots = [(obj, at) for at in range(0, 512, 128)] + [(10 + obj, 0), (10 + obj, 128)]
            for (row, at), block in zip(spots, blocks):
                for half in range(2):
                    narrow_ref[at // 128, pl.ds(128 * half + row, 8, stride=16), :] = (
                        ADAPTER_SCALE * block[8 * half : 8 * half + 8]
                    )
            cot_low.append(
                slow_turned[:16, 128 + obj : 129 + obj] * lead_turned
                - pulled_turned[obj : obj + 1] * low_turned
            )
        jac_down = ADAPTER_SCALE * dot_parts(
            rounded_parts(jnp.concatenate(cot_low, 0), 2), rounded_parts(context, 2), 1, 0
        )
        for obj in range(OBJ):
            for half in range(2):
                start = 16 * obj + 8 * half
                for tile in range(4):
                    narrow_ref[tile, pl.ds(128 * half + 5 + obj, 8, stride=16), :] = jac_down[
                        start : start + 8, 128 * tile : 128 * tile + 128
                    ]
        blank = jnp.zeros((15, 128), jnp.float32)
        repeated_ref[0] = jnp.concatenate([blank, pulled_turned[:5]] * 2, 0)
        repeated_ref[1] = jnp.broadcast_to(lead_turned, (40, 128))


def cotangents(lens, resid, output_weight, side, *others):
    length, width = resid.shape
    query_cols = output_weight.shape[0]

    def chunked(rows):
        return pl.BlockSpec((rows, COT_CHUNK), lambda step: (0, step))

    def fixed(array):
        zeros = (0,) * array.ndim
        return pl.BlockSpec(array.shape, lambda step: zeros)

    shapes = [
        jax.ShapeDtypeStruct((320, 128), jnp.float32),
        jax.ShapeDtypeStruct((4, 256, 128), jnp.float32),
        jax.ShapeDtypeStruct((8, 128), jnp.float32),
        jax.ShapeDtypeStruct((2, 40, 128), jnp.float32),
    ]
    return pl.pallas_call(
        cotangents_body,
        grid=(width // COT_CHUNK,),
        in_specs=[
            pl.BlockSpec(memory_space=pltpu.SMEM),
            chunked(length),
            chunked(query_cols),
            chunked(32),
        ]
        + [fixed(array) for array in others],
        out_specs=[fixed(shape) for shape in shapes],
        out_shape=shapes,
        scratch_shapes=[
            pltpu.VMEM((144, query_cols), jnp.float32),
            pltpu.VMEM((256, 128), jnp.float32),
            pltpu.VMEM((128, 128), jnp.float32),
        ],
        compiler_params=pltpu.CompilerParams(vmem_limit_bytes=40 * 2**20),
        name="cotangents",
    )(lens, resid, output_weight, side, *others)


def jacobian_body(
    factors_ref, tokens_ref, resid_ref, side_ref, repeated_ref, narrow_ref, payload_ref
):
    factors = jnp.sum(factors_ref[...], axis=0)
    row = lax.broadcasted_iota(jnp.int32, (40, 1), 0) % 20
    last = row >= 15
    left = jnp.concatenate(
        [jnp.where(last, 0.0, factors), jnp.where(last, -factors * repeated_ref[0], 0.0)], 1
    )
    left = rounded_parts(left, 2)
    lane = lax.broadcasted_iota(jnp.int32, (40, 16), 1)
    lead = rounded_parts(
        jnp.where(lane == row - 15, lane_sum(factors * repeated_ref[1]), 0.0), 2
    )

    def place(group, _):
        lanes = pl.ds(pl.multiple_of(group * LANES, LANES), LANES)
        right = jnp.concatenate([tokens_ref[:, lanes], resid_ref[:, lanes]], 0)
        rows = dot_parts(left, [right], 1, 0) + dot_parts(lead, [side_ref[16:, lanes]], 1, 0)
        below = jnp.concatenate(
            [narrow_ref[tile, pl.ds(pl.multiple_of(group * 16, 16), 16), :] for tile in range(4)], 1
        )
        payload_ref[group] = jnp.concatenate([rows, below], 0).astype(jnp.bfloat16)
        return 0

    lax.fori_loop(0, 16, place, 0)


def jacobian(*arrays):
    return pl.pallas_call(
        jacobian_body,
        in_specs=whole(len(arrays)),
        out_specs=pl.BlockSpec(memory_space=pltpu.VMEM),
        out_shape=jax.ShapeDtypeStruct((16, PIECE_ROWS, LANES), jnp.bfloat16),
        compiler_params=pltpu.CompilerParams(vmem_limit_bytes=24 * 2**20),
        name="jacobian",
    )(*arrays)


def assemble(part, every, start_a, start_bq, start_bkv, start_ao, start_bo):
    steps = 8
    shapes = [start_a, start_bq, start_bkv, start_ao, start_bo]
    blocks = [
        pl.BlockSpec((3, 16, 2 * LANES), lambda step: (0, 0, step)),
        pl.BlockSpec((16, LANES), lambda step: (0, step)),
        pl.BlockSpec((2, 16, HEAD_SIZE), lambda step: (0, 0, step)),
        pl.BlockSpec((16, LANES), lambda step: (0, step)),
        pl.BlockSpec((16, 2 * LANES), lambda step: (0, step)),
    ]
    return pl.pallas_call(
        assemble_body,
        grid=(steps,),
        in_specs=[
            pl.BlockSpec(memory_space=pltpu.SMEM),
            pl.BlockSpec(every.shape, lambda step: (0, 0, 0)),
        ]
        + blocks,
        out_specs=blocks,
        out_shape=[jax.ShapeDtypeStruct(shape.shape, jnp.float32) for shape in shapes],
        compiler_params=pltpu.CompilerParams(vmem_limit_bytes=32 * 2**20),
        name="assemble",
    )(part, every, start_a, start_bq, start_bkv, start_ao, start_bo)


def local(
    hidden,
    query_weight,
    key_value_weight,
    output_weight,
    head,
    lens,
    partner,
    adapter_down_qkv,
    adapter_up_query,
    adapter_up_key_value,
    adapter_down_output,
    adapter_up_output,
    initial_down_qkv,
    initial_up_query,
    initial_up_key_value,
    initial_down_output,
    initial_up_output,
):
    _, part_length, width = hidden.shape
    shards = lax.axis_size("tensor")
    groups = lax.axis_size("dp")
    tensor_rank = lax.axis_index("tensor")
    group_rank = lax.axis_index("dp")
    query_cols = query_weight.shape[1]
    heads = query_cols // HEAD_SIZE
    length = part_length * shards
    root = 1.0 / math.sqrt(HEAD_SIZE)

    down_qkv = jnp.transpose(adapter_down_qkv, (0, 2, 1))
    down_output = adapter_down_output.T.astype(jnp.float32)
    up_query = adapter_up_query.astype(jnp.float32)
    up_key_value = adapter_up_key_value.astype(jnp.float32)
    head_rows = head.T

    tokens = gather_by_exchange(hidden[0], "tensor").reshape(length, width)

    low = dot_halved(tokens, down_qkv.reshape(48, width), 1, 1)
    low_q, low_k, low_v = low[:, :16], low[:, 16:32], low[:, 32:]
    query = dot_halved(tokens, query_weight, 1, 0) + ADAPTER_SCALE * dot_entire(
        low_q, up_query, 1, 0
    )
    keys = dot_halved(tokens, key_value_weight[0], 1, 0) + ADAPTER_SCALE * dot_entire(
        low_k, up_key_value[0], 1, 0
    )
    values = dot_halved(tokens, key_value_weight[1], 1, 0) + ADAPTER_SCALE * dot_entire(
        low_v, up_key_value[1], 1, 0
    )
    query_split = query.reshape(length, heads, HEAD_SIZE)
    capped = jnp.tanh(
        jnp.einsum("qjd,kd->jqk", query_split, keys, precision=PRECISE) * (root / SCORE_CAP)
    )
    causal = jnp.arange(length)[:, None] >= jnp.arange(length)[None, :]
    weights = jnp.where(causal, jnp.exp(SCORE_CAP * capped), 0.0)
    probabilities = weights / jnp.sum(weights, axis=-1, keepdims=True)
    context_split = jnp.einsum("jqk,kd->qjd", probabilities, values, precision=PRECISE)
    context = context_split.reshape(length, query_cols)
    context_low = dot_entire(down_output, context, 1, 1)
    low_upper, low_lower = two_halves(ADAPTER_SCALE * context_low)
    out_terms = dot_halved(context.astype(jnp.bfloat16), output_weight, 1, 0) + dot_halved(
        jnp.concatenate([low_upper, low_lower], 0),
        jnp.concatenate([adapter_up_output, adapter_up_output], 0),
        0,
        0,
    )
    out_pieces = lax.all_to_all(
        out_terms.astype(jnp.bfloat16).reshape(shards, part_length, width), "tensor", 0, 0
    )
    resid_own = hidden[0].astype(jnp.float32) + jnp.sum(out_pieces.astype(jnp.float32), 0)
    resid = gather_by_exchange(resid_own.astype(jnp.bfloat16), "tensor").reshape(length, width)

    side = jnp.concatenate([adapter_up_output, head_rows, jnp.zeros((11, width), head.dtype)], 0)
    factors, narrow, rewards, repeated = cotangents(
        lens,
        resid,
        output_weight,
        side,
        query,
        keys,
        values,
        probabilities,
        capped,
        context,
        low.T,
        ADAPTER_SCALE * context_low,
        down_output,
        adapter_up_query,
        adapter_up_key_value,
    )
    factors = lax.all_to_all(factors.reshape(shards, 8 * OBJ, length), "tensor", 0, 0)
    payload = jacobian(factors, tokens, resid, side, repeated, narrow)
    spread = lax.all_to_all(payload, "dp", 0, 0)
    jac = (
        spread[:, : PIECES * OBJ]
        .reshape(groups, PIECES, OBJ, LANES)
        .transpose(0, 2, 1, 3)
        .reshape(groups * OBJ, PIECES * LANES)
    )

    own_a = lax.dynamic_slice(
        jnp.transpose(initial_down_qkv, (0, 2, 1)).reshape(3, 2, shards, width),
        (0, 0, tensor_rank, group_rank * LANES),
        (3, 2, 1, LANES),
    ).reshape(3, 2, LANES)
    own_bo = lax.dynamic_slice(
        initial_up_output.reshape(2, shards, width),
        (0, tensor_rank, group_rank * LANES),
        (2, 1, LANES),
    ).reshape(2, LANES)
    own_bq = lax.dynamic_slice(
        initial_up_query, (group_rank, tensor_rank * query_cols), (1, query_cols)
    )
    own_ao = lax.dynamic_slice(
        initial_down_output.T, (group_rank, tensor_rank * query_cols), (1, query_cols)
    )
    own_bkv = lax.dynamic_slice(
        initial_up_key_value, (0, group_rank, tensor_rank * HEAD_SIZE), (2, 1, HEAD_SIZE)
    )
    own_start = jnp.concatenate(
        [
            jnp.concatenate([own_a.transpose(1, 0, 2), own_bo[:, None]], 1).reshape(8, LANES),
            own_bq,
            own_ao,
            jnp.concatenate(
                [own_bkv.reshape(1, 2 * HEAD_SIZE), jnp.zeros((1, LANES - 2 * HEAD_SIZE))], 1
            ),
        ],
        0,
    ).reshape(1, PIECES * LANES)
    own_start = own_start.astype(jnp.float32)
    sequences = jnp.arange(groups)
    leads = sequences < partner
    order = jnp.sum((sequences[None, :] < sequences[:, None]) & leads[None, :], 1)
    chosen = (
        leads[None, :] & (order[None, :] == jnp.arange(groups // 2)[:, None])
    ).astype(jnp.float32)
    differences = chosen - jnp.take(chosen, partner, axis=1)
    pairs = (
        differences[:, None, :, None] * jnp.eye(OBJ, dtype=jnp.float32)[None, :, None, :]
    ).reshape(PAIR_ROWS, groups * OBJ)
    pairs = jnp.pad(pairs, ((0, PACK_ROWS - PAIR_ROWS), (0, 128 - groups * OBJ)))
    packed = pl.pallas_call(
        gram_body,
        in_specs=[pl.BlockSpec(memory_space=pltpu.SMEM)] + whole(4),
        out_specs=pl.BlockSpec(memory_space=pltpu.VMEM),
        out_shape=jax.ShapeDtypeStruct((16, 128), jnp.float32),
        compiler_params=pltpu.CompilerParams(vmem_limit_bytes=32 * 2**20),
        name="gram",
    )(
        jnp.stack([group_rank, tensor_rank]).astype(jnp.int32),
        jac,
        own_start,
        pairs,
        rewards,
    )
    packed = jnp.sum(gather_by_exchange(packed, "dp"), 0)
    packed = gather_by_exchange(packed, "tensor")
    own_result, part = pl.pallas_call(
        lanczos_body,
        in_specs=whole(3),
        out_specs=whole(2),
        out_shape=[
            jax.ShapeDtypeStruct((8, RESULT_LANES), jnp.bfloat16),
            jax.ShapeDtypeStruct((1, 128), jnp.float32),
        ],
        compiler_params=pltpu.CompilerParams(vmem_limit_bytes=32 * 2**20),
        name="lanczos",
    )(packed, pairs, jac)
    every = lax.all_to_all(
        jnp.broadcast_to(own_result[None], (groups * shards,) + own_result.shape),
        ("dp", "tensor"),
        0,
        0,
    )
    next_a, next_bq, next_bkv, next_ao, next_bo = assemble(
        part,
        every,
        jnp.transpose(initial_down_qkv, (0, 2, 1)),
        initial_up_query,
        initial_up_key_value,
        initial_down_output.T,
        initial_up_output,
    )
    return jnp.transpose(next_a, (0, 2, 1)), next_bq, next_bkv, next_ao.T, next_bo


def solution(mesh):
    in_specs = (
        P("dp", "tensor", None),
        P(None, "tensor"),
        P(None, None, "tensor"),
        P("tensor", None),
        P(),
        P("dp"),
        P(),
        P(),
        P(None, "tensor"),
        P(None, None, "tensor"),
        P("tensor", None),
        P(),
        P(),
        P(),
        P(),
        P(),
        P(),
    )
    out_specs = (P(), P(), P(), P(), P())
    return jax.shard_map(local, mesh=mesh, in_specs=in_specs, out_specs=out_specs, check_vma=False)
```

time: 288 us -> 247 us (0.86)
  waiting for transfers between devices: 134 us -> 86.2 us
  blocking collectives: 0 us -> 47 us
  Pallas kernels: 0 us -> 24.1 us
  matrix products: 39.5 us -> 17.1 us
  other arithmetic: 24 us -> 8.27 us
  starting transfers between devices: 44 us -> 30.7 us
  local copies, waits for them, and re-layouts: 37.3 us -> 29.8 us
  between operations: 7.84 us -> 1.81 us
    all_to_all x0 -> x3, blocking collectives: none -> 47 us  [the longest x1 28.2 us: local(): lax.all_to_all(jnp.broadcast_to(own_result[None], (groups * shards,) + ow...]
    all_to_all x2 -> x1, waiting for transfers between devices: 29.9 us -> 5.07 us  [local(): lax.all_to_all(factors.reshape(shards, 8 * OBJ, length), 'tensor', 0, 0)]
    pallas_call x0 -> x5, Pallas kernels: none -> 24.1 us  [the longest x1 11.3 us: cotangents(): pl.pallas_call(cotangents_body, grid=(width // COT_CHUNK,), in_specs=[pl....]
    all_to_all x4 -> x2, waiting for transfers between devices: 64.1 us -> 49.9 us  [gather_by_exchange(): return lax.all_to_all(copies, axis, 0, 0)]
    unnamed x72 -> x84, local copies, waits for them, and re-layouts: 4.87 us -> 17.2 us
    dot_general x14 -> x6, matrix products: 25.4 us -> 13.8 us  [dot_halved(): lax.dot_general(left_side, right_side, (((left_dim,), (right_dim,)), ((),...]
    dot_general x10 -> x0, matrix products: 10.8 us -> none  [the longest x1 2.31 us: local(): jnp.einsum('ojqk,kd->oqjd', cot_score, keys, precision=PRECISE)]
    add x6 -> x0, other arithmetic: 8.69 us -> none  [the longest x1 2.71 us: local(): jnp.transpose(wide[:3], (0, 2, 1)) + start_part * initial_down_qkv]
  transfers between devices with their start and end apart: 8 -> 5, of which waited for: 8 -> 5; matrix products, arithmetic and copies ran while one was open for 3% -> 5% of each run, Pallas kernels for 0% -> 0%
where the time goes in v2:
time: 247 us; the launch traced here: 245 us
  waiting for transfers between devices  86.2 us (35%)
  blocking collectives  47 us (19%)
  starting transfers between devices  30.7 us (12%)
  local copies, waits for them, and re-layouts  29.8 us (12%)
  Pallas kernels  24.1 us (10%)
  matrix products  17.1 us (7%)
  other arithmetic  8.27 us (3%)
    all_to_all x2, waiting for transfers between devices, gather_by_exchange(): return lax.all_to_all(copies, axis, 0, 0)  49.9 us
    all_to_all x1, blocking collectives, local(): lax.all_to_all(jnp.broadcast_to(own_result[None], (groups * shards,) + ow...  28.2 us
    all_to_all x2, blocking collectives, gather_by_exchange(): return lax.all_to_all(copies, axis, 0, 0)  18.8 us
    all_to_all x1, waiting for transfers between devices, local(): lax.all_to_all(out_terms.astype(jnp.bfloat16).reshape(shards, part_length...  17.9 us
    unnamed x84, local copies, waits for them, and re-layouts  17.2 us
    dot_general x6, matrix products, dot_halved(): lax.dot_general(left_side, right_side, (((left_dim,), (right_dim,)), ((),...  13.8 us
    all_to_all x2, starting transfers between devices, gather_by_exchange(): return lax.all_to_all(copies, axis, 0, 0)  13.8 us
    all_to_all x1, waiting for transfers between devices, local(): spread = lax.all_to_all(payload, 'dp', 0, 0)  13.3 us
  transfers between devices with their start and end apart: 5, of which 5 were waited for; matrix products, arithmetic and copies ran while one was open for 5% of the time, Pallas kernels for 0%

profile of v2, /device:TPU:1, one launch (start us, length us, event | category | flops | bytes accessed | tf_op | source)
XLA Modules:
  0.0 245.0 jit_solution(6340789859802718532)
XLA Ops:
  0.6 2.6 %broadcast_in_dim.37 = bf16[8,16,8192]{2,1,0:T(8,128)(2,1)} broadcast(bf16[16,8192]{1,0:T(8,128)(2,1)} %bitcast.125), dimensions={1,2} | broadcast | bytes 2359296 | tf_op jit(solution)/shard_map/broadcast_in_dim | solution.py:60
  3.2 8.5 %all-to-all-start = ((bf16[8,16,8192]{2,1,0:T(8,128)(2,1)}), bf16[8,16,8192]{2,1,0:T(8,128)(2,1)S(1)}, u32[]{:S(2)}, u32[]{:S(2)}) async-start(bf16[8,16,8192]{2,1,0:T(8,128)(2,1)} %broadcast_in_dim.37), calls=%async_computation | async-start | bytes 4194304 | tf_op jit(solution)/shard_map/all_to_all | solution.py:61
  11.8 26.1 %all-to-all-done = bf16[8,16,8192]{2,1,0:T(8,128)(2,1)S(1)} async-done(((bf16[8,16,8192]{2,1,0:T(8,128)(2,1)}), bf16[8,16,8192]{2,1,0:T(8,128)(2,1)S(1)}, u32[]{:S(2)}, u32[]{:S(2)}) %all-to-all-start) | async-done | bytes 2097184 | tf_op jit(solution)/shard_map/all_to_all | solution.py:61
  37.9 0.8 fusion.47
  39.3 4.8 %fusion.48 = f32[128,512]{1,0:T(8,128)S(1)} fusion(bf16[128,8192]{1,0:T(8,128)(2,1)S(1)} %bitcast.106, bf16[8192,512]{1,0:T(8,128)(2,1)} %param.18), kind=kOutput, calls=%fused_computation.79 | convolution fusion | flops 1073741824 | bytes 10747904 | tf_op jit(solution)/shard_map/dot_general | solution.py:24
  44.1 0.7 fusion.13.keys_ref
  44.8 0.7 fusion.10.values_ref
  47.5 1.6 reduce-precision_convert_fusion
  49.0 4.7 %fusion.25 = f32[128,8192]{1,0:T(8,128)S(1)} fusion(bf16[512,8192]{1,0:T(8,128)(2,1)} %weight_ref.1, f32[128,512]{1,0:T(8,128)S(1)} %copy.53.context_ref), kind=kOutput, calls=%fused_computation.34 | convolution fusion | flops 1073807360 | bytes 12845056 | tf_op jit(solution)/shard_map/dot_general | solution.py:24
  53.7 2.0 fusion
  55.8 5.3 %all-to-all-start.1 = ((bf16[8,16,8192]{2,1,0:T(8,128)(2,1)}), bf16[8,16,8192]{2,1,0:T(8,128)(2,1)}, u32[]{:S(2)}, u32[]{:S(2)}) async-start(bf16[8,16,8192]{2,1,0:T(8,128)(2,1)} %bitcast.119), calls=%async_computation.1 | async-start | bytes 4194304 | tf_op jit(solution)/shard_map/all_to_all | solution.py:569
  61.1 1.0 constant_dynamic-slice_fusion.1
  62.1 0.8 constant_dynamic-slice_fusion
  63.6 1.3 dynamic_slice.17
  64.9 1.4 dynamic-slice_bitcast_fusion.1
  66.3 1.4 dynamic-slice_bitcast_fusion
  69.4 17.9 %all-to-all-done.1 = bf16[8,16,8192]{2,1,0:T(8,128)(2,1)} async-done(((bf16[8,16,8192]{2,1,0:T(8,128)(2,1)}), bf16[8,16,8192]{2,1,0:T(8,128)(2,1)}, u32[]{:S(2)}, u32[]{:S(2)}) %all-to-all-start.1) | async-done | bytes 2097184 | tf_op jit(solution)/shard_map/all_to_all | solution.py:569
  87.4 1.9 convert_reduce_fusion
  89.3 1.0 fusion.20
  90.3 1.5 broadcast_in_dim.41
  91.9 5.3 %all-to-all-start.2 = ((bf16[8,16,8192]{2,1,0:T(8,128)(2,1)}), bf16[8,16,8192]{2,1,0:T(8,128)(2,1)}, u32[]{:S(2)}, u32[]{:S(2)}) async-start(bf16[8,16,8192]{2,1,0:T(8,128)(2,1)} %broadcast_in_dim.41), calls=%async_computation.2 | async-start | bytes 4194304 | tf_op jit(solution)/shard_map/all_to_all | solution.py:61
  98.6 1.1 fusion.17.side_ref
  99.7 23.8 %all-to-all-done.2 = bf16[8,16,8192]{2,1,0:T(8,128)(2,1)} async-done(((bf16[8,16,8192]{2,1,0:T(8,128)(2,1)}), bf16[8,16,8192]{2,1,0:T(8,128)(2,1)}, u32[]{:S(2)}, u32[]{:S(2)}) %all-to-all-start.2) | async-done | bytes 2097184 | tf_op jit(solution)/shard_map/all_to_all | solution.py:61
  123.5 3.4 %copy-done.1 = bf16[512,8192]{1,0:T(8,128)(2,1)S(1)} copy-done((bf16[512,8192]{1,0:T(8,128)(2,1)S(1)}, bf16[512,8192]{1,0:T(8,128)(2,1)}, u32[]{:S(2)}) %copy-start.1) | copy-done | bytes 8388632
  126.8 0.9 copy-done.4
  127.8 0.9 copy-done.6
  128.7 0.9 copy-done.8
  129.7 0.9 copy-done.10
  130.6 0.7 copy-done.18
  131.4 0.8 copy-done.21
  133.5 11.3 %cotangents.1 = (f32[320,128]{1,0:T(8,128)S(1)}, f32[4,256,128]{2,1,0:T(8,128)S(1)}, f32[8,128]{1,0:T(8,128)S(1)}, f32[2,40,128]{2,1,0:T(8,128)S(1)}) custom-call(s32[1]{0:T(128)S(6)} %copy.67.lens_ref, bf16[128,8192]{1,0:T(8,128)(2,1)} %bitcast.20.resid_ref, bf16[512,8192]{1,0:T(8,128)(2,1)S(1)} %copy-done.1, bf16[32,8192]{1,0:T(8,128)(2,1)S(1)} %fusion.17.side_ref, ...), custom_call_target="tpu_custom_call" | custom-call | tf_op jit(solution)/shard_map/cotangents/pallas_call | solution.py:418
  144.9 0.8 copy-done.13
  147.5 5.2 %all-to-all-start.3 = ((f32[8,40,128]{2,1,0:T(8,128)}), f32[8,40,128]{2,1,0:T(8,128)}, u32[]{:S(2)}, u32[]{:S(2)}) async-start(f32[8,40,128]{2,1,0:T(8,128)} %bitcast.117), calls=%async_computation.3 | async-start | bytes 327680 | tf_op jit(solution)/shard_map/all_to_all | solution.py:593
  153.4 0.8 copy.58
  154.1 0.7 convert_reduce_fusion.1
  154.9 5.1 %all-to-all-done.3.factors_ref = f32[8,40,128]{2,1,0:T(8,128)} async-done(((f32[8,40,128]{2,1,0:T(8,128)}), f32[8,40,128]{2,1,0:T(8,128)}, u32[]{:S(2)}, u32[]{:S(2)}) %all-to-all-start.3) | async-done | bytes 163872 | tf_op jit(solution)/shard_map/all_to_all | solution.py:593
  159.9 1.0 copy-done.14
  161.0 0.8 copy-done.24
  161.8 5.7 %jacobian.1 = bf16[16,56,512]{2,1,0:T(8,128)(2,1)S(1)} custom-call(f32[8,40,128]{2,1,0:T(8,128)} %all-to-all-done.3.factors_ref, bf16[128,8192]{1,0:T(8,128)(2,1)S(1)} %bitcast.109, bf16[128,8192]{1,0:T(8,128)(2,1)} %bitcast.20.resid_ref, bf16[32,8192]{1,0:T(8,128)(2,1)S(1)} %fusion.17.side_ref, f32[2,40,128]{2,1,0:T(8,128)S(1)} %copy-done.24, ...), custom_call_target="tpu_custom_call" | custom-call | tf_op jit(solution)/shard_map/jacobian/pallas_call | solution.py:469
  167.5 0.9 copy-done.2
  168.4 6.4 %all-to-all-start.4 = ((bf16[16,56,512]{2,1,0:T(8,128)(2,1)}), bf16[16,56,512]{2,1,0:T(8,128)(2,1)S(1)}, u32[]{:S(2)}, u32[]{:S(2)}) async-start(bf16[16,56,512]{2,1,0:T(8,128)(2,1)} %copy-done.2), calls=%async_computation.4 | async-start | bytes 1835008 | tf_op jit(solution)/shard_map/all_to_all | solution.py:595
  175.9 13.3 %all-to-all-done.4 = bf16[16,56,512]{2,1,0:T(8,128)(2,1)S(1)} async-done(((bf16[16,56,512]{2,1,0:T(8,128)(2,1)}), bf16[16,56,512]{2,1,0:T(8,128)(2,1)S(1)}, u32[]{:S(2)}, u32[]{:S(2)}) %all-to-all-start.4) | async-done | bytes 917536 | tf_op jit(solution)/shard_map/all_to_all | solution.py:595
  190.6 1.6 gram.1
  192.2 9.3 %all_to_all.40 = f32[16,16,128]{2,1,0:T(8,128)S(1)} all-to-all(f32[16,16,128]{2,1,0:T(8,128)S(1)} %broadcast_in_dim.78), channel_id=1, replica_groups=mesh['dp'=16,'tensor'=8] {'dp'}, dimensions={0} | all-to-all | bytes 262144 | tf_op jit(solution)/shard_map/all_to_all | solution.py:61
  201.5 9.6 %all_to_all.41.packed_ref = f32[8,16,128]{2,1,0:T(8,128)S(1)} all-to-all(f32[8,16,128]{2,1,0:T(8,128)S(1)} %broadcast_in_dim.79), channel_id=1, replica_groups=mesh['dp'=16,'tensor'=8] {'tensor'}, dimensions={0} | all-to-all | bytes 131072 | tf_op jit(solution)/shard_map/all_to_all | solution.py:61
  211.1 0.9 lanczos.1
  212.2 28.2 %all_to_all.42.every_ref = bf16[128,8,768]{2,1,0:T(8,128)(2,1)S(1)} all-to-all(bf16[128,8,768]{2,1,0:T(8,128)(2,1)S(1)} %broadcast_in_dim.80), channel_id=1, replica_groups=mesh['dp'=16,'tensor'=8] {'dp','tensor'}, dimensions={0} | all-to-all | bytes 3145728 | tf_op jit(solution)/shard_map/all_to_all | solution.py:672
  240.4 4.6 %assemble.1 = (f32[3,16,8192]{2,1,0:T(8,128)}, f32[16,4096]{1,0:T(8,128)}, f32[2,16,1024]{2,1,0:T(8,128)}, f32[16,4096]{1,0:T(8,128)}, f32[16,8192]{1,0:T(8,128)}) custom-call(f32[1,128]{1,0:T(1,128)S(1)} %get-tuple-element.20.part_ref, bf16[128,8,768]{2,1,0:T(8,128)(2,1)S(1)} %all_to_all.42.every_ref, f32[3,16,8192]{2,1,0:T(8,128)S(1)} %bitcast.113, ...), custom_call_target="tpu_custom_call" | custom-call | tf_op jit(solution)/shard_map/assemble/pallas_call | solution.py:489
  (105 shorter events, 12.1 us)
Async XLA Ops:
  0.6 37.2 %copy-start = (bf16[3,8192,16]{1,2,0:T(8,128)(2,1)S(1)}, bf16[3,8192,16]{1,2,0:T(8,128)(2,1)}, u32[]{:S(2)}) copy-start(bf16[3,8192,16]{1,2,0:T(8,128)(2,1)} %param.24) | copy-start | bytes 2359300
  3.2 34.6 %all-to-all-start = ((bf16[8,16,8192]{2,1,0:T(8,128)(2,1)}), bf16[8,16,8192]{2,1,0:T(8,128)(2,1)S(1)}, u32[]{:S(2)}, u32[]{:S(2)}) async-start(bf16[8,16,8192]{2,1,0:T(8,128)(2,1)} %broadcast_in_dim.37), calls=%async_computation | async-start | bytes 4194304 | tf_op jit(solution)/shard_map/all_to_all | solution.py:61
  11.7 27.0 %copy-start.25 = (bf16[2,16,128]{2,1,0:T(8,128)(2,1)S(1)}, bf16[2,16,128]{2,1,0:T(8,128)(2,1)}, u32[]{:S(2)}) copy-start(bf16[2,16,128]{2,1,0:T(8,128)(2,1)} %up_kv_ref.1) | copy-start | bytes 24580
  38.7 6.9 %copy-start.17 = (f32[128,48]{0,1:T(8,128)}, f32[128,48]{0,1:T(8,128)S(1)}, u32[]{:S(2)}) copy-start(f32[128,48]{0,1:T(8,128)S(1)} %fusion.47) | copy-start | bytes 73732
  39.2 4.8 %copy-start.38 = (bf16[2,8192,128]{2,1,0:T(8,128)(2,1)S(1)}, bf16[2,8192,128]{2,1,0:T(8,128)(2,1)}, u32[]{:S(2)}) copy-start(bf16[2,8192,128]{2,1,0:T(8,128)(2,1)} %param.19) | copy-start | bytes 12582916
  44.8 0.8 copy-start.22
  45.9 1.1 copy-start.5
  46.4 0.7 copy-start.7
  46.6 0.7 copy-start.9
  47.4 6.3 %copy-start.3 = (f32[128,512]{1,0:T(8,128)}, f32[128,512]{1,0:T(8,128)S(1)}, u32[]{:S(2)}) copy-start(f32[128,512]{1,0:T(8,128)S(1)} %copy.53.context_ref) | copy-start | bytes 786436
  49.0 4.7 %copy-start.30 = (bf16[16,8192]{1,0:T(8,128)(2,1)S(1)}, bf16[16,8192]{1,0:T(8,128)(2,1)}, u32[]{:S(2)}) copy-start(bf16[16,8192]{1,0:T(8,128)(2,1)} %param.28) | copy-start | bytes 786436
  55.8 11.9 %copy-start.39 = (s32[16]{0:T(128)S(1)}, s32[16]{0:T(128)}, u32[]{:S(2)}) copy-start(s32[16]{0:T(128)} %param.23) | copy-start | bytes 196
  55.8 13.1 %copy-start.31 = (bf16[512,16]{0,1:T(8,128)(2,1)S(1)}, bf16[512,16]{0,1:T(8,128)(2,1)}, u32[]{:S(2)}) copy-start(bf16[512,16]{0,1:T(8,128)(2,1)} %param.27) | copy-start | bytes 49156
  55.8 31.6 %all-to-all-start.1 = ((bf16[8,16,8192]{2,1,0:T(8,128)(2,1)}), bf16[8,16,8192]{2,1,0:T(8,128)(2,1)}, u32[]{:S(2)}, u32[]{:S(2)}) async-start(bf16[8,16,8192]{2,1,0:T(8,128)(2,1)} %bitcast.119), calls=%async_computation.1 | async-start | bytes 4194304 | tf_op jit(solution)/shard_map/all_to_all | solution.py:569
  91.8 5.3 %copy-start.32 = (f32[8,512]{1,0:T(8,128)S(1)}, f32[8,512]{1,0:T(8,128)}, u32[]{:S(2)}) copy-start(f32[8,512]{1,0:T(8,128)} %reshape.135) | copy-start | bytes 49156
  91.8 5.3 %copy-start.33 = (f32[1,512]{1,0:T(1,128)S(1)}, f32[1,512]{1,0:T(1,128)}, u32[]{:S(2)}) copy-start(f32[1,512]{1,0:T(1,128)} %dynamic_slice.17) | copy-start | bytes 6148
  91.8 5.4 %copy-start.34 = (f32[1,512]{1,0:T(1,128)S(1)}, f32[1,512]{1,0:T(1,128)}, u32[]{:S(2)}) copy-start(f32[1,512]{1,0:T(1,128)} %dynamic-slice_bitcast_fusion) | copy-start | bytes 6148
  91.8 5.4 %copy-start.35 = (f32[1,256]{1,0:T(1,128)S(1)}, f32[1,256]{1,0:T(1,128)}, u32[]{:S(2)}) copy-start(f32[1,256]{1,0:T(1,128)} %dynamic-slice_bitcast_fusion.1) | copy-start | bytes 3076
  91.9 31.6 %all-to-all-start.2 = ((bf16[8,16,8192]{2,1,0:T(8,128)(2,1)}), bf16[8,16,8192]{2,1,0:T(8,128)(2,1)}, u32[]{:S(2)}, u32[]{:S(2)}) async-start(bf16[8,16,8192]{2,1,0:T(8,128)(2,1)} %broadcast_in_dim.41), calls=%async_computation.2 | async-start | bytes 4194304 | tf_op jit(solution)/shard_map/all_to_all | solution.py:61
  123.5 3.4 %copy-start.1 = (bf16[512,8192]{1,0:T(8,128)(2,1)S(1)}, bf16[512,8192]{1,0:T(8,128)(2,1)}, u32[]{:S(2)}) copy-start(bf16[512,8192]{1,0:T(8,128)(2,1)} %weight_ref.1) | copy-start | bytes 25165828
  126.8 0.9 copy-start.4
  127.8 0.9 copy-start.6
  128.7 0.9 copy-start.8
  129.7 0.9 copy-start.10
  130.6 0.7 copy-start.18
  131.4 0.8 copy-start.21
  132.1 0.7 copy-start.26
  132.8 0.7 copy-start.27
  144.9 0.8 copy-start.13
  145.7 0.7 copy-start.19
  146.3 0.6 copy-start.23
  146.9 0.6 copy-start.28
  147.5 12.4 %all-to-all-start.3 = ((f32[8,40,128]{2,1,0:T(8,128)}), f32[8,40,128]{2,1,0:T(8,128)}, u32[]{:S(2)}, u32[]{:S(2)}) async-start(f32[8,40,128]{2,1,0:T(8,128)} %bitcast.117), calls=%async_computation.3 | async-start | bytes 327680 | tf_op jit(solution)/shard_map/all_to_all | solution.py:593
  159.9 1.0 copy-start.14
  161.0 0.8 copy-start.24
  161.8 13.0 %copy-start.36 = (pred[16]{0:T(512)(128)(4,1)S(1)}, pred[16]{0:T(512)(128)(4,1)}, u32[]{:S(2)}) copy-start(pred[16]{0:T(512)(128)(4,1)} %get-tuple-element.30) | copy-start | bytes 52
  161.8 13.6 %copy-start.37 = (pred[16]{0:T(512)(128)(4,1)S(1)}, pred[16]{0:T(512)(128)(4,1)}, u32[]{:S(2)}) copy-start(pred[16]{0:T(512)(128)(4,1)} %get-tuple-element.29) | copy-start | bytes 52
  167.4 0.9 copy-start.2
  168.4 20.8 %all-to-all-start.4 = ((bf16[16,56,512]{2,1,0:T(8,128)(2,1)}), bf16[16,56,512]{2,1,0:T(8,128)(2,1)S(1)}, u32[]{:S(2)}, u32[]{:S(2)}) async-start(bf16[16,56,512]{2,1,0:T(8,128)(2,1)} %copy-done.2), calls=%async_computation.4 | async-start | bytes 1835008 | tf_op jit(solution)/shard_map/all_to_all | solution.py:595
  189.5 1.1 copy-start.29
  212.0 28.3 %copy-start.11 = (f32[3,8192,16]{1,2,0:T(8,128)S(1)}, f32[3,8192,16]{1,2,0:T(8,128)}, u32[]{:S(2)}) copy-start(f32[3,8192,16]{1,2,0:T(8,128)} %param.29) | copy-start | bytes 4718596
  212.0 28.3 %copy-start.12 = (f32[16,8192]{1,0:T(8,128)S(1)}, f32[16,8192]{1,0:T(8,128)}, u32[]{:S(2)}) copy-start(f32[16,8192]{1,0:T(8,128)} %bo_ref.1) | copy-start | bytes 1572868
  212.0 28.3 %copy-start.15 = (f32[4096,16]{0,1:T(8,128)S(1)}, f32[4096,16]{0,1:T(8,128)}, u32[]{:S(2)}) copy-start(f32[4096,16]{0,1:T(8,128)} %param.32) | copy-start | bytes 786436
  212.0 28.3 %copy-start.16 = (f32[16,4096]{1,0:T(8,128)S(1)}, f32[16,4096]{1,0:T(8,128)}, u32[]{:S(2)}) copy-start(f32[16,4096]{1,0:T(8,128)} %bq_ref.1) | copy-start | bytes 786436
  212.0 28.3 %copy-start.20 = (f32[2,16,1024]{2,1,0:T(8,128)S(1)}, f32[2,16,1024]{2,1,0:T(8,128)}, u32[]{:S(2)}) copy-start(f32[2,16,1024]{2,1,0:T(8,128)} %bkv_ref.1) | copy-start | bytes 393220

commit v3 on v2

--- a/solution.py
+++ b/solution.py
@@ -36,22 +36,6 @@
         (((left_dim,), (right_dim,)), ((), ())),
         precision=PRECISE,
         preferred_element_type=jnp.float32,
-    )
-
-
-def two_halves(entire):
-    upper = lax.reduce_precision(entire, 8, 7)
-    return upper.astype(jnp.bfloat16), (entire - upper).astype(jnp.bfloat16)
-
-
-def three_halves(entire):
-    upper = lax.reduce_precision(entire, 8, 7)
-    rest = entire - upper
-    middle = lax.reduce_precision(rest, 8, 7)
-    return (
-        upper.astype(jnp.bfloat16),
-        middle.astype(jnp.bfloat16),
-        (rest - middle).astype(jnp.bfloat16),
     )
 
 
@@ -232,22 +216,315 @@
     return [pl.BlockSpec(memory_space=pltpu.VMEM)] * count
 
 
-def dot_parts(left_parts, right_parts, left_dim, right_dim):
-    total = None
-    for left_at, left_part in enumerate(left_parts):
-        for right_at, right_part in enumerate(right_parts):
-            if left_at + right_at < 2:
-                term = dot_halved(left_part, right_part, left_dim, right_dim)
-                total = term if total is None else total + term
-    return total
-
-
-COT_CHUNK = 2048
+def product(left, right, right_dim):
+    left_both = jnp.concatenate(rounded_parts(left, 2), 1)
+    upper, lower = rounded_parts(right, 2)
+    if right_dim == 0:
+        rows = jnp.concatenate([upper, lower], 1)
+        both = dot_halved(left_both, jnp.concatenate([rows, rows], 0), 1, 0)
+    else:
+        rows = jnp.concatenate([upper, lower], 0)
+        both = dot_halved(left_both, jnp.concatenate([rows, rows], 1), 1, 1)
+    size = right.shape[1 - right_dim]
+    return both[:, :size] + both[:, size:]
+
+
+def tall(parts):
+    return jnp.concatenate(parts, 0)
+
+
+def flat(parts):
+    return jnp.concatenate(parts, 1)
+
+
+def corners(both, rows, lanes):
+    upper = both[:rows] + both[rows:]
+    return upper[:, :lanes] + upper[:, lanes:]
+
+
+def stack(rows):
+    return tall([rows[:, at : at + 128] for at in range(0, rows.shape[1], 128)])
+
+
+def unstack(rows):
+    return flat([rows[at : at + 128] for at in range(0, rows.shape[0], 128)])
+
+
+def place_shards(spots_ref, whole_ref, shards, first_half):
+    for at in range(6):
+        rows = pl.ds(pl.multiple_of(spots_ref[at] * 16, 16), 16)
+        whole_ref[rows, :] = shards[at][...]
+    for at in range(2):
+        rows = pl.ds(pl.multiple_of(spots_ref[6 + at] * 16, 16), 16)
+        whole_ref[rows, :] = jnp.where(
+            first_half, shards[6 + 2 * at][...], shards[7 + 2 * at][...]
+        )
+
+
+def shard_specs(last_step):
+    half = last_step // 2
+    full = pl.BlockSpec((16, CHUNK), lambda step: (0, jnp.minimum(step, last_step)))
+    early = pl.BlockSpec((16, CHUNK), lambda step: (0, jnp.minimum(step, half)))
+    late = pl.BlockSpec(
+        (16, CHUNK), lambda step: (0, jnp.clip(step - half - 1, 0, last_step - half - 1))
+    )
+    return [full] * 6 + [early, late] * 2
+
+
+def gather_by_relays(block):
+    half = block.shape[1] // 2
+
+    def permute(array, y_step, z_step):
+        pairs = [
+            (at, ((at // 4 + y_step) % 2) * 4 + (at % 4 + z_step) % 4) for at in range(8)
+        ]
+        return lax.ppermute(array, "tensor", pairs)
+
+    across = permute(block, 1, 0)
+    below = permute(block, 0, 1)
+    above = permute(block, 0, 3)
+    across_below = permute(across, 0, 1)
+    across_above = permute(across, 0, 3)
+    far = [permute(below[:, :half], 0, 1), permute(above[:, half:], 0, 3)]
+    across_far = [
+        permute(across_below[:, :half], 0, 1),
+        permute(across_above[:, half:], 0, 3),
+    ]
+    return [block, across, below, above, across_below, across_above] + far + across_far
+
+
+def shard_spots():
+    rank = lax.axis_index("tensor").astype(jnp.int32)
+    y, z = rank // 4 * 4, rank % 4
+    other = 4 - y
+    return jnp.stack(
+        [
+            y + z,
+            other + z,
+            y + (z + 3) % 4,
+            y + (z + 1) % 4,
+            other + (z + 3) % 4,
+            other + (z + 1) % 4,
+            y + (z + 2) % 4,
+            other + (z + 2) % 4,
+        ]
+    )
+
+
+CHUNK = 2048
+
+
+def forward_body(
+    spots_ref,
+    shard_0,
+    shard_1,
+    shard_2,
+    shard_3,
+    shard_4,
+    shard_5,
+    shard_6,
+    shard_7,
+    shard_8,
+    shard_9,
+    query_weight_ref,
+    kv_weight_ref,
+    down_ref,
+    output_weight_ref,
+    up_output_ref,
+    down_output_ref,
+    up_query_ref,
+    up_kv_ref,
+    tokens_ref,
+    out_ref,
+    query_ref,
+    keys_ref,
+    values_ref,
+    prob_ref,
+    capped_ref,
+    context_ref,
+    low_ref,
+    context_low_ref,
+    query_sum,
+    kv_sum,
+    low_sum,
+    halved_ref,
+    halved_low_ref,
+):
+    step = pl.program_id(0)
+    steps = pl.num_programs(0) // 2
+    shards = [
+        shard_0,
+        shard_1,
+        shard_2,
+        shard_3,
+        shard_4,
+        shard_5,
+        shard_6,
+        shard_7,
+        shard_8,
+        shard_9,
+    ]
+
+    @pl.when(step < steps)
+    def _():
+        place_shards(spots_ref, tokens_ref, shards, step < steps // 2)
+        tokens = tokens_ref[...]
+        query = dot_halved(tokens, query_weight_ref[...], 1, 0)
+        kv = dot_halved(tokens, flat([kv_weight_ref[0], kv_weight_ref[1]]), 1, 0)
+        low = dot_halved(down_ref[...], tokens, 1, 1)
+
+        @pl.when(step == 0)
+        def _():
+            query_sum[...] = query
+            kv_sum[...] = kv
+            low_sum[...] = jnp.zeros(low_sum.shape, jnp.float32)
+            low_sum[:48] = low
+
+        @pl.when(step > 0)
+        def _():
+            query_sum[...] += query
+            kv_sum[...] += kv
+            low_sum[:48] += low
+
+    @pl.when(step == steps - 1)
+    def _():
+        low_turned = low_sum[...]
+        low = low_turned.T
+        low_ref[...] = low_turned[:48]
+        root = 1.0 / math.sqrt(HEAD_SIZE)
+
+        def adapted(total, piece, up):
+            parts = rounded_parts(low[:, 16 * piece : 16 * piece + 16], 2)
+            return total + ADAPTER_SCALE * dot_halved(flat(parts), tall([up, up]), 1, 0)
+
+        query = adapted(query_sum[...], 0, up_query_ref[...])
+        keys = adapted(kv_sum[:, :128], 1, up_kv_ref[0])
+        values = adapted(kv_sum[:, 128:], 2, up_kv_ref[1])
+        capped = jnp.tanh(product(stack(query), keys, 1) * (root / SCORE_CAP))
+        row = lax.broadcasted_iota(jnp.int32, (512, 128), 0) % 128
+        lane = lax.broadcasted_iota(jnp.int32, (512, 128), 1)
+        weights = jnp.where(row >= lane, jnp.exp(SCORE_CAP * capped), 0.0)
+        probs = weights / lane_sum(weights)
+        context = unstack(product(probs, values, 0))
+        low_pair = dot_halved(down_output_ref[...], tall(rounded_parts(context, 2)), 1, 1)
+        context_low = ADAPTER_SCALE * (low_pair[:, :128] + low_pair[:, 128:])
+        query_ref[...] = query
+        keys_ref[...] = keys
+        values_ref[...] = values
+        prob_ref[...] = probs
+        capped_ref[...] = capped
+        context_ref[...] = context
+        context_low_ref[...] = context_low
+        halved_ref[...] = context.astype(jnp.bfloat16)
+        turned = tall([context_low, jnp.zeros((112, 128), jnp.float32)]).T[:, :16]
+        halved_low_ref[...] = flat(rounded_parts(turned, 2))
+
+    @pl.when(step >= steps)
+    def _():
+        up = up_output_ref[...]
+        terms = dot_halved(halved_ref[...], output_weight_ref[...], 1, 0) + dot_halved(
+            halved_low_ref[...], tall([up, up]), 1, 0
+        )
+        out_ref[...] = terms.astype(jnp.bfloat16).reshape(out_ref.shape)
+
+
+def fixed(array):
+    zeros = (0,) * array.ndim
+    return pl.BlockSpec(array.shape, lambda step: zeros)
+
+
+def forward(
+    spots,
+    shards,
+    query_weight,
+    key_value_weight,
+    down_rows,
+    output_weight,
+    up_output,
+    down_output,
+    up_query,
+    up_key_value,
+):
+    width = shards[0].shape[1]
+    steps = width // CHUNK
+    last = steps - 1
+    query_cols = query_weight.shape[1]
+
+    def first_part(step):
+        return jnp.minimum(step, last)
+
+    def second_part(step):
+        return jnp.maximum(step - steps, 0)
+
+    shapes = [
+        jax.ShapeDtypeStruct((128, width), jnp.bfloat16),
+        jax.ShapeDtypeStruct((8, 16, width), jnp.bfloat16),
+        jax.ShapeDtypeStruct((128, query_cols), jnp.float32),
+        jax.ShapeDtypeStruct((128, 128), jnp.float32),
+        jax.ShapeDtypeStruct((128, 128), jnp.float32),
+        jax.ShapeDtypeStruct((512, 128), jnp.float32),
+        jax.ShapeDtypeStruct((512, 128), jnp.float32),
+        jax.ShapeDtypeStruct((128, query_cols), jnp.float32),
+        jax.ShapeDtypeStruct((48, 128), jnp.float32),
+        jax.ShapeDtypeStruct((16, 128), jnp.float32),
+    ]
+    return pl.pallas_call(
+        forward_body,
+        grid=(2 * steps,),
+        in_specs=[pl.BlockSpec(memory_space=pltpu.SMEM)]
+        + shard_specs(last)
+        + [
+            pl.BlockSpec((CHUNK, query_cols), lambda step: (first_part(step), 0)),
+            pl.BlockSpec((2, CHUNK, 128), lambda step: (0, first_part(step), 0)),
+            pl.BlockSpec((48, CHUNK), lambda step: (0, first_part(step))),
+            pl.BlockSpec((query_cols, CHUNK), lambda step: (0, second_part(step))),
+            pl.BlockSpec((16, CHUNK), lambda step: (0, second_part(step))),
+            fixed(down_output),
+            fixed(up_query),
+            fixed(up_key_value),
+        ],
+        out_specs=[
+            pl.BlockSpec((128, CHUNK), lambda step: (0, first_part(step))),
+            pl.BlockSpec((8, 16, CHUNK), lambda step: (0, 0, second_part(step))),
+        ]
+        + [fixed(shape) for shape in shapes[2:]],
+        out_shape=shapes,
+        scratch_shapes=[
+            pltpu.VMEM((128, query_cols), jnp.float32),
+            pltpu.VMEM((128, 256), jnp.float32),
+            pltpu.VMEM((128, 128), jnp.float32),
+            pltpu.VMEM((128, query_cols), jnp.bfloat16),
+            pltpu.VMEM((128, 32), jnp.bfloat16),
+        ],
+        compiler_params=pltpu.CompilerParams(vmem_limit_bytes=24 * 2**20),
+        name="forward",
+    )(
+        spots,
+        *shards,
+        query_weight,
+        key_value_weight,
+        down_rows,
+        output_weight,
+        up_output,
+        down_output,
+        up_query,
+        up_key_value,
+    )
 
 
 def cotangents_body(
     lens_ref,
-    resid_ref,
+    spots_ref,
+    shard_0,
+    shard_1,
+    shard_2,
+    shard_3,
+    shard_4,
+    shard_5,
+    shard_6,
+    shard_7,
+    shard_8,
+    shard_9,
     weight_ref,
     side_ref,
     query_ref,
@@ -261,6 +538,7 @@
     down_ref,
     up_query_ref,
     up_kv_ref,
+    resid_ref,
     factors_ref,
     narrow_ref,
     rewards_ref,
@@ -270,9 +548,22 @@
     square_ref,
 ):
     step = pl.program_id(0)
+    shards = [
+        shard_0,
+        shard_1,
+        shard_2,
+        shard_3,
+        shard_4,
+        shard_5,
+        shard_6,
+        shard_7,
+        shard_8,
+        shard_9,
+    ]
+    place_shards(spots_ref, resid_ref, shards, step < pl.num_programs(0) // 2)
     chunk = resid_ref[...]
     side = side_ref[...]
-    left = jnp.concatenate([chunk, side[16:]], 0)
+    left = tall([chunk, side[16:]])
     through = dot_halved(left, weight_ref[...], 1, 1)
     slow = dot_halved(left, side, 1, 1)
     wide = chunk.astype(jnp.float32)
@@ -320,72 +611,66 @@
         low_turned = slow_turned[:16, :128]
         rewards_ref[...] = jnp.zeros(rewards_ref.shape, jnp.float32)
         rewards_ref[:1, :16] = row_sum(share * logits)
-        through = through_ref[...] + ADAPTER_SCALE * dot_entire(
-            slow[:144, :16], down_ref[...], 1, 0
+        down = down_ref[...]
+        through = through_ref[...] + ADAPTER_SCALE * dot_halved(
+            flat(rounded_parts(slow[:144, :16], 2)), tall([down, down]), 1, 0
         )
-
-        def stack(rows):
-            return jnp.concatenate([rows[:, at : at + 128] for at in range(0, 512, 128)], 0)
-
         narrow_ref[...] = jnp.zeros(narrow_ref.shape, jnp.float32)
         context = context_ref[...]
         context_rows = stack(context)
-        probs = prob_ref[...].reshape(512, 128)
-        capped = capped_ref[...].reshape(512, 128)
+        probs = prob_ref[...]
+        capped = capped_ref[...]
         slope = probs * (1.0 - capped * capped) * root
-        probs_turned = rounded_parts(probs.T, 2)
-        query_turned = rounded_parts(stack(query_ref[...]).T, 2)
-        keys = rounded_parts(keys_ref[...], 2)
-        values = rounded_parts(values_ref[...], 2)
-        low = [rounded_parts(low_ref[16 * piece : 16 * piece + 16], 2) for piece in range(3)]
+        probs_turned = tall(rounded_parts(probs.T, 2))
+        query_turned = tall(rounded_parts(stack(query_ref[...]).T, 2))
+        keys = keys_ref[...]
+        values = values_ref[...]
+        low = [tall(rounded_parts(low_ref[16 * at : 16 * at + 16], 2)) for at in range(3)]
         up_query = up_query_ref[...]
         context_low = context_low_ref[...]
         cot_low = []
         for obj in range(OBJ):
             lead_row = through[128 + obj : 129 + obj]
             cot = stack(lead * lead_row - pulled[:, obj : obj + 1] * through[:128])
-            cot_parts = rounded_parts(cot, 2)
-            cot_prob = dot_parts(cot_parts, values, 1, 1)
+            cot_prob = product(cot, values, 1)
             cot_score = slope * (cot_prob - lane_sum(cot * context_rows))
-            score_parts = rounded_parts(cot_score, 2)
-            cot_query = dot_parts(score_parts, keys, 1, 0)
+            cot_query = unstack(product(cot_score, keys, 0))
+            cot_keys = corners(
+                dot_halved(query_turned, flat(rounded_parts(cot_score, 2)), 1, 0), 128, 128
+            )
+            cot_values = corners(
+                dot_halved(probs_turned, flat(rounded_parts(cot, 2)), 1, 0), 128, 128
+            )
             query_parts = rounded_parts(cot_query, 2)
-            keys_parts = rounded_parts(dot_parts(query_turned, score_parts, 1, 0), 2)
-            values_parts = rounded_parts(dot_parts(probs_turned, cot_parts, 1, 0), 2)
-            factor_query = 0.0
-            jac_query = []
-            for at in range(0, 512, 128):
-                block = [part[at : at + 128] for part in query_parts]
-                factor_query += dot_parts([up_query[:, at : at + 128]], block, 1, 1)
-                jac_query.append(dot_parts(low[0], block, 1, 0))
+            keys_parts = rounded_parts(cot_keys, 2)
+            values_parts = rounded_parts(cot_values, 2)
+            factor_query = dot_halved(up_query, tall(query_parts), 1, 1)
+            factor_keys = dot_halved(up_kv_ref[0], flat(keys_parts), 1, 0)
+            factor_values = dot_halved(up_kv_ref[1], tall(values_parts), 1, 1)
             rows = [
-                ADAPTER_SCALE * factor_query,
-                ADAPTER_SCALE * dot_parts([up_kv_ref[0]], keys_parts, 1, 0),
-                ADAPTER_SCALE * dot_parts([up_kv_ref[1]], values_parts, 1, 1),
-                context_low,
-            ]
+                ADAPTER_SCALE * (factor[:, :128] + factor[:, 128:])
+                for factor in (factor_query, factor_keys, factor_values)
+            ] + [context_low]
             for piece in range(4):
                 for half in range(2):
                     factors_ref[pl.ds(20 * half + 5 * piece + obj, 8, stride=40), :] = rows[
                         piece
                     ][8 * half : 8 * half + 8]
-            blocks = jac_query + [
-                dot_parts(low[1], keys_parts, 1, 1),
-                dot_parts(low[2], values_parts, 1, 0),
-            ]
-            spots = [(obj, at) for at in range(0, 512, 128)] + [(10 + obj, 0), (10 + obj, 128)]
-            for (row, at), block in zip(spots, blocks):
+            jac_query = corners(dot_halved(low[0], flat(query_parts), 1, 0), 16, 512)
+            jac_keys = corners(dot_halved(low[1], tall(keys_parts), 1, 1), 16, 128)
+            jac_values = corners(dot_halved(low[2], flat(values_parts), 1, 0), 16, 128)
+            blocks = [jac_query[:, at : at + 128] for at in range(0, 512, 128)]
+            spots = [(obj, 0), (obj, 1), (obj, 2), (obj, 3), (10 + obj, 0), (10 + obj, 1)]
+            for (row, tile), block in zip(spots, blocks + [jac_keys, jac_values]):
                 for half in range(2):
-                    narrow_ref[at // 128, pl.ds(128 * half + row, 8, stride=16), :] = (
+                    narrow_ref[tile, pl.ds(128 * half + row, 8, stride=16), :] = (
                         ADAPTER_SCALE * block[8 * half : 8 * half + 8]
                     )
             cot_low.append(
                 slow_turned[:16, 128 + obj : 129 + obj] * lead_turned
                 - pulled_turned[obj : obj + 1] * low_turned
             )
-        jac_down = ADAPTER_SCALE * dot_parts(
-            rounded_parts(jnp.concatenate(cot_low, 0), 2), rounded_parts(context, 2), 1, 0
-        )
+        jac_down = ADAPTER_SCALE * product(tall(cot_low), context, 0)
         for obj in range(OBJ):
             for half in range(2):
                 start = 16 * obj + 8 * half
@@ -398,18 +683,16 @@
         repeated_ref[1] = jnp.broadcast_to(lead_turned, (40, 128))
 
 
-def cotangents(lens, resid, output_weight, side, *others):
-    length, width = resid.shape
+def cotangents(lens, spots, shards, output_weight, side, *others):
+    width = shards[0].shape[1]
     query_cols = output_weight.shape[0]
+    steps = width // CHUNK
 
     def chunked(rows):
-        return pl.BlockSpec((rows, COT_CHUNK), lambda step: (0, step))
-
-    def fixed(array):
-        zeros = (0,) * array.ndim
-        return pl.BlockSpec(array.shape, lambda step: zeros)
+        return pl.BlockSpec((rows, CHUNK), lambda step: (0, step))
 
     shapes = [
+        jax.ShapeDtypeStruct((128, width), jnp.bfloat16),
         jax.ShapeDtypeStruct((320, 128), jnp.float32),
         jax.ShapeDtypeStruct((4, 256, 128), jnp.float32),
         jax.ShapeDtypeStruct((8, 128), jnp.float32),
@@ -417,24 +700,21 @@
     ]
     return pl.pallas_call(
         cotangents_body,
-        grid=(width // COT_CHUNK,),
-        in_specs=[
-            pl.BlockSpec(memory_space=pltpu.SMEM),
-            chunked(length),
-            chunked(query_cols),
-            chunked(32),
-        ]
+        grid=(steps,),
+        in_specs=[pl.BlockSpec(memory_space=pltpu.SMEM)] * 2
+        + shard_specs(steps - 1)
+        + [chunked(query_cols), chunked(32)]
         + [fixed(array) for array in others],
-        out_specs=[fixed(shape) for shape in shapes],
+        out_specs=[chunked(128)] + [fixed(shape) for shape in shapes[1:]],
         out_shape=shapes,
         scratch_shapes=[
             pltpu.VMEM((144, query_cols), jnp.float32),
             pltpu.VMEM((256, 128), jnp.float32),
             pltpu.VMEM((128, 128), jnp.float32),
         ],
-        compiler_params=pltpu.CompilerParams(vmem_limit_bytes=40 * 2**20),
+        compiler_params=pltpu.CompilerParams(vmem_limit_bytes=20 * 2**20),
         name="cotangents",
-    )(lens, resid, output_weight, side, *others)
+    )(lens, spots, *shards, output_weight, side, *others)
 
 
 def jacobian_body(
@@ -443,26 +723,28 @@
     factors = jnp.sum(factors_ref[...], axis=0)
     row = lax.broadcasted_iota(jnp.int32, (40, 1), 0) % 20
     last = row >= 15
-    left = jnp.concatenate(
-        [jnp.where(last, 0.0, factors), jnp.where(last, -factors * repeated_ref[0], 0.0)], 1
-    )
-    left = rounded_parts(left, 2)
+    left = flat([jnp.where(last, 0.0, factors), jnp.where(last, -factors * repeated_ref[0], 0.0)])
     lane = lax.broadcasted_iota(jnp.int32, (40, 16), 1)
-    lead = rounded_parts(
-        jnp.where(lane == row - 15, lane_sum(factors * repeated_ref[1]), 0.0), 2
-    )
+    lead = jnp.where(lane == row - 15, lane_sum(factors * repeated_ref[1]), 0.0)
+
+    def both(rows):
+        upper = rows.astype(jnp.bfloat16).astype(jnp.float32)
+        return tall([upper, rows - upper]).astype(jnp.bfloat16)
+
+    left = both(left)
+    lead = both(lead)
 
     def place(group, _):
         lanes = pl.ds(pl.multiple_of(group * LANES, LANES), LANES)
-        right = jnp.concatenate([tokens_ref[:, lanes], resid_ref[:, lanes]], 0)
-        rows = dot_parts(left, [right], 1, 0) + dot_parts(lead, [side_ref[16:, lanes]], 1, 0)
-        below = jnp.concatenate(
-            [narrow_ref[tile, pl.ds(pl.multiple_of(group * 16, 16), 16), :] for tile in range(4)], 1
+        right = tall([tokens_ref[:, lanes], resid_ref[:, lanes]])
+        pair = dot_halved(left, right, 1, 0) + dot_halved(lead, side_ref[16:, lanes], 1, 0)
+        below = flat(
+            [narrow_ref[tile, pl.ds(pl.multiple_of(group * 16, 16), 16), :] for tile in range(4)]
         )
-        payload_ref[group] = jnp.concatenate([rows, below], 0).astype(jnp.bfloat16)
+        payload_ref[group] = tall([pair[:40] + pair[40:], below]).astype(jnp.bfloat16)
         return 0
 
-    lax.fori_loop(0, 16, place, 0)
+    lax.fori_loop(0, 16, place, 0, unroll=4)
 
 
 def jacobian(*arrays):
@@ -471,7 +753,7 @@
         in_specs=whole(len(arrays)),
         out_specs=pl.BlockSpec(memory_space=pltpu.VMEM),
         out_shape=jax.ShapeDtypeStruct((16, PIECE_ROWS, LANES), jnp.bfloat16),
-        compiler_params=pltpu.CompilerParams(vmem_limit_bytes=24 * 2**20),
+        compiler_params=pltpu.CompilerParams(vmem_limit_bytes=12 * 2**20),
         name="jacobian",
     )(*arrays)
 
@@ -496,7 +778,7 @@
         + blocks,
         out_specs=blocks,
         out_shape=[jax.ShapeDtypeStruct(shape.shape, jnp.float32) for shape in shapes],
-        compiler_params=pltpu.CompilerParams(vmem_limit_bytes=32 * 2**20),
+        compiler_params=pltpu.CompilerParams(vmem_limit_bytes=14 * 2**20),
         name="assemble",
     )(part, every, start_a, start_bq, start_bkv, start_ao, start_bo)
 
@@ -526,56 +808,42 @@
     tensor_rank = lax.axis_index("tensor")
     group_rank = lax.axis_index("dp")
     query_cols = query_weight.shape[1]
-    heads = query_cols // HEAD_SIZE
     length = part_length * shards
-    root = 1.0 / math.sqrt(HEAD_SIZE)
-
-    down_qkv = jnp.transpose(adapter_down_qkv, (0, 2, 1))
-    down_output = adapter_down_output.T.astype(jnp.float32)
-    up_query = adapter_up_query.astype(jnp.float32)
-    up_key_value = adapter_up_key_value.astype(jnp.float32)
+
+    down_rows = jnp.transpose(adapter_down_qkv, (0, 2, 1)).reshape(48, width)
+    down_output = adapter_down_output.T
     head_rows = head.T
-
-    tokens = gather_by_exchange(hidden[0], "tensor").reshape(length, width)
-
-    low = dot_halved(tokens, down_qkv.reshape(48, width), 1, 1)
-    low_q, low_k, low_v = low[:, :16], low[:, 16:32], low[:, 32:]
-    query = dot_halved(tokens, query_weight, 1, 0) + ADAPTER_SCALE * dot_entire(
-        low_q, up_query, 1, 0
-    )
-    keys = dot_halved(tokens, key_value_weight[0], 1, 0) + ADAPTER_SCALE * dot_entire(
-        low_k, up_key_value[0], 1, 0
-    )
-    values = dot_halved(tokens, key_value_weight[1], 1, 0) + ADAPTER_SCALE * dot_entire(
-        low_v, up_key_value[1], 1, 0
-    )
-    query_split = query.reshape(length, heads, HEAD_SIZE)
-    capped = jnp.tanh(
-        jnp.einsum("qjd,kd->jqk", query_split, keys, precision=PRECISE) * (root / SCORE_CAP)
-    )
-    causal = jnp.arange(length)[:, None] >= jnp.arange(length)[None, :]
-    weights = jnp.where(causal, jnp.exp(SCORE_CAP * capped), 0.0)
-    probabilities = weights / jnp.sum(weights, axis=-1, keepdims=True)
-    context_split = jnp.einsum("jqk,kd->qjd", probabilities, values, precision=PRECISE)
-    context = context_split.reshape(length, query_cols)
-    context_low = dot_entire(down_output, context, 1, 1)
-    low_upper, low_lower = two_halves(ADAPTER_SCALE * context_low)
-    out_terms = dot_halved(context.astype(jnp.bfloat16), output_weight, 1, 0) + dot_halved(
-        jnp.concatenate([low_upper, low_lower], 0),
-        jnp.concatenate([adapter_up_output, adapter_up_output], 0),
-        0,
-        0,
-    )
-    out_pieces = lax.all_to_all(
-        out_terms.astype(jnp.bfloat16).reshape(shards, part_length, width), "tensor", 0, 0
-    )
+    spots = shard_spots()
+    side = jnp.concatenate([adapter_up_output, head_rows, jnp.zeros((11, width), head.dtype)], 0)
+    (
+        tokens,
+        out_terms,
+        query,
+        keys,
+        values,
+        probabilities,
+        capped,
+        context,
+        low,
+        context_low,
+    ) = forward(
+        spots,
+        gather_by_relays(hidden[0]),
+        query_weight,
+        key_value_weight,
+        down_rows,
+        output_weight,
+        adapter_up_output,
+        down_output,
+        adapter_up_query,
+        adapter_up_key_value,
+    )
+    out_pieces = lax.all_to_all(out_terms, "tensor", 0, 0)
     resid_own = hidden[0].astype(jnp.float32) + jnp.sum(out_pieces.astype(jnp.float32), 0)
-    resid = gather_by_exchange(resid_own.astype(jnp.bfloat16), "tensor").reshape(length, width)
-
-    side = jnp.concatenate([adapter_up_output, head_rows, jnp.zeros((11, width), head.dtype)], 0)
-    factors, narrow, rewards, repeated = cotangents(
+    resid, factors, narrow, rewards, repeated = cotangents(
         lens,
-        resid,
+        spots,
+        gather_by_relays(resid_own.astype(jnp.bfloat16)),
         output_weight,
         side,
         query,
@@ -584,8 +852,8 @@
         probabilities,
         capped,
         context,
-        low.T,
-        ADAPTER_SCALE * context_low,
+        low,
+        context_low,
         down_output,
         adapter_up_query,
         adapter_up_key_value,
@@ -647,7 +915,7 @@
         in_specs=[pl.BlockSpec(memory_space=pltpu.SMEM)] + whole(4),
         out_specs=pl.BlockSpec(memory_space=pltpu.VMEM),
         out_shape=jax.ShapeDtypeStruct((16, 128), jnp.float32),
-        compiler_params=pltpu.CompilerParams(vmem_limit_bytes=32 * 2**20),
+        compiler_params=pltpu.CompilerParams(vmem_limit_bytes=6 * 2**20),
         name="gram",
     )(
         jnp.stack([group_rank, tensor_rank]).astype(jnp.int32),
@@ -666,7 +934,7 @@
             jax.ShapeDtypeStruct((8, RESULT_LANES), jnp.bfloat16),
             jax.ShapeDtypeStruct((1, 128), jnp.float32),
         ],
-        compiler_params=pltpu.CompilerParams(vmem_limit_bytes=32 * 2**20),
+        compiler_params=pltpu.CompilerParams(vmem_limit_bytes=6 * 2**20),
         name="lanczos",
     )(packed, pairs, jac)
     every = lax.all_to_all(

time: 247 us -> 247 us (level)
  waiting for transfers between devices: 86.2 us -> 45.8 us
  local copies, waits for them, and re-layouts: 29.8 us -> 60.2 us
  starting transfers between devices: 30.7 us -> 54.7 us
  matrix products: 17.1 us -> 0 us
  Pallas kernels: 24.1 us -> 28.3 us
    all_to_all x3 -> x1, waiting for transfers between devices: 67.8 us -> 20.5 us  [local(): out_pieces = lax.all_to_all(out_terms, 'tensor', 0, 0)]
    ppermute x0 -> x18, starting transfers between devices: none -> 34.9 us  [permute(): return lax.ppermute(array, 'tensor', pairs)]
    unnamed x84 -> x120, local copies, waits for them, and re-layouts: 17.2 us -> 46.5 us
    dot_general x12 -> x0, matrix products: 17.1 us -> none  [the longest x6 13.8 us: dot_halved(): lax.dot_general(left_side, right_side, (((left_dim,), (right_dim,)), ((),...]
    all_to_all x3 -> x1, starting transfers between devices: 19.2 us -> 6.04 us  [local(): out_pieces = lax.all_to_all(out_terms, 'tensor', 0, 0)]
    pallas_call x1 -> x2, Pallas kernels: 11.3 us -> 18.6 us  [the longest x1 9.54 us: cotangents(): pl.pallas_call(cotangents_body, grid=(steps,), in_specs=[pl.BlockSpec(mem...]
    ppermute x0 -> x18, waiting for transfers between devices: none -> 7.12 us  [permute(): return lax.ppermute(array, 'tensor', pairs)]
    slice x0 -> x8, local copies, waits for them, and re-layouts: none -> 4.49 us  [the longest x2 1.58 us: gather_by_relays(): across_below[:, :half]]
  transfers between devices with their start and end apart: 5 -> 21, of which waited for: 5 -> 8; matrix products, arithmetic and copies ran while one was open for 5% -> 8% of each run, Pallas kernels for 0% -> 0%
where the time goes in v3:
time: 247 us; the launch traced here: 245 us
  local copies, waits for them, and re-layouts  60.2 us (24%)
  starting transfers between devices  54.7 us (22%)
  blocking collectives  47 us (19%)
  waiting for transfers between devices  45.8 us (19%)
  Pallas kernels  28.3 us (11%)
  other arithmetic  7.72 us (3%)
    unnamed x120, local copies, waits for them, and re-layouts  46.5 us
    ppermute x18, starting transfers between devices, permute(): return lax.ppermute(array, 'tensor', pairs)  34.9 us
    all_to_all x1, blocking collectives, local(): lax.all_to_all(jnp.broadcast_to(own_result[None], (groups * shards,) + ow...  28.2 us
    all_to_all x1, waiting for transfers between devices, local(): out_pieces = lax.all_to_all(out_terms, 'tensor', 0, 0)  20.5 us
    all_to_all x2, blocking collectives, gather_by_exchange(): return lax.all_to_all(copies, axis, 0, 0)  18.8 us
    all_to_all x1, waiting for transfers between devices, local(): spread = lax.all_to_all(payload, 'dp', 0, 0)  13.3 us
    pallas_call x1, Pallas kernels, cotangents(): pl.pallas_call(cotangents_body, grid=(steps,), in_specs=[pl.BlockSpec(mem...  9.54 us
    all_to_all x1, starting transfers between devices, local(): spread = lax.all_to_all(payload, 'dp', 0, 0)  9.45 us
  transfers between devices with their start and end apart: 21, of which 8 were waited for; matrix products, arithmetic and copies ran while one was open for 8% of the time, Pallas kernels for 0%

profile of v3, /device:TPU:1, one launch (start us, length us, event | category | flops | bytes accessed | tf_op | source)
XLA Modules:
  0.0 245.4 jit_solution(5879207196208792691)
XLA Ops:
  0.6 3.8 %collective-permute-start = (bf16[16,8192]{1,0:T(8,128)(2,1)}, bf16[16,8192]{1,0:T(8,128)(2,1)S(1)}, u32[]{:S(2)}, u32[]{:S(2)}) collective-permute-start(bf16[16,8192]{1,0:T(8,128)(2,1)} %bitcast.53), channel_id=1, source_target_pairs={{0,4},{1,5},{2,6},{3,7},{4,0},{5,1},{6,2},{7,3},{8,12},{9,13},{10,... | collective-permute-start | bytes 786440 | tf_op jit(solution)/shard_map/ppermute | solution.py:281
  4.5 1.6 collective-permute-start.1
  6.1 2.1 collective-permute-start.2
  8.2 2.2 collective-permute-done.shard_1
  10.4 1.6 collective-permute-start.3
  12.1 2.1 collective-permute-start.4
  14.3 2.7 %collective-permute-start.6 = (bf16[16,4096]{1,0:T(8,128)(2,1)S(1)}, bf16[16,4096]{1,0:T(8,128)(2,1)S(1)}, u32[]{:S(2)}, u32[]{:S(2)}) collective-permute-start(bf16[16,4096]{1,0:T(8,128)(2,1)S(1)} %slice.39), channel_id=1, source_target_pairs={{0,3},{1,0},{2,1},{3,2},{4,7},{5,4},{6,5},{7,6},{8,11},{9,8},{10,9... | collective-permute-start | bytes 393224 | tf_op jit(solution)/shard_map/ppermute | solution.py:281
  17.0 2.2 collective-permute-done.3.shard_4
  19.4 2.7 %collective-permute-start.8 = (bf16[16,4096]{1,0:T(8,128)(2,1)S(1)}, bf16[16,4096]{1,0:T(8,128)(2,1)S(1)}, u32[]{:S(2)}, u32[]{:S(2)}) collective-permute-start(bf16[16,4096]{1,0:T(8,128)(2,1)S(1)} %slice.41), channel_id=1, source_target_pairs={{0,3},{1,0},{2,1},{3,2},{4,7},{5,4},{6,5},{7,6},{8,11},{9,8},{10,9... | collective-permute-start | bytes 393224 | tf_op jit(solution)/shard_map/ppermute | solution.py:281
  22.2 1.0 constant_dynamic-slice_fusion.1
  23.9 1.1 collective-permute-done.7.shard_8
  26.3 3.4 %copy-done = bf16[512,8192]{1,0:T(8,128)(2,1)S(1)} copy-done((bf16[512,8192]{1,0:T(8,128)(2,1)S(1)}, bf16[512,8192]{1,0:T(8,128)(2,1)}, u32[]{:S(2)}) %copy-start) | copy-done | bytes 8388632
  29.7 3.4 %copy-done.2 = bf16[8192,512]{1,0:T(8,128)(2,1)S(1)} copy-done((bf16[8192,512]{1,0:T(8,128)(2,1)S(1)}, bf16[8192,512]{1,0:T(8,128)(2,1)}, u32[]{:S(2)}) %copy-start.2) | copy-done | bytes 8388632
  33.0 2.2 copy-done.3
  37.1 1.1 copy-done.12
  43.1 9.0 %forward.1 = (bf16[128,8192]{1,0:T(8,128)(2,1)S(1)}, bf16[8,16,8192]{2,1,0:T(8,128)(2,1)S(1)}, f32[128,512]{1,0:T(8,128)S(1)}, f32[128,128]{1,0:T(8,128)S(1)}, f...) custom-call(s32[8]{0:T(128)S(1)} %stack.47.spots_ref, ...), custom_call_target="tpu_custom_call" | custom-call | tf_op jit(solution)/shard_map/forward/pallas_call | solution.py:471
  52.2 1.3 copy-done.6
  58.8 6.0 %all-to-all-start = ((bf16[8,16,8192]{2,1,0:T(8,128)(2,1)}), bf16[8,16,8192]{2,1,0:T(8,128)(2,1)}, u32[]{:S(2)}, u32[]{:S(2)}) async-start(bf16[8,16,8192]{2,1,0:T(8,128)(2,1)} %copy-done.6), calls=%async_computation | async-start | bytes 4194304 | tf_op jit(solution)/shard_map/all_to_all | solution.py:841
  66.0 20.5 %all-to-all-done = bf16[8,16,8192]{2,1,0:T(8,128)(2,1)} async-done(((bf16[8,16,8192]{2,1,0:T(8,128)(2,1)}), bf16[8,16,8192]{2,1,0:T(8,128)(2,1)}, u32[]{:S(2)}, u32[]{:S(2)}) %all-to-all-start) | async-done | bytes 2097184 | tf_op jit(solution)/shard_map/all_to_all | solution.py:841
  86.5 1.9 convert_reduce_fusion
  88.6 7.2 %collective-permute-start.9 = (bf16[16,8192]{1,0:T(8,128)(2,1)S(1)}, bf16[16,8192]{1,0:T(8,128)(2,1)}, u32[]{:S(2)}, u32[]{:S(2)}) collective-permute-start(bf16[16,8192]{1,0:T(8,128)(2,1)S(1)} %add_convert_fusion.shard_0), channel_id=1, source_target_pairs={{0,4},{1,5},{2,6},{3,7},{4,0},{5,1},{6,2},{7,3},{8,12},{9,13},{10,... | collective-permute-start | bytes 786440 | tf_op jit(solution)/shard_map/ppermute | solution.py:281
  98.0 1.7 collective-permute-start.11
  100.6 1.2 collective-permute-start.12
  101.9 1.4 collective-permute-start.13
  103.3 1.3 dynamic-slice_bitcast_fusion
  104.6 1.3 compare_and_fusion
  107.3 2.6 %collective-permute-start.15 = (bf16[16,4096]{1,0:T(8,128)(2,1)}, bf16[16,4096]{1,0:T(8,128)(2,1)}, u32[]{:S(2)}, u32[]{:S(2)}) collective-permute-start(bf16[16,4096]{1,0:T(8,128)(2,1)} %slice.43), channel_id=1, source_target_pairs={{0,3},{1,0},{2,1},{3,2},{4,7},{5,4},{6,5},{7,6},{8,11},{9,8},{10,9... | collective-permute-start | bytes 393224 | tf_op jit(solution)/shard_map/ppermute | solution.py:281
  110.5 1.6 slice.44
  112.3 1.6 slice.45
  113.8 2.5 %collective-permute-start.17 = (bf16[16,4096]{1,0:T(8,128)(2,1)}, bf16[16,4096]{1,0:T(8,128)(2,1)}, u32[]{:S(2)}, u32[]{:S(2)}) collective-permute-start(bf16[16,4096]{1,0:T(8,128)(2,1)} %slice.45), channel_id=1, source_target_pairs={{0,3},{1,0},{2,1},{3,2},{4,7},{5,4},{6,5},{7,6},{8,11},{9,8},{10,9... | collective-permute-start | bytes 393224 | tf_op jit(solution)/shard_map/ppermute | solution.py:281
  117.6 1.3 copy.38
  118.9 1.3 reshape.113
  121.0 1.3 fusion
  122.4 3.4 %copy-done.1 = bf16[512,8192]{1,0:T(8,128)(2,1)S(1)} copy-done((bf16[512,8192]{1,0:T(8,128)(2,1)S(1)}, bf16[512,8192]{1,0:T(8,128)(2,1)}, u32[]{:S(2)}) %copy-start.1) | copy-done | bytes 8388632
  134.7 9.5 %cotangents.1 = (bf16[128,8192]{1,0:T(8,128)(2,1)S(1)}, f32[320,128]{1,0:T(8,128)S(1)}, f32[4,256,128]{2,1,0:T(8,128)S(1)}, f32[8,128]{1,0:T(8,128)S(1)}, f32[2,40,128]{2,1,0:T(8,128)S(1)}) custom-call(s32[1]{0:T(128)S(6)} %copy.46.lens_ref, s32[8]{0:T(128)S(1)} %copy-done.51, bf16[16,8192]{1,0:T(8,128)(2,1)S(1)} %add_convert_fusion.shard_0, ...), custom_call_target="tpu_custom_call" | custom-call | tf_op jit(solution)/shard_map/cotangents/pallas_call | solution.py:701
  144.3 1.3 copy-done.4
  148.3 4.3 %all-to-all-start.1 = ((f32[8,40,128]{2,1,0:T(8,128)}), f32[8,40,128]{2,1,0:T(8,128)S(1)}, u32[]{:S(2)}, u32[]{:S(2)}) async-start(f32[8,40,128]{2,1,0:T(8,128)} %bitcast.60), calls=%async_computation.1 | async-start | bytes 327680 | tf_op jit(solution)/shard_map/all_to_all | solution.py:861
  154.8 4.9 %all-to-all-done.1.factors_ref = f32[8,40,128]{2,1,0:T(8,128)S(1)} async-done(((f32[8,40,128]{2,1,0:T(8,128)}), f32[8,40,128]{2,1,0:T(8,128)S(1)}, u32[]{:S(2)}, u32[]{:S(2)}) %all-to-all-start.1) | async-done | bytes 163872 | tf_op jit(solution)/shard_map/all_to_all | solution.py:861
  159.7 1.6 copy-done.5
  161.3 1.0 copy-done.15
  163.1 2.7 %jacobian.1 = bf16[16,56,512]{2,1,0:T(8,128)(2,1)} custom-call(f32[8,40,128]{2,1,0:T(8,128)S(1)} %all-to-all-done.1.factors_ref, bf16[128,8192]{1,0:T(8,128)(2,1)S(1)} %get-tuple-element.37.tokens_ref, bf16[128,8192]{1,0:T(8,128)(2,1)S(1)} %copy-done.5, bf16[32,8192]{1,0:T(8,128)(2,1)S(1)} %maximum_maximum_fusion.side_ref, f32[2,40,128]{2,1,0:T(8,128)S(1)} %copy-done.43, ...), custom_call_target="tpu_custom_call" | custom-call | tf_op jit(solution)/shard_map/jacobian/pallas_call | solution.py:751
  165.8 9.4 %all-to-all-start.2 = ((bf16[16,56,512]{2,1,0:T(8,128)(2,1)}), bf16[16,56,512]{2,1,0:T(8,128)(2,1)S(1)}, u32[]{:S(2)}, u32[]{:S(2)}) async-start(bf16[16,56,512]{2,1,0:T(8,128)(2,1)} %jacobian.1), calls=%async_computation.2 | async-start | bytes 1835008 | tf_op jit(solution)/shard_map/all_to_all | solution.py:863
  176.4 13.3 %all-to-all-done.2 = bf16[16,56,512]{2,1,0:T(8,128)(2,1)S(1)} async-done(((bf16[16,56,512]{2,1,0:T(8,128)(2,1)}), bf16[16,56,512]{2,1,0:T(8,128)(2,1)S(1)}, u32[]{:S(2)}, u32[]{:S(2)}) %all-to-all-start.2) | async-done | bytes 917536 | tf_op jit(solution)/shard_map/all_to_all | solution.py:863
  191.1 1.6 gram.1
  192.7 9.3 %all_to_all.30 = f32[16,16,128]{2,1,0:T(8,128)S(1)} all-to-all(f32[16,16,128]{2,1,0:T(8,128)S(1)} %broadcast_in_dim.24), channel_id=1, replica_groups=mesh['dp'=16,'tensor'=8] {'dp'}, dimensions={0} | all-to-all | bytes 262144 | tf_op jit(solution)/shard_map/all_to_all | solution.py:45
  202.0 9.6 %all_to_all.31.packed_ref = f32[8,16,128]{2,1,0:T(8,128)S(1)} all-to-all(f32[8,16,128]{2,1,0:T(8,128)S(1)} %broadcast_in_dim.25), channel_id=1, replica_groups=mesh['dp'=16,'tensor'=8] {'tensor'}, dimensions={0} | all-to-all | bytes 131072 | tf_op jit(solution)/shard_map/all_to_all | solution.py:45
  212.6 28.2 %all_to_all.32.every_ref = bf16[128,8,768]{2,1,0:T(8,128)(2,1)S(1)} all-to-all(bf16[128,8,768]{2,1,0:T(8,128)(2,1)S(1)} %broadcast_in_dim.26), channel_id=1, replica_groups=mesh['dp'=16,'tensor'=8] {'dp','tensor'}, dimensions={0} | all-to-all | bytes 3145728 | tf_op jit(solution)/shard_map/all_to_all | solution.py:940
  240.8 4.6 %assemble.1 = (f32[3,16,8192]{2,1,0:T(8,128)}, f32[16,4096]{1,0:T(8,128)}, f32[2,16,1024]{2,1,0:T(8,128)}, f32[16,4096]{1,0:T(8,128)}, f32[16,8192]{1,0:T(8,128)}) custom-call(f32[1,128]{1,0:T(1,128)S(1)} %get-tuple-element.42.part_ref, bf16[128,8,768]{2,1,0:T(8,128)(2,1)S(1)} %all_to_all.32.every_ref, f32[3,16,8192]{2,1,0:T(8,128)S(1)} %bitcast.52, ...), custom_call_target="tpu_custom_call" | custom-call | tf_op jit(solution)/shard_map/assemble/pallas_call | solution.py:771
  (165 shorter events, 40.4 us)
Async XLA Ops:
  0.6 9.8 %collective-permute-start = (bf16[16,8192]{1,0:T(8,128)(2,1)}, bf16[16,8192]{1,0:T(8,128)(2,1)S(1)}, u32[]{:S(2)}, u32[]{:S(2)}) collective-permute-start(bf16[16,8192]{1,0:T(8,128)(2,1)} %bitcast.53), channel_id=1, source_target_pairs={{0,4},{1,5},{2,6},{3,7},{4,0},{5,1},{6,2},{7,3},{8,12},{9,13},{10,... | collective-permute-start | bytes 786440 | tf_op jit(solution)/shard_map/ppermute | solution.py:281
  4.5 9.7 %collective-permute-start.1 = (bf16[16,8192]{1,0:T(8,128)(2,1)}, bf16[16,8192]{1,0:T(8,128)(2,1)S(1)}, u32[]{:S(2)}, u32[]{:S(2)}) collective-permute-start(bf16[16,8192]{1,0:T(8,128)(2,1)} %bitcast.54), channel_id=1, source_target_pairs={{0,1},{1,2},{2,3},{3,0},{4,5},{5,6},{6,7},{7,4},{8,9},{9,10},{10,1... | collective-permute-start | bytes 786440 | tf_op jit(solution)/shard_map/ppermute | solution.py:281
  6.1 8.2 %collective-permute-start.2 = (bf16[16,8192]{1,0:T(8,128)(2,1)}, bf16[16,8192]{1,0:T(8,128)(2,1)S(1)}, u32[]{:S(2)}, u32[]{:S(2)}) collective-permute-start(bf16[16,8192]{1,0:T(8,128)(2,1)} %bitcast.55), channel_id=1, source_target_pairs={{0,3},{1,0},{2,1},{3,2},{4,7},{5,4},{6,5},{7,6},{8,11},{9,8},{10,9... | collective-permute-start | bytes 786440 | tf_op jit(solution)/shard_map/ppermute | solution.py:281
  10.4 8.8 %collective-permute-start.3 = (bf16[16,8192]{1,0:T(8,128)(2,1)S(1)}, bf16[16,8192]{1,0:T(8,128)(2,1)S(1)}, u32[]{:S(2)}, u32[]{:S(2)}) collective-permute-start(bf16[16,8192]{1,0:T(8,128)(2,1)S(1)} %collective-permute-done.shard_1), channel_id=1, source_target_pairs={{0,1},{1,2},{2,3},{3,0},{4,5},{5,6},{6,7},{7,4},{8,9},{9,10},{10,1... | collective-permute-start | bytes 786440 | tf_op jit(solution)/shard_map/ppermute | solution.py:281
  12.1 7.3 %collective-permute-start.4 = (bf16[16,8192]{1,0:T(8,128)(2,1)S(1)}, bf16[16,8192]{1,0:T(8,128)(2,1)S(1)}, u32[]{:S(2)}, u32[]{:S(2)}) collective-permute-start(bf16[16,8192]{1,0:T(8,128)(2,1)S(1)} %collective-permute-done.shard_1), channel_id=1, source_target_pairs={{0,3},{1,0},{2,1},{3,2},{4,7},{5,4},{6,5},{7,6},{8,11},{9,8},{10,9... | collective-permute-start | bytes 786440 | tf_op jit(solution)/shard_map/ppermute | solution.py:281
  14.2 9.0 %collective-permute-start.5 = (bf16[16,4096]{1,0:T(8,128)(2,1)S(1)}, bf16[16,4096]{1,0:T(8,128)(2,1)S(1)}, u32[]{:S(2)}, u32[]{:S(2)}) collective-permute-start(bf16[16,4096]{1,0:T(8,128)(2,1)S(1)} %slice.38), channel_id=1, source_target_pairs={{0,1},{1,2},{2,3},{3,0},{4,5},{5,6},{6,7},{7,4},{8,9},{9,10},{10,1... | collective-permute-start | bytes 393224 | tf_op jit(solution)/shard_map/ppermute | solution.py:281
  14.3 8.9 %collective-permute-start.6 = (bf16[16,4096]{1,0:T(8,128)(2,1)S(1)}, bf16[16,4096]{1,0:T(8,128)(2,1)S(1)}, u32[]{:S(2)}, u32[]{:S(2)}) collective-permute-start(bf16[16,4096]{1,0:T(8,128)(2,1)S(1)} %slice.39), channel_id=1, source_target_pairs={{0,3},{1,0},{2,1},{3,2},{4,7},{5,4},{6,5},{7,6},{8,11},{9,8},{10,9... | collective-permute-start | bytes 393224 | tf_op jit(solution)/shard_map/ppermute | solution.py:281
  19.3 5.7 %collective-permute-start.7 = (bf16[16,4096]{1,0:T(8,128)(2,1)S(1)}, bf16[16,4096]{1,0:T(8,128)(2,1)S(1)}, u32[]{:S(2)}, u32[]{:S(2)}) collective-permute-start(bf16[16,4096]{1,0:T(8,128)(2,1)S(1)} %slice.40), channel_id=1, source_target_pairs={{0,1},{1,2},{2,3},{3,0},{4,5},{5,6},{6,7},{7,4},{8,9},{9,10},{10,1... | collective-permute-start | bytes 393224 | tf_op jit(solution)/shard_map/ppermute | solution.py:281
  19.4 6.2 %collective-permute-start.8 = (bf16[16,4096]{1,0:T(8,128)(2,1)S(1)}, bf16[16,4096]{1,0:T(8,128)(2,1)S(1)}, u32[]{:S(2)}, u32[]{:S(2)}) collective-permute-start(bf16[16,4096]{1,0:T(8,128)(2,1)S(1)} %slice.41), channel_id=1, source_target_pairs={{0,3},{1,0},{2,1},{3,2},{4,7},{5,4},{6,5},{7,6},{8,11},{9,8},{10,9... | collective-permute-start | bytes 393224 | tf_op jit(solution)/shard_map/ppermute | solution.py:281
  22.2 30.0 %copy-start.50 = (s32[8]{0:T(128)}, s32[8]{0:T(128)S(1)}, u32[]{:S(2)}) copy-start(s32[8]{0:T(128)S(1)} %stack.47.spots_ref) | copy-start | bytes 100
  26.3 3.4 %copy-start = (bf16[512,8192]{1,0:T(8,128)(2,1)S(1)}, bf16[512,8192]{1,0:T(8,128)(2,1)}, u32[]{:S(2)}) copy-start(bf16[512,8192]{1,0:T(8,128)(2,1)} %weight_ref.1) | copy-start | bytes 25165828
  29.7 3.4 %copy-start.2 = (bf16[8192,512]{1,0:T(8,128)(2,1)S(1)}, bf16[8192,512]{1,0:T(8,128)(2,1)}, u32[]{:S(2)}) copy-start(bf16[8192,512]{1,0:T(8,128)(2,1)} %query_weight_ref.1) | copy-start | bytes 25165828
  33.0 2.2 copy-start.3
  35.2 0.9 copy-start.8
  36.2 0.9 copy-start.10
  37.1 1.1 copy-start.12
  52.2 1.3 copy-start.6
  58.8 7.1 %copy-start.9 = (bf16[16,8192]{1,0:T(8,128)(2,1)S(1)}, bf16[16,8192]{1,0:T(8,128)(2,1)}, u32[]{:S(2)}) copy-start(bf16[16,8192]{1,0:T(8,128)(2,1)} %up_output_ref.1) | copy-start | bytes 786436
  58.8 7.1 %copy-start.54 = (bf16[8192,5]{0,1:T(8,128)(2,1)S(1)}, bf16[8192,5]{0,1:T(8,128)(2,1)}, u32[]{:S(2)}) copy-start(bf16[8192,5]{0,1:T(8,128)(2,1)} %param.21) | copy-start | bytes 245764
  58.8 27.7 %all-to-all-start = ((bf16[8,16,8192]{2,1,0:T(8,128)(2,1)}), bf16[8,16,8192]{2,1,0:T(8,128)(2,1)}, u32[]{:S(2)}, u32[]{:S(2)}) async-start(bf16[8,16,8192]{2,1,0:T(8,128)(2,1)} %copy-done.6), calls=%async_computation | async-start | bytes 4194304 | tf_op jit(solution)/shard_map/all_to_all | solution.py:841
  64.9 23.6 %copy-start.11 = (bf16[1,16,8192]{2,1,0:T(8,128)(2,1)S(1)}, bf16[1,16,8192]{2,1,0:T(8,128)(2,1)}, u32[]{:S(2)}) copy-start(bf16[1,16,8192]{2,1,0:T(8,128)(2,1)} %param.17) | copy-start | bytes 786436
  65.9 30.5 %copy-start.57 = (s32[16]{0:T(128)S(1)}, s32[16]{0:T(128)}, u32[]{:S(2)}) copy-start(s32[16]{0:T(128)} %param.23) | copy-start | bytes 196
  66.0 50.3 %copy-start.27 = (f32[2,16,1024]{2,1,0:T(8,128)S(1)}, f32[2,16,1024]{2,1,0:T(8,128)}, u32[]{:S(2)}) copy-start(f32[2,16,1024]{2,1,0:T(8,128)} %bkv_ref.1) | copy-start | bytes 393220
  66.0 56.4 %copy-start.39 = (bf16[512,16]{0,1:T(8,128)(2,1)S(1)}, bf16[512,16]{0,1:T(8,128)(2,1)}, u32[]{:S(2)}) copy-start(bf16[512,16]{0,1:T(8,128)(2,1)} %param.27) | copy-start | bytes 49156
  88.6 12.1 %collective-permute-start.9 = (bf16[16,8192]{1,0:T(8,128)(2,1)S(1)}, bf16[16,8192]{1,0:T(8,128)(2,1)}, u32[]{:S(2)}, u32[]{:S(2)}) collective-permute-start(bf16[16,8192]{1,0:T(8,128)(2,1)S(1)} %add_convert_fusion.shard_0), channel_id=1, source_target_pairs={{0,4},{1,5},{2,6},{3,7},{4,0},{5,1},{6,2},{7,3},{8,12},{9,13},{10,... | collective-permute-start | bytes 786440 | tf_op jit(solution)/shard_map/ppermute | solution.py:281
  97.0 8.9 %collective-permute-start.10 = (bf16[16,8192]{1,0:T(8,128)(2,1)S(1)}, bf16[16,8192]{1,0:T(8,128)(2,1)S(1)}, u32[]{:S(2)}, u32[]{:S(2)}) collective-permute-start(bf16[16,8192]{1,0:T(8,128)(2,1)S(1)} %add_convert_fusion.shard_0), channel_id=1, source_target_pairs={{0,1},{1,2},{2,3},{3,0},{4,5},{5,6},{6,7},{7,4},{8,9},{9,10},{10,1... | collective-permute-start | bytes 786440 | tf_op jit(solution)/shard_map/ppermute | solution.py:281
  98.0 8.6 %collective-permute-start.11 = (bf16[16,8192]{1,0:T(8,128)(2,1)S(1)}, bf16[16,8192]{1,0:T(8,128)(2,1)S(1)}, u32[]{:S(2)}, u32[]{:S(2)}) collective-permute-start(bf16[16,8192]{1,0:T(8,128)(2,1)S(1)} %add_convert_fusion.shard_0), channel_id=1, source_target_pairs={{0,3},{1,0},{2,1},{3,2},{4,7},{5,4},{6,5},{7,6},{8,11},{9,8},{10,9... | collective-permute-start | bytes 786440 | tf_op jit(solution)/shard_map/ppermute | solution.py:281
  100.6 9.9 %collective-permute-start.12 = (bf16[16,8192]{1,0:T(8,128)(2,1)}, bf16[16,8192]{1,0:T(8,128)(2,1)}, u32[]{:S(2)}, u32[]{:S(2)}) collective-permute-start(bf16[16,8192]{1,0:T(8,128)(2,1)} %collective-permute-done.9.shard_1), channel_id=1, source_target_pairs={{0,1},{1,2},{2,3},{3,0},{4,5},{5,6},{6,7},{7,4},{8,9},{9,10},{10,1... | collective-permute-start | bytes 786440 | tf_op jit(solution)/shard_map/ppermute | solution.py:281
  101.9 10.4 %collective-permute-start.13 = (bf16[16,8192]{1,0:T(8,128)(2,1)}, bf16[16,8192]{1,0:T(8,128)(2,1)}, u32[]{:S(2)}, u32[]{:S(2)}) collective-permute-start(bf16[16,8192]{1,0:T(8,128)(2,1)} %collective-permute-done.9.shard_1), channel_id=1, source_target_pairs={{0,3},{1,0},{2,1},{3,2},{4,7},{5,4},{6,5},{7,6},{8,11},{9,8},{10,9... | collective-permute-start | bytes 786440 | tf_op jit(solution)/shard_map/ppermute | solution.py:281
  106.6 15.8 %collective-permute-start.14 = (bf16[16,4096]{1,0:T(8,128)(2,1)}, bf16[16,4096]{1,0:T(8,128)(2,1)}, u32[]{:S(2)}, u32[]{:S(2)}) collective-permute-start(bf16[16,4096]{1,0:T(8,128)(2,1)} %slice.42), channel_id=1, source_target_pairs={{0,1},{1,2},{2,3},{3,0},{4,5},{5,6},{6,7},{7,4},{8,9},{9,10},{10,1... | collective-permute-start | bytes 393224 | tf_op jit(solution)/shard_map/ppermute | solution.py:281
  107.3 15.1 %collective-permute-start.15 = (bf16[16,4096]{1,0:T(8,128)(2,1)}, bf16[16,4096]{1,0:T(8,128)(2,1)}, u32[]{:S(2)}, u32[]{:S(2)}) collective-permute-start(bf16[16,4096]{1,0:T(8,128)(2,1)} %slice.43), channel_id=1, source_target_pairs={{0,3},{1,0},{2,1},{3,2},{4,7},{5,4},{6,5},{7,6},{8,11},{9,8},{10,9... | collective-permute-start | bytes 393224 | tf_op jit(solution)/shard_map/ppermute | solution.py:281
  112.1 10.3 %collective-permute-start.16 = (bf16[16,4096]{1,0:T(8,128)(2,1)}, bf16[16,4096]{1,0:T(8,128)(2,1)}, u32[]{:S(2)}, u32[]{:S(2)}) collective-permute-start(bf16[16,4096]{1,0:T(8,128)(2,1)} %slice.44), channel_id=1, source_target_pairs={{0,1},{1,2},{2,3},{3,0},{4,5},{5,6},{6,7},{7,4},{8,9},{9,10},{10,1... | collective-permute-start | bytes 393224 | tf_op jit(solution)/shard_map/ppermute | solution.py:281
  113.8 8.6 %collective-permute-start.17 = (bf16[16,4096]{1,0:T(8,128)(2,1)}, bf16[16,4096]{1,0:T(8,128)(2,1)}, u32[]{:S(2)}, u32[]{:S(2)}) collective-permute-start(bf16[16,4096]{1,0:T(8,128)(2,1)} %slice.45), channel_id=1, source_target_pairs={{0,3},{1,0},{2,1},{3,2},{4,7},{5,4},{6,5},{7,6},{8,11},{9,8},{10,9... | collective-permute-start | bytes 393224 | tf_op jit(solution)/shard_map/ppermute | solution.py:281
  122.4 3.4 %copy-start.1 = (bf16[512,8192]{1,0:T(8,128)(2,1)S(1)}, bf16[512,8192]{1,0:T(8,128)(2,1)}, u32[]{:S(2)}) copy-start(bf16[512,8192]{1,0:T(8,128)(2,1)} %weight_ref.1) | copy-start | bytes 25165828
  125.8 0.9 copy-start.19
  126.8 0.9 copy-start.21
  144.3 1.3 copy-start.4
  148.3 11.4 %all-to-all-start.1 = ((f32[8,40,128]{2,1,0:T(8,128)}), f32[8,40,128]{2,1,0:T(8,128)S(1)}, u32[]{:S(2)}, u32[]{:S(2)}) async-start(f32[8,40,128]{2,1,0:T(8,128)} %bitcast.60), calls=%async_computation.1 | async-start | bytes 327680 | tf_op jit(solution)/shard_map/all_to_all | solution.py:861
  159.7 1.6 copy-start.5
  161.3 1.0 copy-start.15
  163.1 12.1 %copy-start.55 = (pred[16]{0:T(512)(128)(4,1)S(1)}, pred[16]{0:T(512)(128)(4,1)}, u32[]{:S(2)}) copy-start(pred[16]{0:T(512)(128)(4,1)} %get-tuple-element.50) | copy-start | bytes 52
  163.1 12.8 %copy-start.56 = (pred[16]{0:T(512)(128)(4,1)S(1)}, pred[16]{0:T(512)(128)(4,1)}, u32[]{:S(2)}) copy-start(pred[16]{0:T(512)(128)(4,1)} %get-tuple-element.49) | copy-start | bytes 52
  165.8 23.9 %all-to-all-start.2 = ((bf16[16,56,512]{2,1,0:T(8,128)(2,1)}), bf16[16,56,512]{2,1,0:T(8,128)(2,1)S(1)}, u32[]{:S(2)}, u32[]{:S(2)}) async-start(bf16[16,56,512]{2,1,0:T(8,128)(2,1)} %jacobian.1), calls=%async_computation.2 | async-start | bytes 1835008 | tf_op jit(solution)/shard_map/all_to_all | solution.py:863
  189.9 1.1 copy-start.53
  212.5 28.3 %copy-start.7 = (f32[3,8192,16]{1,2,0:T(8,128)S(1)}, f32[3,8192,16]{1,2,0:T(8,128)}, u32[]{:S(2)}) copy-start(f32[3,8192,16]{1,2,0:T(8,128)} %param.29) | copy-start | bytes 4718596
  212.5 28.3 %copy-start.13 = (f32[16,8192]{1,0:T(8,128)S(1)}, f32[16,8192]{1,0:T(8,128)}, u32[]{:S(2)}) copy-start(f32[16,8192]{1,0:T(8,128)} %bo_ref.1) | copy-start | bytes 1572868
  212.5 28.3 %copy-start.16 = (f32[4096,16]{0,1:T(8,128)S(1)}, f32[4096,16]{0,1:T(8,128)}, u32[]{:S(2)}) copy-start(f32[4096,16]{0,1:T(8,128)} %param.32) | copy-start | bytes 786436
  212.5 28.3 %copy-start.17 = (f32[16,4096]{1,0:T(8,128)S(1)}, f32[16,4096]{1,0:T(8,128)}, u32[]{:S(2)}) copy-start(f32[16,4096]{1,0:T(8,128)} %bq_ref.1) | copy-start | bytes 786436
  (31 other events, 22.6 us)

commit v4 on v3

--- a/solution.py
+++ b/solution.py
@@ -496,7 +496,7 @@
             pltpu.VMEM((128, query_cols), jnp.bfloat16),
             pltpu.VMEM((128, 32), jnp.bfloat16),
         ],
-        compiler_params=pltpu.CompilerParams(vmem_limit_bytes=24 * 2**20),
+        compiler_params=pltpu.CompilerParams(vmem_limit_bytes=60 * 2**20),
         name="forward",
     )(
         spots,
@@ -712,7 +712,7 @@
             pltpu.VMEM((256, 128), jnp.float32),
             pltpu.VMEM((128, 128), jnp.float32),
         ],
-        compiler_params=pltpu.CompilerParams(vmem_limit_bytes=20 * 2**20),
+        compiler_params=pltpu.CompilerParams(vmem_limit_bytes=60 * 2**20),
         name="cotangents",
     )(lens, spots, *shards, output_weight, side, *others)
 
@@ -753,7 +753,7 @@
         in_specs=whole(len(arrays)),
         out_specs=pl.BlockSpec(memory_space=pltpu.VMEM),
         out_shape=jax.ShapeDtypeStruct((16, PIECE_ROWS, LANES), jnp.bfloat16),
-        compiler_params=pltpu.CompilerParams(vmem_limit_bytes=12 * 2**20),
+        compiler_params=pltpu.CompilerParams(vmem_limit_bytes=60 * 2**20),
         name="jacobian",
     )(*arrays)
 

time: 247 us -> 213 us (0.86)
  local copies, waits for them, and re-layouts: 60.2 us -> 8.57 us
  Pallas kernels: 28.3 us -> 40.1 us
  waiting for transfers between devices: 45.8 us -> 52 us
  starting transfers between devices: 54.7 us -> 59.5 us
  other arithmetic: 7.72 us -> 3.42 us
    unnamed x120 -> x64, local copies, waits for them, and re-layouts: 46.5 us -> 2.64 us
    pallas_call x1, Pallas kernels: 9.05 us -> 15.5 us  [forward(): pl.pallas_call(forward_body, grid=(2 * steps,), in_specs=[pl.BlockSpec(me...]
    ppermute x18, waiting for transfers between devices: 7.12 us -> 11.2 us  [permute(): return lax.ppermute(array, 'tensor', pairs)]
    pallas_call x1, Pallas kernels: 9.54 us -> 12.4 us  [cotangents(): pl.pallas_call(cotangents_body, grid=(steps,), in_specs=[pl.BlockSpec(mem...]
    pallas_call x1, Pallas kernels: 2.65 us -> 5.19 us  [jacobian(): pl.pallas_call(jacobian_body, in_specs=whole(len(arrays)), out_specs=pl.B...]
  transfers between devices with their start and end apart: 21 -> 21, of which waited for: 8 -> 11; matrix products, arithmetic and copies ran while one was open for 8% -> 3% of each run, Pallas kernels for 0% -> 0%
where the time goes in v4:
time: 213 us; the launch traced here: 212 us
  starting transfers between devices  59.5 us (28%)
  waiting for transfers between devices  52 us (24%)
  blocking collectives  47 us (22%)
  Pallas kernels  40.1 us (19%)
  local copies, waits for them, and re-layouts  8.57 us (4%)
  other arithmetic  3.42 us (2%)
    ppermute x18, starting transfers between devices, permute(): return lax.ppermute(array, 'tensor', pairs)  35 us
    all_to_all x1, blocking collectives, local(): lax.all_to_all(jnp.broadcast_to(own_result[None], (groups * shards,) + ow...  28.2 us
    all_to_all x1, waiting for transfers between devices, local(): out_pieces = lax.all_to_all(out_terms, 'tensor', 0, 0)  20.6 us
    all_to_all x2, blocking collectives, gather_by_exchange(): return lax.all_to_all(copies, axis, 0, 0)  18.8 us
    pallas_call x1, Pallas kernels, forward(): pl.pallas_call(forward_body, grid=(2 * steps,), in_specs=[pl.BlockSpec(me...  15.5 us
    all_to_all x1, waiting for transfers between devices, local(): spread = lax.all_to_all(payload, 'dp', 0, 0)  13.3 us
    pallas_call x1, Pallas kernels, cotangents(): pl.pallas_call(cotangents_body, grid=(steps,), in_specs=[pl.BlockSpec(mem...  12.4 us
    all_to_all x1, starting transfers between devices, local(): spread = lax.all_to_all(payload, 'dp', 0, 0)  11.5 us
  transfers between devices with their start and end apart: 21, of which 11 were waited for; matrix products, arithmetic and copies ran while one was open for 3% of the time, Pallas kernels for 0%

profile of v4, /device:TPU:1, one launch (start us, length us, event | category | flops | bytes accessed | tf_op | source)
XLA Modules:
  0.0 212.5 jit_solution(13963689560288741767)
XLA Ops:
  0.6 3.8 %collective-permute-start = (bf16[16,8192]{1,0:T(8,128)(2,1)}, bf16[16,8192]{1,0:T(8,128)(2,1)S(1)}, u32[]{:S(2)}, u32[]{:S(2)}) collective-permute-start(bf16[16,8192]{1,0:T(8,128)(2,1)} %bitcast.59), channel_id=1, source_target_pairs={{0,4},{1,5},{2,6},{3,7},{4,0},{5,1},{6,2},{7,3},{8,12},{9,13},{10,... | collective-permute-start | bytes 786440 | tf_op jit(solution)/shard_map/ppermute | solution.py:281
  4.5 1.6 collective-permute-start.1
  6.1 2.1 collective-permute-start.2
  8.2 2.2 %collective-permute-done.shard_1 = bf16[16,8192]{1,0:T(8,128)(2,1)S(1)} collective-permute-done((bf16[16,8192]{1,0:T(8,128)(2,1)}, bf16[16,8192]{1,0:T(8,128)(2,1)S(1)}, u32[]{:S(2)}, u32[]{:S(2)}) %collective-permute-start) | collective-permute-done | bytes 262176 | tf_op jit(solution)/shard_map/ppermute | solution.py:281
  10.4 1.6 collective-permute-start.3
  12.1 2.1 collective-permute-start.4
  14.3 2.7 %collective-permute-start.6 = (bf16[16,4096]{1,0:T(8,128)(2,1)S(1)}, bf16[16,4096]{1,0:T(8,128)(2,1)S(1)}, u32[]{:S(2)}, u32[]{:S(2)}) collective-permute-start(bf16[16,4096]{1,0:T(8,128)(2,1)S(1)} %slice.39), channel_id=1, source_target_pairs={{0,3},{1,0},{2,1},{3,2},{4,7},{5,4},{6,5},{7,6},{8,11},{9,8},{10,9... | collective-permute-start | bytes 393224 | tf_op jit(solution)/shard_map/ppermute | solution.py:281
  17.0 2.2 %collective-permute-done.3.shard_4 = bf16[16,8192]{1,0:T(8,128)(2,1)S(1)} collective-permute-done((bf16[16,8192]{1,0:T(8,128)(2,1)S(1)}, bf16[16,8192]{1,0:T(8,128)(2,1)S(1)}, u32[]{:S(2)}, u32[]{:S(2)}) %collective-permute-start.3) | collective-permute-done | bytes 262176 | tf_op jit(solution)/shard_map/ppermute | solution.py:281
  19.4 2.7 %collective-permute-start.8 = (bf16[16,4096]{1,0:T(8,128)(2,1)S(1)}, bf16[16,4096]{1,0:T(8,128)(2,1)S(1)}, u32[]{:S(2)}, u32[]{:S(2)}) collective-permute-start(bf16[16,4096]{1,0:T(8,128)(2,1)S(1)} %slice.41), channel_id=1, source_target_pairs={{0,3},{1,0},{2,1},{3,2},{4,7},{5,4},{6,5},{7,6},{8,11},{9,8},{10,9... | collective-permute-start | bytes 393224 | tf_op jit(solution)/shard_map/ppermute | solution.py:281
  22.1 0.6 stack.47.spots_ref
  22.7 1.0 constant_dynamic-slice_fusion.1
  23.7 1.3 collective-permute-done.7.shard_8
  25.0 0.6 copy-done.22
  25.7 15.5 %forward.1 = (bf16[128,8192]{1,0:T(8,128)(2,1)}, bf16[8,16,8192]{2,1,0:T(8,128)(2,1)}, f32[128,512]{1,0:T(8,128)}, f32[128,128]{1,0:T(8,128)}, f32[128,128]{1,0:...) custom-call(s32[8]{0:T(128)} %stack.47.spots_ref, ...), custom_call_target="tpu_custom_call" | custom-call | tf_op jit(solution)/shard_map/forward/pallas_call | solution.py:471
  41.2 6.7 %all-to-all-start = ((bf16[8,16,8192]{2,1,0:T(8,128)(2,1)}), bf16[8,16,8192]{2,1,0:T(8,128)(2,1)}, u32[]{:S(2)}, u32[]{:S(2)}) async-start(bf16[8,16,8192]{2,1,0:T(8,128)(2,1)} %get-tuple-element.27), calls=%async_computation | async-start | bytes 4194304 | tf_op jit(solution)/shard_map/all_to_all | solution.py:841
  48.1 0.9 maximum_maximum_fusion.side_ref
  49.1 20.6 %all-to-all-done = bf16[8,16,8192]{2,1,0:T(8,128)(2,1)} async-done(((bf16[8,16,8192]{2,1,0:T(8,128)(2,1)}), bf16[8,16,8192]{2,1,0:T(8,128)(2,1)}, u32[]{:S(2)}, u32[]{:S(2)}) %all-to-all-start) | async-done | bytes 2097184 | tf_op jit(solution)/shard_map/all_to_all | solution.py:841
  69.6 1.9 convert_reduce_fusion
  71.6 7.2 %collective-permute-start.9 = (bf16[16,8192]{1,0:T(8,128)(2,1)S(1)}, bf16[16,8192]{1,0:T(8,128)(2,1)S(1)}, u32[]{:S(2)}, u32[]{:S(2)}) collective-permute-start(bf16[16,8192]{1,0:T(8,128)(2,1)S(1)} %add_convert_fusion.shard_0), channel_id=1, source_target_pairs={{0,4},{1,5},{2,6},{3,7},{4,0},{5,1},{6,2},{7,3},{8,12},{9,13},{10,... | collective-permute-start | bytes 786440 | tf_op jit(solution)/shard_map/ppermute | solution.py:281
  78.9 1.0 collective-permute-start.10
  79.9 1.7 collective-permute-start.11
  81.6 2.0 collective-permute-done.9.shard_1
  83.6 1.4 collective-permute-start.12
  85.0 1.3 collective-permute-start.13
  87.0 0.7 slice.43
  87.7 2.5 %collective-permute-start.15 = (bf16[16,4096]{1,0:T(8,128)(2,1)}, bf16[16,4096]{1,0:T(8,128)(2,1)S(1)}, u32[]{:S(2)}, u32[]{:S(2)}) collective-permute-start(bf16[16,4096]{1,0:T(8,128)(2,1)} %slice.43), channel_id=1, source_target_pairs={{0,3},{1,0},{2,1},{3,2},{4,7},{5,4},{6,5},{7,6},{8,11},{9,8},{10,9... | collective-permute-start | bytes 393224 | tf_op jit(solution)/shard_map/ppermute | solution.py:281
  90.2 1.8 collective-permute-done.12.shard_4
  92.0 0.7 slice.44
  92.8 0.7 slice.45
  93.5 2.7 %collective-permute-start.17 = (bf16[16,4096]{1,0:T(8,128)(2,1)}, bf16[16,4096]{1,0:T(8,128)(2,1)S(1)}, u32[]{:S(2)}, u32[]{:S(2)}) collective-permute-start(bf16[16,4096]{1,0:T(8,128)(2,1)} %slice.45), channel_id=1, source_target_pairs={{0,3},{1,0},{2,1},{3,2},{4,7},{5,4},{6,5},{7,6},{8,11},{9,8},{10,9... | collective-permute-start | bytes 393224 | tf_op jit(solution)/shard_map/ppermute | solution.py:281
  97.1 0.9 collective-permute-done.16.shard_8
  98.0 0.4 collective-permute-done.17.shard_9
  99.1 12.4 %cotangents.1 = (bf16[128,8192]{1,0:T(8,128)(2,1)}, f32[320,128]{1,0:T(8,128)}, f32[4,256,128]{2,1,0:T(8,128)}, f32[8,128]{1,0:T(8,128)}, f32[2,40,128]{2,1,0:T(8,128)}) custom-call(s32[1]{0:T(128)S(6)} %copy.46.lens_ref, s32[8]{0:T(128)} %stack.47.spots_ref, bf16[16,8192]{1,0:T(8,128)(2,1)} %copy-done.8, bf16[16,8192]{1,0:T(8,128)(2,1)} %copy-done.19, ...), custom_call_target="tpu_custom_call" | custom-call | tf_op jit(solution)/shard_map/cotangents/pallas_call | solution.py:701
  111.5 6.3 %all-to-all-start.1 = ((f32[8,40,128]{2,1,0:T(8,128)}), f32[8,40,128]{2,1,0:T(8,128)S(1)}, u32[]{:S(2)}, u32[]{:S(2)}) async-start(f32[8,40,128]{2,1,0:T(8,128)} %bitcast.64), calls=%async_computation.1 | async-start | bytes 327680 | tf_op jit(solution)/shard_map/all_to_all | solution.py:861
  118.0 7.0 %all-to-all-done.1.factors_ref = f32[8,40,128]{2,1,0:T(8,128)S(1)} async-done(((f32[8,40,128]{2,1,0:T(8,128)}), f32[8,40,128]{2,1,0:T(8,128)S(1)}, u32[]{:S(2)}, u32[]{:S(2)}) %all-to-all-start.1) | async-done | bytes 163872 | tf_op jit(solution)/shard_map/all_to_all | solution.py:861
  125.0 0.7 copy-done.9
  125.6 5.2 %jacobian.1 = bf16[16,56,512]{2,1,0:T(8,128)(2,1)} custom-call(f32[8,40,128]{2,1,0:T(8,128)} %copy-done.9, bf16[128,8192]{1,0:T(8,128)(2,1)} %get-tuple-element.37.tokens_ref, bf16[128,8192]{1,0:T(8,128)(2,1)} %get-tuple-element.38.resid_ref, bf16[32,8192]{1,0:T(8,128)(2,1)} %maximum_maximum_fusion.side_ref, f32[2,40,128]{2,1,0:T(8,128)} %get-tuple-element.39.repeated_ref, ...), custom_call_target="tpu_custom_call" | custom-call | tf_op jit(solution)/shard_map/jacobian/pallas_call | solution.py:751
  130.8 11.5 %all-to-all-start.2 = ((bf16[16,56,512]{2,1,0:T(8,128)(2,1)}), bf16[16,56,512]{2,1,0:T(8,128)(2,1)S(1)}, u32[]{:S(2)}, u32[]{:S(2)}) async-start(bf16[16,56,512]{2,1,0:T(8,128)(2,1)} %jacobian.1), calls=%async_computation.2 | async-start | bytes 1835008 | tf_op jit(solution)/shard_map/all_to_all | solution.py:863
  142.4 0.6 gather_fusion
  143.5 13.3 %all-to-all-done.2 = bf16[16,56,512]{2,1,0:T(8,128)(2,1)S(1)} async-done(((bf16[16,56,512]{2,1,0:T(8,128)(2,1)}), bf16[16,56,512]{2,1,0:T(8,128)(2,1)S(1)}, u32[]{:S(2)}, u32[]{:S(2)}) %all-to-all-start.2) | async-done | bytes 917536 | tf_op jit(solution)/shard_map/all_to_all | solution.py:863
  157.1 0.5 copy.35
  157.6 0.6 copy.42
  158.2 1.6 gram.1
  159.8 9.3 %all_to_all.30 = f32[16,16,128]{2,1,0:T(8,128)S(1)} all-to-all(f32[16,16,128]{2,1,0:T(8,128)S(1)} %broadcast_in_dim.24), channel_id=1, replica_groups=mesh['dp'=16,'tensor'=8] {'dp'}, dimensions={0} | all-to-all | bytes 262144 | tf_op jit(solution)/shard_map/all_to_all | solution.py:45
  169.2 9.5 %all_to_all.31.packed_ref = f32[8,16,128]{2,1,0:T(8,128)S(1)} all-to-all(f32[8,16,128]{2,1,0:T(8,128)S(1)} %broadcast_in_dim.25), channel_id=1, replica_groups=mesh['dp'=16,'tensor'=8] {'tensor'}, dimensions={0} | all-to-all | bytes 131072 | tf_op jit(solution)/shard_map/all_to_all | solution.py:45
  178.7 0.9 lanczos.1
  179.7 28.2 %all_to_all.32.every_ref = bf16[128,8,768]{2,1,0:T(8,128)(2,1)S(1)} all-to-all(bf16[128,8,768]{2,1,0:T(8,128)(2,1)S(1)} %broadcast_in_dim.26), channel_id=1, replica_groups=mesh['dp'=16,'tensor'=8] {'dp','tensor'}, dimensions={0} | all-to-all | bytes 3145728 | tf_op jit(solution)/shard_map/all_to_all | solution.py:940
  207.9 4.6 %assemble.1 = (f32[3,16,8192]{2,1,0:T(8,128)}, f32[16,4096]{1,0:T(8,128)}, f32[2,16,1024]{2,1,0:T(8,128)}, f32[16,4096]{1,0:T(8,128)}, f32[16,8192]{1,0:T(8,128)}) custom-call(f32[1,128]{1,0:T(1,128)S(1)} %get-tuple-element.42.part_ref, bf16[128,8,768]{2,1,0:T(8,128)(2,1)S(1)} %all_to_all.32.every_ref, f32[3,16,8192]{2,1,0:T(8,128)S(1)} %bitcast.52, ...), custom_call_target="tpu_custom_call" | custom-call | tf_op jit(solution)/shard_map/assemble/pallas_call | solution.py:771
  (109 shorter events, 3.3 us)
Async XLA Ops:
  0.6 9.8 %collective-permute-start = (bf16[16,8192]{1,0:T(8,128)(2,1)}, bf16[16,8192]{1,0:T(8,128)(2,1)S(1)}, u32[]{:S(2)}, u32[]{:S(2)}) collective-permute-start(bf16[16,8192]{1,0:T(8,128)(2,1)} %bitcast.59), channel_id=1, source_target_pairs={{0,4},{1,5},{2,6},{3,7},{4,0},{5,1},{6,2},{7,3},{8,12},{9,13},{10,... | collective-permute-start | bytes 786440 | tf_op jit(solution)/shard_map/ppermute | solution.py:281
  4.5 9.7 %collective-permute-start.1 = (bf16[16,8192]{1,0:T(8,128)(2,1)}, bf16[16,8192]{1,0:T(8,128)(2,1)S(1)}, u32[]{:S(2)}, u32[]{:S(2)}) collective-permute-start(bf16[16,8192]{1,0:T(8,128)(2,1)} %bitcast.60), channel_id=1, source_target_pairs={{0,1},{1,2},{2,3},{3,0},{4,5},{5,6},{6,7},{7,4},{8,9},{9,10},{10,1... | collective-permute-start | bytes 786440 | tf_op jit(solution)/shard_map/ppermute | solution.py:281
  6.1 8.2 %collective-permute-start.2 = (bf16[16,8192]{1,0:T(8,128)(2,1)}, bf16[16,8192]{1,0:T(8,128)(2,1)S(1)}, u32[]{:S(2)}, u32[]{:S(2)}) collective-permute-start(bf16[16,8192]{1,0:T(8,128)(2,1)} %bitcast.61), channel_id=1, source_target_pairs={{0,3},{1,0},{2,1},{3,2},{4,7},{5,4},{6,5},{7,6},{8,11},{9,8},{10,9... | collective-permute-start | bytes 786440 | tf_op jit(solution)/shard_map/ppermute | solution.py:281
  10.4 14.6 %copy-start.18 = (bf16[16,8192]{1,0:T(8,128)(2,1)}, bf16[16,8192]{1,0:T(8,128)(2,1)S(1)}, u32[]{:S(2)}) copy-start(bf16[16,8192]{1,0:T(8,128)(2,1)S(1)} %collective-permute-done.shard_1) | copy-start | bytes 786436
  10.4 8.8 %collective-permute-start.3 = (bf16[16,8192]{1,0:T(8,128)(2,1)S(1)}, bf16[16,8192]{1,0:T(8,128)(2,1)S(1)}, u32[]{:S(2)}, u32[]{:S(2)}) collective-permute-start(bf16[16,8192]{1,0:T(8,128)(2,1)S(1)} %collective-permute-done.shard_1), channel_id=1, source_target_pairs={{0,1},{1,2},{2,3},{3,0},{4,5},{5,6},{6,7},{7,4},{8,9},{9,10},{10,1... | collective-permute-start | bytes 786440 | tf_op jit(solution)/shard_map/ppermute | solution.py:281
  12.1 7.3 %collective-permute-start.4 = (bf16[16,8192]{1,0:T(8,128)(2,1)S(1)}, bf16[16,8192]{1,0:T(8,128)(2,1)S(1)}, u32[]{:S(2)}, u32[]{:S(2)}) collective-permute-start(bf16[16,8192]{1,0:T(8,128)(2,1)S(1)} %collective-permute-done.shard_1), channel_id=1, source_target_pairs={{0,3},{1,0},{2,1},{3,2},{4,7},{5,4},{6,5},{7,6},{8,11},{9,8},{10,9... | collective-permute-start | bytes 786440 | tf_op jit(solution)/shard_map/ppermute | solution.py:281
  14.2 10.8 %copy-start.10 = (bf16[16,8192]{1,0:T(8,128)(2,1)}, bf16[16,8192]{1,0:T(8,128)(2,1)S(1)}, u32[]{:S(2)}) copy-start(bf16[16,8192]{1,0:T(8,128)(2,1)S(1)} %collective-permute-done.1.shard_2) | copy-start | bytes 786436
  14.2 9.5 %collective-permute-start.5 = (bf16[16,4096]{1,0:T(8,128)(2,1)S(1)}, bf16[16,4096]{1,0:T(8,128)(2,1)S(1)}, u32[]{:S(2)}, u32[]{:S(2)}) collective-permute-start(bf16[16,4096]{1,0:T(8,128)(2,1)S(1)} %slice.38), channel_id=1, source_target_pairs={{0,1},{1,2},{2,3},{3,0},{4,5},{5,6},{6,7},{7,4},{8,9},{9,10},{10,1... | collective-permute-start | bytes 393224 | tf_op jit(solution)/shard_map/ppermute | solution.py:281
  14.3 10.7 %copy-start.11 = (bf16[16,8192]{1,0:T(8,128)(2,1)}, bf16[16,8192]{1,0:T(8,128)(2,1)S(1)}, u32[]{:S(2)}) copy-start(bf16[16,8192]{1,0:T(8,128)(2,1)S(1)} %collective-permute-done.2.shard_3) | copy-start | bytes 786436
  14.3 9.4 %collective-permute-start.6 = (bf16[16,4096]{1,0:T(8,128)(2,1)S(1)}, bf16[16,4096]{1,0:T(8,128)(2,1)S(1)}, u32[]{:S(2)}, u32[]{:S(2)}) collective-permute-start(bf16[16,4096]{1,0:T(8,128)(2,1)S(1)} %slice.39), channel_id=1, source_target_pairs={{0,3},{1,0},{2,1},{3,2},{4,7},{5,4},{6,5},{7,6},{8,11},{9,8},{10,9... | collective-permute-start | bytes 393224 | tf_op jit(solution)/shard_map/ppermute | solution.py:281
  19.3 5.7 %copy-start.12 = (bf16[16,8192]{1,0:T(8,128)(2,1)}, bf16[16,8192]{1,0:T(8,128)(2,1)S(1)}, u32[]{:S(2)}) copy-start(bf16[16,8192]{1,0:T(8,128)(2,1)S(1)} %collective-permute-done.3.shard_4) | copy-start | bytes 786436
  19.3 5.7 %collective-permute-start.7 = (bf16[16,4096]{1,0:T(8,128)(2,1)S(1)}, bf16[16,4096]{1,0:T(8,128)(2,1)S(1)}, u32[]{:S(2)}, u32[]{:S(2)}) collective-permute-start(bf16[16,4096]{1,0:T(8,128)(2,1)S(1)} %slice.40), channel_id=1, source_target_pairs={{0,1},{1,2},{2,3},{3,0},{4,5},{5,6},{6,7},{7,4},{8,9},{9,10},{10,1... | collective-permute-start | bytes 393224 | tf_op jit(solution)/shard_map/ppermute | solution.py:281
  19.4 5.6 %copy-start.13 = (bf16[16,8192]{1,0:T(8,128)(2,1)}, bf16[16,8192]{1,0:T(8,128)(2,1)S(1)}, u32[]{:S(2)}) copy-start(bf16[16,8192]{1,0:T(8,128)(2,1)S(1)} %collective-permute-done.4.shard_5) | copy-start | bytes 786436
  19.4 5.6 %collective-permute-start.8 = (bf16[16,4096]{1,0:T(8,128)(2,1)S(1)}, bf16[16,4096]{1,0:T(8,128)(2,1)S(1)}, u32[]{:S(2)}, u32[]{:S(2)}) collective-permute-start(bf16[16,4096]{1,0:T(8,128)(2,1)S(1)} %slice.41), channel_id=1, source_target_pairs={{0,3},{1,0},{2,1},{3,2},{4,7},{5,4},{6,5},{7,6},{8,11},{9,8},{10,9... | collective-permute-start | bytes 393224 | tf_op jit(solution)/shard_map/ppermute | solution.py:281
  23.7 1.3 copy-start.20
  23.7 1.3 copy-start.21
  25.0 0.7 copy-start.23
  41.2 6.7 %copy-start.1 = (f32[16,8192]{1,0:T(8,128)S(1)}, f32[16,8192]{1,0:T(8,128)}, u32[]{:S(2)}) copy-start(f32[16,8192]{1,0:T(8,128)} %bo_ref.1) | copy-start | bytes 1572868
  41.2 6.9 %copy-start.6 = (bf16[16,8192]{1,0:T(8,128)(2,1)S(1)}, bf16[16,8192]{1,0:T(8,128)(2,1)}, u32[]{:S(2)}) copy-start(bf16[16,8192]{1,0:T(8,128)(2,1)} %up_output_ref.1) | copy-start | bytes 786436
  41.2 6.9 %copy-start.28 = (bf16[8192,5]{0,1:T(8,128)(2,1)S(1)}, bf16[8192,5]{0,1:T(8,128)(2,1)}, u32[]{:S(2)}) copy-start(bf16[8192,5]{0,1:T(8,128)(2,1)} %param.21) | copy-start | bytes 245764
  41.2 28.4 %all-to-all-start = ((bf16[8,16,8192]{2,1,0:T(8,128)(2,1)}), bf16[8,16,8192]{2,1,0:T(8,128)(2,1)}, u32[]{:S(2)}, u32[]{:S(2)}) async-start(bf16[8,16,8192]{2,1,0:T(8,128)(2,1)} %get-tuple-element.27), calls=%async_computation | async-start | bytes 4194304 | tf_op jit(solution)/shard_map/all_to_all | solution.py:841
  47.9 23.6 %copy-start.7 = (bf16[1,16,8192]{2,1,0:T(8,128)(2,1)S(1)}, bf16[1,16,8192]{2,1,0:T(8,128)(2,1)}, u32[]{:S(2)}) copy-start(bf16[1,16,8192]{2,1,0:T(8,128)(2,1)} %param.17) | copy-start | bytes 786436
  48.1 30.7 %copy-start.29 = (s32[16]{0:T(128)S(1)}, s32[16]{0:T(128)}, u32[]{:S(2)}) copy-start(s32[16]{0:T(128)} %param.23) | copy-start | bytes 196
  48.1 38.2 %copy-start.2 = (f32[4096,16]{0,1:T(8,128)S(1)}, f32[4096,16]{0,1:T(8,128)}, u32[]{:S(2)}) copy-start(f32[4096,16]{0,1:T(8,128)} %param.32) | copy-start | bytes 786436
  49.1 47.1 %copy-start.4 = (f32[2,16,1024]{2,1,0:T(8,128)S(1)}, f32[2,16,1024]{2,1,0:T(8,128)}, u32[]{:S(2)}) copy-start(f32[2,16,1024]{2,1,0:T(8,128)} %bkv_ref.1) | copy-start | bytes 393220
  49.1 47.9 %copy-start.3 = (f32[16,4096]{1,0:T(8,128)S(1)}, f32[16,4096]{1,0:T(8,128)}, u32[]{:S(2)}) copy-start(f32[16,4096]{1,0:T(8,128)} %bq_ref.1) | copy-start | bytes 786436
  71.6 26.8 %copy-start.8 = (bf16[16,8192]{1,0:T(8,128)(2,1)}, bf16[16,8192]{1,0:T(8,128)(2,1)S(1)}, u32[]{:S(2)}) copy-start(bf16[16,8192]{1,0:T(8,128)(2,1)S(1)} %add_convert_fusion.shard_0) | copy-start | bytes 786436
  71.6 12.0 %collective-permute-start.9 = (bf16[16,8192]{1,0:T(8,128)(2,1)S(1)}, bf16[16,8192]{1,0:T(8,128)(2,1)S(1)}, u32[]{:S(2)}, u32[]{:S(2)}) collective-permute-start(bf16[16,8192]{1,0:T(8,128)(2,1)S(1)} %add_convert_fusion.shard_0), channel_id=1, source_target_pairs={{0,4},{1,5},{2,6},{3,7},{4,0},{5,1},{6,2},{7,3},{8,12},{9,13},{10,... | collective-permute-start | bytes 786440 | tf_op jit(solution)/shard_map/ppermute | solution.py:281
  78.9 7.9 %collective-permute-start.10 = (bf16[16,8192]{1,0:T(8,128)(2,1)S(1)}, bf16[16,8192]{1,0:T(8,128)(2,1)S(1)}, u32[]{:S(2)}, u32[]{:S(2)}) collective-permute-start(bf16[16,8192]{1,0:T(8,128)(2,1)S(1)} %add_convert_fusion.shard_0), channel_id=1, source_target_pairs={{0,1},{1,2},{2,3},{3,0},{4,5},{5,6},{6,7},{7,4},{8,9},{9,10},{10,1... | collective-permute-start | bytes 786440 | tf_op jit(solution)/shard_map/ppermute | solution.py:281
  79.9 7.1 %collective-permute-start.11 = (bf16[16,8192]{1,0:T(8,128)(2,1)S(1)}, bf16[16,8192]{1,0:T(8,128)(2,1)S(1)}, u32[]{:S(2)}, u32[]{:S(2)}) collective-permute-start(bf16[16,8192]{1,0:T(8,128)(2,1)S(1)} %add_convert_fusion.shard_0), channel_id=1, source_target_pairs={{0,3},{1,0},{2,1},{3,2},{4,7},{5,4},{6,5},{7,6},{8,11},{9,8},{10,9... | collective-permute-start | bytes 786440 | tf_op jit(solution)/shard_map/ppermute | solution.py:281
  83.6 14.9 %copy-start.19 = (bf16[16,8192]{1,0:T(8,128)(2,1)}, bf16[16,8192]{1,0:T(8,128)(2,1)S(1)}, u32[]{:S(2)}) copy-start(bf16[16,8192]{1,0:T(8,128)(2,1)S(1)} %collective-permute-done.9.shard_1) | copy-start | bytes 786436
  83.6 8.4 %collective-permute-start.12 = (bf16[16,8192]{1,0:T(8,128)(2,1)S(1)}, bf16[16,8192]{1,0:T(8,128)(2,1)S(1)}, u32[]{:S(2)}, u32[]{:S(2)}) collective-permute-start(bf16[16,8192]{1,0:T(8,128)(2,1)S(1)} %collective-permute-done.9.shard_1), channel_id=1, source_target_pairs={{0,1},{1,2},{2,3},{3,0},{4,5},{5,6},{6,7},{7,4},{8,9},{9,10},{10,1... | collective-permute-start | bytes 786440 | tf_op jit(solution)/shard_map/ppermute | solution.py:281
  85.0 7.8 %collective-permute-start.13 = (bf16[16,8192]{1,0:T(8,128)(2,1)S(1)}, bf16[16,8192]{1,0:T(8,128)(2,1)S(1)}, u32[]{:S(2)}, u32[]{:S(2)}) collective-permute-start(bf16[16,8192]{1,0:T(8,128)(2,1)S(1)} %collective-permute-done.9.shard_1), channel_id=1, source_target_pairs={{0,3},{1,0},{2,1},{3,2},{4,7},{5,4},{6,5},{7,6},{8,11},{9,8},{10,9... | collective-permute-start | bytes 786440 | tf_op jit(solution)/shard_map/ppermute | solution.py:281
  86.7 11.7 %copy-start.14 = (bf16[16,8192]{1,0:T(8,128)(2,1)}, bf16[16,8192]{1,0:T(8,128)(2,1)S(1)}, u32[]{:S(2)}) copy-start(bf16[16,8192]{1,0:T(8,128)(2,1)S(1)} %collective-permute-done.10.shard_2) | copy-start | bytes 786436
  86.8 10.3 %collective-permute-start.14 = (bf16[16,4096]{1,0:T(8,128)(2,1)S(1)}, bf16[16,4096]{1,0:T(8,128)(2,1)S(1)}, u32[]{:S(2)}, u32[]{:S(2)}) collective-permute-start(bf16[16,4096]{1,0:T(8,128)(2,1)S(1)} %slice.42), channel_id=1, source_target_pairs={{0,1},{1,2},{2,3},{3,0},{4,5},{5,6},{6,7},{7,4},{8,9},{9,10},{10,1... | collective-permute-start | bytes 393224 | tf_op jit(solution)/shard_map/ppermute | solution.py:281
  87.0 11.4 %copy-start.15 = (bf16[16,8192]{1,0:T(8,128)(2,1)}, bf16[16,8192]{1,0:T(8,128)(2,1)S(1)}, u32[]{:S(2)}) copy-start(bf16[16,8192]{1,0:T(8,128)(2,1)S(1)} %collective-permute-done.11.shard_3) | copy-start | bytes 786436
  87.7 9.3 %collective-permute-start.15 = (bf16[16,4096]{1,0:T(8,128)(2,1)}, bf16[16,4096]{1,0:T(8,128)(2,1)S(1)}, u32[]{:S(2)}, u32[]{:S(2)}) collective-permute-start(bf16[16,4096]{1,0:T(8,128)(2,1)} %slice.43), channel_id=1, source_target_pairs={{0,3},{1,0},{2,1},{3,2},{4,7},{5,4},{6,5},{7,6},{8,11},{9,8},{10,9... | collective-permute-start | bytes 393224 | tf_op jit(solution)/shard_map/ppermute | solution.py:281
  92.0 6.4 %copy-start.16 = (bf16[16,8192]{1,0:T(8,128)(2,1)}, bf16[16,8192]{1,0:T(8,128)(2,1)S(1)}, u32[]{:S(2)}) copy-start(bf16[16,8192]{1,0:T(8,128)(2,1)S(1)} %collective-permute-done.12.shard_4) | copy-start | bytes 786436
  92.8 5.3 %collective-permute-start.16 = (bf16[16,4096]{1,0:T(8,128)(2,1)}, bf16[16,4096]{1,0:T(8,128)(2,1)S(1)}, u32[]{:S(2)}, u32[]{:S(2)}) collective-permute-start(bf16[16,4096]{1,0:T(8,128)(2,1)} %slice.44), channel_id=1, source_target_pairs={{0,1},{1,2},{2,3},{3,0},{4,5},{5,6},{6,7},{7,4},{8,9},{9,10},{10,1... | collective-permute-start | bytes 393224 | tf_op jit(solution)/shard_map/ppermute | solution.py:281
  92.8 5.7 %copy-start.17 = (bf16[16,8192]{1,0:T(8,128)(2,1)}, bf16[16,8192]{1,0:T(8,128)(2,1)S(1)}, u32[]{:S(2)}) copy-start(bf16[16,8192]{1,0:T(8,128)(2,1)S(1)} %collective-permute-done.13.shard_5) | copy-start | bytes 786436
  93.5 4.9 %collective-permute-start.17 = (bf16[16,4096]{1,0:T(8,128)(2,1)}, bf16[16,4096]{1,0:T(8,128)(2,1)S(1)}, u32[]{:S(2)}, u32[]{:S(2)}) collective-permute-start(bf16[16,4096]{1,0:T(8,128)(2,1)} %slice.45), channel_id=1, source_target_pairs={{0,3},{1,0},{2,1},{3,2},{4,7},{5,4},{6,5},{7,6},{8,11},{9,8},{10,9... | collective-permute-start | bytes 393224 | tf_op jit(solution)/shard_map/ppermute | solution.py:281
  97.1 1.4 copy-start.24
  97.1 1.4 copy-start.25
  111.5 13.4 %all-to-all-start.1 = ((f32[8,40,128]{2,1,0:T(8,128)}), f32[8,40,128]{2,1,0:T(8,128)S(1)}, u32[]{:S(2)}, u32[]{:S(2)}) async-start(f32[8,40,128]{2,1,0:T(8,128)} %bitcast.64), calls=%async_computation.1 | async-start | bytes 327680 | tf_op jit(solution)/shard_map/all_to_all | solution.py:861
  125.0 0.7 copy-start.9
  130.8 26.0 %all-to-all-start.2 = ((bf16[16,56,512]{2,1,0:T(8,128)(2,1)}), bf16[16,56,512]{2,1,0:T(8,128)(2,1)S(1)}, u32[]{:S(2)}, u32[]{:S(2)}) async-start(bf16[16,56,512]{2,1,0:T(8,128)(2,1)} %jacobian.1), calls=%async_computation.2 | async-start | bytes 1835008 | tf_op jit(solution)/shard_map/all_to_all | solution.py:863
  157.1 1.1 copy-start.5
  179.6 28.3 %copy-start = (f32[3,8192,16]{1,2,0:T(8,128)S(1)}, f32[3,8192,16]{1,2,0:T(8,128)}, u32[]{:S(2)}) copy-start(f32[3,8192,16]{1,2,0:T(8,128)} %param.29) | copy-start | bytes 4718596
  (3 other events, 2.0 us)

commit v5 on v4

--- a/solution.py
+++ b/solution.py
@@ -165,8 +165,10 @@
 
 
 def assemble_body(
+    core_ref,
     part_ref,
-    every_ref,
+    own_ref,
+    other_ref,
     a_ref,
     bq_ref,
     bkv_ref,
@@ -191,15 +193,21 @@
     lane = lax.broadcasted_iota(jnp.int32, (64, 64), 1)
     wanted = (row % 8) * 8 + ((row % 16) // 8) * 4 + row // 16
     moved = jnp.where(lane == wanted, 1.0, 0.0).astype(jnp.bfloat16)
+
+    def pick(core, spot, lanes):
+        return jnp.where(
+            core_ref[0] == core, own_ref[spot, :, lanes], other_ref[spot, :, lanes]
+        )
+
     for half in range(2):
-        group = 2 * step + half
-        block = every_ref[pl.ds(8 * group, 8), :, :LANES].reshape(64, LANES)
+        spot = pl.ds(pl.multiple_of(8 * step, 8), 8)
+        block = pick(half, spot, slice(0, LANES)).reshape(64, LANES)
         placed = dot_halved(moved, block, 1, 0).reshape(4, 16, LANES)
         lanes = slice(half * LANES, (half + 1) * LANES)
         out_a_ref[:, :, lanes] = placed[:3] + part * a_ref[:, :, lanes]
         out_bo_ref[:, lanes] = placed[3] + part * bo_ref[:, lanes]
     block = jnp.concatenate(
-        [every_ref[8 * group + step, :, LANES:] for group in range(16)], 0
+        [pick(at % 2, 8 * (at // 2) + step, slice(LANES, None)) for at in range(16)], 0
     )
     placed = dot_halved(one_hot(128, 8, 16), block, 1, 0)
     for chunk in range(4):
@@ -250,25 +258,53 @@
     return flat([rows[at : at + 128] for at in range(0, rows.shape[0], 128)])
 
 
-def place_shards(spots_ref, whole_ref, shards, first_half):
-    for at in range(6):
-        rows = pl.ds(pl.multiple_of(spots_ref[at] * 16, 16), 16)
-        whole_ref[rows, :] = shards[at][...]
-    for at in range(2):
-        rows = pl.ds(pl.multiple_of(spots_ref[6 + at] * 16, 16), 16)
-        whole_ref[rows, :] = jnp.where(
-            first_half, shards[6 + 2 * at][...], shards[7 + 2 * at][...]
-        )
-
-
-def shard_specs(last_step):
-    half = last_step // 2
-    full = pl.BlockSpec((16, CHUNK), lambda step: (0, jnp.minimum(step, last_step)))
-    early = pl.BlockSpec((16, CHUNK), lambda step: (0, jnp.minimum(step, half)))
-    late = pl.BlockSpec(
-        (16, CHUNK), lambda step: (0, jnp.clip(step - half - 1, 0, last_step - half - 1))
-    )
-    return [full] * 6 + [early, late] * 2
+def place_shards(spots_ref, whole_ref, shards, semaphores):
+    half = whole_ref.shape[1] // 2
+    copies = []
+    for at, shard in enumerate(shards):
+        spot = at if at < 6 else 6 + (at - 6) // 2
+        rows = pl.ds(pl.multiple_of(spots_ref[spot] * 16, 16), 16)
+        if at < 6:
+            target = whole_ref.at[rows, :]
+        else:
+            target = whole_ref.at[rows, pl.ds((at % 2) * half, half)]
+        copies.append(pltpu.make_async_copy(shard, target, semaphores.at[at]))
+    for copy in copies:
+        copy.start()
+    return copies
+
+
+def launch(pairs, semaphores, first):
+    copies = prepared(pairs, semaphores, first)
+    begin(copies)
+    return copies
+
+
+def finish(copies):
+    for copy in copies:
+        copy.wait()
+
+
+def prepared(pairs, semaphores, first):
+    return [
+        pltpu.make_async_copy(source, target, semaphores.at[first + at])
+        for at, (source, target) in enumerate(pairs)
+    ]
+
+
+def begin(copies):
+    for copy in copies:
+        copy.start()
+
+
+def span_of(step):
+    if isinstance(step, int):
+        return pl.ds(step * CHUNK, CHUNK)
+    return pl.ds(pl.multiple_of(step * CHUNK, CHUNK), CHUNK)
+
+
+ANYWHERE = pl.BlockSpec(memory_space=pl.ANY)
+LARGE = 60 * 2**20
 
 
 def gather_by_relays(block):
@@ -312,6 +348,7 @@
 
 
 CHUNK = 2048
+STATE_ROWS = 2368
 
 
 def forward_body(
@@ -326,32 +363,29 @@
     shard_7,
     shard_8,
     shard_9,
+    query_weight_hbm,
+    kv_weight_hbm,
+    down_hbm,
+    output_weight_hbm,
+    up_output_hbm,
+    small_hbm,
+    tokens_hbm,
+    out_hbm,
+    state_hbm,
+    tokens_ref,
     query_weight_ref,
     kv_weight_ref,
     down_ref,
     output_weight_ref,
     up_output_ref,
-    down_output_ref,
-    up_query_ref,
-    up_kv_ref,
-    tokens_ref,
+    small_ref,
     out_ref,
-    query_ref,
-    keys_ref,
-    values_ref,
-    prob_ref,
-    capped_ref,
-    context_ref,
-    low_ref,
-    context_low_ref,
+    state_ref,
     query_sum,
     kv_sum,
     low_sum,
-    halved_ref,
-    halved_low_ref,
+    semaphores,
 ):
-    step = pl.program_id(0)
-    steps = pl.num_programs(0) // 2
     shards = [
         shard_0,
         shard_1,
@@ -364,152 +398,133 @@
         shard_8,
         shard_9,
     ]
-
-    @pl.when(step < steps)
-    def _():
-        place_shards(spots_ref, tokens_ref, shards, step < steps // 2)
-        tokens = tokens_ref[...]
-        query = dot_halved(tokens, query_weight_ref[...], 1, 0)
-        kv = dot_halved(tokens, flat([kv_weight_ref[0], kv_weight_ref[1]]), 1, 0)
-        low = dot_halved(down_ref[...], tokens, 1, 1)
-
-        @pl.when(step == 0)
-        def _():
-            query_sum[...] = query
-            kv_sum[...] = kv
-            low_sum[...] = jnp.zeros(low_sum.shape, jnp.float32)
-            low_sum[:48] = low
-
-        @pl.when(step > 0)
-        def _():
-            query_sum[...] += query
-            kv_sum[...] += kv
-            low_sum[:48] += low
-
-    @pl.when(step == steps - 1)
-    def _():
-        low_turned = low_sum[...]
-        low = low_turned.T
-        low_ref[...] = low_turned[:48]
-        root = 1.0 / math.sqrt(HEAD_SIZE)
-
-        def adapted(total, piece, up):
-            parts = rounded_parts(low[:, 16 * piece : 16 * piece + 16], 2)
-            return total + ADAPTER_SCALE * dot_halved(flat(parts), tall([up, up]), 1, 0)
-
-        query = adapted(query_sum[...], 0, up_query_ref[...])
-        keys = adapted(kv_sum[:, :128], 1, up_kv_ref[0])
-        values = adapted(kv_sum[:, 128:], 2, up_kv_ref[1])
-        capped = jnp.tanh(product(stack(query), keys, 1) * (root / SCORE_CAP))
-        row = lax.broadcasted_iota(jnp.int32, (512, 128), 0) % 128
-        lane = lax.broadcasted_iota(jnp.int32, (512, 128), 1)
-        weights = jnp.where(row >= lane, jnp.exp(SCORE_CAP * capped), 0.0)
-        probs = weights / lane_sum(weights)
-        context = unstack(product(probs, values, 0))
-        low_pair = dot_halved(down_output_ref[...], tall(rounded_parts(context, 2)), 1, 1)
-        context_low = ADAPTER_SCALE * (low_pair[:, :128] + low_pair[:, 128:])
-        query_ref[...] = query
-        keys_ref[...] = keys
-        values_ref[...] = values
-        prob_ref[...] = probs
-        capped_ref[...] = capped
-        context_ref[...] = context
-        context_low_ref[...] = context_low
-        halved_ref[...] = context.astype(jnp.bfloat16)
-        turned = tall([context_low, jnp.zeros((112, 128), jnp.float32)]).T[:, :16]
-        halved_low_ref[...] = flat(rounded_parts(turned, 2))
-
-    @pl.when(step >= steps)
-    def _():
-        up = up_output_ref[...]
-        terms = dot_halved(halved_ref[...], output_weight_ref[...], 1, 0) + dot_halved(
-            halved_low_ref[...], tall([up, up]), 1, 0
+    placed = place_shards(spots_ref, tokens_ref, shards, semaphores)
+    count = tokens_ref.shape[1] // CHUNK
+
+    def early(step):
+        span = span_of(step)
+        pairs = [
+            (query_weight_hbm.at[span, :], query_weight_ref.at[span, :]),
+            (kv_weight_hbm.at[:, span, :], kv_weight_ref.at[:, span, :]),
+            (down_hbm.at[:, span], down_ref.at[:, span]),
+        ]
+        return prepared(pairs, semaphores, 10 + 3 * step)
+
+    def late(step):
+        span = span_of(step)
+        pairs = [
+            (output_weight_hbm.at[:, span], output_weight_ref.at[:, span]),
+            (up_output_hbm.at[:, span], up_output_ref.at[:, span]),
+        ]
+        return prepared(pairs, semaphores, 10 + 3 * count + 2 * step)
+
+    def departing(step):
+        span = span_of(step)
+        pairs = [(out_ref.at[:, :, span], out_hbm.at[:, :, span])]
+        return prepared(pairs, semaphores, 10 + 5 * count + step)
+
+    for step in range(count):
+        begin(early(step))
+    small_copy = launch([(small_hbm, small_ref)], semaphores, 10 + 6 * count)
+    for step in range(count):
+        begin(late(step))
+    finish(placed)
+    leaving = launch([(tokens_ref, tokens_hbm)], semaphores, 11 + 6 * count)
+    query_sum[...] = jnp.zeros(query_sum.shape, jnp.float32)
+    kv_sum[...] = jnp.zeros(kv_sum.shape, jnp.float32)
+    low_sum[...] = jnp.zeros(low_sum.shape, jnp.float32)
+
+    def project(step, _):
+        finish(early(step))
+        span = span_of(step)
+        tokens = tokens_ref[:, span]
+        query_sum[...] += dot_halved(tokens, query_weight_ref[span, :], 1, 0)
+        kv_sum[...] += dot_halved(
+            tokens, flat([kv_weight_ref[0, span, :], kv_weight_ref[1, span, :]]), 1, 0
         )
-        out_ref[...] = terms.astype(jnp.bfloat16).reshape(out_ref.shape)
-
-
-def fixed(array):
-    zeros = (0,) * array.ndim
-    return pl.BlockSpec(array.shape, lambda step: zeros)
+        low_sum[:48] += dot_halved(down_ref[:, span], tokens, 1, 1)
+        return 0
+
+    lax.fori_loop(0, count, project, 0)
+    finish(small_copy)
+    low_turned = low_sum[...]
+    low = low_turned.T
+    root = 1.0 / math.sqrt(HEAD_SIZE)
+
+    def adapted(total, piece, up):
+        parts = rounded_parts(low[:, 16 * piece : 16 * piece + 16], 2)
+        return total + ADAPTER_SCALE * dot_halved(flat(parts), tall([up, up]), 1, 0)
+
+    query = stack(adapted(query_sum[...], 0, small_ref[:, 512:1024]))
+    keys = adapted(kv_sum[:, :128], 1, small_ref[:, 1024:1152])
+    values = adapted(kv_sum[:, 128:], 2, small_ref[:, 1152:])
+    capped = jnp.tanh(product(query, keys, 1) * (root / SCORE_CAP))
+    row = lax.broadcasted_iota(jnp.int32, (512, 128), 0) % 128
+    lane = lax.broadcasted_iota(jnp.int32, (512, 128), 1)
+    weights = jnp.where(row >= lane, jnp.exp(SCORE_CAP * capped), 0.0)
+    probs = weights / lane_sum(weights)
+    context_rows = product(probs, values, 0)
+    context = unstack(context_rows)
+    low_pair = dot_halved(small_ref[:, :512], tall(rounded_parts(context, 2)), 1, 1)
+    context_low = ADAPTER_SCALE * (low_pair[:, :128] + low_pair[:, 128:])
+    state_ref[0:512] = query
+    state_ref[512:1024] = context_rows
+    state_ref[1024:1536] = probs
+    state_ref[1536:2048] = capped
+    state_ref[2048:2176] = keys
+    state_ref[2176:2304] = values
+    state_ref[2304:2352] = low_turned[:48]
+    state_ref[2352:2368] = context_low
+    halved = context.astype(jnp.bfloat16)
+    turned = tall([context_low, jnp.zeros((112, 128), jnp.float32)]).T[:, :16]
+    halved_low = flat(rounded_parts(turned, 2))
+    leaving += launch([(state_ref, state_hbm)], semaphores, 12 + 6 * count)
+
+    def write(step, _):
+        finish(late(step))
+        span = span_of(step)
+        up = up_output_ref[:, span]
+        terms = dot_halved(halved, output_weight_ref[:, span], 1, 0) + dot_halved(
+            halved_low, tall([up, up]), 1, 0
+        )
+        out_ref[:, :, span] = terms.astype(jnp.bfloat16).reshape(8, 16, CHUNK)
+        begin(departing(step))
+        return 0
+
+    lax.fori_loop(0, count, write, 0)
+    for step in range(count):
+        finish(departing(step))
+    finish(leaving)
 
 
 def forward(
-    spots,
-    shards,
-    query_weight,
-    key_value_weight,
-    down_rows,
-    output_weight,
-    up_output,
-    down_output,
-    up_query,
-    up_key_value,
+    spots, shards, query_weight, key_value_weight, down_rows, output_weight, up_output, small
 ):
     width = shards[0].shape[1]
-    steps = width // CHUNK
-    last = steps - 1
     query_cols = query_weight.shape[1]
-
-    def first_part(step):
-        return jnp.minimum(step, last)
-
-    def second_part(step):
-        return jnp.maximum(step - steps, 0)
-
-    shapes = [
+    arrays = (query_weight, key_value_weight, down_rows, output_weight, up_output, small)
+    results = [
         jax.ShapeDtypeStruct((128, width), jnp.bfloat16),
         jax.ShapeDtypeStruct((8, 16, width), jnp.bfloat16),
-        jax.ShapeDtypeStruct((128, query_cols), jnp.float32),
-        jax.ShapeDtypeStruct((128, 128), jnp.float32),
-        jax.ShapeDtypeStruct((128, 128), jnp.float32),
-        jax.ShapeDtypeStruct((512, 128), jnp.float32),
-        jax.ShapeDtypeStruct((512, 128), jnp.float32),
-        jax.ShapeDtypeStruct((128, query_cols), jnp.float32),
-        jax.ShapeDtypeStruct((48, 128), jnp.float32),
-        jax.ShapeDtypeStruct((16, 128), jnp.float32),
+        jax.ShapeDtypeStruct((STATE_ROWS, 128), jnp.float32),
     ]
+    scratch = [results[0], *arrays, results[1], results[2]]
     return pl.pallas_call(
         forward_body,
-        grid=(2 * steps,),
         in_specs=[pl.BlockSpec(memory_space=pltpu.SMEM)]
-        + shard_specs(last)
+        + [ANYWHERE] * (len(shards) + len(arrays)),
+        out_specs=[ANYWHERE] * 3,
+        out_shape=results,
+        scratch_shapes=[pltpu.VMEM(array.shape, array.dtype) for array in scratch]
         + [
-            pl.BlockSpec((CHUNK, query_cols), lambda step: (first_part(step), 0)),
-            pl.BlockSpec((2, CHUNK, 128), lambda step: (0, first_part(step), 0)),
-            pl.BlockSpec((48, CHUNK), lambda step: (0, first_part(step))),
-            pl.BlockSpec((query_cols, CHUNK), lambda step: (0, second_part(step))),
-            pl.BlockSpec((16, CHUNK), lambda step: (0, second_part(step))),
-            fixed(down_output),
-            fixed(up_query),
-            fixed(up_key_value),
-        ],
-        out_specs=[
-            pl.BlockSpec((128, CHUNK), lambda step: (0, first_part(step))),
-            pl.BlockSpec((8, 16, CHUNK), lambda step: (0, 0, second_part(step))),
-        ]
-        + [fixed(shape) for shape in shapes[2:]],
-        out_shape=shapes,
-        scratch_shapes=[
             pltpu.VMEM((128, query_cols), jnp.float32),
             pltpu.VMEM((128, 256), jnp.float32),
             pltpu.VMEM((128, 128), jnp.float32),
-            pltpu.VMEM((128, query_cols), jnp.bfloat16),
-            pltpu.VMEM((128, 32), jnp.bfloat16),
+            pltpu.SemaphoreType.DMA((13 + 6 * (width // CHUNK),)),
         ],
-        compiler_params=pltpu.CompilerParams(vmem_limit_bytes=60 * 2**20),
+        compiler_params=pltpu.CompilerParams(vmem_limit_bytes=LARGE),
         name="forward",
-    )(
-        spots,
-        *shards,
-        query_weight,
-        key_value_weight,
-        down_rows,
-        output_weight,
-        up_output,
-        down_output,
-        up_query,
-        up_key_value,
-    )
+    )(spots, *shards, *arrays)
 
 
 def cotangents_body(
@@ -525,29 +540,24 @@
     shard_7,
     shard_8,
     shard_9,
+    weight_hbm,
+    side_hbm,
+    state_hbm,
+    small_hbm,
+    resid_hbm,
+    factors_ref,
+    narrow_ref,
+    scalars_ref,
+    resid_ref,
     weight_ref,
     side_ref,
-    query_ref,
-    keys_ref,
-    values_ref,
-    prob_ref,
-    capped_ref,
-    context_ref,
-    low_ref,
-    context_low_ref,
-    down_ref,
-    up_query_ref,
-    up_kv_ref,
-    resid_ref,
-    factors_ref,
-    narrow_ref,
-    rewards_ref,
-    repeated_ref,
+    state_ref,
+    small_ref,
     through_ref,
     slow_ref,
     square_ref,
+    semaphores,
 ):
-    step = pl.program_id(0)
     shards = [
         shard_0,
         shard_1,
@@ -560,33 +570,74 @@
         shard_8,
         shard_9,
     ]
-    place_shards(spots_ref, resid_ref, shards, step < pl.num_programs(0) // 2)
-    chunk = resid_ref[...]
-    side = side_ref[...]
-    left = tall([chunk, side[16:]])
-    through = dot_halved(left, weight_ref[...], 1, 1)
-    slow = dot_halved(left, side, 1, 1)
-    wide = chunk.astype(jnp.float32)
-    square = jnp.zeros((128, 128), jnp.float32)
-    for at in range(0, chunk.shape[1], 128):
-        square = square + wide[:, at : at + 128] * wide[:, at : at + 128]
-
-    @pl.when(step == 0)
-    def _():
-        slow_ref[...] = jnp.zeros(slow_ref.shape, jnp.float32)
-        through_ref[...] = through
-        slow_ref[:144, :32] = slow
-        square_ref[...] = square
-
-    @pl.when(step > 0)
-    def _():
-        through_ref[...] += through
-        slow_ref[:144, :32] += slow
+    placed = place_shards(spots_ref, resid_ref, shards, semaphores)
+    count = resid_ref.shape[1] // CHUNK
+
+    def early(step):
+        span = span_of(step)
+        pairs = [
+            (weight_hbm.at[:, span], weight_ref.at[:, span]),
+            (side_hbm.at[:, span], side_ref.at[:, span]),
+        ]
+        return prepared(pairs, semaphores, 10 + 2 * step)
+
+    for step in range(count):
+        begin(early(step))
+    first = 10 + 2 * count
+    others = launch([(state_hbm, state_ref), (small_hbm, small_ref)], semaphores, first)
+    slow_ref[...] = jnp.zeros(slow_ref.shape, jnp.float32)
+    through_ref[...] = jnp.zeros(through_ref.shape, jnp.float32)
+    square_ref[...] = jnp.zeros(square_ref.shape, jnp.float32)
+    narrow_ref[...] = jnp.zeros(narrow_ref.shape, jnp.float32)
+    width = resid_ref.shape[1]
+    finish(placed)
+    leaving = launch([(resid_ref, resid_hbm)], semaphores, first + 2)
+
+    def project(step, _):
+        finish(early(step))
+        span = span_of(step)
+        chunk = resid_ref[:, span]
+        side = side_ref[:, span]
+        left = tall([chunk, side[16:]])
+        through_ref[...] += dot_halved(left, weight_ref[:, span], 1, 1)
+        slow_ref[:144, :32] += dot_halved(left, side, 1, 1)
+        wide = chunk.astype(jnp.float32)
+        square = jnp.zeros((128, 128), jnp.float32)
+        for lanes in range(0, CHUNK, 128):
+            square = square + wide[:, lanes : lanes + 128] * wide[:, lanes : lanes + 128]
         square_ref[...] += square
-
-    @pl.when(step == pl.num_programs(0) - 1)
-    def _():
-        width = chunk.shape[1] * pl.num_programs(0)
+        return 0
+
+    lax.fori_loop(0, count, project, 0)
+    finish(others)
+    finish_cotangents(
+        lens_ref,
+        width,
+        state_ref,
+        small_ref,
+        factors_ref,
+        narrow_ref,
+        scalars_ref,
+        through_ref,
+        slow_ref,
+        square_ref,
+    )
+    finish(leaving)
+
+
+def finish_cotangents(
+    lens_ref,
+    width,
+    state_ref,
+    small_ref,
+    factors_ref,
+    narrow_ref,
+    scalars_ref,
+    through_ref,
+    slow_ref,
+    square_ref,
+):
+    if True:
         length_own = lens_ref[0]
         root = 1.0 / math.sqrt(HEAD_SIZE)
         slow = slow_ref[...]
@@ -609,29 +660,39 @@
             lead_turned * inverse_turned * inverse_turned * slow_turned[16:32, :128] / width
         )
         low_turned = slow_turned[:16, :128]
-        rewards_ref[...] = jnp.zeros(rewards_ref.shape, jnp.float32)
-        rewards_ref[:1, :16] = row_sum(share * logits)
-        down = down_ref[...]
+        scalars_ref[:8] = jnp.zeros((8, 128), jnp.float32)
+        scalars_ref[:1, :16] = row_sum(share * logits)
+        down = small_ref[:, :512]
         through = through_ref[...] + ADAPTER_SCALE * dot_halved(
             flat(rounded_parts(slow[:144, :16], 2)), tall([down, down]), 1, 0
         )
-        narrow_ref[...] = jnp.zeros(narrow_ref.shape, jnp.float32)
-        context = context_ref[...]
-        context_rows = stack(context)
-        probs = prob_ref[...]
-        capped = capped_ref[...]
+        context_rows = state_ref[512:1024]
+        context = unstack(context_rows)
+        probs = state_ref[1024:1536]
+        capped = state_ref[1536:2048]
         slope = probs * (1.0 - capped * capped) * root
         probs_turned = tall(rounded_parts(probs.T, 2))
-        query_turned = tall(rounded_parts(stack(query_ref[...]).T, 2))
-        keys = keys_ref[...]
-        values = values_ref[...]
-        low = [tall(rounded_parts(low_ref[16 * at : 16 * at + 16], 2)) for at in range(3)]
-        up_query = up_query_ref[...]
-        context_low = context_low_ref[...]
-        cot_low = []
-        for obj in range(OBJ):
-            lead_row = through[128 + obj : 129 + obj]
-            cot = stack(lead * lead_row - pulled[:, obj : obj + 1] * through[:128])
+        query_turned = tall(rounded_parts(state_ref[0:512].T, 2))
+        keys = state_ref[2048:2176]
+        values = state_ref[2176:2304]
+        low = [
+            tall(rounded_parts(state_ref[2304 + 16 * at : 2320 + 16 * at], 2)) for at in range(3)
+        ]
+        up_query = small_ref[:, 512:1024]
+        up_keys = small_ref[:, 1024:1152]
+        up_values = small_ref[:, 1152:]
+        context_low = state_ref[2352:2368]
+        through_ref[...] = through
+        through_tokens = through[:128]
+        heads_low = slow_turned[:16, 128:]
+        lane_pulled = lax.broadcasted_iota(jnp.int32, pulled.shape, 1)
+        lane_low = lax.broadcasted_iota(jnp.int32, heads_low.shape, 1)
+        row_pulled = lax.broadcasted_iota(jnp.int32, pulled_turned.shape, 0)
+
+        def objective(obj, _):
+            pulled_own = lane_sum(jnp.where(lane_pulled == obj, pulled, 0.0))
+            lead_row = through_ref[pl.ds(128 + obj, 1), :]
+            cot = stack(lead * lead_row - pulled_own * through_tokens)
             cot_prob = product(cot, values, 1)
             cot_score = slope * (cot_prob - lane_sum(cot * context_rows))
             cot_query = unstack(product(cot_score, keys, 0))
@@ -645,8 +706,8 @@
             keys_parts = rounded_parts(cot_keys, 2)
             values_parts = rounded_parts(cot_values, 2)
             factor_query = dot_halved(up_query, tall(query_parts), 1, 1)
-            factor_keys = dot_halved(up_kv_ref[0], flat(keys_parts), 1, 0)
-            factor_values = dot_halved(up_kv_ref[1], tall(values_parts), 1, 1)
+            factor_keys = dot_halved(up_keys, flat(keys_parts), 1, 0)
+            factor_values = dot_halved(up_values, tall(values_parts), 1, 1)
             rows = [
                 ADAPTER_SCALE * (factor[:, :128] + factor[:, 128:])
                 for factor in (factor_query, factor_keys, factor_values)
@@ -659,73 +720,102 @@
             jac_query = corners(dot_halved(low[0], flat(query_parts), 1, 0), 16, 512)
             jac_keys = corners(dot_halved(low[1], tall(keys_parts), 1, 1), 16, 128)
             jac_values = corners(dot_halved(low[2], flat(values_parts), 1, 0), 16, 128)
+            pulled_row = row_sum(jnp.where(row_pulled == obj, pulled_turned, 0.0))
+            head_low = lane_sum(jnp.where(lane_low == obj, heads_low, 0.0))
+            jac_down = product(head_low * lead_turned - pulled_row * low_turned, context, 0)
             blocks = [jac_query[:, at : at + 128] for at in range(0, 512, 128)]
-            spots = [(obj, 0), (obj, 1), (obj, 2), (obj, 3), (10 + obj, 0), (10 + obj, 1)]
+            blocks += [jac_down[:, at : at + 128] for at in range(0, 512, 128)]
+            spots = [(0, 0), (0, 1), (0, 2), (0, 3), (5, 0), (5, 1), (5, 2), (5, 3)]
+            spots += [(10, 0), (10, 1)]
             for (row, tile), block in zip(spots, blocks + [jac_keys, jac_values]):
                 for half in range(2):
-                    narrow_ref[tile, pl.ds(128 * half + row, 8, stride=16), :] = (
+                    narrow_ref[tile, pl.ds(128 * half + row + obj, 8, stride=16), :] = (
                         ADAPTER_SCALE * block[8 * half : 8 * half + 8]
                     )
-            cot_low.append(
-                slow_turned[:16, 128 + obj : 129 + obj] * lead_turned
-                - pulled_turned[obj : obj + 1] * low_turned
-            )
-        jac_down = ADAPTER_SCALE * product(tall(cot_low), context, 0)
-        for obj in range(OBJ):
-            for half in range(2):
-                start = 16 * obj + 8 * half
-                for tile in range(4):
-                    narrow_ref[tile, pl.ds(128 * half + 5 + obj, 8, stride=16), :] = jac_down[
-                        start : start + 8, 128 * tile : 128 * tile + 128
-                    ]
+            return 0
+
+        lax.fori_loop(0, OBJ, objective, 0, unroll=True)
         blank = jnp.zeros((15, 128), jnp.float32)
-        repeated_ref[0] = jnp.concatenate([blank, pulled_turned[:5]] * 2, 0)
-        repeated_ref[1] = jnp.broadcast_to(lead_turned, (40, 128))
-
-
-def cotangents(lens, spots, shards, output_weight, side, *others):
+        scalars_ref[8:48] = jnp.concatenate([blank, pulled_turned[:5]] * 2, 0)
+        scalars_ref[48:] = jnp.broadcast_to(lead_turned, (40, 128))
+
+
+def cotangents(lens, spots, shards, output_weight, side, state, small):
     width = shards[0].shape[1]
     query_cols = output_weight.shape[0]
-    steps = width // CHUNK
-
-    def chunked(rows):
-        return pl.BlockSpec((rows, CHUNK), lambda step: (0, step))
-
-    shapes = [
+    arrays = (output_weight, side, state, small)
+    results = [
         jax.ShapeDtypeStruct((128, width), jnp.bfloat16),
         jax.ShapeDtypeStruct((320, 128), jnp.float32),
         jax.ShapeDtypeStruct((4, 256, 128), jnp.float32),
-        jax.ShapeDtypeStruct((8, 128), jnp.float32),
-        jax.ShapeDtypeStruct((2, 40, 128), jnp.float32),
+        jax.ShapeDtypeStruct((88, 128), jnp.float32),
     ]
     return pl.pallas_call(
         cotangents_body,
-        grid=(steps,),
         in_specs=[pl.BlockSpec(memory_space=pltpu.SMEM)] * 2
-        + shard_specs(steps - 1)
-        + [chunked(query_cols), chunked(32)]
-        + [fixed(array) for array in others],
-        out_specs=[chunked(128)] + [fixed(shape) for shape in shapes[1:]],
-        out_shape=shapes,
-        scratch_shapes=[
+        + [ANYWHERE] * (len(shards) + len(arrays)),
+        out_specs=[ANYWHERE] + whole(3),
+        out_shape=results,
+        scratch_shapes=[pltpu.VMEM(array.shape, array.dtype) for array in (results[0], *arrays)]
+        + [
             pltpu.VMEM((144, query_cols), jnp.float32),
             pltpu.VMEM((256, 128), jnp.float32),
             pltpu.VMEM((128, 128), jnp.float32),
+            pltpu.SemaphoreType.DMA((13 + 2 * (width // CHUNK),)),
         ],
-        compiler_params=pltpu.CompilerParams(vmem_limit_bytes=60 * 2**20),
+        compiler_params=pltpu.CompilerParams(vmem_limit_bytes=LARGE),
         name="cotangents",
-    )(lens, spots, *shards, output_weight, side, *others)
+    )(lens, spots, *shards, *arrays)
 
 
 def jacobian_body(
-    factors_ref, tokens_ref, resid_ref, side_ref, repeated_ref, narrow_ref, payload_ref
+    factors_hbm,
+    tokens_hbm,
+    resid_hbm,
+    side_hbm,
+    scalars_hbm,
+    narrow_hbm,
+    payload_hbm,
+    factors_ref,
+    tokens_ref,
+    resid_ref,
+    side_ref,
+    scalars_ref,
+    narrow_ref,
+    payload_ref,
+    semaphores,
 ):
+    early = launch([(factors_hbm, factors_ref), (scalars_hbm, scalars_ref)], semaphores, 0)
+    count = tokens_ref.shape[1] // CHUNK
+    per_step = CHUNK // LANES
+
+    def arriving(step):
+        span = span_of(step)
+        pairs = [
+            (tokens_hbm.at[:, span], tokens_ref.at[:, span]),
+            (resid_hbm.at[:, span], resid_ref.at[:, span]),
+            (side_hbm.at[:, span], side_ref.at[:, span]),
+        ]
+        return prepared(pairs, semaphores, 3 + 3 * step)
+
+    def departing(step):
+        groups = pl.ds(step * per_step, per_step)
+        pairs = [(payload_ref.at[groups], payload_hbm.at[groups])]
+        return prepared(pairs, semaphores, 3 + 3 * count + step)
+
+    begin(arriving(0))
+    early += launch([(narrow_hbm, narrow_ref)], semaphores, 2)
+    for step in range(1, count):
+        begin(arriving(step))
+    finish(early)
     factors = jnp.sum(factors_ref[...], axis=0)
     row = lax.broadcasted_iota(jnp.int32, (40, 1), 0) % 20
     last = row >= 15
-    left = flat([jnp.where(last, 0.0, factors), jnp.where(last, -factors * repeated_ref[0], 0.0)])
+    left = flat(
+        [jnp.where(last, 0.0, factors), jnp.where(last, -factors * scalars_ref[8:48], 0.0)]
+    )
     lane = lax.broadcasted_iota(jnp.int32, (40, 16), 1)
-    lead = jnp.where(lane == row - 15, lane_sum(factors * repeated_ref[1]), 0.0)
+    lead = jnp.where(lane == row - 15, lane_sum(factors * scalars_ref[48:]), 0.0)
 
     def both(rows):
         upper = rows.astype(jnp.bfloat16).astype(jnp.float32)
@@ -734,31 +824,46 @@
     left = both(left)
     lead = both(lead)
 
-    def place(group, _):
-        lanes = pl.ds(pl.multiple_of(group * LANES, LANES), LANES)
-        right = tall([tokens_ref[:, lanes], resid_ref[:, lanes]])
-        pair = dot_halved(left, right, 1, 0) + dot_halved(lead, side_ref[16:, lanes], 1, 0)
-        below = flat(
-            [narrow_ref[tile, pl.ds(pl.multiple_of(group * 16, 16), 16), :] for tile in range(4)]
-        )
-        payload_ref[group] = tall([pair[:40] + pair[40:], below]).astype(jnp.bfloat16)
+    def place(step, _):
+        finish(arriving(step))
+        span = span_of(step)
+        right = tall([tokens_ref[:, span], resid_ref[:, span]])
+        pair = dot_halved(left, right, 1, 0) + dot_halved(lead, side_ref[16:, span], 1, 0)
+        rows = pair[:40] + pair[40:]
+        for inner in range(per_step):
+            group = step * per_step + inner
+            below = flat(
+                [
+                    narrow_ref[tile, pl.ds(pl.multiple_of(group * 16, 16), 16), :]
+                    for tile in range(4)
+                ]
+            )
+            block = tall([rows[:, inner * LANES : (inner + 1) * LANES], below])
+            payload_ref[group] = block.astype(jnp.bfloat16)
+        begin(departing(step))
         return 0
 
-    lax.fori_loop(0, 16, place, 0, unroll=4)
+    lax.fori_loop(0, count, place, 0)
+    for step in range(count):
+        finish(departing(step))
 
 
 def jacobian(*arrays):
+    result = jax.ShapeDtypeStruct((16, PIECE_ROWS, LANES), jnp.bfloat16)
+    steps = arrays[1].shape[1] // CHUNK
     return pl.pallas_call(
         jacobian_body,
-        in_specs=whole(len(arrays)),
-        out_specs=pl.BlockSpec(memory_space=pltpu.VMEM),
-        out_shape=jax.ShapeDtypeStruct((16, PIECE_ROWS, LANES), jnp.bfloat16),
-        compiler_params=pltpu.CompilerParams(vmem_limit_bytes=60 * 2**20),
+        in_specs=[ANYWHERE] * len(arrays),
+        out_specs=ANYWHERE,
+        out_shape=result,
+        scratch_shapes=[pltpu.VMEM(array.shape, array.dtype) for array in (*arrays, result)]
+        + [pltpu.SemaphoreType.DMA((3 + 4 * steps,))],
+        compiler_params=pltpu.CompilerParams(vmem_limit_bytes=LARGE),
         name="jacobian",
     )(*arrays)
 
 
-def assemble(part, every, start_a, start_bq, start_bkv, start_ao, start_bo):
+def assemble(core, part, own, other, start_a, start_bq, start_bkv, start_ao, start_bo):
     steps = 8
     shapes = [start_a, start_bq, start_bkv, start_ao, start_bo]
     blocks = [
@@ -773,14 +878,16 @@
         grid=(steps,),
         in_specs=[
             pl.BlockSpec(memory_space=pltpu.SMEM),
-            pl.BlockSpec(every.shape, lambda step: (0, 0, 0)),
+            pl.BlockSpec(memory_space=pltpu.SMEM),
+            pl.BlockSpec(own.shape, lambda step: (0, 0, 0)),
+            pl.BlockSpec(other.shape, lambda step: (0, 0, 0)),
         ]
         + blocks,
         out_specs=blocks,
         out_shape=[jax.ShapeDtypeStruct(shape.shape, jnp.float32) for shape in shapes],
         compiler_params=pltpu.CompilerParams(vmem_limit_bytes=14 * 2**20),
         name="assemble",
-    )(part, every, start_a, start_bq, start_bkv, start_ao, start_bo)
+    )(core, part, own, other, *(pltpu.with_memory_space_constraint(x, pltpu.HBM) for x in shapes))
 
 
 def local(
@@ -815,18 +922,10 @@
     head_rows = head.T
     spots = shard_spots()
     side = jnp.concatenate([adapter_up_output, head_rows, jnp.zeros((11, width), head.dtype)], 0)
-    (
-        tokens,
-        out_terms,
-        query,
-        keys,
-        values,
-        probabilities,
-        capped,
-        context,
-        low,
-        context_low,
-    ) = forward(
+    small = jnp.concatenate(
+        [down_output, adapter_up_query, adapter_up_key_value[0], adapter_up_key_value[1]], 1
+    )
+    tokens, out_terms, state = forward(
         spots,
         gather_by_relays(hidden[0]),
         query_weight,
@@ -834,32 +933,21 @@
         down_rows,
         output_weight,
         adapter_up_output,
-        down_output,
-        adapter_up_query,
-        adapter_up_key_value,
+        small,
     )
     out_pieces = lax.all_to_all(out_terms, "tensor", 0, 0)
     resid_own = hidden[0].astype(jnp.float32) + jnp.sum(out_pieces.astype(jnp.float32), 0)
-    resid, factors, narrow, rewards, repeated = cotangents(
+    resid, factors, narrow, scalars = cotangents(
         lens,
         spots,
         gather_by_relays(resid_own.astype(jnp.bfloat16)),
         output_weight,
         side,
-        query,
-        keys,
-        values,
-        probabilities,
-        capped,
-        context,
-        low,
-        context_low,
-        down_output,
-        adapter_up_query,
-        adapter_up_key_value,
+        state,
+        small,
     )
     factors = lax.all_to_all(factors.reshape(shards, 8 * OBJ, length), "tensor", 0, 0)
-    payload = jacobian(factors, tokens, resid, side, repeated, narrow)
+    payload = jacobian(factors, tokens, resid, side, scalars, narrow)
     spread = lax.all_to_all(payload, "dp", 0, 0)
     jac = (
         spread[:, : PIECES * OBJ]
@@ -922,7 +1010,7 @@
         jac,
         own_start,
         pairs,
-        rewards,
+        scalars[:8],
     )
     packed = jnp.sum(gather_by_exchange(packed, "dp"), 0)
     packed = gather_by_exchange(packed, "tensor")
@@ -937,15 +1025,23 @@
         compiler_params=pltpu.CompilerParams(vmem_limit_bytes=6 * 2**20),
         name="lanczos",
     )(packed, pairs, jac)
-    every = lax.all_to_all(
-        jnp.broadcast_to(own_result[None], (groups * shards,) + own_result.shape),
+    half = groups * shards // 2
+    same_core = [
+        [at for at in range(2 * half) if (at // shards) % 2 == core] for core in range(2)
+    ]
+    own_half = lax.all_to_all(
+        jnp.broadcast_to(own_result[None], (half,) + own_result.shape),
         ("dp", "tensor"),
         0,
         0,
-    )
+        axis_index_groups=same_core,
+    )
+    other_half = lax.ppermute(own_half, "dp", [(at, at ^ 1) for at in range(groups)])
     next_a, next_bq, next_bkv, next_ao, next_bo = assemble(
+        (group_rank % 2).astype(jnp.int32).reshape(1),
         part,
-        every,
+        own_half,
+        other_half,
         jnp.transpose(initial_down_qkv, (0, 2, 1)),
         initial_up_query,
         initial_up_key_value,

time: 213 us -> 202 us (0.948)
  blocking collectives: 47 us -> 36.2 us
  Pallas kernels: 40.1 us -> 37.4 us
  starting transfers between devices: 59.5 us -> 62.1 us
  waiting for transfers between devices: 52 us -> 49.6 us
  local copies, waits for them, and re-layouts: 8.57 us -> 10.8 us
    all_to_all x1, blocking collectives: 28.2 us -> 17.4 us  [local(): lax.all_to_all(jnp.broadcast_to(own_result[None], (half,) + own_result.sh...]
    pallas_call x3, Pallas kernels: 33.1 us -> 28.3 us  [the longest x1 12.2 us: cotangents(): pl.pallas_call(cotangents_body, in_specs=[pl.BlockSpec(memory_space=pltpu...]
    ppermute x0 -> x1, starting transfers between devices: none -> 3.36 us  [local(): lax.ppermute(own_half, 'dp', [(at, at ^ 1) for at in range(groups)])]
    ppermute x18, waiting for transfers between devices: 11.2 us -> 8.45 us  [permute(): return lax.ppermute(array, 'tensor', pairs)]
  transfers between devices with their start and end apart: 21 -> 22, of which waited for: 11 -> 9; matrix products, arithmetic and copies ran while one was open for 3% -> 5% of each run, Pallas kernels for 0% -> 0%
where the time goes in v5:
time: 202 us; the launch traced here: 201 us
  starting transfers between devices  62.1 us (31%)
  waiting for transfers between devices  49.6 us (25%)
  Pallas kernels  37.4 us (19%)
  blocking collectives  36.2 us (18%)
  local copies, waits for them, and re-layouts  10.8 us (5%)
  other arithmetic  3.12 us (2%)
    ppermute x18, starting transfers between devices, permute(): return lax.ppermute(array, 'tensor', pairs)  35.3 us
    all_to_all x1, waiting for transfers between devices, local(): out_pieces = lax.all_to_all(out_terms, 'tensor', 0, 0)  19.7 us
    all_to_all x2, blocking collectives, gather_by_exchange(): return lax.all_to_all(copies, axis, 0, 0)  18.9 us
    all_to_all x1, blocking collectives, local(): lax.all_to_all(jnp.broadcast_to(own_result[None], (half,) + own_result.sh...  17.4 us
    all_to_all x1, waiting for transfers between devices, local(): spread = lax.all_to_all(payload, 'dp', 0, 0)  12.6 us
    pallas_call x1, Pallas kernels, cotangents(): pl.pallas_call(cotangents_body, in_specs=[pl.BlockSpec(memory_space=pltpu...  12.2 us
    pallas_call x1, Pallas kernels, forward(): pl.pallas_call(forward_body, in_specs=[pl.BlockSpec(memory_space=pltpu.SM...  12 us
    all_to_all x1, starting transfers between devices, local(): spread = lax.all_to_all(payload, 'dp', 0, 0)  10.6 us
  transfers between devices with their start and end apart: 22, of which 9 were waited for; matrix products, arithmetic and copies ran while one was open for 5% of the time, Pallas kernels for 0%

profile of v5, /device:TPU:1, one launch (start us, length us, event | category | flops | bytes accessed | tf_op | source)
XLA Modules:
  0.0 201.2 jit_solution(498648185116672311)
XLA Ops:
  0.6 3.8 %collective-permute-start = (bf16[16,8192]{1,0:T(8,128)(2,1)}, bf16[16,8192]{1,0:T(8,128)(2,1)S(1)}, u32[]{:S(2)}, u32[]{:S(2)}) collective-permute-start(bf16[16,8192]{1,0:T(8,128)(2,1)} %bitcast.62), channel_id=1, source_target_pairs={{0,4},{1,5},{2,6},{3,7},{4,0},{5,1},{6,2},{7,3},{8,12},{9,13},{10,... | collective-permute-start | bytes 786440 | tf_op jit(solution)/shard_map/ppermute | solution.py:317
  4.5 1.6 collective-permute-start.1
  6.1 2.1 %collective-permute-start.2 = (bf16[16,8192]{1,0:T(8,128)(2,1)}, bf16[16,8192]{1,0:T(8,128)(2,1)S(1)}, u32[]{:S(2)}, u32[]{:S(2)}) collective-permute-start(bf16[16,8192]{1,0:T(8,128)(2,1)} %bitcast.64), channel_id=1, source_target_pairs={{0,3},{1,0},{2,1},{3,2},{4,7},{5,4},{6,5},{7,6},{8,11},{9,8},{10,9... | collective-permute-start | bytes 786440 | tf_op jit(solution)/shard_map/ppermute | solution.py:317
  8.2 2.2 %collective-permute-done.shard_1 = bf16[16,8192]{1,0:T(8,128)(2,1)S(1)} collective-permute-done((bf16[16,8192]{1,0:T(8,128)(2,1)}, bf16[16,8192]{1,0:T(8,128)(2,1)S(1)}, u32[]{:S(2)}, u32[]{:S(2)}) %collective-permute-start) | collective-permute-done | bytes 262176 | tf_op jit(solution)/shard_map/ppermute | solution.py:317
  10.4 1.6 collective-permute-start.3
  12.1 2.1 %collective-permute-start.4 = (bf16[16,8192]{1,0:T(8,128)(2,1)S(1)}, bf16[16,8192]{1,0:T(8,128)(2,1)S(1)}, u32[]{:S(2)}, u32[]{:S(2)}) collective-permute-start(bf16[16,8192]{1,0:T(8,128)(2,1)S(1)} %collective-permute-done.shard_1), channel_id=1, source_target_pairs={{0,3},{1,0},{2,1},{3,2},{4,7},{5,4},{6,5},{7,6},{8,11},{9,8},{10,9... | collective-permute-start | bytes 786440 | tf_op jit(solution)/shard_map/ppermute | solution.py:317
  14.2 0.7 slice_bitcast_fusion.1
  15.0 2.7 %collective-permute-start.6 = (bf16[16,4096]{1,0:T(8,128)(2,1)S(1)}, bf16[16,4096]{1,0:T(8,128)(2,1)S(1)}, u32[]{:S(2)}, u32[]{:S(2)}) collective-permute-start(bf16[16,4096]{1,0:T(8,128)(2,1)S(1)} %slice.51), channel_id=1, source_target_pairs={{0,3},{1,0},{2,1},{3,2},{4,7},{5,4},{6,5},{7,6},{8,11},{9,8},{10,9... | collective-permute-start | bytes 393224 | tf_op jit(solution)/shard_map/ppermute | solution.py:317
  17.8 1.5 collective-permute-done.3.shard_4
  19.4 2.7 %collective-permute-start.8 = (bf16[16,4096]{1,0:T(8,128)(2,1)S(1)}, bf16[16,4096]{1,0:T(8,128)(2,1)S(1)}, u32[]{:S(2)}, u32[]{:S(2)}) collective-permute-start(bf16[16,4096]{1,0:T(8,128)(2,1)S(1)} %slice.53), channel_id=1, source_target_pairs={{0,3},{1,0},{2,1},{3,2},{4,7},{5,4},{6,5},{7,6},{8,11},{9,8},{10,9... | collective-permute-start | bytes 393224 | tf_op jit(solution)/shard_map/ppermute | solution.py:317
  22.1 1.4 pad_maximum_fusion.small_hbm
  23.5 0.7 stack.47.spots_ref
  24.1 1.0 constant_dynamic-slice_fusion.1
  25.9 12.0 %forward.1 = (bf16[128,8192]{1,0:T(8,128)(2,1)}, bf16[8,16,8192]{2,1,0:T(8,128)(2,1)}, f32[2368,128]{1,0:T(8,128)}) custom-call(s32[8]{0:T(128)} %stack.47.spots_ref, bf16[16,8192]{1,0:T(8,128)(2,1)} %bitcast.65, bf16[16,8192]{1,0:T(8,128)(2,1)} %copy-done.12, bf16[16,8192]{1,0:T(8,128)(2,1)} %copy-done.4, bf16[16,8192]{1,0:T(8,128)(2,1)} %copy-done.5, ...), custom_call_target="tpu_custom_call" | custom-call | tf_op jit(solution)/shard_map/forward/pallas_call | solution.py:512
  38.0 6.4 %all-to-all-start = ((bf16[8,16,8192]{2,1,0:T(8,128)(2,1)}), bf16[8,16,8192]{2,1,0:T(8,128)(2,1)S(1)}, u32[]{:S(2)}, u32[]{:S(2)}) async-start(bf16[8,16,8192]{2,1,0:T(8,128)(2,1)} %get-tuple-element.19), calls=%async_computation | async-start | bytes 4194304 | tf_op jit(solution)/shard_map/all_to_all | solution.py:938
  44.4 0.9 constant_dynamic-slice_fusion
  45.4 0.9 maximum_maximum_fusion.side_hbm
  46.3 19.7 %all-to-all-done = bf16[8,16,8192]{2,1,0:T(8,128)(2,1)S(1)} async-done(((bf16[8,16,8192]{2,1,0:T(8,128)(2,1)}), bf16[8,16,8192]{2,1,0:T(8,128)(2,1)S(1)}, u32[]{:S(2)}, u32[]{:S(2)}) %all-to-all-start) | async-done | bytes 2097184 | tf_op jit(solution)/shard_map/all_to_all | solution.py:938
  66.4 7.2 %collective-permute-start.9 = (bf16[16,8192]{1,0:T(8,128)(2,1)S(1)}, bf16[16,8192]{1,0:T(8,128)(2,1)S(1)}, u32[]{:S(2)}, u32[]{:S(2)}) collective-permute-start(bf16[16,8192]{1,0:T(8,128)(2,1)S(1)} %add_convert_fusion.shard_0), channel_id=1, source_target_pairs={{0,4},{1,5},{2,6},{3,7},{4,0},{5,1},{6,2},{7,3},{8,12},{9,13},{10,... | collective-permute-start | bytes 786440 | tf_op jit(solution)/shard_map/ppermute | solution.py:317
  73.6 1.0 collective-permute-start.10
  74.7 1.7 collective-permute-start.11
  76.4 2.0 collective-permute-done.9.shard_1
  78.3 1.4 collective-permute-start.12
  79.7 1.3 collective-permute-start.13
  81.0 0.8 dynamic-slice_bitcast_fusion
  82.1 2.6 %collective-permute-start.15 = (bf16[16,4096]{1,0:T(8,128)(2,1)S(1)}, bf16[16,4096]{1,0:T(8,128)(2,1)S(1)}, u32[]{:S(2)}, u32[]{:S(2)}) collective-permute-start(bf16[16,4096]{1,0:T(8,128)(2,1)S(1)} %slice.55), channel_id=1, source_target_pairs={{0,3},{1,0},{2,1},{3,2},{4,7},{5,4},{6,5},{7,6},{8,11},{9,8},{10,9... | collective-permute-start | bytes 393224 | tf_op jit(solution)/shard_map/ppermute | solution.py:317
  84.7 2.1 %collective-permute-done.12.shard_4 = bf16[16,8192]{1,0:T(8,128)(2,1)S(1)} collective-permute-done((bf16[16,8192]{1,0:T(8,128)(2,1)S(1)}, bf16[16,8192]{1,0:T(8,128)(2,1)S(1)}, u32[]{:S(2)}, u32[]{:S(2)}) %collective-permute-start.12) | collective-permute-done | bytes 262176 | tf_op jit(solution)/shard_map/ppermute | solution.py:317
  86.9 2.9 %collective-permute-start.17 = (bf16[16,4096]{1,0:T(8,128)(2,1)S(1)}, bf16[16,4096]{1,0:T(8,128)(2,1)S(1)}, u32[]{:S(2)}, u32[]{:S(2)}) collective-permute-start(bf16[16,4096]{1,0:T(8,128)(2,1)S(1)} %slice.57), channel_id=1, source_target_pairs={{0,3},{1,0},{2,1},{3,2},{4,7},{5,4},{6,5},{7,6},{8,11},{9,8},{10,9... | collective-permute-start | bytes 393224 | tf_op jit(solution)/shard_map/ppermute | solution.py:317
  89.8 0.8 dynamic-slice_bitcast_fusion.1
  91.3 0.8 dynamic_slice.17
  92.1 0.6 collective-permute-done.16.shard_8
  93.5 12.2 %cotangents.1 = (bf16[128,8192]{1,0:T(8,128)(2,1)}, f32[320,128]{1,0:T(8,128)}, f32[4,256,128]{2,1,0:T(8,128)}, f32[88,128]{1,0:T(8,128)}) custom-call(s32[1]{0:T(128)S(6)} %copy.46.lens_ref, s32[8]{0:T(128)} %stack.47.spots_ref, bf16[16,8192]{1,0:T(8,128)(2,1)} %copy-done.2, bf16[16,8192]{1,0:T(8,128)(2,1)} %copy-done.13, bf16[16,8192]{1,0:T(8,128)(2,1)} %copy-done.8, ...), custom_call_target="tpu_custom_call" | custom-call | tf_op jit(solution)/shard_map/cotangents/pallas_call | solution.py:753
  105.7 6.3 %all-to-all-start.1 = ((f32[8,40,128]{2,1,0:T(8,128)}), f32[8,40,128]{2,1,0:T(8,128)S(1)}, u32[]{:S(2)}, u32[]{:S(2)}) async-start(f32[8,40,128]{2,1,0:T(8,128)} %bitcast.69), calls=%async_computation.1 | async-start | bytes 327680 | tf_op jit(solution)/shard_map/all_to_all | solution.py:949
  112.2 7.0 %all-to-all-done.1.factors_hbm = f32[8,40,128]{2,1,0:T(8,128)S(1)} async-done(((f32[8,40,128]{2,1,0:T(8,128)}), f32[8,40,128]{2,1,0:T(8,128)S(1)}, u32[]{:S(2)}, u32[]{:S(2)}) %all-to-all-start.1) | async-done | bytes 163872 | tf_op jit(solution)/shard_map/all_to_all | solution.py:949
  119.1 0.7 copy-done.3
  119.8 4.1 %jacobian.1 = bf16[16,56,512]{2,1,0:T(8,128)(2,1)} custom-call(f32[8,40,128]{2,1,0:T(8,128)} %copy-done.3, bf16[128,8192]{1,0:T(8,128)(2,1)} %get-tuple-element.22.tokens_hbm, bf16[128,8192]{1,0:T(8,128)(2,1)} %get-tuple-element.23.resid_hbm, bf16[32,8192]{1,0:T(8,128)(2,1)} %maximum_maximum_fusion.side_hbm, f32[88,128]{1,0:T(8,128)} %get-tuple-element.24.scalars_hbm, ...), custom_call_target="tpu_custom_call" | custom-call | tf_op jit(solution)/shard_map/jacobian/pallas_call | solution.py:854
  123.8 10.6 %all-to-all-start.2 = ((bf16[16,56,512]{2,1,0:T(8,128)(2,1)}), bf16[16,56,512]{2,1,0:T(8,128)(2,1)S(1)}, u32[]{:S(2)}, u32[]{:S(2)}) async-start(bf16[16,56,512]{2,1,0:T(8,128)(2,1)} %jacobian.1), calls=%async_computation.2 | async-start | bytes 1835008 | tf_op jit(solution)/shard_map/all_to_all | solution.py:951
  135.6 0.7 slice.47.rewards_ref
  136.3 12.6 %all-to-all-done.2 = bf16[16,56,512]{2,1,0:T(8,128)(2,1)S(1)} async-done(((bf16[16,56,512]{2,1,0:T(8,128)(2,1)}), bf16[16,56,512]{2,1,0:T(8,128)(2,1)S(1)}, u32[]{:S(2)}, u32[]{:S(2)}) %all-to-all-start.2) | async-done | bytes 917536 | tf_op jit(solution)/shard_map/all_to_all | solution.py:951
  149.7 0.6 copy.42
  150.3 1.6 gram.1
  151.9 9.3 %all_to_all.30 = f32[16,16,128]{2,1,0:T(8,128)S(1)} all-to-all(f32[16,16,128]{2,1,0:T(8,128)S(1)} %broadcast_in_dim.24), channel_id=1, replica_groups=mesh['dp'=16,'tensor'=8] {'dp'}, dimensions={0} | all-to-all | bytes 262144 | tf_op jit(solution)/shard_map/all_to_all | solution.py:45
  161.3 9.6 %all_to_all.31.packed_ref = f32[8,16,128]{2,1,0:T(8,128)S(1)} all-to-all(f32[8,16,128]{2,1,0:T(8,128)S(1)} %broadcast_in_dim.25), channel_id=1, replica_groups=mesh['dp'=16,'tensor'=8] {'tensor'}, dimensions={0} | all-to-all | bytes 131072 | tf_op jit(solution)/shard_map/all_to_all | solution.py:45
  170.8 0.9 lanczos.1
  171.8 17.4 %all_to_all.32.own_ref = bf16[64,8,768]{2,1,0:T(8,128)(2,1)S(1)} all-to-all(bf16[64,8,768]{2,1,0:T(8,128)(2,1)S(1)} %broadcast_in_dim.26), channel_id=1, replica_groups={{0,1,2,3,4,5,6,7,16,17,18,19,20,21,22,23,32,33,34,35,36,37,38,39,48,49,..., dimensions={0} | all-to-all | bytes 1572864 | tf_op jit(solution)/shard_map/all_to_all | solution.py:1032
  189.2 3.4 %collective-permute-start.18 = (bf16[64,8,768]{2,1,0:T(8,128)(2,1)S(1)}, bf16[64,8,768]{2,1,0:T(8,128)(2,1)S(1)}, u32[]{:S(2)}, u32[]{:S(2)}) collective-permute-start(bf16[64,8,768]{2,1,0:T(8,128)(2,1)S(1)} %all_to_all.32.own_ref), channel_id=1, source_target_pairs={{0,8},{8,0},{16,24},{24,16},{32,40},{40,32},{48,56},{56,48},{64,72... | collective-permute-start | bytes 2359304 | tf_op jit(solution)/shard_map/ppermute | solution.py:1039
  192.5 1.9 collective-permute-done.18.other_ref
  194.4 6.6 %assemble.1 = (f32[3,16,8192]{2,1,0:T(8,128)}, f32[16,4096]{1,0:T(8,128)}, f32[2,16,1024]{2,1,0:T(8,128)}, f32[16,4096]{1,0:T(8,128)}, f32[16,8192]{1,0:T(8,128)}) custom-call(s32[1]{0:T(128)} %bitcast.core_ref, f32[1,128]{1,0:T(1,128)S(1)} %get-tuple-element.26.part_ref, bf16[64,8,768]{2,1,0:T(8,128)(2,1)S(1)} %all_to_all.32.own_ref, ...), custom_call_target="tpu_custom_call" | custom-call | tf_op jit(solution)/shard_map/assemble/pallas_call | solution.py:876
  (102 shorter events, 4.6 us)
Async XLA Ops:
  0.6 9.8 %collective-permute-start = (bf16[16,8192]{1,0:T(8,128)(2,1)}, bf16[16,8192]{1,0:T(8,128)(2,1)S(1)}, u32[]{:S(2)}, u32[]{:S(2)}) collective-permute-start(bf16[16,8192]{1,0:T(8,128)(2,1)} %bitcast.62), channel_id=1, source_target_pairs={{0,4},{1,5},{2,6},{3,7},{4,0},{5,1},{6,2},{7,3},{8,12},{9,13},{10,... | collective-permute-start | bytes 786440 | tf_op jit(solution)/shard_map/ppermute | solution.py:317
  4.5 10.4 %collective-permute-start.1 = (bf16[16,8192]{1,0:T(8,128)(2,1)}, bf16[16,8192]{1,0:T(8,128)(2,1)S(1)}, u32[]{:S(2)}, u32[]{:S(2)}) collective-permute-start(bf16[16,8192]{1,0:T(8,128)(2,1)} %bitcast.63), channel_id=1, source_target_pairs={{0,1},{1,2},{2,3},{3,0},{4,5},{5,6},{6,7},{7,4},{8,9},{9,10},{10,1... | collective-permute-start | bytes 786440 | tf_op jit(solution)/shard_map/ppermute | solution.py:317
  6.1 8.9 %collective-permute-start.2 = (bf16[16,8192]{1,0:T(8,128)(2,1)}, bf16[16,8192]{1,0:T(8,128)(2,1)S(1)}, u32[]{:S(2)}, u32[]{:S(2)}) collective-permute-start(bf16[16,8192]{1,0:T(8,128)(2,1)} %bitcast.64), channel_id=1, source_target_pairs={{0,3},{1,0},{2,1},{3,2},{4,7},{5,4},{6,5},{7,6},{8,11},{9,8},{10,9... | collective-permute-start | bytes 786440 | tf_op jit(solution)/shard_map/ppermute | solution.py:317
  10.4 14.8 %copy-start.12 = (bf16[16,8192]{1,0:T(8,128)(2,1)}, bf16[16,8192]{1,0:T(8,128)(2,1)S(1)}, u32[]{:S(2)}) copy-start(bf16[16,8192]{1,0:T(8,128)(2,1)S(1)} %collective-permute-done.shard_1) | copy-start | bytes 786436
  10.4 8.8 %collective-permute-start.3 = (bf16[16,8192]{1,0:T(8,128)(2,1)S(1)}, bf16[16,8192]{1,0:T(8,128)(2,1)S(1)}, u32[]{:S(2)}, u32[]{:S(2)}) collective-permute-start(bf16[16,8192]{1,0:T(8,128)(2,1)S(1)} %collective-permute-done.shard_1), channel_id=1, source_target_pairs={{0,1},{1,2},{2,3},{3,0},{4,5},{5,6},{6,7},{7,4},{8,9},{9,10},{10,1... | collective-permute-start | bytes 786440 | tf_op jit(solution)/shard_map/ppermute | solution.py:317
  12.1 7.3 %collective-permute-start.4 = (bf16[16,8192]{1,0:T(8,128)(2,1)S(1)}, bf16[16,8192]{1,0:T(8,128)(2,1)S(1)}, u32[]{:S(2)}, u32[]{:S(2)}) collective-permute-start(bf16[16,8192]{1,0:T(8,128)(2,1)S(1)} %collective-permute-done.shard_1), channel_id=1, source_target_pairs={{0,3},{1,0},{2,1},{3,2},{4,7},{5,4},{6,5},{7,6},{8,11},{9,8},{10,9... | collective-permute-start | bytes 786440 | tf_op jit(solution)/shard_map/ppermute | solution.py:317
  14.9 10.3 %copy-start.4 = (bf16[16,8192]{1,0:T(8,128)(2,1)}, bf16[16,8192]{1,0:T(8,128)(2,1)S(1)}, u32[]{:S(2)}) copy-start(bf16[16,8192]{1,0:T(8,128)(2,1)S(1)} %collective-permute-done.1.shard_2) | copy-start | bytes 786436
  14.9 10.2 %collective-permute-start.5 = (bf16[16,4096]{1,0:T(8,128)(2,1)S(1)}, bf16[16,4096]{1,0:T(8,128)(2,1)S(1)}, u32[]{:S(2)}, u32[]{:S(2)}) collective-permute-start(bf16[16,4096]{1,0:T(8,128)(2,1)S(1)} %slice.50), channel_id=1, source_target_pairs={{0,1},{1,2},{2,3},{3,0},{4,5},{5,6},{6,7},{7,4},{8,9},{9,10},{10,1... | collective-permute-start | bytes 393224 | tf_op jit(solution)/shard_map/ppermute | solution.py:317
  15.0 10.2 %copy-start.5 = (bf16[16,8192]{1,0:T(8,128)(2,1)}, bf16[16,8192]{1,0:T(8,128)(2,1)S(1)}, u32[]{:S(2)}) copy-start(bf16[16,8192]{1,0:T(8,128)(2,1)S(1)} %collective-permute-done.2.shard_3) | copy-start | bytes 786436
  15.0 10.1 %collective-permute-start.6 = (bf16[16,4096]{1,0:T(8,128)(2,1)S(1)}, bf16[16,4096]{1,0:T(8,128)(2,1)S(1)}, u32[]{:S(2)}, u32[]{:S(2)}) collective-permute-start(bf16[16,4096]{1,0:T(8,128)(2,1)S(1)} %slice.51), channel_id=1, source_target_pairs={{0,3},{1,0},{2,1},{3,2},{4,7},{5,4},{6,5},{7,6},{8,11},{9,8},{10,9... | collective-permute-start | bytes 393224 | tf_op jit(solution)/shard_map/ppermute | solution.py:317
  19.3 6.0 %copy-start.6 = (bf16[16,8192]{1,0:T(8,128)(2,1)}, bf16[16,8192]{1,0:T(8,128)(2,1)S(1)}, u32[]{:S(2)}) copy-start(bf16[16,8192]{1,0:T(8,128)(2,1)S(1)} %collective-permute-done.3.shard_4) | copy-start | bytes 786436
  19.3 5.9 %collective-permute-start.7 = (bf16[16,4096]{1,0:T(8,128)(2,1)S(1)}, bf16[16,4096]{1,0:T(8,128)(2,1)S(1)}, u32[]{:S(2)}, u32[]{:S(2)}) collective-permute-start(bf16[16,4096]{1,0:T(8,128)(2,1)S(1)} %slice.52), channel_id=1, source_target_pairs={{0,1},{1,2},{2,3},{3,0},{4,5},{5,6},{6,7},{7,4},{8,9},{9,10},{10,1... | collective-permute-start | bytes 393224 | tf_op jit(solution)/shard_map/ppermute | solution.py:317
  19.4 5.9 %copy-start.7 = (bf16[16,8192]{1,0:T(8,128)(2,1)}, bf16[16,8192]{1,0:T(8,128)(2,1)S(1)}, u32[]{:S(2)}) copy-start(bf16[16,8192]{1,0:T(8,128)(2,1)S(1)} %collective-permute-done.4.shard_5) | copy-start | bytes 786436
  19.4 5.8 %collective-permute-start.8 = (bf16[16,4096]{1,0:T(8,128)(2,1)S(1)}, bf16[16,4096]{1,0:T(8,128)(2,1)S(1)}, u32[]{:S(2)}, u32[]{:S(2)}) collective-permute-start(bf16[16,4096]{1,0:T(8,128)(2,1)S(1)} %slice.53), channel_id=1, source_target_pairs={{0,3},{1,0},{2,1},{3,2},{4,7},{5,4},{6,5},{7,6},{8,11},{9,8},{10,9... | collective-permute-start | bytes 393224 | tf_op jit(solution)/shard_map/ppermute | solution.py:317
  25.1 0.7 copy-start.14
  25.2 0.7 copy-start.15
  25.2 0.7 copy-start.16
  25.2 0.7 copy-start.17
  37.9 7.5 %copy-start = (bf16[16,8192]{1,0:T(8,128)(2,1)S(1)}, bf16[16,8192]{1,0:T(8,128)(2,1)}, u32[]{:S(2)}) copy-start(bf16[16,8192]{1,0:T(8,128)(2,1)} %up_output_hbm.1) | copy-start | bytes 786436
  38.0 7.5 %copy-start.22 = (bf16[8192,5]{0,1:T(8,128)(2,1)S(1)}, bf16[8192,5]{0,1:T(8,128)(2,1)}, u32[]{:S(2)}) copy-start(bf16[8192,5]{0,1:T(8,128)(2,1)} %param.21) | copy-start | bytes 245764
  38.0 28.0 %all-to-all-start = ((bf16[8,16,8192]{2,1,0:T(8,128)(2,1)}), bf16[8,16,8192]{2,1,0:T(8,128)(2,1)S(1)}, u32[]{:S(2)}, u32[]{:S(2)}) async-start(bf16[8,16,8192]{2,1,0:T(8,128)(2,1)} %get-tuple-element.19), calls=%async_computation | async-start | bytes 4194304 | tf_op jit(solution)/shard_map/all_to_all | solution.py:938
  44.4 21.9 %copy-start.1 = (bf16[1,16,8192]{2,1,0:T(8,128)(2,1)S(1)}, bf16[1,16,8192]{2,1,0:T(8,128)(2,1)}, u32[]{:S(2)}) copy-start(bf16[1,16,8192]{2,1,0:T(8,128)(2,1)} %param.17) | copy-start | bytes 786436
  45.4 28.2 %copy-start.23 = (s32[16]{0:T(128)S(1)}, s32[16]{0:T(128)}, u32[]{:S(2)}) copy-start(s32[16]{0:T(128)} %param.23) | copy-start | bytes 196
  66.4 26.4 %copy-start.2 = (bf16[16,8192]{1,0:T(8,128)(2,1)}, bf16[16,8192]{1,0:T(8,128)(2,1)S(1)}, u32[]{:S(2)}) copy-start(bf16[16,8192]{1,0:T(8,128)(2,1)S(1)} %add_convert_fusion.shard_0) | copy-start | bytes 786436
  66.4 12.0 %collective-permute-start.9 = (bf16[16,8192]{1,0:T(8,128)(2,1)S(1)}, bf16[16,8192]{1,0:T(8,128)(2,1)S(1)}, u32[]{:S(2)}, u32[]{:S(2)}) collective-permute-start(bf16[16,8192]{1,0:T(8,128)(2,1)S(1)} %add_convert_fusion.shard_0), channel_id=1, source_target_pairs={{0,4},{1,5},{2,6},{3,7},{4,0},{5,1},{6,2},{7,3},{8,12},{9,13},{10,... | collective-permute-start | bytes 786440 | tf_op jit(solution)/shard_map/ppermute | solution.py:317
  73.6 8.2 %collective-permute-start.10 = (bf16[16,8192]{1,0:T(8,128)(2,1)S(1)}, bf16[16,8192]{1,0:T(8,128)(2,1)S(1)}, u32[]{:S(2)}, u32[]{:S(2)}) collective-permute-start(bf16[16,8192]{1,0:T(8,128)(2,1)S(1)} %add_convert_fusion.shard_0), channel_id=1, source_target_pairs={{0,1},{1,2},{2,3},{3,0},{4,5},{5,6},{6,7},{7,4},{8,9},{9,10},{10,1... | collective-permute-start | bytes 786440 | tf_op jit(solution)/shard_map/ppermute | solution.py:317
  74.7 7.4 %collective-permute-start.11 = (bf16[16,8192]{1,0:T(8,128)(2,1)S(1)}, bf16[16,8192]{1,0:T(8,128)(2,1)S(1)}, u32[]{:S(2)}, u32[]{:S(2)}) collective-permute-start(bf16[16,8192]{1,0:T(8,128)(2,1)S(1)} %add_convert_fusion.shard_0), channel_id=1, source_target_pairs={{0,3},{1,0},{2,1},{3,2},{4,7},{5,4},{6,5},{7,6},{8,11},{9,8},{10,9... | collective-permute-start | bytes 786440 | tf_op jit(solution)/shard_map/ppermute | solution.py:317
  78.3 14.4 %copy-start.13 = (bf16[16,8192]{1,0:T(8,128)(2,1)}, bf16[16,8192]{1,0:T(8,128)(2,1)S(1)}, u32[]{:S(2)}) copy-start(bf16[16,8192]{1,0:T(8,128)(2,1)S(1)} %collective-permute-done.9.shard_1) | copy-start | bytes 786436
  78.3 8.4 %collective-permute-start.12 = (bf16[16,8192]{1,0:T(8,128)(2,1)S(1)}, bf16[16,8192]{1,0:T(8,128)(2,1)S(1)}, u32[]{:S(2)}, u32[]{:S(2)}) collective-permute-start(bf16[16,8192]{1,0:T(8,128)(2,1)S(1)} %collective-permute-done.9.shard_1), channel_id=1, source_target_pairs={{0,1},{1,2},{2,3},{3,0},{4,5},{5,6},{6,7},{7,4},{8,9},{9,10},{10,1... | collective-permute-start | bytes 786440 | tf_op jit(solution)/shard_map/ppermute | solution.py:317
  79.7 7.2 %collective-permute-start.13 = (bf16[16,8192]{1,0:T(8,128)(2,1)S(1)}, bf16[16,8192]{1,0:T(8,128)(2,1)S(1)}, u32[]{:S(2)}, u32[]{:S(2)}) collective-permute-start(bf16[16,8192]{1,0:T(8,128)(2,1)S(1)} %collective-permute-done.9.shard_1), channel_id=1, source_target_pairs={{0,3},{1,0},{2,1},{3,2},{4,7},{5,4},{6,5},{7,6},{8,11},{9,8},{10,9... | collective-permute-start | bytes 786440 | tf_op jit(solution)/shard_map/ppermute | solution.py:317
  81.8 11.0 %copy-start.8 = (bf16[16,8192]{1,0:T(8,128)(2,1)}, bf16[16,8192]{1,0:T(8,128)(2,1)S(1)}, u32[]{:S(2)}) copy-start(bf16[16,8192]{1,0:T(8,128)(2,1)S(1)} %collective-permute-done.10.shard_2) | copy-start | bytes 786436
  81.9 10.2 %collective-permute-start.14 = (bf16[16,4096]{1,0:T(8,128)(2,1)S(1)}, bf16[16,4096]{1,0:T(8,128)(2,1)S(1)}, u32[]{:S(2)}, u32[]{:S(2)}) collective-permute-start(bf16[16,4096]{1,0:T(8,128)(2,1)S(1)} %slice.54), channel_id=1, source_target_pairs={{0,1},{1,2},{2,3},{3,0},{4,5},{5,6},{6,7},{7,4},{8,9},{9,10},{10,1... | collective-permute-start | bytes 393224 | tf_op jit(solution)/shard_map/ppermute | solution.py:317
  82.1 10.7 %copy-start.9 = (bf16[16,8192]{1,0:T(8,128)(2,1)}, bf16[16,8192]{1,0:T(8,128)(2,1)S(1)}, u32[]{:S(2)}) copy-start(bf16[16,8192]{1,0:T(8,128)(2,1)S(1)} %collective-permute-done.11.shard_3) | copy-start | bytes 786436
  82.1 10.0 %collective-permute-start.15 = (bf16[16,4096]{1,0:T(8,128)(2,1)S(1)}, bf16[16,4096]{1,0:T(8,128)(2,1)S(1)}, u32[]{:S(2)}, u32[]{:S(2)}) collective-permute-start(bf16[16,4096]{1,0:T(8,128)(2,1)S(1)} %slice.55), channel_id=1, source_target_pairs={{0,3},{1,0},{2,1},{3,2},{4,7},{5,4},{6,5},{7,6},{8,11},{9,8},{10,9... | collective-permute-start | bytes 393224 | tf_op jit(solution)/shard_map/ppermute | solution.py:317
  86.8 6.0 %copy-start.10 = (bf16[16,8192]{1,0:T(8,128)(2,1)}, bf16[16,8192]{1,0:T(8,128)(2,1)S(1)}, u32[]{:S(2)}) copy-start(bf16[16,8192]{1,0:T(8,128)(2,1)S(1)} %collective-permute-done.12.shard_4) | copy-start | bytes 786436
  86.8 6.0 %collective-permute-start.16 = (bf16[16,4096]{1,0:T(8,128)(2,1)S(1)}, bf16[16,4096]{1,0:T(8,128)(2,1)S(1)}, u32[]{:S(2)}, u32[]{:S(2)}) collective-permute-start(bf16[16,4096]{1,0:T(8,128)(2,1)S(1)} %slice.56), channel_id=1, source_target_pairs={{0,1},{1,2},{2,3},{3,0},{4,5},{5,6},{6,7},{7,4},{8,9},{9,10},{10,1... | collective-permute-start | bytes 393224 | tf_op jit(solution)/shard_map/ppermute | solution.py:317
  86.9 5.9 %copy-start.11 = (bf16[16,8192]{1,0:T(8,128)(2,1)}, bf16[16,8192]{1,0:T(8,128)(2,1)S(1)}, u32[]{:S(2)}) copy-start(bf16[16,8192]{1,0:T(8,128)(2,1)S(1)} %collective-permute-done.13.shard_5) | copy-start | bytes 786436
  86.9 5.9 %collective-permute-start.17 = (bf16[16,4096]{1,0:T(8,128)(2,1)S(1)}, bf16[16,4096]{1,0:T(8,128)(2,1)S(1)}, u32[]{:S(2)}, u32[]{:S(2)}) collective-permute-start(bf16[16,4096]{1,0:T(8,128)(2,1)S(1)} %slice.57), channel_id=1, source_target_pairs={{0,3},{1,0},{2,1},{3,2},{4,7},{5,4},{6,5},{7,6},{8,11},{9,8},{10,9... | collective-permute-start | bytes 393224 | tf_op jit(solution)/shard_map/ppermute | solution.py:317
  92.1 0.7 copy-start.18
  92.1 0.7 copy-start.19
  92.8 0.7 copy-start.20
  92.8 0.7 copy-start.21
  105.7 13.4 %all-to-all-start.1 = ((f32[8,40,128]{2,1,0:T(8,128)}), f32[8,40,128]{2,1,0:T(8,128)S(1)}, u32[]{:S(2)}, u32[]{:S(2)}) async-start(f32[8,40,128]{2,1,0:T(8,128)} %bitcast.69), calls=%async_computation.1 | async-start | bytes 327680 | tf_op jit(solution)/shard_map/all_to_all | solution.py:949
  119.1 0.7 copy-start.3
  123.8 25.1 %all-to-all-start.2 = ((bf16[16,56,512]{2,1,0:T(8,128)(2,1)}), bf16[16,56,512]{2,1,0:T(8,128)(2,1)S(1)}, u32[]{:S(2)}, u32[]{:S(2)}) async-start(bf16[16,56,512]{2,1,0:T(8,128)(2,1)} %jacobian.1), calls=%async_computation.2 | async-start | bytes 1835008 | tf_op jit(solution)/shard_map/all_to_all | solution.py:951
  189.2 5.3 %collective-permute-start.18 = (bf16[64,8,768]{2,1,0:T(8,128)(2,1)S(1)}, bf16[64,8,768]{2,1,0:T(8,128)(2,1)S(1)}, u32[]{:S(2)}, u32[]{:S(2)}) collective-permute-start(bf16[64,8,768]{2,1,0:T(8,128)(2,1)S(1)} %all_to_all.32.own_ref), channel_id=1, source_target_pairs={{0,8},{8,0},{16,24},{24,16},{32,40},{40,32},{48,56},{56,48},{64,72... | collective-permute-start | bytes 2359304 | tf_op jit(solution)/shard_map/ppermute | solution.py:1039

commit v6 on v5

--- a/solution.py
+++ b/solution.py
@@ -68,19 +68,55 @@
     return jnp.sum(values, axis=0, keepdims=True)
 
 
-def gram_body(rank_ref, jac_ref, start_ref, pairs_ref, rewards_ref, packed_ref):
+def gram_body(
+    jac_ref,
+    pairs_ref,
+    rewards_ref,
+    a_hbm,
+    bq_hbm,
+    bkv_hbm,
+    ao_hbm,
+    bo_hbm,
+    packed_ref,
+    a_ref,
+    bq_ref,
+    bkv_ref,
+    ao_ref,
+    bo_ref,
+    semaphores,
+):
+    group = lax.axis_index("dp").astype(jnp.int32)
+    rank = lax.axis_index("tensor").astype(jnp.int32)
+    by_group = pl.ds(pl.multiple_of(group * LANES, LANES), LANES)
+    by_rank = pl.ds(pl.multiple_of(rank * LANES, LANES), LANES)
+    narrow = pl.ds(pl.multiple_of(rank * HEAD_SIZE, HEAD_SIZE), HEAD_SIZE)
+    pairs = [
+        (a_hbm.at[:, :, by_group], a_ref),
+        (bq_hbm.at[:, by_rank], bq_ref),
+        (bkv_hbm.at[:, :, narrow], bkv_ref),
+        (ao_hbm.at[:, by_rank], ao_ref),
+        (bo_hbm.at[:, by_group], bo_ref),
+    ]
+    copies = launch(pairs, semaphores, 0)
     jac = jac_ref[...]
-    start = start_ref[...]
     pairs = pairs_ref[...]
     rows = jac.shape[0]
     gram = dot_halved(jac, jac, 1, 1)
+    finish(copies)
+    blocks = []
+    for row in (rank, rank + 8):
+        blocks += [a_ref[piece, pl.ds(row, 1), :] for piece in range(3)]
+        blocks.append(bo_ref[pl.ds(row, 1), :])
+    blocks += [bq_ref[pl.ds(group, 1), :], ao_ref[pl.ds(group, 1), :]]
+    blocks += [bkv_ref[piece, pl.ds(group, 1), :] for piece in range(2)]
+    start = flat(blocks + [jnp.zeros((1, LANES - 2 * HEAD_SIZE), jnp.float32)])
     starts = jnp.concatenate(rounded_parts(start, 3), 0)
     along = lane_sum(dot_halved(jac, starts, 1, 1))
     own_pairs = pairs[:, :rows]
     gram = dot_entire(dot_entire(own_pairs, gram, 1, 0), own_pairs, 1, 1)
     along = dot_entire(own_pairs, jnp.broadcast_to(along, (rows, 128)), 1, 0)
-    rewards = pltpu.roll(rewards_ref[...], OBJ * rank_ref[0], axis=1)[:1]
-    rewards = jnp.where(rank_ref[1] == 0, rewards, 0.0)
+    rewards = pltpu.roll(rewards_ref[...], OBJ * group, axis=1)[:1]
+    rewards = jnp.where(rank == 0, rewards, 0.0)
     apart = lane_sum(pairs * rewards)
     square = jnp.sum(start * start)
     lane = lax.broadcasted_iota(jnp.int32, (PACK_ROWS, 128), 1)
@@ -165,7 +201,6 @@
 
 
 def assemble_body(
-    core_ref,
     part_ref,
     own_ref,
     other_ref,
@@ -194,30 +229,39 @@
     wanted = (row % 8) * 8 + ((row % 16) // 8) * 4 + row // 16
     moved = jnp.where(lane == wanted, 1.0, 0.0).astype(jnp.bfloat16)
 
+    mine = lax.axis_index("dp").astype(jnp.int32) % 2
+
     def pick(core, spot, lanes):
         return jnp.where(
-            core_ref[0] == core, own_ref[spot, :, lanes], other_ref[spot, :, lanes]
+            mine == core, own_ref[spot, :, lanes], other_ref[spot, :, lanes]
         )
 
-    for half in range(2):
-        spot = pl.ds(pl.multiple_of(8 * step, 8), 8)
-        block = pick(half, spot, slice(0, LANES)).reshape(64, LANES)
+    for half in range(4):
+        spot = pl.ds(pl.multiple_of(16 * step + 8 * (half // 2), 8), 8)
+        block = pick(half % 2, spot, slice(0, LANES)).reshape(64, LANES)
         placed = dot_halved(moved, block, 1, 0).reshape(4, 16, LANES)
         lanes = slice(half * LANES, (half + 1) * LANES)
         out_a_ref[:, :, lanes] = placed[:3] + part * a_ref[:, :, lanes]
         out_bo_ref[:, lanes] = placed[3] + part * bo_ref[:, lanes]
-    block = jnp.concatenate(
-        [pick(at % 2, 8 * (at // 2) + step, slice(LANES, None)) for at in range(16)], 0
-    )
-    placed = dot_halved(one_hot(128, 8, 16), block, 1, 0)
-    for chunk in range(4):
-        lanes = slice(chunk * 128, (chunk + 1) * 128)
-        out_bq_ref[:, lanes] = placed[16 * chunk : 16 * chunk + 16, :128] + part * bq_ref[:, lanes]
-        out_ao_ref[:, lanes] = (
-            placed[64 + 16 * chunk : 80 + 16 * chunk, :128] + part * ao_ref[:, lanes]
+    turned = one_hot(128, 8, 16)
+    for sub in range(2):
+        block = jnp.concatenate(
+            [
+                pick(at % 2, 8 * (at // 2) + 2 * step + sub, slice(LANES, None))
+                for at in range(16)
+            ],
+            0,
         )
-    out_bkv_ref[0] = placed[:16, 128:] + part * bkv_ref[0]
-    out_bkv_ref[1] = placed[16:32, 128:] + part * bkv_ref[1]
+        placed = dot_halved(turned, block, 1, 0)
+        for chunk in range(4):
+            lanes = slice(sub * LANES + chunk * 128, sub * LANES + (chunk + 1) * 128)
+            rows = slice(16 * chunk, 16 * chunk + 16)
+            out_bq_ref[:, lanes] = placed[rows, :128] + part * bq_ref[:, lanes]
+            rows = slice(64 + 16 * chunk, 80 + 16 * chunk)
+            out_ao_ref[:, lanes] = placed[rows, :128] + part * ao_ref[:, lanes]
+        lanes = slice(sub * HEAD_SIZE, (sub + 1) * HEAD_SIZE)
+        out_bkv_ref[0, :, lanes] = placed[:16, 128:] + part * bkv_ref[0, :, lanes]
+        out_bkv_ref[1, :, lanes] = placed[16:32, 128:] + part * bkv_ref[1, :, lanes]
 
 
 def whole(count):
@@ -258,12 +302,13 @@
     return flat([rows[at : at + 128] for at in range(0, rows.shape[0], 128)])
 
 
-def place_shards(spots_ref, whole_ref, shards, semaphores):
+def place_shards(whole_ref, shards, semaphores):
+    spots = shard_spots()
     half = whole_ref.shape[1] // 2
     copies = []
     for at, shard in enumerate(shards):
         spot = at if at < 6 else 6 + (at - 6) // 2
-        rows = pl.ds(pl.multiple_of(spots_ref[spot] * 16, 16), 16)
+        rows = pl.ds(pl.multiple_of(spots[spot] * 16, 16), 16)
         if at < 6:
             target = whole_ref.at[rows, :]
         else:
@@ -333,18 +378,25 @@
     rank = lax.axis_index("tensor").astype(jnp.int32)
     y, z = rank // 4 * 4, rank % 4
     other = 4 - y
-    return jnp.stack(
-        [
-            y + z,
-            other + z,
-            y + (z + 3) % 4,
-            y + (z + 1) % 4,
-            other + (z + 3) % 4,
-            other + (z + 1) % 4,
-            y + (z + 2) % 4,
-            other + (z + 2) % 4,
-        ]
-    )
+    return [
+        y + z,
+        other + z,
+        y + (z + 3) % 4,
+        y + (z + 1) % 4,
+        other + (z + 3) % 4,
+        other + (z + 1) % 4,
+        y + (z + 2) % 4,
+        other + (z + 2) % 4,
+    ]
+
+
+def small_pairs(down_hbm, up_query_hbm, up_kv_hbm, small_ref):
+    return [
+        (down_hbm, small_ref.at[:, 0:512]),
+        (up_query_hbm, small_ref.at[:, 512:1024]),
+        (up_kv_hbm.at[0], small_ref.at[:, 1024:1152]),
+        (up_kv_hbm.at[1], small_ref.at[:, 1152:1280]),
+    ]
 
 
 CHUNK = 2048
@@ -352,7 +404,6 @@
 
 
 def forward_body(
-    spots_ref,
     shard_0,
     shard_1,
     shard_2,
@@ -368,7 +419,9 @@
     down_hbm,
     output_weight_hbm,
     up_output_hbm,
-    small_hbm,
+    small_down_hbm,
+    small_query_hbm,
+    small_kv_hbm,
     tokens_hbm,
     out_hbm,
     state_hbm,
@@ -398,7 +451,7 @@
         shard_8,
         shard_9,
     ]
-    placed = place_shards(spots_ref, tokens_ref, shards, semaphores)
+    placed = place_shards(tokens_ref, shards, semaphores)
     count = tokens_ref.shape[1] // CHUNK
 
     def early(step):
@@ -425,17 +478,17 @@
 
     for step in range(count):
         begin(early(step))
-    small_copy = launch([(small_hbm, small_ref)], semaphores, 10 + 6 * count)
-    for step in range(count):
-        begin(late(step))
+    pairs = small_pairs(small_down_hbm, small_query_hbm, small_kv_hbm, small_ref)
+    small_copy = launch(pairs, semaphores, 12 + 6 * count)
     finish(placed)
-    leaving = launch([(tokens_ref, tokens_hbm)], semaphores, 11 + 6 * count)
+    leaving = launch([(tokens_ref, tokens_hbm)], semaphores, 10 + 6 * count)
     query_sum[...] = jnp.zeros(query_sum.shape, jnp.float32)
     kv_sum[...] = jnp.zeros(kv_sum.shape, jnp.float32)
     low_sum[...] = jnp.zeros(low_sum.shape, jnp.float32)
 
     def project(step, _):
         finish(early(step))
+        begin(late(step))
         span = span_of(step)
         tokens = tokens_ref[:, span]
         query_sum[...] += dot_halved(tokens, query_weight_ref[span, :], 1, 0)
@@ -478,7 +531,7 @@
     halved = context.astype(jnp.bfloat16)
     turned = tall([context_low, jnp.zeros((112, 128), jnp.float32)]).T[:, :16]
     halved_low = flat(rounded_parts(turned, 2))
-    leaving += launch([(state_ref, state_hbm)], semaphores, 12 + 6 * count)
+    leaving += launch([(state_ref, state_hbm)], semaphores, 11 + 6 * count)
 
     def write(step, _):
         finish(late(step))
@@ -498,21 +551,22 @@
 
 
 def forward(
-    spots, shards, query_weight, key_value_weight, down_rows, output_weight, up_output, small
+    shards, query_weight, key_value_weight, down_rows, output_weight, up_output, *adapters
 ):
     width = shards[0].shape[1]
     query_cols = query_weight.shape[1]
-    arrays = (query_weight, key_value_weight, down_rows, output_weight, up_output, small)
+    weights = (query_weight, key_value_weight, down_rows, output_weight, up_output)
+    arrays = (*weights, *adapters)
+    small = jax.ShapeDtypeStruct((16, 1280), jnp.bfloat16)
     results = [
         jax.ShapeDtypeStruct((128, width), jnp.bfloat16),
         jax.ShapeDtypeStruct((8, 16, width), jnp.bfloat16),
         jax.ShapeDtypeStruct((STATE_ROWS, 128), jnp.float32),
     ]
-    scratch = [results[0], *arrays, results[1], results[2]]
+    scratch = [results[0], *weights, small, results[1], results[2]]
     return pl.pallas_call(
         forward_body,
-        in_specs=[pl.BlockSpec(memory_space=pltpu.SMEM)]
-        + [ANYWHERE] * (len(shards) + len(arrays)),
+        in_specs=[ANYWHERE] * (len(shards) + len(arrays)),
         out_specs=[ANYWHERE] * 3,
         out_shape=results,
         scratch_shapes=[pltpu.VMEM(array.shape, array.dtype) for array in scratch]
@@ -520,16 +574,15 @@
             pltpu.VMEM((128, query_cols), jnp.float32),
             pltpu.VMEM((128, 256), jnp.float32),
             pltpu.VMEM((128, 128), jnp.float32),
-            pltpu.SemaphoreType.DMA((13 + 6 * (width // CHUNK),)),
+            pltpu.SemaphoreType.DMA((16 + 6 * (width // CHUNK),)),
         ],
         compiler_params=pltpu.CompilerParams(vmem_limit_bytes=LARGE),
         name="forward",
-    )(spots, *shards, *arrays)
+    )(*shards, *arrays)
 
 
 def cotangents_body(
     lens_ref,
-    spots_ref,
     shard_0,
     shard_1,
     shard_2,
@@ -543,7 +596,9 @@
     weight_hbm,
     side_hbm,
     state_hbm,
-    small_hbm,
+    small_down_hbm,
+    small_query_hbm,
+    small_kv_hbm,
     resid_hbm,
     factors_ref,
     narrow_ref,
@@ -570,7 +625,7 @@
         shard_8,
         shard_9,
     ]
-    placed = place_shards(spots_ref, resid_ref, shards, semaphores)
+    placed = place_shards(resid_ref, shards, semaphores)
     count = resid_ref.shape[1] // CHUNK
 
     def early(step):
@@ -584,14 +639,15 @@
     for step in range(count):
         begin(early(step))
     first = 10 + 2 * count
-    others = launch([(state_hbm, state_ref), (small_hbm, small_ref)], semaphores, first)
+    pairs = small_pairs(small_down_hbm, small_query_hbm, small_kv_hbm, small_ref)
+    others = launch([(state_hbm, state_ref)] + pairs, semaphores, first)
     slow_ref[...] = jnp.zeros(slow_ref.shape, jnp.float32)
     through_ref[...] = jnp.zeros(through_ref.shape, jnp.float32)
     square_ref[...] = jnp.zeros(square_ref.shape, jnp.float32)
     narrow_ref[...] = jnp.zeros(narrow_ref.shape, jnp.float32)
     width = resid_ref.shape[1]
     finish(placed)
-    leaving = launch([(resid_ref, resid_hbm)], semaphores, first + 2)
+    leaving = launch([(resid_ref, resid_hbm)], semaphores, first + 5)
 
     def project(step, _):
         finish(early(step))
@@ -740,10 +796,12 @@
         scalars_ref[48:] = jnp.broadcast_to(lead_turned, (40, 128))
 
 
-def cotangents(lens, spots, shards, output_weight, side, state, small):
+def cotangents(lens, shards, output_weight, side, state, *adapters):
     width = shards[0].shape[1]
     query_cols = output_weight.shape[0]
-    arrays = (output_weight, side, state, small)
+    arrays = (output_weight, side, state, *adapters)
+    small = jax.ShapeDtypeStruct((16, 1280), jnp.bfloat16)
+    scratch = [output_weight, side, state, small]
     results = [
         jax.ShapeDtypeStruct((128, width), jnp.bfloat16),
         jax.ShapeDtypeStruct((320, 128), jnp.float32),
@@ -752,34 +810,34 @@
     ]
     return pl.pallas_call(
         cotangents_body,
-        in_specs=[pl.BlockSpec(memory_space=pltpu.SMEM)] * 2
+        in_specs=[pl.BlockSpec(memory_space=pltpu.SMEM)]
         + [ANYWHERE] * (len(shards) + len(arrays)),
         out_specs=[ANYWHERE] + whole(3),
         out_shape=results,
-        scratch_shapes=[pltpu.VMEM(array.shape, array.dtype) for array in (results[0], *arrays)]
+        scratch_shapes=[pltpu.VMEM(array.shape, array.dtype) for array in (results[0], *scratch)]
         + [
             pltpu.VMEM((144, query_cols), jnp.float32),
             pltpu.VMEM((256, 128), jnp.float32),
             pltpu.VMEM((128, 128), jnp.float32),
-            pltpu.SemaphoreType.DMA((13 + 2 * (width // CHUNK),)),
+            pltpu.SemaphoreType.DMA((16 + 2 * (width // CHUNK),)),
         ],
         compiler_params=pltpu.CompilerParams(vmem_limit_bytes=LARGE),
         name="cotangents",
-    )(lens, spots, *shards, *arrays)
+    )(lens, *shards, *arrays)
 
 
 def jacobian_body(
     factors_hbm,
     tokens_hbm,
     resid_hbm,
-    side_hbm,
+    heads_hbm,
     scalars_hbm,
     narrow_hbm,
     payload_hbm,
     factors_ref,
     tokens_ref,
     resid_ref,
-    side_ref,
+    heads_ref,
     scalars_ref,
     narrow_ref,
     payload_ref,
@@ -794,7 +852,7 @@
         pairs = [
             (tokens_hbm.at[:, span], tokens_ref.at[:, span]),
             (resid_hbm.at[:, span], resid_ref.at[:, span]),
-            (side_hbm.at[:, span], side_ref.at[:, span]),
+            (heads_hbm.at[:, span], heads_ref.at[:, span]),
         ]
         return prepared(pairs, semaphores, 3 + 3 * step)
 
@@ -814,22 +872,20 @@
     left = flat(
         [jnp.where(last, 0.0, factors), jnp.where(last, -factors * scalars_ref[8:48], 0.0)]
     )
-    lane = lax.broadcasted_iota(jnp.int32, (40, 16), 1)
-    lead = jnp.where(lane == row - 15, lane_sum(factors * scalars_ref[48:]), 0.0)
+    lead = lane_sum(factors * scalars_ref[48:])
 
     def both(rows):
         upper = rows.astype(jnp.bfloat16).astype(jnp.float32)
         return tall([upper, rows - upper]).astype(jnp.bfloat16)
 
     left = both(left)
-    lead = both(lead)
 
     def place(step, _):
         finish(arriving(step))
         span = span_of(step)
         right = tall([tokens_ref[:, span], resid_ref[:, span]])
-        pair = dot_halved(left, right, 1, 0) + dot_halved(lead, side_ref[16:, span], 1, 0)
-        rows = pair[:40] + pair[40:]
+        pair = dot_halved(left, right, 1, 0)
+        rows = pair[:40] + pair[40:] + lead * heads_ref[:40, span].astype(jnp.float32)
         for inner in range(per_step):
             group = step * per_step + inner
             below = flat(
@@ -863,21 +919,19 @@
     )(*arrays)
 
 
-def assemble(core, part, own, other, start_a, start_bq, start_bkv, start_ao, start_bo):
-    steps = 8
-    shapes = [start_a, start_bq, start_bkv, start_ao, start_bo]
+def assemble(part, own, other, *shapes):
+    steps = 4
     blocks = [
-        pl.BlockSpec((3, 16, 2 * LANES), lambda step: (0, 0, step)),
-        pl.BlockSpec((16, LANES), lambda step: (0, step)),
-        pl.BlockSpec((2, 16, HEAD_SIZE), lambda step: (0, 0, step)),
-        pl.BlockSpec((16, LANES), lambda step: (0, step)),
+        pl.BlockSpec((3, 16, 4 * LANES), lambda step: (0, 0, step)),
         pl.BlockSpec((16, 2 * LANES), lambda step: (0, step)),
+        pl.BlockSpec((2, 16, 2 * HEAD_SIZE), lambda step: (0, 0, step)),
+        pl.BlockSpec((16, 2 * LANES), lambda step: (0, step)),
+        pl.BlockSpec((16, 4 * LANES), lambda step: (0, step)),
     ]
     return pl.pallas_call(
         assemble_body,
         grid=(steps,),
         in_specs=[
-            pl.BlockSpec(memory_space=pltpu.SMEM),
             pl.BlockSpec(memory_space=pltpu.SMEM),
             pl.BlockSpec(own.shape, lambda step: (0, 0, 0)),
             pl.BlockSpec(other.shape, lambda step: (0, 0, 0)),
@@ -887,7 +941,7 @@
         out_shape=[jax.ShapeDtypeStruct(shape.shape, jnp.float32) for shape in shapes],
         compiler_params=pltpu.CompilerParams(vmem_limit_bytes=14 * 2**20),
         name="assemble",
-    )(core, part, own, other, *(pltpu.with_memory_space_constraint(x, pltpu.HBM) for x in shapes))
+    )(part, own, other, *shapes)
 
 
 def local(
@@ -920,34 +974,31 @@
     down_rows = jnp.transpose(adapter_down_qkv, (0, 2, 1)).reshape(48, width)
     down_output = adapter_down_output.T
     head_rows = head.T
-    spots = shard_spots()
     side = jnp.concatenate([adapter_up_output, head_rows, jnp.zeros((11, width), head.dtype)], 0)
-    small = jnp.concatenate(
-        [down_output, adapter_up_query, adapter_up_key_value[0], adapter_up_key_value[1]], 1
-    )
+    heads = jnp.pad(head_rows, ((15, 0), (0, 0)))
+    heads = jnp.pad(jnp.concatenate([heads, heads], 0), ((0, 8), (0, 0)))
+    adapters = (down_output, adapter_up_query, adapter_up_key_value)
     tokens, out_terms, state = forward(
-        spots,
         gather_by_relays(hidden[0]),
         query_weight,
         key_value_weight,
         down_rows,
         output_weight,
         adapter_up_output,
-        small,
+        *adapters,
     )
     out_pieces = lax.all_to_all(out_terms, "tensor", 0, 0)
     resid_own = hidden[0].astype(jnp.float32) + jnp.sum(out_pieces.astype(jnp.float32), 0)
     resid, factors, narrow, scalars = cotangents(
         lens,
-        spots,
         gather_by_relays(resid_own.astype(jnp.bfloat16)),
         output_weight,
         side,
         state,
-        small,
+        *adapters,
     )
     factors = lax.all_to_all(factors.reshape(shards, 8 * OBJ, length), "tensor", 0, 0)
-    payload = jacobian(factors, tokens, resid, side, scalars, narrow)
+    payload = jacobian(factors, tokens, resid, heads, scalars, narrow)
     spread = lax.all_to_all(payload, "dp", 0, 0)
     jac = (
         spread[:, : PIECES * OBJ]
@@ -956,37 +1007,14 @@
         .reshape(groups * OBJ, PIECES * LANES)
     )
 
-    own_a = lax.dynamic_slice(
-        jnp.transpose(initial_down_qkv, (0, 2, 1)).reshape(3, 2, shards, width),
-        (0, 0, tensor_rank, group_rank * LANES),
-        (3, 2, 1, LANES),
-    ).reshape(3, 2, LANES)
-    own_bo = lax.dynamic_slice(
-        initial_up_output.reshape(2, shards, width),
-        (0, tensor_rank, group_rank * LANES),
-        (2, 1, LANES),
-    ).reshape(2, LANES)
-    own_bq = lax.dynamic_slice(
-        initial_up_query, (group_rank, tensor_rank * query_cols), (1, query_cols)
-    )
-    own_ao = lax.dynamic_slice(
-        initial_down_output.T, (group_rank, tensor_rank * query_cols), (1, query_cols)
-    )
-    own_bkv = lax.dynamic_slice(
-        initial_up_key_value, (0, group_rank, tensor_rank * HEAD_SIZE), (2, 1, HEAD_SIZE)
-    )
-    own_start = jnp.concatenate(
-        [
-            jnp.concatenate([own_a.transpose(1, 0, 2), own_bo[:, None]], 1).reshape(8, LANES),
-            own_bq,
-            own_ao,
-            jnp.concatenate(
-                [own_bkv.reshape(1, 2 * HEAD_SIZE), jnp.zeros((1, LANES - 2 * HEAD_SIZE))], 1
-            ),
-        ],
-        0,
-    ).reshape(1, PIECES * LANES)
-    own_start = own_start.astype(jnp.float32)
+    starts = (
+        jnp.transpose(initial_down_qkv, (0, 2, 1)),
+        initial_up_query,
+        initial_up_key_value,
+        initial_down_output.T,
+        initial_up_output,
+    )
+    starts = [pltpu.with_memory_space_constraint(start, pltpu.HBM) for start in starts]
     sequences = jnp.arange(groups)
     leads = sequences < partner
     order = jnp.sum((sequences[None, :] < sequences[:, None]) & leads[None, :], 1)
@@ -1000,18 +1028,20 @@
     pairs = jnp.pad(pairs, ((0, PACK_ROWS - PAIR_ROWS), (0, 128 - groups * OBJ)))
     packed = pl.pallas_call(
         gram_body,
-        in_specs=[pl.BlockSpec(memory_space=pltpu.SMEM)] + whole(4),
+        in_specs=whole(3) + [ANYWHERE] * 5,
         out_specs=pl.BlockSpec(memory_space=pltpu.VMEM),
         out_shape=jax.ShapeDtypeStruct((16, 128), jnp.float32),
+        scratch_shapes=[
+            pltpu.VMEM((3, 16, LANES), jnp.float32),
+            pltpu.VMEM((16, LANES), jnp.float32),
+            pltpu.VMEM((2, 16, HEAD_SIZE), jnp.float32),
+            pltpu.VMEM((16, LANES), jnp.float32),
+            pltpu.VMEM((16, LANES), jnp.float32),
+            pltpu.SemaphoreType.DMA((5,)),
+        ],
         compiler_params=pltpu.CompilerParams(vmem_limit_bytes=6 * 2**20),
         name="gram",
-    )(
-        jnp.stack([group_rank, tensor_rank]).astype(jnp.int32),
-        jac,
-        own_start,
-        pairs,
-        scalars[:8],
-    )
+    )(jac, pairs, scalars[:8], *starts)
     packed = jnp.sum(gather_by_exchange(packed, "dp"), 0)
     packed = gather_by_exchange(packed, "tensor")
     own_result, part = pl.pallas_call(
@@ -1037,17 +1067,7 @@
         axis_index_groups=same_core,
     )
     other_half = lax.ppermute(own_half, "dp", [(at, at ^ 1) for at in range(groups)])
-    next_a, next_bq, next_bkv, next_ao, next_bo = assemble(
-        (group_rank % 2).astype(jnp.int32).reshape(1),
-        part,
-        own_half,
-        other_half,
-        jnp.transpose(initial_down_qkv, (0, 2, 1)),
-        initial_up_query,
-        initial_up_key_value,
-        initial_down_output.T,
-        initial_up_output,
-    )
+    next_a, next_bq, next_bkv, next_ao, next_bo = assemble(part, own_half, other_half, *starts)
     return jnp.transpose(next_a, (0, 2, 1)), next_bq, next_bkv, next_ao.T, next_bo
 
 

time: 202 us -> 198 us (0.980)
  waiting for transfers between devices: 49.6 us -> 56.4 us
  local copies, waits for them, and re-layouts: 10.8 us -> 5.19 us
  Pallas kernels: 37.4 us -> 34.4 us
    ppermute x18, waiting for transfers between devices: 8.45 us -> 13.4 us  [permute(): return lax.ppermute(array, 'tensor', pairs)]
    dynamic_slice x4 -> x0, local copies, waits for them, and re-layouts: 3.46 us -> none  [the longest x1 0.98 us: local(): lax.dynamic_slice(jnp.transpose(initial_down_qkv, (0, 2, 1)).reshape(3, 2...]
    pallas_call x1, Pallas kernels: 6.65 us -> 4.39 us  [assemble(): pl.pallas_call(assemble_body, grid=(steps,), in_specs=[pl.BlockSpec(memor...]
  transfers between devices with their start and end apart: 22 -> 22, of which waited for: 9 -> 10; matrix products, arithmetic and copies ran while one was open for 5% -> 2% of each run, Pallas kernels for 0% -> 0%
where the time goes in v6:
time: 198 us
  starting transfers between devices  60.9 us (31%)
  waiting for transfers between devices  56.4 us (28%)
  blocking collectives  36.2 us (18%)
  Pallas kernels  34.4 us (17%)
  local copies, waits for them, and re-layouts  5.19 us (3%)
  other arithmetic  2.7 us (1%)
    ppermute x18, starting transfers between devices, permute(): return lax.ppermute(array, 'tensor', pairs)  35.4 us
    all_to_all x1, waiting for transfers between devices, local(): out_pieces = lax.all_to_all(out_terms, 'tensor', 0, 0)  21.5 us
    all_to_all x2, blocking collectives, gather_by_exchange(): return lax.all_to_all(copies, axis, 0, 0)  18.8 us
    all_to_all x1, blocking collectives, local(): lax.all_to_all(jnp.broadcast_to(own_result[None], (half,) + own_result.sh...  17.4 us
    ppermute x18, waiting for transfers between devices, permute(): return lax.ppermute(array, 'tensor', pairs)  13.4 us
    all_to_all x1, waiting for transfers between devices, local(): spread = lax.all_to_all(payload, 'dp', 0, 0)  12.7 us
    pallas_call x1, Pallas kernels, cotangents(): pl.pallas_call(cotangents_body, in_specs=[pl.BlockSpec(memory_space=pltpu...  11.6 us
    pallas_call x1, Pallas kernels, forward(): pl.pallas_call(forward_body, in_specs=[ANYWHERE] * (len(shards) + len(arr...  11.4 us
  transfers between devices with their start and end apart: 22, of which 10 were waited for; matrix products, arithmetic and copies ran while one was open for 2% of the time, Pallas kernels for 0%

profile of v6, /device:TPU:1, one launch (start us, length us, event | category | flops | bytes accessed | tf_op | source)
XLA Modules:
  0.0 197.7 jit_solution(3417296689933108852)
XLA Ops:
  0.6 3.8 %collective-permute-start = (bf16[16,8192]{1,0:T(8,128)(2,1)}, bf16[16,8192]{1,0:T(8,128)(2,1)S(1)}, u32[]{:S(2)}, u32[]{:S(2)}) collective-permute-start(bf16[16,8192]{1,0:T(8,128)(2,1)} %bitcast.30), channel_id=1, source_target_pairs={{0,4},{1,5},{2,6},{3,7},{4,0},{5,1},{6,2},{7,3},{8,12},{9,13},{10,... | collective-permute-start | bytes 786440 | tf_op jit(solution)/shard_map/ppermute | solution.py:362
  4.5 1.6 collective-permute-start.1
  6.1 2.1 %collective-permute-start.2 = (bf16[16,8192]{1,0:T(8,128)(2,1)}, bf16[16,8192]{1,0:T(8,128)(2,1)S(1)}, u32[]{:S(2)}, u32[]{:S(2)}) collective-permute-start(bf16[16,8192]{1,0:T(8,128)(2,1)} %bitcast.32), channel_id=1, source_target_pairs={{0,3},{1,0},{2,1},{3,2},{4,7},{5,4},{6,5},{7,6},{8,11},{9,8},{10,9... | collective-permute-start | bytes 786440 | tf_op jit(solution)/shard_map/ppermute | solution.py:362
  8.2 2.2 %collective-permute-done.shard_1 = bf16[16,8192]{1,0:T(8,128)(2,1)S(1)} collective-permute-done((bf16[16,8192]{1,0:T(8,128)(2,1)}, bf16[16,8192]{1,0:T(8,128)(2,1)S(1)}, u32[]{:S(2)}, u32[]{:S(2)}) %collective-permute-start) | collective-permute-done | bytes 262176 | tf_op jit(solution)/shard_map/ppermute | solution.py:362
  10.4 1.6 collective-permute-start.3
  12.1 2.1 %collective-permute-start.4 = (bf16[16,8192]{1,0:T(8,128)(2,1)S(1)}, bf16[16,8192]{1,0:T(8,128)(2,1)S(1)}, u32[]{:S(2)}, u32[]{:S(2)}) collective-permute-start(bf16[16,8192]{1,0:T(8,128)(2,1)S(1)} %collective-permute-done.shard_1), channel_id=1, source_target_pairs={{0,3},{1,0},{2,1},{3,2},{4,7},{5,4},{6,5},{7,6},{8,11},{9,8},{10,9... | collective-permute-start | bytes 786440 | tf_op jit(solution)/shard_map/ppermute | solution.py:362
  14.3 2.7 %collective-permute-start.6 = (bf16[16,4096]{1,0:T(8,128)(2,1)S(1)}, bf16[16,4096]{1,0:T(8,128)(2,1)S(1)}, u32[]{:S(2)}, u32[]{:S(2)}) collective-permute-start(bf16[16,4096]{1,0:T(8,128)(2,1)S(1)} %slice.43), channel_id=1, source_target_pairs={{0,3},{1,0},{2,1},{3,2},{4,7},{5,4},{6,5},{7,6},{8,11},{9,8},{10,9... | collective-permute-start | bytes 393224 | tf_op jit(solution)/shard_map/ppermute | solution.py:362
  17.0 2.2 %collective-permute-done.3.shard_4 = bf16[16,8192]{1,0:T(8,128)(2,1)S(1)} collective-permute-done((bf16[16,8192]{1,0:T(8,128)(2,1)S(1)}, bf16[16,8192]{1,0:T(8,128)(2,1)S(1)}, u32[]{:S(2)}, u32[]{:S(2)}) %collective-permute-start.3) | collective-permute-done | bytes 262176 | tf_op jit(solution)/shard_map/ppermute | solution.py:362
  19.4 2.7 %collective-permute-start.8 = (bf16[16,4096]{1,0:T(8,128)(2,1)S(1)}, bf16[16,4096]{1,0:T(8,128)(2,1)S(1)}, u32[]{:S(2)}, u32[]{:S(2)}) collective-permute-start(bf16[16,4096]{1,0:T(8,128)(2,1)S(1)} %slice.45), channel_id=1, source_target_pairs={{0,3},{1,0},{2,1},{3,2},{4,7},{5,4},{6,5},{7,6},{8,11},{9,8},{10,9... | collective-permute-start | bytes 393224 | tf_op jit(solution)/shard_map/ppermute | solution.py:362
  22.1 2.8 %collective-permute-done.7.shard_8 = bf16[16,4096]{1,0:T(8,128)(2,1)S(1)} collective-permute-done((bf16[16,4096]{1,0:T(8,128)(2,1)S(1)}, bf16[16,4096]{1,0:T(8,128)(2,1)S(1)}, u32[]{:S(2)}, u32[]{:S(2)}) %collective-permute-start.7) | collective-permute-done | bytes 131104 | tf_op jit(solution)/shard_map/ppermute | solution.py:362
  25.0 0.6 copy-done.21
  25.7 11.4 %forward.1 = (bf16[128,8192]{1,0:T(8,128)(2,1)}, bf16[8,16,8192]{2,1,0:T(8,128)(2,1)}, f32[2368,128]{1,0:T(8,128)}) custom-call(bf16[16,8192]{1,0:T(8,128)(2,1)} %bitcast.33, bf16[16,8192]{1,0:T(8,128)(2,1)} %copy-done.13, bf16[16,8192]{1,0:T(8,128)(2,1)} %copy-done.4, bf16[16,8192]{1,0:T(8,128)(2,1)} %copy-done.5, bf16[16,8192]{1,0:T(8,128)(2,1)} %copy-done.6, ...), custom_call_target="tpu_custom_call" | custom-call | tf_op jit(solution)/shard_map/forward/pallas_call | solution.py:567
  37.0 6.5 %all-to-all-start = ((bf16[8,16,8192]{2,1,0:T(8,128)(2,1)}), bf16[8,16,8192]{2,1,0:T(8,128)(2,1)S(1)}, u32[]{:S(2)}, u32[]{:S(2)}) async-start(bf16[8,16,8192]{2,1,0:T(8,128)(2,1)} %get-tuple-element.19), calls=%async_computation | async-start | bytes 4194304 | tf_op jit(solution)/shard_map/all_to_all | solution.py:990
  43.7 21.5 %all-to-all-done = bf16[8,16,8192]{2,1,0:T(8,128)(2,1)S(1)} async-done(((bf16[8,16,8192]{2,1,0:T(8,128)(2,1)}), bf16[8,16,8192]{2,1,0:T(8,128)(2,1)S(1)}, u32[]{:S(2)}, u32[]{:S(2)}) %all-to-all-start) | async-done | bytes 2097184 | tf_op jit(solution)/shard_map/all_to_all | solution.py:990
  65.2 0.3 convert_reduce_fusion
  65.6 7.2 %collective-permute-start.9 = (bf16[16,8192]{1,0:T(8,128)(2,1)S(1)}, bf16[16,8192]{1,0:T(8,128)(2,1)S(1)}, u32[]{:S(2)}, u32[]{:S(2)}) collective-permute-start(bf16[16,8192]{1,0:T(8,128)(2,1)S(1)} %add_convert_fusion.shard_0), channel_id=1, source_target_pairs={{0,4},{1,5},{2,6},{3,7},{4,0},{5,1},{6,2},{7,3},{8,12},{9,13},{10,... | collective-permute-start | bytes 786440 | tf_op jit(solution)/shard_map/ppermute | solution.py:362
  72.8 0.9 maximum_maximum_fusion.side_hbm
  73.8 1.0 collective-permute-start.10
  74.8 1.7 collective-permute-start.11
  76.5 1.0 collective-permute-done.9.shard_1
  77.5 1.4 collective-permute-start.12
  78.9 1.3 collective-permute-start.13
  80.2 1.0 fusion.2.heads_hbm
  82.2 2.6 %collective-permute-start.15 = (bf16[16,4096]{1,0:T(8,128)(2,1)S(1)}, bf16[16,4096]{1,0:T(8,128)(2,1)S(1)}, u32[]{:S(2)}, u32[]{:S(2)}) collective-permute-start(bf16[16,4096]{1,0:T(8,128)(2,1)S(1)} %slice.47), channel_id=1, source_target_pairs={{0,3},{1,0},{2,1},{3,2},{4,7},{5,4},{6,5},{7,6},{8,11},{9,8},{10,9... | collective-permute-start | bytes 393224 | tf_op jit(solution)/shard_map/ppermute | solution.py:362
  84.8 2.5 %collective-permute-done.12.shard_4 = bf16[16,8192]{1,0:T(8,128)(2,1)S(1)} collective-permute-done((bf16[16,8192]{1,0:T(8,128)(2,1)S(1)}, bf16[16,8192]{1,0:T(8,128)(2,1)S(1)}, u32[]{:S(2)}, u32[]{:S(2)}) %collective-permute-start.12) | collective-permute-done | bytes 262176 | tf_op jit(solution)/shard_map/ppermute | solution.py:362
  87.5 2.7 %collective-permute-start.17 = (bf16[16,4096]{1,0:T(8,128)(2,1)S(1)}, bf16[16,4096]{1,0:T(8,128)(2,1)S(1)}, u32[]{:S(2)}, u32[]{:S(2)}) collective-permute-start(bf16[16,4096]{1,0:T(8,128)(2,1)S(1)} %slice.49), channel_id=1, source_target_pairs={{0,3},{1,0},{2,1},{3,2},{4,7},{5,4},{6,5},{7,6},{8,11},{9,8},{10,9... | collective-permute-start | bytes 393224 | tf_op jit(solution)/shard_map/ppermute | solution.py:362
  90.3 2.6 %collective-permute-done.16.shard_8 = bf16[16,4096]{1,0:T(8,128)(2,1)S(1)} collective-permute-done((bf16[16,4096]{1,0:T(8,128)(2,1)S(1)}, bf16[16,4096]{1,0:T(8,128)(2,1)S(1)}, u32[]{:S(2)}, u32[]{:S(2)}) %collective-permute-start.16) | collective-permute-done | bytes 131104 | tf_op jit(solution)/shard_map/ppermute | solution.py:362
  93.0 0.6 copy-done.18
  93.6 11.6 %cotangents.1 = (bf16[128,8192]{1,0:T(8,128)(2,1)}, f32[320,128]{1,0:T(8,128)}, f32[4,256,128]{2,1,0:T(8,128)}, f32[88,128]{1,0:T(8,128)}) custom-call(s32[1]{0:T(128)S(6)} %copy.31.lens_ref, bf16[16,8192]{1,0:T(8,128)(2,1)} %copy-done.2, bf16[16,8192]{1,0:T(8,128)(2,1)} %copy-done.14, bf16[16,8192]{1,0:T(8,128)(2,1)} %copy-done.8, ...), custom_call_target="tpu_custom_call" | custom-call | tf_op jit(solution)/shard_map/cotangents/pallas_call | solution.py:811
  105.3 6.1 %all-to-all-start.1 = ((f32[8,40,128]{2,1,0:T(8,128)}), f32[8,40,128]{2,1,0:T(8,128)S(1)}, u32[]{:S(2)}, u32[]{:S(2)}) async-start(f32[8,40,128]{2,1,0:T(8,128)} %bitcast.39), calls=%async_computation.1 | async-start | bytes 327680 | tf_op jit(solution)/shard_map/all_to_all | solution.py:1000
  111.5 7.0 %all-to-all-done.1.factors_hbm = f32[8,40,128]{2,1,0:T(8,128)S(1)} async-done(((f32[8,40,128]{2,1,0:T(8,128)}), f32[8,40,128]{2,1,0:T(8,128)S(1)}, u32[]{:S(2)}, u32[]{:S(2)}) %all-to-all-start.1) | async-done | bytes 163872 | tf_op jit(solution)/shard_map/all_to_all | solution.py:1000
  118.4 0.7 copy-done.3
  119.1 3.8 %jacobian.1 = bf16[16,56,512]{2,1,0:T(8,128)(2,1)} custom-call(f32[8,40,128]{2,1,0:T(8,128)} %copy-done.3, bf16[128,8192]{1,0:T(8,128)(2,1)} %get-tuple-element.22.tokens_hbm, bf16[128,8192]{1,0:T(8,128)(2,1)} %get-tuple-element.23.resid_hbm, bf16[48,8192]{1,0:T(8,128)(2,1)} %fusion.2.heads_hbm, f32[88,128]{1,0:T(8,128)} %get-tuple-element.24.scalars_hbm, ...), custom_call_target="tpu_custom_call" | custom-call | tf_op jit(solution)/shard_map/jacobian/pallas_call | solution.py:910
  122.9 9.6 %all-to-all-start.2 = ((bf16[16,56,512]{2,1,0:T(8,128)(2,1)}), bf16[16,56,512]{2,1,0:T(8,128)(2,1)S(1)}, u32[]{:S(2)}, u32[]{:S(2)}) async-start(bf16[16,56,512]{2,1,0:T(8,128)(2,1)} %jacobian.1), calls=%async_computation.2 | async-start | bytes 1835008 | tf_op jit(solution)/shard_map/all_to_all | solution.py:1002
  132.6 0.6 gather_fusion
  133.6 0.7 slice.39.rewards_ref
  134.3 12.7 %all-to-all-done.2 = bf16[16,56,512]{2,1,0:T(8,128)(2,1)S(1)} async-done(((bf16[16,56,512]{2,1,0:T(8,128)(2,1)}), bf16[16,56,512]{2,1,0:T(8,128)(2,1)S(1)}, u32[]{:S(2)}, u32[]{:S(2)}) %all-to-all-start.2) | async-done | bytes 917536 | tf_op jit(solution)/shard_map/all_to_all | solution.py:1002
  146.9 0.3 copy.27
  147.2 0.5 copy.28
  147.7 0.6 copy.30
  148.3 2.3 %gram.1 = f32[16,128]{1,0:T(8,128)S(1)} custom-call(bf16[80,5632]{1,0:T(8,128)(2,1)S(1)} %bitcast.23, f32[48,128]{1,0:T(8,128)S(1)} %pad.14.pairs_ref, f32[8,128]{1,0:T(8,128)S(1)} %slice.39.rewards_ref, f32[3,16,8192]{2,1,0:T(8,128)} %bitcast.25, f32[16,4096]{1,0:T(8,128)} %bq_ref.1, f32[2,16,1024]{2,1,0:T(8,128)} %bkv_ref.1, f32[16,4096]{1,0:T(8,128)} %bitcast.34, ...), custom_call_target="tpu_custom_call" | custom-call | tf_op jit(solution)/shard_map/gram/pallas_call | solution.py:1029
  150.7 9.3 %all_to_all.30 = f32[16,16,128]{2,1,0:T(8,128)S(1)} all-to-all(f32[16,16,128]{2,1,0:T(8,128)S(1)} %broadcast_in_dim.24), channel_id=1, replica_groups=mesh['dp'=16,'tensor'=8] {'dp'}, dimensions={0} | all-to-all | bytes 262144 | tf_op jit(solution)/shard_map/all_to_all | solution.py:45
  160.0 9.6 %all_to_all.31.packed_ref = f32[8,16,128]{2,1,0:T(8,128)S(1)} all-to-all(f32[8,16,128]{2,1,0:T(8,128)S(1)} %broadcast_in_dim.25), channel_id=1, replica_groups=mesh['dp'=16,'tensor'=8] {'tensor'}, dimensions={0} | all-to-all | bytes 131072 | tf_op jit(solution)/shard_map/all_to_all | solution.py:45
  169.6 0.9 lanczos.1
  170.5 17.4 %all_to_all.32.own_ref = bf16[64,8,768]{2,1,0:T(8,128)(2,1)S(1)} all-to-all(bf16[64,8,768]{2,1,0:T(8,128)(2,1)S(1)} %broadcast_in_dim.26), channel_id=1, replica_groups={{0,1,2,3,4,5,6,7,16,17,18,19,20,21,22,23,32,33,34,35,36,37,38,39,48,49,..., dimensions={0} | all-to-all | bytes 1572864 | tf_op jit(solution)/shard_map/all_to_all | solution.py:1062
  187.9 3.4 %collective-permute-start.18 = (bf16[64,8,768]{2,1,0:T(8,128)(2,1)S(1)}, bf16[64,8,768]{2,1,0:T(8,128)(2,1)S(1)}, u32[]{:S(2)}, u32[]{:S(2)}) collective-permute-start(bf16[64,8,768]{2,1,0:T(8,128)(2,1)S(1)} %all_to_all.32.own_ref), channel_id=1, source_target_pairs={{0,8},{8,0},{16,24},{24,16},{32,40},{40,32},{48,56},{56,48},{64,72... | collective-permute-start | bytes 2359304 | tf_op jit(solution)/shard_map/ppermute | solution.py:1069
  191.3 1.9 collective-permute-done.18.other_ref
  193.2 4.4 %assemble.1 = (f32[3,16,8192]{2,1,0:T(8,128)}, f32[16,4096]{1,0:T(8,128)}, f32[2,16,1024]{2,1,0:T(8,128)}, f32[16,4096]{1,0:T(8,128)}, f32[16,8192]{1,0:T(8,128)}) custom-call(f32[1,128]{1,0:T(1,128)S(1)} %get-tuple-element.26.part_ref, bf16[64,8,768]{2,1,0:T(8,128)(2,1)S(1)} %all_to_all.32.own_ref, ...), custom_call_target="tpu_custom_call" | custom-call | tf_op jit(solution)/shard_map/assemble/pallas_call | solution.py:931
  (88 shorter events, 1.9 us)
Async XLA Ops:
  0.6 9.8 %collective-permute-start = (bf16[16,8192]{1,0:T(8,128)(2,1)}, bf16[16,8192]{1,0:T(8,128)(2,1)S(1)}, u32[]{:S(2)}, u32[]{:S(2)}) collective-permute-start(bf16[16,8192]{1,0:T(8,128)(2,1)} %bitcast.30), channel_id=1, source_target_pairs={{0,4},{1,5},{2,6},{3,7},{4,0},{5,1},{6,2},{7,3},{8,12},{9,13},{10,... | collective-permute-start | bytes 786440 | tf_op jit(solution)/shard_map/ppermute | solution.py:362
  4.5 9.7 %collective-permute-start.1 = (bf16[16,8192]{1,0:T(8,128)(2,1)}, bf16[16,8192]{1,0:T(8,128)(2,1)S(1)}, u32[]{:S(2)}, u32[]{:S(2)}) collective-permute-start(bf16[16,8192]{1,0:T(8,128)(2,1)} %bitcast.31), channel_id=1, source_target_pairs={{0,1},{1,2},{2,3},{3,0},{4,5},{5,6},{6,7},{7,4},{8,9},{9,10},{10,1... | collective-permute-start | bytes 786440 | tf_op jit(solution)/shard_map/ppermute | solution.py:362
  6.1 8.2 %collective-permute-start.2 = (bf16[16,8192]{1,0:T(8,128)(2,1)}, bf16[16,8192]{1,0:T(8,128)(2,1)S(1)}, u32[]{:S(2)}, u32[]{:S(2)}) collective-permute-start(bf16[16,8192]{1,0:T(8,128)(2,1)} %bitcast.32), channel_id=1, source_target_pairs={{0,3},{1,0},{2,1},{3,2},{4,7},{5,4},{6,5},{7,6},{8,11},{9,8},{10,9... | collective-permute-start | bytes 786440 | tf_op jit(solution)/shard_map/ppermute | solution.py:362
  10.4 14.6 %copy-start.13 = (bf16[16,8192]{1,0:T(8,128)(2,1)}, bf16[16,8192]{1,0:T(8,128)(2,1)S(1)}, u32[]{:S(2)}) copy-start(bf16[16,8192]{1,0:T(8,128)(2,1)S(1)} %collective-permute-done.shard_1) | copy-start | bytes 786436
  10.4 8.8 %collective-permute-start.3 = (bf16[16,8192]{1,0:T(8,128)(2,1)S(1)}, bf16[16,8192]{1,0:T(8,128)(2,1)S(1)}, u32[]{:S(2)}, u32[]{:S(2)}) collective-permute-start(bf16[16,8192]{1,0:T(8,128)(2,1)S(1)} %collective-permute-done.shard_1), channel_id=1, source_target_pairs={{0,1},{1,2},{2,3},{3,0},{4,5},{5,6},{6,7},{7,4},{8,9},{9,10},{10,1... | collective-permute-start | bytes 786440 | tf_op jit(solution)/shard_map/ppermute | solution.py:362
  12.1 7.3 %collective-permute-start.4 = (bf16[16,8192]{1,0:T(8,128)(2,1)S(1)}, bf16[16,8192]{1,0:T(8,128)(2,1)S(1)}, u32[]{:S(2)}, u32[]{:S(2)}) collective-permute-start(bf16[16,8192]{1,0:T(8,128)(2,1)S(1)} %collective-permute-done.shard_1), channel_id=1, source_target_pairs={{0,3},{1,0},{2,1},{3,2},{4,7},{5,4},{6,5},{7,6},{8,11},{9,8},{10,9... | collective-permute-start | bytes 786440 | tf_op jit(solution)/shard_map/ppermute | solution.py:362
  14.2 10.8 %copy-start.4 = (bf16[16,8192]{1,0:T(8,128)(2,1)}, bf16[16,8192]{1,0:T(8,128)(2,1)S(1)}, u32[]{:S(2)}) copy-start(bf16[16,8192]{1,0:T(8,128)(2,1)S(1)} %collective-permute-done.1.shard_2) | copy-start | bytes 786436
  14.2 7.9 %collective-permute-start.5 = (bf16[16,4096]{1,0:T(8,128)(2,1)S(1)}, bf16[16,4096]{1,0:T(8,128)(2,1)S(1)}, u32[]{:S(2)}, u32[]{:S(2)}) collective-permute-start(bf16[16,4096]{1,0:T(8,128)(2,1)S(1)} %slice.42), channel_id=1, source_target_pairs={{0,1},{1,2},{2,3},{3,0},{4,5},{5,6},{6,7},{7,4},{8,9},{9,10},{10,1... | collective-permute-start | bytes 393224 | tf_op jit(solution)/shard_map/ppermute | solution.py:362
  14.3 10.7 %copy-start.5 = (bf16[16,8192]{1,0:T(8,128)(2,1)}, bf16[16,8192]{1,0:T(8,128)(2,1)S(1)}, u32[]{:S(2)}) copy-start(bf16[16,8192]{1,0:T(8,128)(2,1)S(1)} %collective-permute-done.2.shard_3) | copy-start | bytes 786436
  14.3 7.8 %collective-permute-start.6 = (bf16[16,4096]{1,0:T(8,128)(2,1)S(1)}, bf16[16,4096]{1,0:T(8,128)(2,1)S(1)}, u32[]{:S(2)}, u32[]{:S(2)}) collective-permute-start(bf16[16,4096]{1,0:T(8,128)(2,1)S(1)} %slice.43), channel_id=1, source_target_pairs={{0,3},{1,0},{2,1},{3,2},{4,7},{5,4},{6,5},{7,6},{8,11},{9,8},{10,9... | collective-permute-start | bytes 393224 | tf_op jit(solution)/shard_map/ppermute | solution.py:362
  19.3 5.7 %copy-start.6 = (bf16[16,8192]{1,0:T(8,128)(2,1)}, bf16[16,8192]{1,0:T(8,128)(2,1)S(1)}, u32[]{:S(2)}) copy-start(bf16[16,8192]{1,0:T(8,128)(2,1)S(1)} %collective-permute-done.3.shard_4) | copy-start | bytes 786436
  19.3 5.7 %collective-permute-start.7 = (bf16[16,4096]{1,0:T(8,128)(2,1)S(1)}, bf16[16,4096]{1,0:T(8,128)(2,1)S(1)}, u32[]{:S(2)}, u32[]{:S(2)}) collective-permute-start(bf16[16,4096]{1,0:T(8,128)(2,1)S(1)} %slice.44), channel_id=1, source_target_pairs={{0,1},{1,2},{2,3},{3,0},{4,5},{5,6},{6,7},{7,4},{8,9},{9,10},{10,1... | collective-permute-start | bytes 393224 | tf_op jit(solution)/shard_map/ppermute | solution.py:362
  19.4 5.6 %copy-start.7 = (bf16[16,8192]{1,0:T(8,128)(2,1)}, bf16[16,8192]{1,0:T(8,128)(2,1)S(1)}, u32[]{:S(2)}) copy-start(bf16[16,8192]{1,0:T(8,128)(2,1)S(1)} %collective-permute-done.4.shard_5) | copy-start | bytes 786436
  19.4 5.6 %collective-permute-start.8 = (bf16[16,4096]{1,0:T(8,128)(2,1)S(1)}, bf16[16,4096]{1,0:T(8,128)(2,1)S(1)}, u32[]{:S(2)}, u32[]{:S(2)}) collective-permute-start(bf16[16,4096]{1,0:T(8,128)(2,1)S(1)} %slice.45), channel_id=1, source_target_pairs={{0,3},{1,0},{2,1},{3,2},{4,7},{5,4},{6,5},{7,6},{8,11},{9,8},{10,9... | collective-permute-start | bytes 393224 | tf_op jit(solution)/shard_map/ppermute | solution.py:362
  22.1 2.9 %copy-start.17 = (bf16[16,4096]{1,0:T(8,128)(2,1)}, bf16[16,4096]{1,0:T(8,128)(2,1)S(1)}, u32[]{:S(2)}) copy-start(bf16[16,4096]{1,0:T(8,128)(2,1)S(1)} %collective-permute-done.5.shard_6) | copy-start | bytes 393220
  22.1 2.9 %copy-start.19 = (bf16[16,4096]{1,0:T(8,128)(2,1)}, bf16[16,4096]{1,0:T(8,128)(2,1)S(1)}, u32[]{:S(2)}) copy-start(bf16[16,4096]{1,0:T(8,128)(2,1)S(1)} %collective-permute-done.6.shard_7) | copy-start | bytes 393220
  25.0 0.7 copy-start.21
  25.0 0.7 copy-start.22
  37.0 28.1 %all-to-all-start = ((bf16[8,16,8192]{2,1,0:T(8,128)(2,1)}), bf16[8,16,8192]{2,1,0:T(8,128)(2,1)S(1)}, u32[]{:S(2)}, u32[]{:S(2)}) async-start(bf16[8,16,8192]{2,1,0:T(8,128)(2,1)} %get-tuple-element.19), calls=%async_computation | async-start | bytes 4194304 | tf_op jit(solution)/shard_map/all_to_all | solution.py:990
  43.6 21.9 %copy-start.1 = (bf16[1,16,8192]{2,1,0:T(8,128)(2,1)S(1)}, bf16[1,16,8192]{2,1,0:T(8,128)(2,1)}, u32[]{:S(2)}) copy-start(bf16[1,16,8192]{2,1,0:T(8,128)(2,1)} %param.17) | copy-start | bytes 786436
  43.6 29.2 %copy-start = (bf16[16,8192]{1,0:T(8,128)(2,1)S(1)}, bf16[16,8192]{1,0:T(8,128)(2,1)}, u32[]{:S(2)}) copy-start(bf16[16,8192]{1,0:T(8,128)(2,1)} %up_output_hbm.1) | copy-start | bytes 786436
  43.6 29.2 %copy-start.12 = (bf16[8192,5]{0,1:T(8,128)(2,1)S(1)}, bf16[8192,5]{0,1:T(8,128)(2,1)}, u32[]{:S(2)}) copy-start(bf16[8192,5]{0,1:T(8,128)(2,1)} %param.21) | copy-start | bytes 245764
  65.5 27.4 %copy-start.2 = (bf16[16,8192]{1,0:T(8,128)(2,1)}, bf16[16,8192]{1,0:T(8,128)(2,1)S(1)}, u32[]{:S(2)}) copy-start(bf16[16,8192]{1,0:T(8,128)(2,1)S(1)} %add_convert_fusion.shard_0) | copy-start | bytes 786436
  65.6 24.7 %copy-start.23 = (s32[16]{0:T(128)S(1)}, s32[16]{0:T(128)}, u32[]{:S(2)}) copy-start(s32[16]{0:T(128)} %param.23) | copy-start | bytes 196
  65.6 12.0 %collective-permute-start.9 = (bf16[16,8192]{1,0:T(8,128)(2,1)S(1)}, bf16[16,8192]{1,0:T(8,128)(2,1)S(1)}, u32[]{:S(2)}, u32[]{:S(2)}) collective-permute-start(bf16[16,8192]{1,0:T(8,128)(2,1)S(1)} %add_convert_fusion.shard_0), channel_id=1, source_target_pairs={{0,4},{1,5},{2,6},{3,7},{4,0},{5,1},{6,2},{7,3},{8,12},{9,13},{10,... | collective-permute-start | bytes 786440 | tf_op jit(solution)/shard_map/ppermute | solution.py:362
  73.8 8.1 %collective-permute-start.10 = (bf16[16,8192]{1,0:T(8,128)(2,1)S(1)}, bf16[16,8192]{1,0:T(8,128)(2,1)S(1)}, u32[]{:S(2)}, u32[]{:S(2)}) collective-permute-start(bf16[16,8192]{1,0:T(8,128)(2,1)S(1)} %add_convert_fusion.shard_0), channel_id=1, source_target_pairs={{0,1},{1,2},{2,3},{3,0},{4,5},{5,6},{6,7},{7,4},{8,9},{9,10},{10,1... | collective-permute-start | bytes 786440 | tf_op jit(solution)/shard_map/ppermute | solution.py:362
  74.8 7.3 %collective-permute-start.11 = (bf16[16,8192]{1,0:T(8,128)(2,1)S(1)}, bf16[16,8192]{1,0:T(8,128)(2,1)S(1)}, u32[]{:S(2)}, u32[]{:S(2)}) collective-permute-start(bf16[16,8192]{1,0:T(8,128)(2,1)S(1)} %add_convert_fusion.shard_0), channel_id=1, source_target_pairs={{0,3},{1,0},{2,1},{3,2},{4,7},{5,4},{6,5},{7,6},{8,11},{9,8},{10,9... | collective-permute-start | bytes 786440 | tf_op jit(solution)/shard_map/ppermute | solution.py:362
  77.5 15.4 %copy-start.14 = (bf16[16,8192]{1,0:T(8,128)(2,1)}, bf16[16,8192]{1,0:T(8,128)(2,1)S(1)}, u32[]{:S(2)}) copy-start(bf16[16,8192]{1,0:T(8,128)(2,1)S(1)} %collective-permute-done.9.shard_1) | copy-start | bytes 786436
  77.5 9.7 %collective-permute-start.12 = (bf16[16,8192]{1,0:T(8,128)(2,1)S(1)}, bf16[16,8192]{1,0:T(8,128)(2,1)S(1)}, u32[]{:S(2)}, u32[]{:S(2)}) collective-permute-start(bf16[16,8192]{1,0:T(8,128)(2,1)S(1)} %collective-permute-done.9.shard_1), channel_id=1, source_target_pairs={{0,1},{1,2},{2,3},{3,0},{4,5},{5,6},{6,7},{7,4},{8,9},{9,10},{10,1... | collective-permute-start | bytes 786440 | tf_op jit(solution)/shard_map/ppermute | solution.py:362
  78.9 8.6 %collective-permute-start.13 = (bf16[16,8192]{1,0:T(8,128)(2,1)S(1)}, bf16[16,8192]{1,0:T(8,128)(2,1)S(1)}, u32[]{:S(2)}, u32[]{:S(2)}) collective-permute-start(bf16[16,8192]{1,0:T(8,128)(2,1)S(1)} %collective-permute-done.9.shard_1), channel_id=1, source_target_pairs={{0,3},{1,0},{2,1},{3,2},{4,7},{5,4},{6,5},{7,6},{8,11},{9,8},{10,9... | collective-permute-start | bytes 786440 | tf_op jit(solution)/shard_map/ppermute | solution.py:362
  81.9 11.0 %copy-start.8 = (bf16[16,8192]{1,0:T(8,128)(2,1)}, bf16[16,8192]{1,0:T(8,128)(2,1)S(1)}, u32[]{:S(2)}) copy-start(bf16[16,8192]{1,0:T(8,128)(2,1)S(1)} %collective-permute-done.10.shard_2) | copy-start | bytes 786436
  81.9 8.4 %collective-permute-start.14 = (bf16[16,4096]{1,0:T(8,128)(2,1)S(1)}, bf16[16,4096]{1,0:T(8,128)(2,1)S(1)}, u32[]{:S(2)}, u32[]{:S(2)}) collective-permute-start(bf16[16,4096]{1,0:T(8,128)(2,1)S(1)} %slice.46), channel_id=1, source_target_pairs={{0,1},{1,2},{2,3},{3,0},{4,5},{5,6},{6,7},{7,4},{8,9},{9,10},{10,1... | collective-permute-start | bytes 393224 | tf_op jit(solution)/shard_map/ppermute | solution.py:362
  82.1 10.8 %copy-start.9 = (bf16[16,8192]{1,0:T(8,128)(2,1)}, bf16[16,8192]{1,0:T(8,128)(2,1)S(1)}, u32[]{:S(2)}) copy-start(bf16[16,8192]{1,0:T(8,128)(2,1)S(1)} %collective-permute-done.11.shard_3) | copy-start | bytes 786436
  82.2 8.2 %collective-permute-start.15 = (bf16[16,4096]{1,0:T(8,128)(2,1)S(1)}, bf16[16,4096]{1,0:T(8,128)(2,1)S(1)}, u32[]{:S(2)}, u32[]{:S(2)}) collective-permute-start(bf16[16,4096]{1,0:T(8,128)(2,1)S(1)} %slice.47), channel_id=1, source_target_pairs={{0,3},{1,0},{2,1},{3,2},{4,7},{5,4},{6,5},{7,6},{8,11},{9,8},{10,9... | collective-permute-start | bytes 393224 | tf_op jit(solution)/shard_map/ppermute | solution.py:362
  87.3 5.7 %copy-start.10 = (bf16[16,8192]{1,0:T(8,128)(2,1)}, bf16[16,8192]{1,0:T(8,128)(2,1)S(1)}, u32[]{:S(2)}) copy-start(bf16[16,8192]{1,0:T(8,128)(2,1)S(1)} %collective-permute-done.12.shard_4) | copy-start | bytes 786436
  87.3 5.7 %collective-permute-start.16 = (bf16[16,4096]{1,0:T(8,128)(2,1)S(1)}, bf16[16,4096]{1,0:T(8,128)(2,1)S(1)}, u32[]{:S(2)}, u32[]{:S(2)}) collective-permute-start(bf16[16,4096]{1,0:T(8,128)(2,1)S(1)} %slice.48), channel_id=1, source_target_pairs={{0,1},{1,2},{2,3},{3,0},{4,5},{5,6},{6,7},{7,4},{8,9},{9,10},{10,1... | collective-permute-start | bytes 393224 | tf_op jit(solution)/shard_map/ppermute | solution.py:362
  87.5 5.4 %copy-start.11 = (bf16[16,8192]{1,0:T(8,128)(2,1)}, bf16[16,8192]{1,0:T(8,128)(2,1)S(1)}, u32[]{:S(2)}) copy-start(bf16[16,8192]{1,0:T(8,128)(2,1)S(1)} %collective-permute-done.13.shard_5) | copy-start | bytes 786436
  87.5 5.4 %collective-permute-start.17 = (bf16[16,4096]{1,0:T(8,128)(2,1)S(1)}, bf16[16,4096]{1,0:T(8,128)(2,1)S(1)}, u32[]{:S(2)}, u32[]{:S(2)}) collective-permute-start(bf16[16,4096]{1,0:T(8,128)(2,1)S(1)} %slice.49), channel_id=1, source_target_pairs={{0,3},{1,0},{2,1},{3,2},{4,7},{5,4},{6,5},{7,6},{8,11},{9,8},{10,9... | collective-permute-start | bytes 393224 | tf_op jit(solution)/shard_map/ppermute | solution.py:362
  90.3 2.7 %copy-start.15 = (bf16[16,4096]{1,0:T(8,128)(2,1)}, bf16[16,4096]{1,0:T(8,128)(2,1)S(1)}, u32[]{:S(2)}) copy-start(bf16[16,4096]{1,0:T(8,128)(2,1)S(1)} %collective-permute-done.14.shard_6) | copy-start | bytes 393220
  90.3 2.7 %copy-start.16 = (bf16[16,4096]{1,0:T(8,128)(2,1)}, bf16[16,4096]{1,0:T(8,128)(2,1)S(1)}, u32[]{:S(2)}) copy-start(bf16[16,4096]{1,0:T(8,128)(2,1)S(1)} %collective-permute-done.15.shard_7) | copy-start | bytes 393220
  92.9 0.6 copy-start.18
  92.9 0.7 copy-start.20
  105.3 13.2 %all-to-all-start.1 = ((f32[8,40,128]{2,1,0:T(8,128)}), f32[8,40,128]{2,1,0:T(8,128)S(1)}, u32[]{:S(2)}, u32[]{:S(2)}) async-start(f32[8,40,128]{2,1,0:T(8,128)} %bitcast.39), calls=%async_computation.1 | async-start | bytes 327680 | tf_op jit(solution)/shard_map/all_to_all | solution.py:1000
  118.4 0.7 copy-start.3
  122.9 24.0 %all-to-all-start.2 = ((bf16[16,56,512]{2,1,0:T(8,128)(2,1)}), bf16[16,56,512]{2,1,0:T(8,128)(2,1)S(1)}, u32[]{:S(2)}, u32[]{:S(2)}) async-start(bf16[16,56,512]{2,1,0:T(8,128)(2,1)} %jacobian.1), calls=%async_computation.2 | async-start | bytes 1835008 | tf_op jit(solution)/shard_map/all_to_all | solution.py:1002
  187.9 5.3 %collective-permute-start.18 = (bf16[64,8,768]{2,1,0:T(8,128)(2,1)S(1)}, bf16[64,8,768]{2,1,0:T(8,128)(2,1)S(1)}, u32[]{:S(2)}, u32[]{:S(2)}) collective-permute-start(bf16[64,8,768]{2,1,0:T(8,128)(2,1)S(1)} %all_to_all.32.own_ref), channel_id=1, source_target_pairs={{0,8},{8,0},{16,24},{24,16},{32,40},{40,32},{48,56},{56,48},{64,72... | collective-permute-start | bytes 2359304 | tf_op jit(solution)/shard_map/ppermute | solution.py:1069

commit v7 on v6

--- a/solution.py
+++ b/solution.py
@@ -289,11 +289,6 @@
     return jnp.concatenate(parts, 1)
 
 
-def corners(both, rows, lanes):
-    upper = both[:rows] + both[rows:]
-    return upper[:, :lanes] + upper[:, lanes:]
-
-
 def stack(rows):
     return tall([rows[:, at : at + 128] for at in range(0, rows.shape[1], 128)])
 
@@ -722,75 +717,134 @@
         through = through_ref[...] + ADAPTER_SCALE * dot_halved(
             flat(rounded_parts(slow[:144, :16], 2)), tall([down, down]), 1, 0
         )
+        query = state_ref[0:512]
         context_rows = state_ref[512:1024]
-        context = unstack(context_rows)
         probs = state_ref[1024:1536]
         capped = state_ref[1536:2048]
-        slope = probs * (1.0 - capped * capped) * root
-        probs_turned = tall(rounded_parts(probs.T, 2))
-        query_turned = tall(rounded_parts(state_ref[0:512].T, 2))
         keys = state_ref[2048:2176]
         values = state_ref[2176:2304]
-        low = [
-            tall(rounded_parts(state_ref[2304 + 16 * at : 2320 + 16 * at], 2)) for at in range(3)
+        low_q = state_ref[2304:2320]
+        low_k = state_ref[2320:2336]
+        low_v = state_ref[2336:2352]
+        context_low = state_ref[2352:2368]
+        small = small_ref[:, 512:].astype(jnp.float32)
+        up_query, up_keys, up_values = small[:, :512], small[:, 512:640], small[:, 640:]
+        objectives = range(OBJ)
+        head_spots = range(4)
+        across = stack(through[:128])
+        heads = stack(through[128:136])
+        on_values = product(tall([across, heads]), values, 1)
+        heads_on_values = on_values[512:]
+        slope = probs * (1.0 - capped * capped) * root
+        shared = slope * (on_values[:512] - lane_sum(across * context_rows))
+        leading = slope * tall([lead] * 4)
+        heads_on_context = product(heads, context_rows, 1)
+        query_on_keys = product(stack(up_query), keys, 1)
+        keys_on_query = product(up_keys, query, 1)
+        padded = tall([across, heads, jnp.zeros((96, 128), jnp.float32)])
+        values_on_cot = product(up_values, padded, 1)
+        low_on_probs = product(low_v, probs, 1)
+
+        def block(array, head):
+            return array[:, 128 * head : 128 * head + 128]
+
+        def row_of(array, row):
+            return array[row : row + 1]
+
+        left_values = []
+        right_values = []
+        for obj in objectives:
+            pull = row_of(pulled_turned, obj)
+            parts = []
+            for head in head_spots:
+                spot = 512 + 8 * head + obj
+                parts.append(
+                    values_on_cot[:, spot : spot + 1] * lead_turned
+                    - pull * block(values_on_cot, head)
+                )
+            left_values.append(flat(parts))
+            right_values.append(low_on_probs * flat([pull] * 4))
+        factor_values = product(tall(left_values), probs, 0)
+        jac_values = -product(tall(right_values), across, 0)
+        low_lead = [lane_sum(block(low_on_probs, head) * lead_turned) for head in head_spots]
+        factor_query = [0.0] * OBJ
+        factor_keys = [0.0] * OBJ
+        query_rows = [[] for _ in objectives]
+        keys_rows = [[] for _ in objectives]
+        for head in head_spots:
+            rows = slice(128 * head, 128 * head + 128)
+            score_lead, score_shared = leading[rows], shared[rows]
+            on_context = block(heads_on_context, head)[8 * head : 8 * head + 8]
+            on_value = heads_on_values[8 * head : 8 * head + 8]
+            base = tall([low_q, block(keys_on_query, head)])
+            first = product(
+                tall([base] + [base * row_of(on_context, obj) for obj in objectives]),
+                score_lead,
+                0,
+            )
+            second = product(
+                tall([base * row_of(pulled_turned, obj) for obj in objectives]), score_shared, 0
+            )
+            base = tall([query_on_keys[16 * head : 16 * head + 16], low_k])
+            third = product(
+                tall([base] + [base * row_of(on_value, obj) for obj in objectives]),
+                score_lead,
+                1,
+            )
+            fourth = product(base, score_shared, 1)
+            for obj in objectives:
+                spot = slice(32 + 32 * obj, 64 + 32 * obj)
+                by_rows = (
+                    first[:32] * row_of(on_value, obj)
+                    - first[spot]
+                    - second[32 * obj : 32 * obj + 32]
+                )
+                by_lanes = (
+                    third[spot]
+                    - row_of(on_context, obj) * third[:32]
+                    - row_of(pulled_turned, obj) * fourth
+                )
+                query_rows[obj].append(by_rows[:16])
+                factor_keys[obj] += by_rows[16:]
+                factor_query[obj] += by_lanes[:16]
+                keys_rows[obj].append(by_lanes[16:])
+        jac_query = product(tall([tall(rows) for rows in query_rows]), keys, 0)
+        jac_keys = product(tall([flat(rows) for rows in keys_rows]), query, 0)
+        cot_low = [
+            slow_turned[:16, 128 + obj : 129 + obj] * lead_turned
+            - row_of(pulled_turned, obj) * low_turned
+            for obj in objectives
         ]
-        up_query = small_ref[:, 512:1024]
-        up_keys = small_ref[:, 1024:1152]
-        up_values = small_ref[:, 1152:]
-        context_low = state_ref[2352:2368]
-        through_ref[...] = through
-        through_tokens = through[:128]
-        heads_low = slow_turned[:16, 128:]
-        lane_pulled = lax.broadcasted_iota(jnp.int32, pulled.shape, 1)
-        lane_low = lax.broadcasted_iota(jnp.int32, heads_low.shape, 1)
-        row_pulled = lax.broadcasted_iota(jnp.int32, pulled_turned.shape, 0)
-
-        def objective(obj, _):
-            pulled_own = lane_sum(jnp.where(lane_pulled == obj, pulled, 0.0))
-            lead_row = through_ref[pl.ds(128 + obj, 1), :]
-            cot = stack(lead * lead_row - pulled_own * through_tokens)
-            cot_prob = product(cot, values, 1)
-            cot_score = slope * (cot_prob - lane_sum(cot * context_rows))
-            cot_query = unstack(product(cot_score, keys, 0))
-            cot_keys = corners(
-                dot_halved(query_turned, flat(rounded_parts(cot_score, 2)), 1, 0), 128, 128
-            )
-            cot_values = corners(
-                dot_halved(probs_turned, flat(rounded_parts(cot, 2)), 1, 0), 128, 128
-            )
-            query_parts = rounded_parts(cot_query, 2)
-            keys_parts = rounded_parts(cot_keys, 2)
-            values_parts = rounded_parts(cot_values, 2)
-            factor_query = dot_halved(up_query, tall(query_parts), 1, 1)
-            factor_keys = dot_halved(up_keys, flat(keys_parts), 1, 0)
-            factor_values = dot_halved(up_values, tall(values_parts), 1, 1)
+        jac_down = product(tall(cot_low), unstack(context_rows), 0)
+        for obj in objectives:
+            own = slice(16 * obj, 16 * obj + 16)
             rows = [
-                ADAPTER_SCALE * (factor[:, :128] + factor[:, 128:])
-                for factor in (factor_query, factor_keys, factor_values)
-            ] + [context_low]
+                ADAPTER_SCALE * factor_query[obj],
+                ADAPTER_SCALE * factor_keys[obj],
+                ADAPTER_SCALE * factor_values[own],
+                context_low,
+            ]
             for piece in range(4):
                 for half in range(2):
                     factors_ref[pl.ds(20 * half + 5 * piece + obj, 8, stride=40), :] = rows[
                         piece
                     ][8 * half : 8 * half + 8]
-            jac_query = corners(dot_halved(low[0], flat(query_parts), 1, 0), 16, 512)
-            jac_keys = corners(dot_halved(low[1], tall(keys_parts), 1, 1), 16, 128)
-            jac_values = corners(dot_halved(low[2], flat(values_parts), 1, 0), 16, 128)
-            pulled_row = row_sum(jnp.where(row_pulled == obj, pulled_turned, 0.0))
-            head_low = lane_sum(jnp.where(lane_low == obj, heads_low, 0.0))
-            jac_down = product(head_low * lead_turned - pulled_row * low_turned, context, 0)
-            blocks = [jac_query[:, at : at + 128] for at in range(0, 512, 128)]
-            blocks += [jac_down[:, at : at + 128] for at in range(0, 512, 128)]
+            own_values = jac_values[own]
+            for head in head_spots:
+                own_values += low_lead[head] * row_of(heads, 8 * head + obj)
+            blocks = [
+                jac_query[64 * obj + 16 * head : 64 * obj + 16 * head + 16]
+                for head in head_spots
+            ]
+            blocks += [block(jac_down, head)[own] for head in head_spots]
+            blocks += [jac_keys[own], own_values]
             spots = [(0, 0), (0, 1), (0, 2), (0, 3), (5, 0), (5, 1), (5, 2), (5, 3)]
             spots += [(10, 0), (10, 1)]
-            for (row, tile), block in zip(spots, blocks + [jac_keys, jac_values]):
+            for (row, tile), part in zip(spots, blocks):
                 for half in range(2):
                     narrow_ref[tile, pl.ds(128 * half + row + obj, 8, stride=16), :] = (
-                        ADAPTER_SCALE * block[8 * half : 8 * half + 8]
+                        ADAPTER_SCALE * part[8 * half : 8 * half + 8]
                     )
-            return 0
-
-        lax.fori_loop(0, OBJ, objective, 0, unroll=True)
         blank = jnp.zeros((15, 128), jnp.float32)
         scalars_ref[8:48] = jnp.concatenate([blank, pulled_turned[:5]] * 2, 0)
         scalars_ref[48:] = jnp.broadcast_to(lead_turned, (40, 128))

time: 198 us -> 196 us (0.990)
  no operation moved by 1% of the time
where the time goes in v7:
time: 196 us
  starting transfers between devices  60.9 us (31%)
  waiting for transfers between devices  56.4 us (29%)
  blocking collectives  36.2 us (18%)
  Pallas kernels  32.6 us (17%)
  local copies, waits for them, and re-layouts  5.19 us (3%)
  other arithmetic  2.7 us (1%)
    ppermute x18, starting transfers between devices, permute(): return lax.ppermute(array, 'tensor', pairs)  35.4 us
    all_to_all x1, waiting for transfers between devices, local(): out_pieces = lax.all_to_all(out_terms, 'tensor', 0, 0)  21.5 us
    all_to_all x2, blocking collectives, gather_by_exchange(): return lax.all_to_all(copies, axis, 0, 0)  18.8 us
    all_to_all x1, blocking collectives, local(): lax.all_to_all(jnp.broadcast_to(own_result[None], (half,) + own_result.sh...  17.4 us
    ppermute x18, waiting for transfers between devices, permute(): return lax.ppermute(array, 'tensor', pairs)  13.4 us
    all_to_all x1, waiting for transfers between devices, local(): spread = lax.all_to_all(payload, 'dp', 0, 0)  12.7 us
    pallas_call x1, Pallas kernels, forward(): pl.pallas_call(forward_body, in_specs=[ANYWHERE] * (len(shards) + len(arr...  11.4 us
    pallas_call x1, Pallas kernels, cotangents(): pl.pallas_call(cotangents_body, in_specs=[pl.BlockSpec(memory_space=pltpu...  9.82 us
  transfers between devices with their start and end apart: 22, of which 10 were waited for; matrix products, arithmetic and copies ran while one was open for 2% of the time, Pallas kernels for 0%

profile of v7, /device:TPU:1, one launch (start us, length us, event | category | flops | bytes accessed | tf_op | source)
XLA Modules:
  0.0 195.9 jit_solution(2767897296360417882)
XLA Ops:
  0.6 3.8 %collective-permute-start = (bf16[16,8192]{1,0:T(8,128)(2,1)}, bf16[16,8192]{1,0:T(8,128)(2,1)S(1)}, u32[]{:S(2)}, u32[]{:S(2)}) collective-permute-start(bf16[16,8192]{1,0:T(8,128)(2,1)} %bitcast.30), channel_id=1, source_target_pairs={{0,4},{1,5},{2,6},{3,7},{4,0},{5,1},{6,2},{7,3},{8,12},{9,13},{10,... | collective-permute-start | bytes 786440 | tf_op jit(solution)/shard_map/ppermute | solution.py:357
  4.5 1.6 collective-permute-start.1
  6.1 2.1 %collective-permute-start.2 = (bf16[16,8192]{1,0:T(8,128)(2,1)}, bf16[16,8192]{1,0:T(8,128)(2,1)S(1)}, u32[]{:S(2)}, u32[]{:S(2)}) collective-permute-start(bf16[16,8192]{1,0:T(8,128)(2,1)} %bitcast.32), channel_id=1, source_target_pairs={{0,3},{1,0},{2,1},{3,2},{4,7},{5,4},{6,5},{7,6},{8,11},{9,8},{10,9... | collective-permute-start | bytes 786440 | tf_op jit(solution)/shard_map/ppermute | solution.py:357
  8.2 2.2 %collective-permute-done.shard_1 = bf16[16,8192]{1,0:T(8,128)(2,1)S(1)} collective-permute-done((bf16[16,8192]{1,0:T(8,128)(2,1)}, bf16[16,8192]{1,0:T(8,128)(2,1)S(1)}, u32[]{:S(2)}, u32[]{:S(2)}) %collective-permute-start) | collective-permute-done | bytes 262176 | tf_op jit(solution)/shard_map/ppermute | solution.py:357
  10.4 1.6 collective-permute-start.3
  12.1 2.1 %collective-permute-start.4 = (bf16[16,8192]{1,0:T(8,128)(2,1)S(1)}, bf16[16,8192]{1,0:T(8,128)(2,1)S(1)}, u32[]{:S(2)}, u32[]{:S(2)}) collective-permute-start(bf16[16,8192]{1,0:T(8,128)(2,1)S(1)} %collective-permute-done.shard_1), channel_id=1, source_target_pairs={{0,3},{1,0},{2,1},{3,2},{4,7},{5,4},{6,5},{7,6},{8,11},{9,8},{10,9... | collective-permute-start | bytes 786440 | tf_op jit(solution)/shard_map/ppermute | solution.py:357
  14.3 2.7 %collective-permute-start.6 = (bf16[16,4096]{1,0:T(8,128)(2,1)S(1)}, bf16[16,4096]{1,0:T(8,128)(2,1)S(1)}, u32[]{:S(2)}, u32[]{:S(2)}) collective-permute-start(bf16[16,4096]{1,0:T(8,128)(2,1)S(1)} %slice.43), channel_id=1, source_target_pairs={{0,3},{1,0},{2,1},{3,2},{4,7},{5,4},{6,5},{7,6},{8,11},{9,8},{10,9... | collective-permute-start | bytes 393224 | tf_op jit(solution)/shard_map/ppermute | solution.py:357
  17.0 2.2 %collective-permute-done.3.shard_4 = bf16[16,8192]{1,0:T(8,128)(2,1)S(1)} collective-permute-done((bf16[16,8192]{1,0:T(8,128)(2,1)S(1)}, bf16[16,8192]{1,0:T(8,128)(2,1)S(1)}, u32[]{:S(2)}, u32[]{:S(2)}) %collective-permute-start.3) | collective-permute-done | bytes 262176 | tf_op jit(solution)/shard_map/ppermute | solution.py:357
  19.4 2.7 %collective-permute-start.8 = (bf16[16,4096]{1,0:T(8,128)(2,1)S(1)}, bf16[16,4096]{1,0:T(8,128)(2,1)S(1)}, u32[]{:S(2)}, u32[]{:S(2)}) collective-permute-start(bf16[16,4096]{1,0:T(8,128)(2,1)S(1)} %slice.45), channel_id=1, source_target_pairs={{0,3},{1,0},{2,1},{3,2},{4,7},{5,4},{6,5},{7,6},{8,11},{9,8},{10,9... | collective-permute-start | bytes 393224 | tf_op jit(solution)/shard_map/ppermute | solution.py:357
  22.1 2.8 %collective-permute-done.7.shard_8 = bf16[16,4096]{1,0:T(8,128)(2,1)S(1)} collective-permute-done((bf16[16,4096]{1,0:T(8,128)(2,1)S(1)}, bf16[16,4096]{1,0:T(8,128)(2,1)S(1)}, u32[]{:S(2)}, u32[]{:S(2)}) %collective-permute-start.7) | collective-permute-done | bytes 131104 | tf_op jit(solution)/shard_map/ppermute | solution.py:357
  25.0 0.6 copy-done.21
  25.7 11.4 %forward.1 = (bf16[128,8192]{1,0:T(8,128)(2,1)}, bf16[8,16,8192]{2,1,0:T(8,128)(2,1)}, f32[2368,128]{1,0:T(8,128)}) custom-call(bf16[16,8192]{1,0:T(8,128)(2,1)} %bitcast.33, bf16[16,8192]{1,0:T(8,128)(2,1)} %copy-done.13, bf16[16,8192]{1,0:T(8,128)(2,1)} %copy-done.4, bf16[16,8192]{1,0:T(8,128)(2,1)} %copy-done.5, bf16[16,8192]{1,0:T(8,128)(2,1)} %copy-done.6, ...), custom_call_target="tpu_custom_call" | custom-call | tf_op jit(solution)/shard_map/forward/pallas_call | solution.py:562
  37.0 6.5 %all-to-all-start = ((bf16[8,16,8192]{2,1,0:T(8,128)(2,1)}), bf16[8,16,8192]{2,1,0:T(8,128)(2,1)S(1)}, u32[]{:S(2)}, u32[]{:S(2)}) async-start(bf16[8,16,8192]{2,1,0:T(8,128)(2,1)} %get-tuple-element.19), calls=%async_computation | async-start | bytes 4194304 | tf_op jit(solution)/shard_map/all_to_all | solution.py:1044
  43.7 21.5 %all-to-all-done = bf16[8,16,8192]{2,1,0:T(8,128)(2,1)S(1)} async-done(((bf16[8,16,8192]{2,1,0:T(8,128)(2,1)}), bf16[8,16,8192]{2,1,0:T(8,128)(2,1)S(1)}, u32[]{:S(2)}, u32[]{:S(2)}) %all-to-all-start) | async-done | bytes 2097184 | tf_op jit(solution)/shard_map/all_to_all | solution.py:1044
  65.2 0.3 convert_reduce_fusion
  65.6 7.2 %collective-permute-start.9 = (bf16[16,8192]{1,0:T(8,128)(2,1)S(1)}, bf16[16,8192]{1,0:T(8,128)(2,1)S(1)}, u32[]{:S(2)}, u32[]{:S(2)}) collective-permute-start(bf16[16,8192]{1,0:T(8,128)(2,1)S(1)} %add_convert_fusion.shard_0), channel_id=1, source_target_pairs={{0,4},{1,5},{2,6},{3,7},{4,0},{5,1},{6,2},{7,3},{8,12},{9,13},{10,... | collective-permute-start | bytes 786440 | tf_op jit(solution)/shard_map/ppermute | solution.py:357
  72.8 0.9 maximum_maximum_fusion.side_hbm
  73.8 1.0 collective-permute-start.10
  74.8 1.7 collective-permute-start.11
  76.5 1.0 collective-permute-done.9.shard_1
  77.5 1.4 collective-permute-start.12
  78.9 1.3 collective-permute-start.13
  80.2 1.0 fusion.2.heads_hbm
  82.2 2.6 %collective-permute-start.15 = (bf16[16,4096]{1,0:T(8,128)(2,1)S(1)}, bf16[16,4096]{1,0:T(8,128)(2,1)S(1)}, u32[]{:S(2)}, u32[]{:S(2)}) collective-permute-start(bf16[16,4096]{1,0:T(8,128)(2,1)S(1)} %slice.47), channel_id=1, source_target_pairs={{0,3},{1,0},{2,1},{3,2},{4,7},{5,4},{6,5},{7,6},{8,11},{9,8},{10,9... | collective-permute-start | bytes 393224 | tf_op jit(solution)/shard_map/ppermute | solution.py:357
  84.8 2.5 %collective-permute-done.12.shard_4 = bf16[16,8192]{1,0:T(8,128)(2,1)S(1)} collective-permute-done((bf16[16,8192]{1,0:T(8,128)(2,1)S(1)}, bf16[16,8192]{1,0:T(8,128)(2,1)S(1)}, u32[]{:S(2)}, u32[]{:S(2)}) %collective-permute-start.12) | collective-permute-done | bytes 262176 | tf_op jit(solution)/shard_map/ppermute | solution.py:357
  87.5 2.7 %collective-permute-start.17 = (bf16[16,4096]{1,0:T(8,128)(2,1)S(1)}, bf16[16,4096]{1,0:T(8,128)(2,1)S(1)}, u32[]{:S(2)}, u32[]{:S(2)}) collective-permute-start(bf16[16,4096]{1,0:T(8,128)(2,1)S(1)} %slice.49), channel_id=1, source_target_pairs={{0,3},{1,0},{2,1},{3,2},{4,7},{5,4},{6,5},{7,6},{8,11},{9,8},{10,9... | collective-permute-start | bytes 393224 | tf_op jit(solution)/shard_map/ppermute | solution.py:357
  90.3 2.6 %collective-permute-done.16.shard_8 = bf16[16,4096]{1,0:T(8,128)(2,1)S(1)} collective-permute-done((bf16[16,4096]{1,0:T(8,128)(2,1)S(1)}, bf16[16,4096]{1,0:T(8,128)(2,1)S(1)}, u32[]{:S(2)}, u32[]{:S(2)}) %collective-permute-start.16) | collective-permute-done | bytes 131104 | tf_op jit(solution)/shard_map/ppermute | solution.py:357
  93.0 0.6 copy-done.18
  93.6 9.8 %cotangents.1 = (bf16[128,8192]{1,0:T(8,128)(2,1)}, f32[320,128]{1,0:T(8,128)}, f32[4,256,128]{2,1,0:T(8,128)}, f32[88,128]{1,0:T(8,128)}) custom-call(s32[1]{0:T(128)S(6)} %copy.31.lens_ref, bf16[16,8192]{1,0:T(8,128)(2,1)} %copy-done.2, bf16[16,8192]{1,0:T(8,128)(2,1)} %copy-done.14, bf16[16,8192]{1,0:T(8,128)(2,1)} %copy-done.8, ...), custom_call_target="tpu_custom_call" | custom-call | tf_op jit(solution)/shard_map/cotangents/pallas_call | solution.py:865
  103.4 6.1 %all-to-all-start.1 = ((f32[8,40,128]{2,1,0:T(8,128)}), f32[8,40,128]{2,1,0:T(8,128)S(1)}, u32[]{:S(2)}, u32[]{:S(2)}) async-start(f32[8,40,128]{2,1,0:T(8,128)} %bitcast.39), calls=%async_computation.1 | async-start | bytes 327680 | tf_op jit(solution)/shard_map/all_to_all | solution.py:1054
  109.6 7.0 %all-to-all-done.1.factors_hbm = f32[8,40,128]{2,1,0:T(8,128)S(1)} async-done(((f32[8,40,128]{2,1,0:T(8,128)}), f32[8,40,128]{2,1,0:T(8,128)S(1)}, u32[]{:S(2)}, u32[]{:S(2)}) %all-to-all-start.1) | async-done | bytes 163872 | tf_op jit(solution)/shard_map/all_to_all | solution.py:1054
  116.6 0.7 copy-done.3
  117.3 3.8 %jacobian.1 = bf16[16,56,512]{2,1,0:T(8,128)(2,1)} custom-call(f32[8,40,128]{2,1,0:T(8,128)} %copy-done.3, bf16[128,8192]{1,0:T(8,128)(2,1)} %get-tuple-element.22.tokens_hbm, bf16[128,8192]{1,0:T(8,128)(2,1)} %get-tuple-element.23.resid_hbm, bf16[48,8192]{1,0:T(8,128)(2,1)} %fusion.2.heads_hbm, f32[88,128]{1,0:T(8,128)} %get-tuple-element.24.scalars_hbm, ...), custom_call_target="tpu_custom_call" | custom-call | tf_op jit(solution)/shard_map/jacobian/pallas_call | solution.py:964
  121.1 9.6 %all-to-all-start.2 = ((bf16[16,56,512]{2,1,0:T(8,128)(2,1)}), bf16[16,56,512]{2,1,0:T(8,128)(2,1)S(1)}, u32[]{:S(2)}, u32[]{:S(2)}) async-start(bf16[16,56,512]{2,1,0:T(8,128)(2,1)} %jacobian.1), calls=%async_computation.2 | async-start | bytes 1835008 | tf_op jit(solution)/shard_map/all_to_all | solution.py:1056
  130.8 0.6 gather_fusion
  131.8 0.7 slice.39.rewards_ref
  132.4 12.7 %all-to-all-done.2 = bf16[16,56,512]{2,1,0:T(8,128)(2,1)S(1)} async-done(((bf16[16,56,512]{2,1,0:T(8,128)(2,1)}), bf16[16,56,512]{2,1,0:T(8,128)(2,1)S(1)}, u32[]{:S(2)}, u32[]{:S(2)}) %all-to-all-start.2) | async-done | bytes 917536 | tf_op jit(solution)/shard_map/all_to_all | solution.py:1056
  145.1 0.3 copy.27
  145.4 0.5 copy.28
  145.9 0.6 copy.30
  146.5 2.3 %gram.1 = f32[16,128]{1,0:T(8,128)S(1)} custom-call(bf16[80,5632]{1,0:T(8,128)(2,1)S(1)} %bitcast.23, f32[48,128]{1,0:T(8,128)S(1)} %pad.14.pairs_ref, f32[8,128]{1,0:T(8,128)S(1)} %slice.39.rewards_ref, f32[3,16,8192]{2,1,0:T(8,128)} %bitcast.25, f32[16,4096]{1,0:T(8,128)} %bq_ref.1, f32[2,16,1024]{2,1,0:T(8,128)} %bkv_ref.1, f32[16,4096]{1,0:T(8,128)} %bitcast.34, ...), custom_call_target="tpu_custom_call" | custom-call | tf_op jit(solution)/shard_map/gram/pallas_call | solution.py:1083
  148.9 9.3 %all_to_all.30 = f32[16,16,128]{2,1,0:T(8,128)S(1)} all-to-all(f32[16,16,128]{2,1,0:T(8,128)S(1)} %broadcast_in_dim.24), channel_id=1, replica_groups=mesh['dp'=16,'tensor'=8] {'dp'}, dimensions={0} | all-to-all | bytes 262144 | tf_op jit(solution)/shard_map/all_to_all | solution.py:45
  158.2 9.6 %all_to_all.31.packed_ref = f32[8,16,128]{2,1,0:T(8,128)S(1)} all-to-all(f32[8,16,128]{2,1,0:T(8,128)S(1)} %broadcast_in_dim.25), channel_id=1, replica_groups=mesh['dp'=16,'tensor'=8] {'tensor'}, dimensions={0} | all-to-all | bytes 131072 | tf_op jit(solution)/shard_map/all_to_all | solution.py:45
  167.7 0.9 lanczos.1
  168.7 17.4 %all_to_all.32.own_ref = bf16[64,8,768]{2,1,0:T(8,128)(2,1)S(1)} all-to-all(bf16[64,8,768]{2,1,0:T(8,128)(2,1)S(1)} %broadcast_in_dim.26), channel_id=1, replica_groups={{0,1,2,3,4,5,6,7,16,17,18,19,20,21,22,23,32,33,34,35,36,37,38,39,48,49,..., dimensions={0} | all-to-all | bytes 1572864 | tf_op jit(solution)/shard_map/all_to_all | solution.py:1116
  186.1 3.4 %collective-permute-start.18 = (bf16[64,8,768]{2,1,0:T(8,128)(2,1)S(1)}, bf16[64,8,768]{2,1,0:T(8,128)(2,1)S(1)}, u32[]{:S(2)}, u32[]{:S(2)}) collective-permute-start(bf16[64,8,768]{2,1,0:T(8,128)(2,1)S(1)} %all_to_all.32.own_ref), channel_id=1, source_target_pairs={{0,8},{8,0},{16,24},{24,16},{32,40},{40,32},{48,56},{56,48},{64,72... | collective-permute-start | bytes 2359304 | tf_op jit(solution)/shard_map/ppermute | solution.py:1123
  189.5 1.9 collective-permute-done.18.other_ref
  191.4 4.4 %assemble.1 = (f32[3,16,8192]{2,1,0:T(8,128)}, f32[16,4096]{1,0:T(8,128)}, f32[2,16,1024]{2,1,0:T(8,128)}, f32[16,4096]{1,0:T(8,128)}, f32[16,8192]{1,0:T(8,128)}) custom-call(f32[1,128]{1,0:T(1,128)S(1)} %get-tuple-element.26.part_ref, bf16[64,8,768]{2,1,0:T(8,128)(2,1)S(1)} %all_to_all.32.own_ref, ...), custom_call_target="tpu_custom_call" | custom-call | tf_op jit(solution)/shard_map/assemble/pallas_call | solution.py:985
  (88 shorter events, 1.9 us)
Async XLA Ops:
  0.6 9.8 %collective-permute-start = (bf16[16,8192]{1,0:T(8,128)(2,1)}, bf16[16,8192]{1,0:T(8,128)(2,1)S(1)}, u32[]{:S(2)}, u32[]{:S(2)}) collective-permute-start(bf16[16,8192]{1,0:T(8,128)(2,1)} %bitcast.30), channel_id=1, source_target_pairs={{0,4},{1,5},{2,6},{3,7},{4,0},{5,1},{6,2},{7,3},{8,12},{9,13},{10,... | collective-permute-start | bytes 786440 | tf_op jit(solution)/shard_map/ppermute | solution.py:357
  4.5 9.7 %collective-permute-start.1 = (bf16[16,8192]{1,0:T(8,128)(2,1)}, bf16[16,8192]{1,0:T(8,128)(2,1)S(1)}, u32[]{:S(2)}, u32[]{:S(2)}) collective-permute-start(bf16[16,8192]{1,0:T(8,128)(2,1)} %bitcast.31), channel_id=1, source_target_pairs={{0,1},{1,2},{2,3},{3,0},{4,5},{5,6},{6,7},{7,4},{8,9},{9,10},{10,1... | collective-permute-start | bytes 786440 | tf_op jit(solution)/shard_map/ppermute | solution.py:357
  6.1 8.2 %collective-permute-start.2 = (bf16[16,8192]{1,0:T(8,128)(2,1)}, bf16[16,8192]{1,0:T(8,128)(2,1)S(1)}, u32[]{:S(2)}, u32[]{:S(2)}) collective-permute-start(bf16[16,8192]{1,0:T(8,128)(2,1)} %bitcast.32), channel_id=1, source_target_pairs={{0,3},{1,0},{2,1},{3,2},{4,7},{5,4},{6,5},{7,6},{8,11},{9,8},{10,9... | collective-permute-start | bytes 786440 | tf_op jit(solution)/shard_map/ppermute | solution.py:357
  10.4 14.6 %copy-start.13 = (bf16[16,8192]{1,0:T(8,128)(2,1)}, bf16[16,8192]{1,0:T(8,128)(2,1)S(1)}, u32[]{:S(2)}) copy-start(bf16[16,8192]{1,0:T(8,128)(2,1)S(1)} %collective-permute-done.shard_1) | copy-start | bytes 786436
  10.4 8.8 %collective-permute-start.3 = (bf16[16,8192]{1,0:T(8,128)(2,1)S(1)}, bf16[16,8192]{1,0:T(8,128)(2,1)S(1)}, u32[]{:S(2)}, u32[]{:S(2)}) collective-permute-start(bf16[16,8192]{1,0:T(8,128)(2,1)S(1)} %collective-permute-done.shard_1), channel_id=1, source_target_pairs={{0,1},{1,2},{2,3},{3,0},{4,5},{5,6},{6,7},{7,4},{8,9},{9,10},{10,1... | collective-permute-start | bytes 786440 | tf_op jit(solution)/shard_map/ppermute | solution.py:357
  12.1 7.3 %collective-permute-start.4 = (bf16[16,8192]{1,0:T(8,128)(2,1)S(1)}, bf16[16,8192]{1,0:T(8,128)(2,1)S(1)}, u32[]{:S(2)}, u32[]{:S(2)}) collective-permute-start(bf16[16,8192]{1,0:T(8,128)(2,1)S(1)} %collective-permute-done.shard_1), channel_id=1, source_target_pairs={{0,3},{1,0},{2,1},{3,2},{4,7},{5,4},{6,5},{7,6},{8,11},{9,8},{10,9... | collective-permute-start | bytes 786440 | tf_op jit(solution)/shard_map/ppermute | solution.py:357
  14.2 10.8 %copy-start.4 = (bf16[16,8192]{1,0:T(8,128)(2,1)}, bf16[16,8192]{1,0:T(8,128)(2,1)S(1)}, u32[]{:S(2)}) copy-start(bf16[16,8192]{1,0:T(8,128)(2,1)S(1)} %collective-permute-done.1.shard_2) | copy-start | bytes 786436
  14.2 7.9 %collective-permute-start.5 = (bf16[16,4096]{1,0:T(8,128)(2,1)S(1)}, bf16[16,4096]{1,0:T(8,128)(2,1)S(1)}, u32[]{:S(2)}, u32[]{:S(2)}) collective-permute-start(bf16[16,4096]{1,0:T(8,128)(2,1)S(1)} %slice.42), channel_id=1, source_target_pairs={{0,1},{1,2},{2,3},{3,0},{4,5},{5,6},{6,7},{7,4},{8,9},{9,10},{10,1... | collective-permute-start | bytes 393224 | tf_op jit(solution)/shard_map/ppermute | solution.py:357
  14.3 10.7 %copy-start.5 = (bf16[16,8192]{1,0:T(8,128)(2,1)}, bf16[16,8192]{1,0:T(8,128)(2,1)S(1)}, u32[]{:S(2)}) copy-start(bf16[16,8192]{1,0:T(8,128)(2,1)S(1)} %collective-permute-done.2.shard_3) | copy-start | bytes 786436
  14.3 7.8 %collective-permute-start.6 = (bf16[16,4096]{1,0:T(8,128)(2,1)S(1)}, bf16[16,4096]{1,0:T(8,128)(2,1)S(1)}, u32[]{:S(2)}, u32[]{:S(2)}) collective-permute-start(bf16[16,4096]{1,0:T(8,128)(2,1)S(1)} %slice.43), channel_id=1, source_target_pairs={{0,3},{1,0},{2,1},{3,2},{4,7},{5,4},{6,5},{7,6},{8,11},{9,8},{10,9... | collective-permute-start | bytes 393224 | tf_op jit(solution)/shard_map/ppermute | solution.py:357
  19.3 5.7 %copy-start.6 = (bf16[16,8192]{1,0:T(8,128)(2,1)}, bf16[16,8192]{1,0:T(8,128)(2,1)S(1)}, u32[]{:S(2)}) copy-start(bf16[16,8192]{1,0:T(8,128)(2,1)S(1)} %collective-permute-done.3.shard_4) | copy-start | bytes 786436
  19.3 5.7 %collective-permute-start.7 = (bf16[16,4096]{1,0:T(8,128)(2,1)S(1)}, bf16[16,4096]{1,0:T(8,128)(2,1)S(1)}, u32[]{:S(2)}, u32[]{:S(2)}) collective-permute-start(bf16[16,4096]{1,0:T(8,128)(2,1)S(1)} %slice.44), channel_id=1, source_target_pairs={{0,1},{1,2},{2,3},{3,0},{4,5},{5,6},{6,7},{7,4},{8,9},{9,10},{10,1... | collective-permute-start | bytes 393224 | tf_op jit(solution)/shard_map/ppermute | solution.py:357
  19.4 5.6 %copy-start.7 = (bf16[16,8192]{1,0:T(8,128)(2,1)}, bf16[16,8192]{1,0:T(8,128)(2,1)S(1)}, u32[]{:S(2)}) copy-start(bf16[16,8192]{1,0:T(8,128)(2,1)S(1)} %collective-permute-done.4.shard_5) | copy-start | bytes 786436
  19.4 5.6 %collective-permute-start.8 = (bf16[16,4096]{1,0:T(8,128)(2,1)S(1)}, bf16[16,4096]{1,0:T(8,128)(2,1)S(1)}, u32[]{:S(2)}, u32[]{:S(2)}) collective-permute-start(bf16[16,4096]{1,0:T(8,128)(2,1)S(1)} %slice.45), channel_id=1, source_target_pairs={{0,3},{1,0},{2,1},{3,2},{4,7},{5,4},{6,5},{7,6},{8,11},{9,8},{10,9... | collective-permute-start | bytes 393224 | tf_op jit(solution)/shard_map/ppermute | solution.py:357
  22.1 2.9 %copy-start.17 = (bf16[16,4096]{1,0:T(8,128)(2,1)}, bf16[16,4096]{1,0:T(8,128)(2,1)S(1)}, u32[]{:S(2)}) copy-start(bf16[16,4096]{1,0:T(8,128)(2,1)S(1)} %collective-permute-done.5.shard_6) | copy-start | bytes 393220
  22.1 2.9 %copy-start.19 = (bf16[16,4096]{1,0:T(8,128)(2,1)}, bf16[16,4096]{1,0:T(8,128)(2,1)S(1)}, u32[]{:S(2)}) copy-start(bf16[16,4096]{1,0:T(8,128)(2,1)S(1)} %collective-permute-done.6.shard_7) | copy-start | bytes 393220
  25.0 0.7 copy-start.21
  25.0 0.7 copy-start.22
  37.0 28.1 %all-to-all-start = ((bf16[8,16,8192]{2,1,0:T(8,128)(2,1)}), bf16[8,16,8192]{2,1,0:T(8,128)(2,1)S(1)}, u32[]{:S(2)}, u32[]{:S(2)}) async-start(bf16[8,16,8192]{2,1,0:T(8,128)(2,1)} %get-tuple-element.19), calls=%async_computation | async-start | bytes 4194304 | tf_op jit(solution)/shard_map/all_to_all | solution.py:1044
  43.6 21.9 %copy-start.1 = (bf16[1,16,8192]{2,1,0:T(8,128)(2,1)S(1)}, bf16[1,16,8192]{2,1,0:T(8,128)(2,1)}, u32[]{:S(2)}) copy-start(bf16[1,16,8192]{2,1,0:T(8,128)(2,1)} %param.17) | copy-start | bytes 786436
  43.6 29.2 %copy-start = (bf16[16,8192]{1,0:T(8,128)(2,1)S(1)}, bf16[16,8192]{1,0:T(8,128)(2,1)}, u32[]{:S(2)}) copy-start(bf16[16,8192]{1,0:T(8,128)(2,1)} %up_output_hbm.1) | copy-start | bytes 786436
  43.6 29.2 %copy-start.12 = (bf16[8192,5]{0,1:T(8,128)(2,1)S(1)}, bf16[8192,5]{0,1:T(8,128)(2,1)}, u32[]{:S(2)}) copy-start(bf16[8192,5]{0,1:T(8,128)(2,1)} %param.21) | copy-start | bytes 245764
  65.5 27.4 %copy-start.2 = (bf16[16,8192]{1,0:T(8,128)(2,1)}, bf16[16,8192]{1,0:T(8,128)(2,1)S(1)}, u32[]{:S(2)}) copy-start(bf16[16,8192]{1,0:T(8,128)(2,1)S(1)} %add_convert_fusion.shard_0) | copy-start | bytes 786436
  65.6 24.7 %copy-start.23 = (s32[16]{0:T(128)S(1)}, s32[16]{0:T(128)}, u32[]{:S(2)}) copy-start(s32[16]{0:T(128)} %param.23) | copy-start | bytes 196
  65.6 12.0 %collective-permute-start.9 = (bf16[16,8192]{1,0:T(8,128)(2,1)S(1)}, bf16[16,8192]{1,0:T(8,128)(2,1)S(1)}, u32[]{:S(2)}, u32[]{:S(2)}) collective-permute-start(bf16[16,8192]{1,0:T(8,128)(2,1)S(1)} %add_convert_fusion.shard_0), channel_id=1, source_target_pairs={{0,4},{1,5},{2,6},{3,7},{4,0},{5,1},{6,2},{7,3},{8,12},{9,13},{10,... | collective-permute-start | bytes 786440 | tf_op jit(solution)/shard_map/ppermute | solution.py:357
  73.8 8.1 %collective-permute-start.10 = (bf16[16,8192]{1,0:T(8,128)(2,1)S(1)}, bf16[16,8192]{1,0:T(8,128)(2,1)S(1)}, u32[]{:S(2)}, u32[]{:S(2)}) collective-permute-start(bf16[16,8192]{1,0:T(8,128)(2,1)S(1)} %add_convert_fusion.shard_0), channel_id=1, source_target_pairs={{0,1},{1,2},{2,3},{3,0},{4,5},{5,6},{6,7},{7,4},{8,9},{9,10},{10,1... | collective-permute-start | bytes 786440 | tf_op jit(solution)/shard_map/ppermute | solution.py:357
  74.8 7.3 %collective-permute-start.11 = (bf16[16,8192]{1,0:T(8,128)(2,1)S(1)}, bf16[16,8192]{1,0:T(8,128)(2,1)S(1)}, u32[]{:S(2)}, u32[]{:S(2)}) collective-permute-start(bf16[16,8192]{1,0:T(8,128)(2,1)S(1)} %add_convert_fusion.shard_0), channel_id=1, source_target_pairs={{0,3},{1,0},{2,1},{3,2},{4,7},{5,4},{6,5},{7,6},{8,11},{9,8},{10,9... | collective-permute-start | bytes 786440 | tf_op jit(solution)/shard_map/ppermute | solution.py:357
  77.5 15.4 %copy-start.14 = (bf16[16,8192]{1,0:T(8,128)(2,1)}, bf16[16,8192]{1,0:T(8,128)(2,1)S(1)}, u32[]{:S(2)}) copy-start(bf16[16,8192]{1,0:T(8,128)(2,1)S(1)} %collective-permute-done.9.shard_1) | copy-start | bytes 786436
  77.5 9.7 %collective-permute-start.12 = (bf16[16,8192]{1,0:T(8,128)(2,1)S(1)}, bf16[16,8192]{1,0:T(8,128)(2,1)S(1)}, u32[]{:S(2)}, u32[]{:S(2)}) collective-permute-start(bf16[16,8192]{1,0:T(8,128)(2,1)S(1)} %collective-permute-done.9.shard_1), channel_id=1, source_target_pairs={{0,1},{1,2},{2,3},{3,0},{4,5},{5,6},{6,7},{7,4},{8,9},{9,10},{10,1... | collective-permute-start | bytes 786440 | tf_op jit(solution)/shard_map/ppermute | solution.py:357
  78.9 8.6 %collective-permute-start.13 = (bf16[16,8192]{1,0:T(8,128)(2,1)S(1)}, bf16[16,8192]{1,0:T(8,128)(2,1)S(1)}, u32[]{:S(2)}, u32[]{:S(2)}) collective-permute-start(bf16[16,8192]{1,0:T(8,128)(2,1)S(1)} %collective-permute-done.9.shard_1), channel_id=1, source_target_pairs={{0,3},{1,0},{2,1},{3,2},{4,7},{5,4},{6,5},{7,6},{8,11},{9,8},{10,9... | collective-permute-start | bytes 786440 | tf_op jit(solution)/shard_map/ppermute | solution.py:357
  81.9 11.0 %copy-start.8 = (bf16[16,8192]{1,0:T(8,128)(2,1)}, bf16[16,8192]{1,0:T(8,128)(2,1)S(1)}, u32[]{:S(2)}) copy-start(bf16[16,8192]{1,0:T(8,128)(2,1)S(1)} %collective-permute-done.10.shard_2) | copy-start | bytes 786436
  81.9 8.4 %collective-permute-start.14 = (bf16[16,4096]{1,0:T(8,128)(2,1)S(1)}, bf16[16,4096]{1,0:T(8,128)(2,1)S(1)}, u32[]{:S(2)}, u32[]{:S(2)}) collective-permute-start(bf16[16,4096]{1,0:T(8,128)(2,1)S(1)} %slice.46), channel_id=1, source_target_pairs={{0,1},{1,2},{2,3},{3,0},{4,5},{5,6},{6,7},{7,4},{8,9},{9,10},{10,1... | collective-permute-start | bytes 393224 | tf_op jit(solution)/shard_map/ppermute | solution.py:357
  82.1 10.8 %copy-start.9 = (bf16[16,8192]{1,0:T(8,128)(2,1)}, bf16[16,8192]{1,0:T(8,128)(2,1)S(1)}, u32[]{:S(2)}) copy-start(bf16[16,8192]{1,0:T(8,128)(2,1)S(1)} %collective-permute-done.11.shard_3) | copy-start | bytes 786436
  82.2 8.2 %collective-permute-start.15 = (bf16[16,4096]{1,0:T(8,128)(2,1)S(1)}, bf16[16,4096]{1,0:T(8,128)(2,1)S(1)}, u32[]{:S(2)}, u32[]{:S(2)}) collective-permute-start(bf16[16,4096]{1,0:T(8,128)(2,1)S(1)} %slice.47), channel_id=1, source_target_pairs={{0,3},{1,0},{2,1},{3,2},{4,7},{5,4},{6,5},{7,6},{8,11},{9,8},{10,9... | collective-permute-start | bytes 393224 | tf_op jit(solution)/shard_map/ppermute | solution.py:357
  87.3 5.7 %copy-start.10 = (bf16[16,8192]{1,0:T(8,128)(2,1)}, bf16[16,8192]{1,0:T(8,128)(2,1)S(1)}, u32[]{:S(2)}) copy-start(bf16[16,8192]{1,0:T(8,128)(2,1)S(1)} %collective-permute-done.12.shard_4) | copy-start | bytes 786436
  87.3 5.7 %collective-permute-start.16 = (bf16[16,4096]{1,0:T(8,128)(2,1)S(1)}, bf16[16,4096]{1,0:T(8,128)(2,1)S(1)}, u32[]{:S(2)}, u32[]{:S(2)}) collective-permute-start(bf16[16,4096]{1,0:T(8,128)(2,1)S(1)} %slice.48), channel_id=1, source_target_pairs={{0,1},{1,2},{2,3},{3,0},{4,5},{5,6},{6,7},{7,4},{8,9},{9,10},{10,1... | collective-permute-start | bytes 393224 | tf_op jit(solution)/shard_map/ppermute | solution.py:357
  87.5 5.4 %copy-start.11 = (bf16[16,8192]{1,0:T(8,128)(2,1)}, bf16[16,8192]{1,0:T(8,128)(2,1)S(1)}, u32[]{:S(2)}) copy-start(bf16[16,8192]{1,0:T(8,128)(2,1)S(1)} %collective-permute-done.13.shard_5) | copy-start | bytes 786436
  87.5 5.4 %collective-permute-start.17 = (bf16[16,4096]{1,0:T(8,128)(2,1)S(1)}, bf16[16,4096]{1,0:T(8,128)(2,1)S(1)}, u32[]{:S(2)}, u32[]{:S(2)}) collective-permute-start(bf16[16,4096]{1,0:T(8,128)(2,1)S(1)} %slice.49), channel_id=1, source_target_pairs={{0,3},{1,0},{2,1},{3,2},{4,7},{5,4},{6,5},{7,6},{8,11},{9,8},{10,9... | collective-permute-start | bytes 393224 | tf_op jit(solution)/shard_map/ppermute | solution.py:357
  90.3 2.7 %copy-start.15 = (bf16[16,4096]{1,0:T(8,128)(2,1)}, bf16[16,4096]{1,0:T(8,128)(2,1)S(1)}, u32[]{:S(2)}) copy-start(bf16[16,4096]{1,0:T(8,128)(2,1)S(1)} %collective-permute-done.14.shard_6) | copy-start | bytes 393220
  90.3 2.7 %copy-start.16 = (bf16[16,4096]{1,0:T(8,128)(2,1)}, bf16[16,4096]{1,0:T(8,128)(2,1)S(1)}, u32[]{:S(2)}) copy-start(bf16[16,4096]{1,0:T(8,128)(2,1)S(1)} %collective-permute-done.15.shard_7) | copy-start | bytes 393220
  92.9 0.6 copy-start.18
  92.9 0.7 copy-start.20
  103.4 13.2 %all-to-all-start.1 = ((f32[8,40,128]{2,1,0:T(8,128)}), f32[8,40,128]{2,1,0:T(8,128)S(1)}, u32[]{:S(2)}, u32[]{:S(2)}) async-start(f32[8,40,128]{2,1,0:T(8,128)} %bitcast.39), calls=%async_computation.1 | async-start | bytes 327680 | tf_op jit(solution)/shard_map/all_to_all | solution.py:1054
  116.6 0.7 copy-start.3
  121.1 24.0 %all-to-all-start.2 = ((bf16[16,56,512]{2,1,0:T(8,128)(2,1)}), bf16[16,56,512]{2,1,0:T(8,128)(2,1)S(1)}, u32[]{:S(2)}, u32[]{:S(2)}) async-start(bf16[16,56,512]{2,1,0:T(8,128)(2,1)} %jacobian.1), calls=%async_computation.2 | async-start | bytes 1835008 | tf_op jit(solution)/shard_map/all_to_all | solution.py:1056
  186.1 5.3 %collective-permute-start.18 = (bf16[64,8,768]{2,1,0:T(8,128)(2,1)S(1)}, bf16[64,8,768]{2,1,0:T(8,128)(2,1)S(1)}, u32[]{:S(2)}, u32[]{:S(2)}) collective-permute-start(bf16[64,8,768]{2,1,0:T(8,128)(2,1)S(1)} %all_to_all.32.own_ref), channel_id=1, source_target_pairs={{0,8},{8,0},{16,24},{24,16},{32,40},{40,32},{48,56},{56,48},{64,72... | collective-permute-start | bytes 2359304 | tf_op jit(solution)/shard_map/ppermute | solution.py:1123

commit v8 on v7

--- a/solution.py
+++ b/solution.py
@@ -344,7 +344,14 @@
 
 
 ANYWHERE = pl.BlockSpec(memory_space=pl.ANY)
-LARGE = 60 * 2**20
+
+
+def in_hbm(arrays):
+    return [pltpu.with_memory_space_constraint(array, pltpu.HBM) for array in arrays]
+
+
+def hbm_like(results):
+    return [pltpu.HBM(result.shape, result.dtype) for result in results]
 
 
 def gather_by_relays(block):
@@ -563,7 +570,7 @@
         forward_body,
         in_specs=[ANYWHERE] * (len(shards) + len(arrays)),
         out_specs=[ANYWHERE] * 3,
-        out_shape=results,
+        out_shape=hbm_like(results),
         scratch_shapes=[pltpu.VMEM(array.shape, array.dtype) for array in scratch]
         + [
             pltpu.VMEM((128, query_cols), jnp.float32),
@@ -571,9 +578,9 @@
             pltpu.VMEM((128, 128), jnp.float32),
             pltpu.SemaphoreType.DMA((16 + 6 * (width // CHUNK),)),
         ],
-        compiler_params=pltpu.CompilerParams(vmem_limit_bytes=LARGE),
+        compiler_params=pltpu.CompilerParams(vmem_limit_bytes=40 * 2**20),
         name="forward",
-    )(*shards, *arrays)
+    )(*in_hbm(shards[:1]), *shards[1:], *in_hbm(arrays))
 
 
 def cotangents_body(
@@ -867,7 +874,7 @@
         in_specs=[pl.BlockSpec(memory_space=pltpu.SMEM)]
         + [ANYWHERE] * (len(shards) + len(arrays)),
         out_specs=[ANYWHERE] + whole(3),
-        out_shape=results,
+        out_shape=hbm_like(results),
         scratch_shapes=[pltpu.VMEM(array.shape, array.dtype) for array in (results[0], *scratch)]
         + [
             pltpu.VMEM((144, query_cols), jnp.float32),
@@ -875,9 +882,9 @@
             pltpu.VMEM((128, 128), jnp.float32),
             pltpu.SemaphoreType.DMA((16 + 2 * (width // CHUNK),)),
         ],
-        compiler_params=pltpu.CompilerParams(vmem_limit_bytes=LARGE),
+        compiler_params=pltpu.CompilerParams(vmem_limit_bytes=32 * 2**20),
         name="cotangents",
-    )(lens, *shards, *arrays)
+    )(lens, *shards, *in_hbm(arrays))
 
 
 def jacobian_body(
@@ -965,12 +972,12 @@
         jacobian_body,
         in_specs=[ANYWHERE] * len(arrays),
         out_specs=ANYWHERE,
-        out_shape=result,
+        out_shape=hbm_like([result])[0],
         scratch_shapes=[pltpu.VMEM(array.shape, array.dtype) for array in (*arrays, result)]
         + [pltpu.SemaphoreType.DMA((3 + 4 * steps,))],
-        compiler_params=pltpu.CompilerParams(vmem_limit_bytes=LARGE),
+        compiler_params=pltpu.CompilerParams(vmem_limit_bytes=24 * 2**20),
         name="jacobian",
-    )(*arrays)
+    )(arrays[0], *in_hbm(arrays[1:]))
 
 
 def assemble(part, own, other, *shapes):

time: 196 us -> 195 us (level)
  local copies, waits for them, and re-layouts: 5.19 us -> 3.22 us
    unnamed x49 -> x9, local copies, waits for them, and re-layouts: 2.58 us -> 0.61 us
where the time goes in v8:
time: 195 us; the launch traced here: 194 us
  starting transfers between devices  61.1 us (31%)
  waiting for transfers between devices  56.5 us (29%)
  blocking collectives  36.2 us (19%)
  Pallas kernels  32.5 us (17%)
  local copies, waits for them, and re-layouts  3.22 us (2%)
  other arithmetic  2.67 us (1%)
    ppermute x18, starting transfers between devices, permute(): return lax.ppermute(array, 'tensor', pairs)  35.4 us
    all_to_all x1, waiting for transfers between devices, local(): out_pieces = lax.all_to_all(out_terms, 'tensor', 0, 0)  21.5 us
    all_to_all x2, blocking collectives, gather_by_exchange(): return lax.all_to_all(copies, axis, 0, 0)  18.8 us
    all_to_all x1, blocking collectives, local(): lax.all_to_all(jnp.broadcast_to(own_result[None], (half,) + own_result.sh...  17.4 us
    ppermute x18, waiting for transfers between devices, permute(): return lax.ppermute(array, 'tensor', pairs)  13.4 us
    all_to_all x1, waiting for transfers between devices, local(): spread = lax.all_to_all(payload, 'dp', 0, 0)  12.7 us
    pallas_call x1, Pallas kernels, forward(): pl.pallas_call(forward_body, in_specs=[ANYWHERE] * (len(shards) + len(arr...  11.2 us
    pallas_call x1, Pallas kernels, cotangents(): pl.pallas_call(cotangents_body, in_specs=[pl.BlockSpec(memory_space=pltpu...  9.86 us
  transfers between devices with their start and end apart: 22, of which 10 were waited for; matrix products, arithmetic and copies ran while one was open for 2% of the time, Pallas kernels for 0%

profile of v8, /device:TPU:1, one launch (start us, length us, event | category | flops | bytes accessed | tf_op | source)
XLA Modules:
  0.0 193.9 jit_solution(8475628451334910474)
XLA Ops:
  0.6 3.8 %collective-permute-start = (bf16[16,8192]{1,0:T(8,128)(2,1)}, bf16[16,8192]{1,0:T(8,128)(2,1)S(1)}, u32[]{:S(2)}, u32[]{:S(2)}) collective-permute-start(bf16[16,8192]{1,0:T(8,128)(2,1)} %bitcast.30), channel_id=1, source_target_pairs={{0,4},{1,5},{2,6},{3,7},{4,0},{5,1},{6,2},{7,3},{8,12},{9,13},{10,... | collective-permute-start | bytes 786440 | tf_op jit(solution)/shard_map/ppermute | solution.py:364
  4.5 1.6 collective-permute-start.1
  6.1 2.1 %collective-permute-start.2 = (bf16[16,8192]{1,0:T(8,128)(2,1)}, bf16[16,8192]{1,0:T(8,128)(2,1)S(1)}, u32[]{:S(2)}, u32[]{:S(2)}) collective-permute-start(bf16[16,8192]{1,0:T(8,128)(2,1)} %bitcast.32), channel_id=1, source_target_pairs={{0,3},{1,0},{2,1},{3,2},{4,7},{5,4},{6,5},{7,6},{8,11},{9,8},{10,9... | collective-permute-start | bytes 786440 | tf_op jit(solution)/shard_map/ppermute | solution.py:364
  8.2 2.2 %collective-permute-done.shard_1 = bf16[16,8192]{1,0:T(8,128)(2,1)S(1)} collective-permute-done((bf16[16,8192]{1,0:T(8,128)(2,1)}, bf16[16,8192]{1,0:T(8,128)(2,1)S(1)}, u32[]{:S(2)}, u32[]{:S(2)}) %collective-permute-start) | collective-permute-done | bytes 262176 | tf_op jit(solution)/shard_map/ppermute | solution.py:364
  10.4 1.6 collective-permute-start.3
  12.1 2.1 %collective-permute-start.4 = (bf16[16,8192]{1,0:T(8,128)(2,1)S(1)}, bf16[16,8192]{1,0:T(8,128)(2,1)S(1)}, u32[]{:S(2)}, u32[]{:S(2)}) collective-permute-start(bf16[16,8192]{1,0:T(8,128)(2,1)S(1)} %collective-permute-done.shard_1), channel_id=1, source_target_pairs={{0,3},{1,0},{2,1},{3,2},{4,7},{5,4},{6,5},{7,6},{8,11},{9,8},{10,9... | collective-permute-start | bytes 786440 | tf_op jit(solution)/shard_map/ppermute | solution.py:364
  14.3 2.7 %collective-permute-start.6 = (bf16[16,4096]{1,0:T(8,128)(2,1)S(1)}, bf16[16,4096]{1,0:T(8,128)(2,1)S(1)}, u32[]{:S(2)}, u32[]{:S(2)}) collective-permute-start(bf16[16,4096]{1,0:T(8,128)(2,1)S(1)} %slice.43), channel_id=1, source_target_pairs={{0,3},{1,0},{2,1},{3,2},{4,7},{5,4},{6,5},{7,6},{8,11},{9,8},{10,9... | collective-permute-start | bytes 393224 | tf_op jit(solution)/shard_map/ppermute | solution.py:364
  17.0 2.2 %collective-permute-done.3.shard_4 = bf16[16,8192]{1,0:T(8,128)(2,1)S(1)} collective-permute-done((bf16[16,8192]{1,0:T(8,128)(2,1)S(1)}, bf16[16,8192]{1,0:T(8,128)(2,1)S(1)}, u32[]{:S(2)}, u32[]{:S(2)}) %collective-permute-start.3) | collective-permute-done | bytes 262176 | tf_op jit(solution)/shard_map/ppermute | solution.py:364
  19.4 2.7 %collective-permute-start.8 = (bf16[16,4096]{1,0:T(8,128)(2,1)S(1)}, bf16[16,4096]{1,0:T(8,128)(2,1)S(1)}, u32[]{:S(2)}, u32[]{:S(2)}) collective-permute-start(bf16[16,4096]{1,0:T(8,128)(2,1)S(1)} %slice.45), channel_id=1, source_target_pairs={{0,3},{1,0},{2,1},{3,2},{4,7},{5,4},{6,5},{7,6},{8,11},{9,8},{10,9... | collective-permute-start | bytes 393224 | tf_op jit(solution)/shard_map/ppermute | solution.py:364
  22.1 2.9 %collective-permute-done.7.shard_8 = bf16[16,4096]{1,0:T(8,128)(2,1)S(1)} collective-permute-done((bf16[16,4096]{1,0:T(8,128)(2,1)S(1)}, bf16[16,4096]{1,0:T(8,128)(2,1)S(1)}, u32[]{:S(2)}, u32[]{:S(2)}) %collective-permute-start.7) | collective-permute-done | bytes 131104 | tf_op jit(solution)/shard_map/ppermute | solution.py:364
  25.0 11.2 %forward.1 = (bf16[128,8192]{1,0:T(8,128)(2,1)}, bf16[8,16,8192]{2,1,0:T(8,128)(2,1)}, f32[2368,128]{1,0:T(8,128)}) custom-call(bf16[16,8192]{1,0:T(8,128)(2,1)} %bitcast.33, bf16[16,8192]{1,0:T(8,128)(2,1)S(1)} %collective-permute-done.shard_1, bf16[16,8192]{1,0:T(8,128)(2,1)S(1)} %collective-permute-done.1.shard_2, ...), custom_call_target="tpu_custom_call" | custom-call | tf_op jit(solution)/shard_map/forward/pallas_call | solution.py:569
  36.2 6.6 %all-to-all-start = ((bf16[8,16,8192]{2,1,0:T(8,128)(2,1)}), bf16[8,16,8192]{2,1,0:T(8,128)(2,1)S(1)}, u32[]{:S(2)}, u32[]{:S(2)}) async-start(bf16[8,16,8192]{2,1,0:T(8,128)(2,1)} %get-tuple-element.19), calls=%async_computation | async-start | bytes 4194304 | tf_op jit(solution)/shard_map/all_to_all | solution.py:1051
  42.9 21.5 %all-to-all-done = bf16[8,16,8192]{2,1,0:T(8,128)(2,1)S(1)} async-done(((bf16[8,16,8192]{2,1,0:T(8,128)(2,1)}), bf16[8,16,8192]{2,1,0:T(8,128)(2,1)S(1)}, u32[]{:S(2)}, u32[]{:S(2)}) %all-to-all-start) | async-done | bytes 2097184 | tf_op jit(solution)/shard_map/all_to_all | solution.py:1051
  64.4 0.3 convert_reduce_fusion
  64.7 7.2 %collective-permute-start.9 = (bf16[16,8192]{1,0:T(8,128)(2,1)S(1)}, bf16[16,8192]{1,0:T(8,128)(2,1)S(1)}, u32[]{:S(2)}, u32[]{:S(2)}) collective-permute-start(bf16[16,8192]{1,0:T(8,128)(2,1)S(1)} %add_convert_fusion.shard_0), channel_id=1, source_target_pairs={{0,4},{1,5},{2,6},{3,7},{4,0},{5,1},{6,2},{7,3},{8,12},{9,13},{10,... | collective-permute-start | bytes 786440 | tf_op jit(solution)/shard_map/ppermute | solution.py:364
  71.9 0.9 maximum_maximum_fusion.side_hbm
  72.9 1.0 collective-permute-start.10
  74.0 1.7 collective-permute-start.11
  75.7 1.0 collective-permute-done.9.shard_1
  76.7 1.4 collective-permute-start.12
  78.0 1.3 collective-permute-start.13
  79.4 1.0 fusion.2.heads_hbm
  81.1 0.2 collective-permute-start.14
  81.3 2.6 %collective-permute-start.15 = (bf16[16,4096]{1,0:T(8,128)(2,1)S(1)}, bf16[16,4096]{1,0:T(8,128)(2,1)S(1)}, u32[]{:S(2)}, u32[]{:S(2)}) collective-permute-start(bf16[16,4096]{1,0:T(8,128)(2,1)S(1)} %slice.47), channel_id=1, source_target_pairs={{0,3},{1,0},{2,1},{3,2},{4,7},{5,4},{6,5},{7,6},{8,11},{9,8},{10,9... | collective-permute-start | bytes 393224 | tf_op jit(solution)/shard_map/ppermute | solution.py:364
  83.9 2.5 %collective-permute-done.12.shard_4 = bf16[16,8192]{1,0:T(8,128)(2,1)S(1)} collective-permute-done((bf16[16,8192]{1,0:T(8,128)(2,1)S(1)}, bf16[16,8192]{1,0:T(8,128)(2,1)S(1)}, u32[]{:S(2)}, u32[]{:S(2)}) %collective-permute-start.12) | collective-permute-done | bytes 262176 | tf_op jit(solution)/shard_map/ppermute | solution.py:364
  86.4 0.3 collective-permute-start.16
  86.7 2.7 %collective-permute-start.17 = (bf16[16,4096]{1,0:T(8,128)(2,1)S(1)}, bf16[16,4096]{1,0:T(8,128)(2,1)S(1)}, u32[]{:S(2)}, u32[]{:S(2)}) collective-permute-start(bf16[16,4096]{1,0:T(8,128)(2,1)S(1)} %slice.49), channel_id=1, source_target_pairs={{0,3},{1,0},{2,1},{3,2},{4,7},{5,4},{6,5},{7,6},{8,11},{9,8},{10,9... | collective-permute-start | bytes 393224 | tf_op jit(solution)/shard_map/ppermute | solution.py:364
  89.5 2.6 %collective-permute-done.16.shard_8 = bf16[16,4096]{1,0:T(8,128)(2,1)S(1)} collective-permute-done((bf16[16,4096]{1,0:T(8,128)(2,1)S(1)}, bf16[16,4096]{1,0:T(8,128)(2,1)S(1)}, u32[]{:S(2)}, u32[]{:S(2)}) %collective-permute-start.16) | collective-permute-done | bytes 131104 | tf_op jit(solution)/shard_map/ppermute | solution.py:364
  92.1 9.9 %cotangents.1 = (bf16[128,8192]{1,0:T(8,128)(2,1)}, f32[320,128]{1,0:T(8,128)}, f32[4,256,128]{2,1,0:T(8,128)}, f32[88,128]{1,0:T(8,128)}) custom-call(s32[1]{0:T(128)S(6)} %copy.31.lens_ref, bf16[16,8192]{1,0:T(8,128)(2,1)S(1)} %add_convert_fusion.shard_0, bf16[16,8192]{1,0:T(8,128)(2,1)S(1)} %collective-permute-done.9.shard_1, ...), custom_call_target="tpu_custom_call" | custom-call | tf_op jit(solution)/shard_map/cotangents/pallas_call | solution.py:872
  102.0 6.1 %all-to-all-start.1 = ((f32[8,40,128]{2,1,0:T(8,128)}), f32[8,40,128]{2,1,0:T(8,128)S(1)}, u32[]{:S(2)}, u32[]{:S(2)}) async-start(f32[8,40,128]{2,1,0:T(8,128)} %bitcast.39), calls=%async_computation.1 | async-start | bytes 327680 | tf_op jit(solution)/shard_map/all_to_all | solution.py:1061
  108.1 7.0 %all-to-all-done.1.factors_hbm = f32[8,40,128]{2,1,0:T(8,128)S(1)} async-done(((f32[8,40,128]{2,1,0:T(8,128)}), f32[8,40,128]{2,1,0:T(8,128)S(1)}, u32[]{:S(2)}, u32[]{:S(2)}) %all-to-all-start.1) | async-done | bytes 163872 | tf_op jit(solution)/shard_map/all_to_all | solution.py:1061
  115.1 3.9 %jacobian.1 = bf16[16,56,512]{2,1,0:T(8,128)(2,1)} custom-call(f32[8,40,128]{2,1,0:T(8,128)S(1)} %all-to-all-done.1.factors_hbm, bf16[128,8192]{1,0:T(8,128)(2,1)} %get-tuple-element.22.tokens_hbm, bf16[128,8192]{1,0:T(8,128)(2,1)} %get-tuple-element.23.resid_hbm, bf16[48,8192]{1,0:T(8,128)(2,1)} %fusion.2.heads_hbm, ...), custom_call_target="tpu_custom_call" | custom-call | tf_op jit(solution)/shard_map/jacobian/pallas_call | solution.py:971
  119.0 9.6 %all-to-all-start.2 = ((bf16[16,56,512]{2,1,0:T(8,128)(2,1)}), bf16[16,56,512]{2,1,0:T(8,128)(2,1)S(1)}, u32[]{:S(2)}, u32[]{:S(2)}) async-start(bf16[16,56,512]{2,1,0:T(8,128)(2,1)} %jacobian.1), calls=%async_computation.2 | async-start | bytes 1835008 | tf_op jit(solution)/shard_map/all_to_all | solution.py:1063
  128.8 0.6 gather_fusion
  129.6 0.2 mul.20
  129.8 0.7 slice.39.rewards_ref
  130.5 12.7 %all-to-all-done.2 = bf16[16,56,512]{2,1,0:T(8,128)(2,1)S(1)} async-done(((bf16[16,56,512]{2,1,0:T(8,128)(2,1)}), bf16[16,56,512]{2,1,0:T(8,128)(2,1)S(1)}, u32[]{:S(2)}, u32[]{:S(2)}) %all-to-all-start.2) | async-done | bytes 917536 | tf_op jit(solution)/shard_map/all_to_all | solution.py:1063
  143.1 0.3 copy.27
  143.4 0.5 copy.28
  144.0 0.6 copy.30
  144.5 2.3 %gram.1 = f32[16,128]{1,0:T(8,128)S(1)} custom-call(bf16[80,5632]{1,0:T(8,128)(2,1)S(1)} %bitcast.23, f32[48,128]{1,0:T(8,128)S(1)} %pad.14.pairs_ref, f32[8,128]{1,0:T(8,128)S(1)} %slice.39.rewards_ref, f32[3,16,8192]{2,1,0:T(8,128)} %bitcast.25, f32[16,4096]{1,0:T(8,128)} %bq_ref.1, f32[2,16,1024]{2,1,0:T(8,128)} %bkv_ref.1, f32[16,4096]{1,0:T(8,128)} %bitcast.34, ...), custom_call_target="tpu_custom_call" | custom-call | tf_op jit(solution)/shard_map/gram/pallas_call | solution.py:1090
  146.9 9.3 %all_to_all.30 = f32[16,16,128]{2,1,0:T(8,128)S(1)} all-to-all(f32[16,16,128]{2,1,0:T(8,128)S(1)} %broadcast_in_dim.24), channel_id=1, replica_groups=mesh['dp'=16,'tensor'=8] {'dp'}, dimensions={0} | all-to-all | bytes 262144 | tf_op jit(solution)/shard_map/all_to_all | solution.py:45
  156.2 9.6 %all_to_all.31.packed_ref = f32[8,16,128]{2,1,0:T(8,128)S(1)} all-to-all(f32[8,16,128]{2,1,0:T(8,128)S(1)} %broadcast_in_dim.25), channel_id=1, replica_groups=mesh['dp'=16,'tensor'=8] {'tensor'}, dimensions={0} | all-to-all | bytes 131072 | tf_op jit(solution)/shard_map/all_to_all | solution.py:45
  165.8 0.9 lanczos.1
  166.7 17.4 %all_to_all.32.own_ref = bf16[64,8,768]{2,1,0:T(8,128)(2,1)S(1)} all-to-all(bf16[64,8,768]{2,1,0:T(8,128)(2,1)S(1)} %broadcast_in_dim.26), channel_id=1, replica_groups={{0,1,2,3,4,5,6,7,16,17,18,19,20,21,22,23,32,33,34,35,36,37,38,39,48,49,..., dimensions={0} | all-to-all | bytes 1572864 | tf_op jit(solution)/shard_map/all_to_all | solution.py:1123
  184.1 3.4 %collective-permute-start.18 = (bf16[64,8,768]{2,1,0:T(8,128)(2,1)S(1)}, bf16[64,8,768]{2,1,0:T(8,128)(2,1)S(1)}, u32[]{:S(2)}, u32[]{:S(2)}) collective-permute-start(bf16[64,8,768]{2,1,0:T(8,128)(2,1)S(1)} %all_to_all.32.own_ref), channel_id=1, source_target_pairs={{0,8},{8,0},{16,24},{24,16},{32,40},{40,32},{48,56},{56,48},{64,72... | collective-permute-start | bytes 2359304 | tf_op jit(solution)/shard_map/ppermute | solution.py:1130
  187.5 1.9 collective-permute-done.18.other_ref
  189.4 4.4 %assemble.1 = (f32[3,16,8192]{2,1,0:T(8,128)}, f32[16,4096]{1,0:T(8,128)}, f32[2,16,1024]{2,1,0:T(8,128)}, f32[16,4096]{1,0:T(8,128)}, f32[16,8192]{1,0:T(8,128)}) custom-call(f32[1,128]{1,0:T(1,128)S(1)} %get-tuple-element.26.part_ref, bf16[64,8,768]{2,1,0:T(8,128)(2,1)S(1)} %all_to_all.32.own_ref, ...), custom_call_target="tpu_custom_call" | custom-call | tf_op jit(solution)/shard_map/assemble/pallas_call | solution.py:992
  (48 shorter events, 1.0 us)
Async XLA Ops:
  0.6 9.8 %collective-permute-start = (bf16[16,8192]{1,0:T(8,128)(2,1)}, bf16[16,8192]{1,0:T(8,128)(2,1)S(1)}, u32[]{:S(2)}, u32[]{:S(2)}) collective-permute-start(bf16[16,8192]{1,0:T(8,128)(2,1)} %bitcast.30), channel_id=1, source_target_pairs={{0,4},{1,5},{2,6},{3,7},{4,0},{5,1},{6,2},{7,3},{8,12},{9,13},{10,... | collective-permute-start | bytes 786440 | tf_op jit(solution)/shard_map/ppermute | solution.py:364
  4.5 9.7 %collective-permute-start.1 = (bf16[16,8192]{1,0:T(8,128)(2,1)}, bf16[16,8192]{1,0:T(8,128)(2,1)S(1)}, u32[]{:S(2)}, u32[]{:S(2)}) collective-permute-start(bf16[16,8192]{1,0:T(8,128)(2,1)} %bitcast.31), channel_id=1, source_target_pairs={{0,1},{1,2},{2,3},{3,0},{4,5},{5,6},{6,7},{7,4},{8,9},{9,10},{10,1... | collective-permute-start | bytes 786440 | tf_op jit(solution)/shard_map/ppermute | solution.py:364
  6.1 8.2 %collective-permute-start.2 = (bf16[16,8192]{1,0:T(8,128)(2,1)}, bf16[16,8192]{1,0:T(8,128)(2,1)S(1)}, u32[]{:S(2)}, u32[]{:S(2)}) collective-permute-start(bf16[16,8192]{1,0:T(8,128)(2,1)} %bitcast.32), channel_id=1, source_target_pairs={{0,3},{1,0},{2,1},{3,2},{4,7},{5,4},{6,5},{7,6},{8,11},{9,8},{10,9... | collective-permute-start | bytes 786440 | tf_op jit(solution)/shard_map/ppermute | solution.py:364
  10.4 8.8 %collective-permute-start.3 = (bf16[16,8192]{1,0:T(8,128)(2,1)S(1)}, bf16[16,8192]{1,0:T(8,128)(2,1)S(1)}, u32[]{:S(2)}, u32[]{:S(2)}) collective-permute-start(bf16[16,8192]{1,0:T(8,128)(2,1)S(1)} %collective-permute-done.shard_1), channel_id=1, source_target_pairs={{0,1},{1,2},{2,3},{3,0},{4,5},{5,6},{6,7},{7,4},{8,9},{9,10},{10,1... | collective-permute-start | bytes 786440 | tf_op jit(solution)/shard_map/ppermute | solution.py:364
  12.1 7.3 %collective-permute-start.4 = (bf16[16,8192]{1,0:T(8,128)(2,1)S(1)}, bf16[16,8192]{1,0:T(8,128)(2,1)S(1)}, u32[]{:S(2)}, u32[]{:S(2)}) collective-permute-start(bf16[16,8192]{1,0:T(8,128)(2,1)S(1)} %collective-permute-done.shard_1), channel_id=1, source_target_pairs={{0,3},{1,0},{2,1},{3,2},{4,7},{5,4},{6,5},{7,6},{8,11},{9,8},{10,9... | collective-permute-start | bytes 786440 | tf_op jit(solution)/shard_map/ppermute | solution.py:364
  14.2 7.9 %collective-permute-start.5 = (bf16[16,4096]{1,0:T(8,128)(2,1)S(1)}, bf16[16,4096]{1,0:T(8,128)(2,1)S(1)}, u32[]{:S(2)}, u32[]{:S(2)}) collective-permute-start(bf16[16,4096]{1,0:T(8,128)(2,1)S(1)} %slice.42), channel_id=1, source_target_pairs={{0,1},{1,2},{2,3},{3,0},{4,5},{5,6},{6,7},{7,4},{8,9},{9,10},{10,1... | collective-permute-start | bytes 393224 | tf_op jit(solution)/shard_map/ppermute | solution.py:364
  14.3 7.8 %collective-permute-start.6 = (bf16[16,4096]{1,0:T(8,128)(2,1)S(1)}, bf16[16,4096]{1,0:T(8,128)(2,1)S(1)}, u32[]{:S(2)}, u32[]{:S(2)}) collective-permute-start(bf16[16,4096]{1,0:T(8,128)(2,1)S(1)} %slice.43), channel_id=1, source_target_pairs={{0,3},{1,0},{2,1},{3,2},{4,7},{5,4},{6,5},{7,6},{8,11},{9,8},{10,9... | collective-permute-start | bytes 393224 | tf_op jit(solution)/shard_map/ppermute | solution.py:364
  19.3 5.7 %collective-permute-start.7 = (bf16[16,4096]{1,0:T(8,128)(2,1)S(1)}, bf16[16,4096]{1,0:T(8,128)(2,1)S(1)}, u32[]{:S(2)}, u32[]{:S(2)}) collective-permute-start(bf16[16,4096]{1,0:T(8,128)(2,1)S(1)} %slice.44), channel_id=1, source_target_pairs={{0,1},{1,2},{2,3},{3,0},{4,5},{5,6},{6,7},{7,4},{8,9},{9,10},{10,1... | collective-permute-start | bytes 393224 | tf_op jit(solution)/shard_map/ppermute | solution.py:364
  19.4 5.6 %collective-permute-start.8 = (bf16[16,4096]{1,0:T(8,128)(2,1)S(1)}, bf16[16,4096]{1,0:T(8,128)(2,1)S(1)}, u32[]{:S(2)}, u32[]{:S(2)}) collective-permute-start(bf16[16,4096]{1,0:T(8,128)(2,1)S(1)} %slice.45), channel_id=1, source_target_pairs={{0,3},{1,0},{2,1},{3,2},{4,7},{5,4},{6,5},{7,6},{8,11},{9,8},{10,9... | collective-permute-start | bytes 393224 | tf_op jit(solution)/shard_map/ppermute | solution.py:364
  36.2 28.2 %all-to-all-start = ((bf16[8,16,8192]{2,1,0:T(8,128)(2,1)}), bf16[8,16,8192]{2,1,0:T(8,128)(2,1)S(1)}, u32[]{:S(2)}, u32[]{:S(2)}) async-start(bf16[8,16,8192]{2,1,0:T(8,128)(2,1)} %get-tuple-element.19), calls=%async_computation | async-start | bytes 4194304 | tf_op jit(solution)/shard_map/all_to_all | solution.py:1051
  42.8 21.9 %copy-start.1 = (bf16[1,16,8192]{2,1,0:T(8,128)(2,1)S(1)}, bf16[1,16,8192]{2,1,0:T(8,128)(2,1)}, u32[]{:S(2)}) copy-start(bf16[1,16,8192]{2,1,0:T(8,128)(2,1)} %param.17) | copy-start | bytes 786436
  42.8 29.2 %copy-start = (bf16[16,8192]{1,0:T(8,128)(2,1)S(1)}, bf16[16,8192]{1,0:T(8,128)(2,1)}, u32[]{:S(2)}) copy-start(bf16[16,8192]{1,0:T(8,128)(2,1)} %up_output_hbm.1) | copy-start | bytes 786436
  42.8 29.2 %copy-start.2 = (bf16[8192,5]{0,1:T(8,128)(2,1)S(1)}, bf16[8192,5]{0,1:T(8,128)(2,1)}, u32[]{:S(2)}) copy-start(bf16[8192,5]{0,1:T(8,128)(2,1)} %param.21) | copy-start | bytes 245764
  64.7 24.7 %copy-start.3 = (s32[16]{0:T(128)S(1)}, s32[16]{0:T(128)}, u32[]{:S(2)}) copy-start(s32[16]{0:T(128)} %param.23) | copy-start | bytes 196
  64.7 12.0 %collective-permute-start.9 = (bf16[16,8192]{1,0:T(8,128)(2,1)S(1)}, bf16[16,8192]{1,0:T(8,128)(2,1)S(1)}, u32[]{:S(2)}, u32[]{:S(2)}) collective-permute-start(bf16[16,8192]{1,0:T(8,128)(2,1)S(1)} %add_convert_fusion.shard_0), channel_id=1, source_target_pairs={{0,4},{1,5},{2,6},{3,7},{4,0},{5,1},{6,2},{7,3},{8,12},{9,13},{10,... | collective-permute-start | bytes 786440 | tf_op jit(solution)/shard_map/ppermute | solution.py:364
  72.9 8.1 %collective-permute-start.10 = (bf16[16,8192]{1,0:T(8,128)(2,1)S(1)}, bf16[16,8192]{1,0:T(8,128)(2,1)S(1)}, u32[]{:S(2)}, u32[]{:S(2)}) collective-permute-start(bf16[16,8192]{1,0:T(8,128)(2,1)S(1)} %add_convert_fusion.shard_0), channel_id=1, source_target_pairs={{0,1},{1,2},{2,3},{3,0},{4,5},{5,6},{6,7},{7,4},{8,9},{9,10},{10,1... | collective-permute-start | bytes 786440 | tf_op jit(solution)/shard_map/ppermute | solution.py:364
  74.0 7.3 %collective-permute-start.11 = (bf16[16,8192]{1,0:T(8,128)(2,1)S(1)}, bf16[16,8192]{1,0:T(8,128)(2,1)S(1)}, u32[]{:S(2)}, u32[]{:S(2)}) collective-permute-start(bf16[16,8192]{1,0:T(8,128)(2,1)S(1)} %add_convert_fusion.shard_0), channel_id=1, source_target_pairs={{0,3},{1,0},{2,1},{3,2},{4,7},{5,4},{6,5},{7,6},{8,11},{9,8},{10,9... | collective-permute-start | bytes 786440 | tf_op jit(solution)/shard_map/ppermute | solution.py:364
  76.7 9.7 %collective-permute-start.12 = (bf16[16,8192]{1,0:T(8,128)(2,1)S(1)}, bf16[16,8192]{1,0:T(8,128)(2,1)S(1)}, u32[]{:S(2)}, u32[]{:S(2)}) collective-permute-start(bf16[16,8192]{1,0:T(8,128)(2,1)S(1)} %collective-permute-done.9.shard_1), channel_id=1, source_target_pairs={{0,1},{1,2},{2,3},{3,0},{4,5},{5,6},{6,7},{7,4},{8,9},{9,10},{10,1... | collective-permute-start | bytes 786440 | tf_op jit(solution)/shard_map/ppermute | solution.py:364
  78.0 8.6 %collective-permute-start.13 = (bf16[16,8192]{1,0:T(8,128)(2,1)S(1)}, bf16[16,8192]{1,0:T(8,128)(2,1)S(1)}, u32[]{:S(2)}, u32[]{:S(2)}) collective-permute-start(bf16[16,8192]{1,0:T(8,128)(2,1)S(1)} %collective-permute-done.9.shard_1), channel_id=1, source_target_pairs={{0,3},{1,0},{2,1},{3,2},{4,7},{5,4},{6,5},{7,6},{8,11},{9,8},{10,9... | collective-permute-start | bytes 786440 | tf_op jit(solution)/shard_map/ppermute | solution.py:364
  81.1 8.4 %collective-permute-start.14 = (bf16[16,4096]{1,0:T(8,128)(2,1)S(1)}, bf16[16,4096]{1,0:T(8,128)(2,1)S(1)}, u32[]{:S(2)}, u32[]{:S(2)}) collective-permute-start(bf16[16,4096]{1,0:T(8,128)(2,1)S(1)} %slice.46), channel_id=1, source_target_pairs={{0,1},{1,2},{2,3},{3,0},{4,5},{5,6},{6,7},{7,4},{8,9},{9,10},{10,1... | collective-permute-start | bytes 393224 | tf_op jit(solution)/shard_map/ppermute | solution.py:364
  81.3 8.2 %collective-permute-start.15 = (bf16[16,4096]{1,0:T(8,128)(2,1)S(1)}, bf16[16,4096]{1,0:T(8,128)(2,1)S(1)}, u32[]{:S(2)}, u32[]{:S(2)}) collective-permute-start(bf16[16,4096]{1,0:T(8,128)(2,1)S(1)} %slice.47), channel_id=1, source_target_pairs={{0,3},{1,0},{2,1},{3,2},{4,7},{5,4},{6,5},{7,6},{8,11},{9,8},{10,9... | collective-permute-start | bytes 393224 | tf_op jit(solution)/shard_map/ppermute | solution.py:364
  86.4 5.7 %collective-permute-start.16 = (bf16[16,4096]{1,0:T(8,128)(2,1)S(1)}, bf16[16,4096]{1,0:T(8,128)(2,1)S(1)}, u32[]{:S(2)}, u32[]{:S(2)}) collective-permute-start(bf16[16,4096]{1,0:T(8,128)(2,1)S(1)} %slice.48), channel_id=1, source_target_pairs={{0,1},{1,2},{2,3},{3,0},{4,5},{5,6},{6,7},{7,4},{8,9},{9,10},{10,1... | collective-permute-start | bytes 393224 | tf_op jit(solution)/shard_map/ppermute | solution.py:364
  86.7 5.4 %collective-permute-start.17 = (bf16[16,4096]{1,0:T(8,128)(2,1)S(1)}, bf16[16,4096]{1,0:T(8,128)(2,1)S(1)}, u32[]{:S(2)}, u32[]{:S(2)}) collective-permute-start(bf16[16,4096]{1,0:T(8,128)(2,1)S(1)} %slice.49), channel_id=1, source_target_pairs={{0,3},{1,0},{2,1},{3,2},{4,7},{5,4},{6,5},{7,6},{8,11},{9,8},{10,9... | collective-permute-start | bytes 393224 | tf_op jit(solution)/shard_map/ppermute | solution.py:364
  102.0 13.2 %all-to-all-start.1 = ((f32[8,40,128]{2,1,0:T(8,128)}), f32[8,40,128]{2,1,0:T(8,128)S(1)}, u32[]{:S(2)}, u32[]{:S(2)}) async-start(f32[8,40,128]{2,1,0:T(8,128)} %bitcast.39), calls=%async_computation.1 | async-start | bytes 327680 | tf_op jit(solution)/shard_map/all_to_all | solution.py:1061
  119.0 24.1 %all-to-all-start.2 = ((bf16[16,56,512]{2,1,0:T(8,128)(2,1)}), bf16[16,56,512]{2,1,0:T(8,128)(2,1)S(1)}, u32[]{:S(2)}, u32[]{:S(2)}) async-start(bf16[16,56,512]{2,1,0:T(8,128)(2,1)} %jacobian.1), calls=%async_computation.2 | async-start | bytes 1835008 | tf_op jit(solution)/shard_map/all_to_all | solution.py:1063
  184.1 5.3 %collective-permute-start.18 = (bf16[64,8,768]{2,1,0:T(8,128)(2,1)S(1)}, bf16[64,8,768]{2,1,0:T(8,128)(2,1)S(1)}, u32[]{:S(2)}, u32[]{:S(2)}) collective-permute-start(bf16[64,8,768]{2,1,0:T(8,128)(2,1)S(1)} %all_to_all.32.own_ref), channel_id=1, source_target_pairs={{0,8},{8,0},{16,24},{24,16},{32,40},{40,32},{48,56},{56,48},{64,72... | collective-permute-start | bytes 2359304 | tf_op jit(solution)/shard_map/ppermute | solution.py:1130

commit v9 on v8

--- a/solution.py
+++ b/solution.py
@@ -603,7 +603,7 @@
     small_kv_hbm,
     resid_hbm,
     factors_ref,
-    narrow_ref,
+    later_ref,
     scalars_ref,
     resid_ref,
     weight_ref,
@@ -646,7 +646,6 @@
     slow_ref[...] = jnp.zeros(slow_ref.shape, jnp.float32)
     through_ref[...] = jnp.zeros(through_ref.shape, jnp.float32)
     square_ref[...] = jnp.zeros(square_ref.shape, jnp.float32)
-    narrow_ref[...] = jnp.zeros(narrow_ref.shape, jnp.float32)
     width = resid_ref.shape[1]
     finish(placed)
     leaving = launch([(resid_ref, resid_hbm)], semaphores, first + 5)
@@ -674,7 +673,7 @@
         state_ref,
         small_ref,
         factors_ref,
-        narrow_ref,
+        later_ref,
         scalars_ref,
         through_ref,
         slow_ref,
@@ -689,7 +688,7 @@
     state_ref,
     small_ref,
     factors_ref,
-    narrow_ref,
+    later_ref,
     scalars_ref,
     through_ref,
     slow_ref,
@@ -759,7 +758,6 @@
             return array[row : row + 1]
 
         left_values = []
-        right_values = []
         for obj in objectives:
             pull = row_of(pulled_turned, obj)
             parts = []
@@ -770,10 +768,7 @@
                     - pull * block(values_on_cot, head)
                 )
             left_values.append(flat(parts))
-            right_values.append(low_on_probs * flat([pull] * 4))
         factor_values = product(tall(left_values), probs, 0)
-        jac_values = -product(tall(right_values), across, 0)
-        low_lead = [lane_sum(block(low_on_probs, head) * lead_turned) for head in head_spots]
         factor_query = [0.0] * OBJ
         factor_keys = [0.0] * OBJ
         query_rows = [[] for _ in objectives]
@@ -815,14 +810,20 @@
                 factor_keys[obj] += by_rows[16:]
                 factor_query[obj] += by_lanes[:16]
                 keys_rows[obj].append(by_lanes[16:])
-        jac_query = product(tall([tall(rows) for rows in query_rows]), keys, 0)
-        jac_keys = product(tall([flat(rows) for rows in keys_rows]), query, 0)
+        later_ref[0:320] = tall([tall(rows) for rows in query_rows])
+        for head in head_spots:
+            spot = 320 + 80 * head
+            later_ref[spot : spot + 80] = tall([rows[head] for rows in keys_rows])
+            spot = 1264 + 16 * head
+            later_ref[spot : spot + 16] = block(low_on_probs, head)
+        later_ref[720:1232] = across
+        later_ref[1232:1264] = heads
         cot_low = [
             slow_turned[:16, 128 + obj : 129 + obj] * lead_turned
             - row_of(pulled_turned, obj) * low_turned
             for obj in objectives
         ]
-        jac_down = product(tall(cot_low), unstack(context_rows), 0)
+        later_ref[640:720] = tall(cot_low)
         for obj in objectives:
             own = slice(16 * obj, 16 * obj + 16)
             rows = [
@@ -836,22 +837,6 @@
                     factors_ref[pl.ds(20 * half + 5 * piece + obj, 8, stride=40), :] = rows[
                         piece
                     ][8 * half : 8 * half + 8]
-            own_values = jac_values[own]
-            for head in head_spots:
-                own_values += low_lead[head] * row_of(heads, 8 * head + obj)
-            blocks = [
-                jac_query[64 * obj + 16 * head : 64 * obj + 16 * head + 16]
-                for head in head_spots
-            ]
-            blocks += [block(jac_down, head)[own] for head in head_spots]
-            blocks += [jac_keys[own], own_values]
-            spots = [(0, 0), (0, 1), (0, 2), (0, 3), (5, 0), (5, 1), (5, 2), (5, 3)]
-            spots += [(10, 0), (10, 1)]
-            for (row, tile), part in zip(spots, blocks):
-                for half in range(2):
-                    narrow_ref[tile, pl.ds(128 * half + row + obj, 8, stride=16), :] = (
-                        ADAPTER_SCALE * part[8 * half : 8 * half + 8]
-                    )
         blank = jnp.zeros((15, 128), jnp.float32)
         scalars_ref[8:48] = jnp.concatenate([blank, pulled_turned[:5]] * 2, 0)
         scalars_ref[48:] = jnp.broadcast_to(lead_turned, (40, 128))
@@ -866,7 +851,7 @@
     results = [
         jax.ShapeDtypeStruct((128, width), jnp.bfloat16),
         jax.ShapeDtypeStruct((320, 128), jnp.float32),
-        jax.ShapeDtypeStruct((4, 256, 128), jnp.float32),
+        jax.ShapeDtypeStruct((1328, 128), jnp.float32),
         jax.ShapeDtypeStruct((88, 128), jnp.float32),
     ]
     return pl.pallas_call(
@@ -885,6 +870,68 @@
         compiler_params=pltpu.CompilerParams(vmem_limit_bytes=32 * 2**20),
         name="cotangents",
     )(lens, *shards, *in_hbm(arrays))
+
+
+def narrow_body(
+    later_hbm, state_hbm, scalars_hbm, narrow_ref, later_ref, state_ref, scalars_ref, semaphores
+):
+    pairs = [(later_hbm, later_ref), (state_hbm, state_ref), (scalars_hbm, scalars_ref)]
+    copies = launch(pairs, semaphores, 0)
+    narrow_ref[...] = jnp.zeros(narrow_ref.shape, jnp.float32)
+    finish(copies)
+    objectives = range(OBJ)
+    head_spots = range(4)
+    across = later_ref[720:1232]
+    heads = later_ref[1232:1264]
+    low_on_probs = flat([later_ref[1264 + 16 * at : 1280 + 16 * at] for at in head_spots])
+    pulls = [scalars_ref[23 + obj : 24 + obj] for obj in objectives]
+    lead_turned = scalars_ref[48:49]
+
+    def block(array, head):
+        return array[:, 128 * head : 128 * head + 128]
+
+    def row_of(array, row):
+        return array[row : row + 1]
+
+    right_values = [low_on_probs * flat([pull] * 4) for pull in pulls]
+    jac_values = -product(tall(right_values), across, 0)
+    low_lead = [lane_sum(block(low_on_probs, head) * lead_turned) for head in head_spots]
+    jac_query = product(later_ref[0:320], state_ref[2048:2176], 0)
+    keys_rows = flat([later_ref[320 + 80 * at : 400 + 80 * at] for at in head_spots])
+    jac_keys = product(keys_rows, state_ref[0:512], 0)
+    jac_down = product(later_ref[640:720], unstack(state_ref[512:1024]), 0)
+    for obj in objectives:
+        own = slice(16 * obj, 16 * obj + 16)
+        own_values = jac_values[own]
+        for head in head_spots:
+            own_values += low_lead[head] * row_of(heads, 8 * head + obj)
+        blocks = [
+            jac_query[64 * obj + 16 * head : 64 * obj + 16 * head + 16]
+            for head in head_spots
+        ]
+        blocks += [block(jac_down, head)[own] for head in head_spots]
+        blocks += [jac_keys[own], own_values]
+        spots = [(0, 0), (0, 1), (0, 2), (0, 3), (5, 0), (5, 1), (5, 2), (5, 3)]
+        spots += [(10, 0), (10, 1)]
+        for (row, tile), part in zip(spots, blocks):
+            for half in range(2):
+                narrow_ref[tile, pl.ds(128 * half + row + obj, 8, stride=16), :] = (
+                    ADAPTER_SCALE * part[8 * half : 8 * half + 8]
+                )
+
+
+def narrow_rows(*arrays):
+    return pl.pallas_call(
+        narrow_body,
+        in_specs=[ANYWHERE] * 3,
+        out_specs=pl.BlockSpec(memory_space=pltpu.VMEM),
+        out_shape=pltpu.HBM((4, 256, 128), jnp.float32),
+        scratch_shapes=[pltpu.VMEM(array.shape, array.dtype) for array in arrays]
+        + [pltpu.SemaphoreType.DMA((3,))],
+        compiler_params=pltpu.CompilerParams(vmem_limit_bytes=16 * 2**20),
+        cost_estimate=pl.CostEstimate(flops=0, bytes_accessed=8_000_000, transcendentals=0),
+        name="narrow_rows",
+    )(*in_hbm(arrays))
 
 
 def jacobian_body(
@@ -1050,7 +1097,7 @@
     )
     out_pieces = lax.all_to_all(out_terms, "tensor", 0, 0)
     resid_own = hidden[0].astype(jnp.float32) + jnp.sum(out_pieces.astype(jnp.float32), 0)
-    resid, factors, narrow, scalars = cotangents(
+    resid, factors, later, scalars = cotangents(
         lens,
         gather_by_relays(resid_own.astype(jnp.bfloat16)),
         output_weight,
@@ -1059,6 +1106,7 @@
         *adapters,
     )
     factors = lax.all_to_all(factors.reshape(shards, 8 * OBJ, length), "tensor", 0, 0)
+    narrow = narrow_rows(later, state, scalars)
     payload = jacobian(factors, tokens, resid, heads, scalars, narrow)
     spread = lax.all_to_all(payload, "dp", 0, 0)
     jac = (

time: 195 us -> 194 us (level)
  waiting for transfers between devices: 56.5 us -> 53.7 us
  Pallas kernels: 32.5 us -> 35 us
    all_to_all x1, waiting for transfers between devices: 6.99 us -> 4.19 us  [local(): lax.all_to_all(factors.reshape(shards, 8 * OBJ, length), 'tensor', 0, 0)]
    pallas_call x0 -> x1, Pallas kernels: none -> 2.79 us  [narrow_rows(): pl.pallas_call(narrow_body, in_specs=[ANYWHERE] * 3, out_specs=pl.BlockSp...]
  transfers between devices with their start and end apart: 22 -> 22, of which waited for: 10 -> 10; matrix products, arithmetic and copies ran while one was open for 2% -> 2% of each run, Pallas kernels for 0% -> 1%
where the time goes in v9:
time: 194 us
  starting transfers between devices  61 us (31%)
  waiting for transfers between devices  53.7 us (28%)
  blocking collectives  36.2 us (19%)
  Pallas kernels  35 us (18%)
  local copies, waits for them, and re-layouts  3.22 us (2%)
  other arithmetic  2.67 us (1%)
    ppermute x18, starting transfers between devices, permute(): return lax.ppermute(array, 'tensor', pairs)  35.4 us
    all_to_all x1, waiting for transfers between devices, local(): out_pieces = lax.all_to_all(out_terms, 'tensor', 0, 0)  21.5 us
    all_to_all x2, blocking collectives, gather_by_exchange(): return lax.all_to_all(copies, axis, 0, 0)  18.8 us
    all_to_all x1, blocking collectives, local(): lax.all_to_all(jnp.broadcast_to(own_result[None], (half,) + own_result.sh...  17.4 us
    ppermute x18, waiting for transfers between devices, permute(): return lax.ppermute(array, 'tensor', pairs)  13.4 us
    all_to_all x1, waiting for transfers between devices, local(): spread = lax.all_to_all(payload, 'dp', 0, 0)  12.7 us
    pallas_call x1, Pallas kernels, forward(): pl.pallas_call(forward_body, in_specs=[ANYWHERE] * (len(shards) + len(arr...  11.2 us
    all_to_all x1, starting transfers between devices, local(): spread = lax.all_to_all(payload, 'dp', 0, 0)  9.64 us
  transfers between devices with their start and end apart: 22, of which 10 were waited for; matrix products, arithmetic and copies ran while one was open for 2% of the time, Pallas kernels for 1%

profile of v9, /device:TPU:1, one launch (start us, length us, event | category | flops | bytes accessed | tf_op | source)
XLA Modules:
  0.0 193.6 jit_solution(1120902220401161795)
XLA Ops:
  0.6 3.8 %collective-permute-start = (bf16[16,8192]{1,0:T(8,128)(2,1)}, bf16[16,8192]{1,0:T(8,128)(2,1)S(1)}, u32[]{:S(2)}, u32[]{:S(2)}) collective-permute-start(bf16[16,8192]{1,0:T(8,128)(2,1)} %bitcast.30), channel_id=1, source_target_pairs={{0,4},{1,5},{2,6},{3,7},{4,0},{5,1},{6,2},{7,3},{8,12},{9,13},{10,... | collective-permute-start | bytes 786440 | tf_op jit(solution)/shard_map/ppermute | solution.py:364
  4.5 1.6 collective-permute-start.1
  6.1 2.1 %collective-permute-start.2 = (bf16[16,8192]{1,0:T(8,128)(2,1)}, bf16[16,8192]{1,0:T(8,128)(2,1)S(1)}, u32[]{:S(2)}, u32[]{:S(2)}) collective-permute-start(bf16[16,8192]{1,0:T(8,128)(2,1)} %bitcast.32), channel_id=1, source_target_pairs={{0,3},{1,0},{2,1},{3,2},{4,7},{5,4},{6,5},{7,6},{8,11},{9,8},{10,9... | collective-permute-start | bytes 786440 | tf_op jit(solution)/shard_map/ppermute | solution.py:364
  8.2 2.2 %collective-permute-done.shard_1 = bf16[16,8192]{1,0:T(8,128)(2,1)S(1)} collective-permute-done((bf16[16,8192]{1,0:T(8,128)(2,1)}, bf16[16,8192]{1,0:T(8,128)(2,1)S(1)}, u32[]{:S(2)}, u32[]{:S(2)}) %collective-permute-start) | collective-permute-done | bytes 262176 | tf_op jit(solution)/shard_map/ppermute | solution.py:364
  10.4 1.6 collective-permute-start.3
  12.1 2.1 %collective-permute-start.4 = (bf16[16,8192]{1,0:T(8,128)(2,1)S(1)}, bf16[16,8192]{1,0:T(8,128)(2,1)S(1)}, u32[]{:S(2)}, u32[]{:S(2)}) collective-permute-start(bf16[16,8192]{1,0:T(8,128)(2,1)S(1)} %collective-permute-done.shard_1), channel_id=1, source_target_pairs={{0,3},{1,0},{2,1},{3,2},{4,7},{5,4},{6,5},{7,6},{8,11},{9,8},{10,9... | collective-permute-start | bytes 786440 | tf_op jit(solution)/shard_map/ppermute | solution.py:364
  14.3 2.7 %collective-permute-start.6 = (bf16[16,4096]{1,0:T(8,128)(2,1)S(1)}, bf16[16,4096]{1,0:T(8,128)(2,1)S(1)}, u32[]{:S(2)}, u32[]{:S(2)}) collective-permute-start(bf16[16,4096]{1,0:T(8,128)(2,1)S(1)} %slice.43), channel_id=1, source_target_pairs={{0,3},{1,0},{2,1},{3,2},{4,7},{5,4},{6,5},{7,6},{8,11},{9,8},{10,9... | collective-permute-start | bytes 393224 | tf_op jit(solution)/shard_map/ppermute | solution.py:364
  17.0 2.2 %collective-permute-done.3.shard_4 = bf16[16,8192]{1,0:T(8,128)(2,1)S(1)} collective-permute-done((bf16[16,8192]{1,0:T(8,128)(2,1)S(1)}, bf16[16,8192]{1,0:T(8,128)(2,1)S(1)}, u32[]{:S(2)}, u32[]{:S(2)}) %collective-permute-start.3) | collective-permute-done | bytes 262176 | tf_op jit(solution)/shard_map/ppermute | solution.py:364
  19.4 2.7 %collective-permute-start.8 = (bf16[16,4096]{1,0:T(8,128)(2,1)S(1)}, bf16[16,4096]{1,0:T(8,128)(2,1)S(1)}, u32[]{:S(2)}, u32[]{:S(2)}) collective-permute-start(bf16[16,4096]{1,0:T(8,128)(2,1)S(1)} %slice.45), channel_id=1, source_target_pairs={{0,3},{1,0},{2,1},{3,2},{4,7},{5,4},{6,5},{7,6},{8,11},{9,8},{10,9... | collective-permute-start | bytes 393224 | tf_op jit(solution)/shard_map/ppermute | solution.py:364
  22.1 2.9 %collective-permute-done.7.shard_8 = bf16[16,4096]{1,0:T(8,128)(2,1)S(1)} collective-permute-done((bf16[16,4096]{1,0:T(8,128)(2,1)S(1)}, bf16[16,4096]{1,0:T(8,128)(2,1)S(1)}, u32[]{:S(2)}, u32[]{:S(2)}) %collective-permute-start.7) | collective-permute-done | bytes 131104 | tf_op jit(solution)/shard_map/ppermute | solution.py:364
  25.0 11.2 %forward.1 = (bf16[128,8192]{1,0:T(8,128)(2,1)}, bf16[8,16,8192]{2,1,0:T(8,128)(2,1)}, f32[2368,128]{1,0:T(8,128)}) custom-call(bf16[16,8192]{1,0:T(8,128)(2,1)} %bitcast.33, bf16[16,8192]{1,0:T(8,128)(2,1)S(1)} %collective-permute-done.shard_1, bf16[16,8192]{1,0:T(8,128)(2,1)S(1)} %collective-permute-done.1.shard_2, ...), custom_call_target="tpu_custom_call" | custom-call | tf_op jit(solution)/shard_map/forward/pallas_call | solution.py:569
  36.2 6.6 %all-to-all-start = ((bf16[8,16,8192]{2,1,0:T(8,128)(2,1)}), bf16[8,16,8192]{2,1,0:T(8,128)(2,1)S(1)}, u32[]{:S(2)}, u32[]{:S(2)}) async-start(bf16[8,16,8192]{2,1,0:T(8,128)(2,1)} %get-tuple-element.19), calls=%async_computation | async-start | bytes 4194304 | tf_op jit(solution)/shard_map/all_to_all | solution.py:1098
  42.9 21.5 %all-to-all-done = bf16[8,16,8192]{2,1,0:T(8,128)(2,1)S(1)} async-done(((bf16[8,16,8192]{2,1,0:T(8,128)(2,1)}), bf16[8,16,8192]{2,1,0:T(8,128)(2,1)S(1)}, u32[]{:S(2)}, u32[]{:S(2)}) %all-to-all-start) | async-done | bytes 2097184 | tf_op jit(solution)/shard_map/all_to_all | solution.py:1098
  64.4 0.3 convert_reduce_fusion
  64.7 7.2 %collective-permute-start.9 = (bf16[16,8192]{1,0:T(8,128)(2,1)S(1)}, bf16[16,8192]{1,0:T(8,128)(2,1)S(1)}, u32[]{:S(2)}, u32[]{:S(2)}) collective-permute-start(bf16[16,8192]{1,0:T(8,128)(2,1)S(1)} %add_convert_fusion.shard_0), channel_id=1, source_target_pairs={{0,4},{1,5},{2,6},{3,7},{4,0},{5,1},{6,2},{7,3},{8,12},{9,13},{10,... | collective-permute-start | bytes 786440 | tf_op jit(solution)/shard_map/ppermute | solution.py:364
  71.9 0.9 maximum_maximum_fusion.side_hbm
  72.9 1.0 collective-permute-start.10
  74.0 1.7 collective-permute-start.11
  75.7 1.0 collective-permute-done.9.shard_1
  76.7 1.4 collective-permute-start.12
  78.0 1.3 collective-permute-start.13
  79.4 1.0 fusion.2.heads_hbm
  81.1 0.2 collective-permute-start.14
  81.3 2.6 %collective-permute-start.15 = (bf16[16,4096]{1,0:T(8,128)(2,1)S(1)}, bf16[16,4096]{1,0:T(8,128)(2,1)S(1)}, u32[]{:S(2)}, u32[]{:S(2)}) collective-permute-start(bf16[16,4096]{1,0:T(8,128)(2,1)S(1)} %slice.47), channel_id=1, source_target_pairs={{0,3},{1,0},{2,1},{3,2},{4,7},{5,4},{6,5},{7,6},{8,11},{9,8},{10,9... | collective-permute-start | bytes 393224 | tf_op jit(solution)/shard_map/ppermute | solution.py:364
  83.9 2.5 %collective-permute-done.12.shard_4 = bf16[16,8192]{1,0:T(8,128)(2,1)S(1)} collective-permute-done((bf16[16,8192]{1,0:T(8,128)(2,1)S(1)}, bf16[16,8192]{1,0:T(8,128)(2,1)S(1)}, u32[]{:S(2)}, u32[]{:S(2)}) %collective-permute-start.12) | collective-permute-done | bytes 262176 | tf_op jit(solution)/shard_map/ppermute | solution.py:364
  86.4 0.3 collective-permute-start.16
  86.7 2.7 %collective-permute-start.17 = (bf16[16,4096]{1,0:T(8,128)(2,1)S(1)}, bf16[16,4096]{1,0:T(8,128)(2,1)S(1)}, u32[]{:S(2)}, u32[]{:S(2)}) collective-permute-start(bf16[16,4096]{1,0:T(8,128)(2,1)S(1)} %slice.49), channel_id=1, source_target_pairs={{0,3},{1,0},{2,1},{3,2},{4,7},{5,4},{6,5},{7,6},{8,11},{9,8},{10,9... | collective-permute-start | bytes 393224 | tf_op jit(solution)/shard_map/ppermute | solution.py:364
  89.5 2.6 %collective-permute-done.16.shard_8 = bf16[16,4096]{1,0:T(8,128)(2,1)S(1)} collective-permute-done((bf16[16,4096]{1,0:T(8,128)(2,1)S(1)}, bf16[16,4096]{1,0:T(8,128)(2,1)S(1)}, u32[]{:S(2)}, u32[]{:S(2)}) %collective-permute-start.16) | collective-permute-done | bytes 131104 | tf_op jit(solution)/shard_map/ppermute | solution.py:364
  92.1 9.6 %cotangents.1 = (bf16[128,8192]{1,0:T(8,128)(2,1)}, f32[320,128]{1,0:T(8,128)}, f32[1328,128]{1,0:T(8,128)}, f32[88,128]{1,0:T(8,128)}) custom-call(s32[1]{0:T(128)S(6)} %copy.31.lens_ref, bf16[16,8192]{1,0:T(8,128)(2,1)S(1)} %add_convert_fusion.shard_0, bf16[16,8192]{1,0:T(8,128)(2,1)S(1)} %collective-permute-done.9.shard_1, ...), custom_call_target="tpu_custom_call" | custom-call | tf_op jit(solution)/shard_map/cotangents/pallas_call | solution.py:857
  101.7 6.1 %all-to-all-start.1 = ((f32[8,40,128]{2,1,0:T(8,128)}), f32[8,40,128]{2,1,0:T(8,128)S(1)}, u32[]{:S(2)}, u32[]{:S(2)}) async-start(f32[8,40,128]{2,1,0:T(8,128)} %bitcast.39), calls=%async_computation.1 | async-start | bytes 327680 | tf_op jit(solution)/shard_map/all_to_all | solution.py:1108
  107.9 2.8 %narrow_rows.1.narrow_hbm = f32[4,256,128]{2,1,0:T(8,128)} custom-call(f32[1328,128]{1,0:T(8,128)} %get-tuple-element.25.later_hbm, f32[2368,128]{1,0:T(8,128)} %get-tuple-element.20.state_hbm, f32[88,128]{1,0:T(8,128)} %get-tuple-element.24.scalars_hbm), custom_call_target="tpu_custom_call" | custom-call | bytes 8000000 | tf_op jit(solution)/shard_map/narrow_rows/pallas_call | solution.py:924
  110.7 4.2 %all-to-all-done.1.factors_hbm = f32[8,40,128]{2,1,0:T(8,128)S(1)} async-done(((f32[8,40,128]{2,1,0:T(8,128)}), f32[8,40,128]{2,1,0:T(8,128)S(1)}, u32[]{:S(2)}, u32[]{:S(2)}) %all-to-all-start.1) | async-done | bytes 163872 | tf_op jit(solution)/shard_map/all_to_all | solution.py:1108
  114.8 3.9 %jacobian.1 = bf16[16,56,512]{2,1,0:T(8,128)(2,1)} custom-call(f32[8,40,128]{2,1,0:T(8,128)S(1)} %all-to-all-done.1.factors_hbm, bf16[128,8192]{1,0:T(8,128)(2,1)} %get-tuple-element.22.tokens_hbm, bf16[128,8192]{1,0:T(8,128)(2,1)} %get-tuple-element.23.resid_hbm, bf16[48,8192]{1,0:T(8,128)(2,1)} %fusion.2.heads_hbm, ...), custom_call_target="tpu_custom_call" | custom-call | tf_op jit(solution)/shard_map/jacobian/pallas_call | solution.py:1018
  118.8 9.6 %all-to-all-start.2 = ((bf16[16,56,512]{2,1,0:T(8,128)(2,1)}), bf16[16,56,512]{2,1,0:T(8,128)(2,1)S(1)}, u32[]{:S(2)}, u32[]{:S(2)}) async-start(bf16[16,56,512]{2,1,0:T(8,128)(2,1)} %jacobian.1), calls=%async_computation.2 | async-start | bytes 1835008 | tf_op jit(solution)/shard_map/all_to_all | solution.py:1111
  128.5 0.6 gather_fusion
  129.5 0.7 slice.39.rewards_ref
  130.2 12.7 %all-to-all-done.2 = bf16[16,56,512]{2,1,0:T(8,128)(2,1)S(1)} async-done(((bf16[16,56,512]{2,1,0:T(8,128)(2,1)}), bf16[16,56,512]{2,1,0:T(8,128)(2,1)S(1)}, u32[]{:S(2)}, u32[]{:S(2)}) %all-to-all-start.2) | async-done | bytes 917536 | tf_op jit(solution)/shard_map/all_to_all | solution.py:1111
  142.9 0.3 copy.27
  143.1 0.5 copy.28
  143.7 0.6 copy.30
  144.3 2.3 %gram.1 = f32[16,128]{1,0:T(8,128)S(1)} custom-call(bf16[80,5632]{1,0:T(8,128)(2,1)S(1)} %bitcast.23, f32[48,128]{1,0:T(8,128)S(1)} %pad.14.pairs_ref, f32[8,128]{1,0:T(8,128)S(1)} %slice.39.rewards_ref, f32[3,16,8192]{2,1,0:T(8,128)} %bitcast.25, f32[16,4096]{1,0:T(8,128)} %bq_ref.1, f32[2,16,1024]{2,1,0:T(8,128)} %bkv_ref.1, f32[16,4096]{1,0:T(8,128)} %bitcast.34, ...), custom_call_target="tpu_custom_call" | custom-call | tf_op jit(solution)/shard_map/gram/pallas_call | solution.py:1138
  146.6 9.3 %all_to_all.30 = f32[16,16,128]{2,1,0:T(8,128)S(1)} all-to-all(f32[16,16,128]{2,1,0:T(8,128)S(1)} %broadcast_in_dim.24), channel_id=1, replica_groups=mesh['dp'=16,'tensor'=8] {'dp'}, dimensions={0} | all-to-all | bytes 262144 | tf_op jit(solution)/shard_map/all_to_all | solution.py:45
  155.9 9.6 %all_to_all.31.packed_ref = f32[8,16,128]{2,1,0:T(8,128)S(1)} all-to-all(f32[8,16,128]{2,1,0:T(8,128)S(1)} %broadcast_in_dim.25), channel_id=1, replica_groups=mesh['dp'=16,'tensor'=8] {'tensor'}, dimensions={0} | all-to-all | bytes 131072 | tf_op jit(solution)/shard_map/all_to_all | solution.py:45
  165.5 0.9 lanczos.1
  166.4 17.4 %all_to_all.32.own_ref = bf16[64,8,768]{2,1,0:T(8,128)(2,1)S(1)} all-to-all(bf16[64,8,768]{2,1,0:T(8,128)(2,1)S(1)} %broadcast_in_dim.26), channel_id=1, replica_groups={{0,1,2,3,4,5,6,7,16,17,18,19,20,21,22,23,32,33,34,35,36,37,38,39,48,49,..., dimensions={0} | all-to-all | bytes 1572864 | tf_op jit(solution)/shard_map/all_to_all | solution.py:1171
  183.8 3.4 %collective-permute-start.18 = (bf16[64,8,768]{2,1,0:T(8,128)(2,1)S(1)}, bf16[64,8,768]{2,1,0:T(8,128)(2,1)S(1)}, u32[]{:S(2)}, u32[]{:S(2)}) collective-permute-start(bf16[64,8,768]{2,1,0:T(8,128)(2,1)S(1)} %all_to_all.32.own_ref), channel_id=1, source_target_pairs={{0,8},{8,0},{16,24},{24,16},{32,40},{40,32},{48,56},{56,48},{64,72... | collective-permute-start | bytes 2359304 | tf_op jit(solution)/shard_map/ppermute | solution.py:1178
  187.2 1.9 collective-permute-done.18.other_ref
  189.1 4.4 %assemble.1 = (f32[3,16,8192]{2,1,0:T(8,128)}, f32[16,4096]{1,0:T(8,128)}, f32[2,16,1024]{2,1,0:T(8,128)}, f32[16,4096]{1,0:T(8,128)}, f32[16,8192]{1,0:T(8,128)}) custom-call(f32[1,128]{1,0:T(1,128)S(1)} %get-tuple-element.26.part_ref, bf16[64,8,768]{2,1,0:T(8,128)(2,1)S(1)} %all_to_all.32.own_ref, ...), custom_call_target="tpu_custom_call" | custom-call | tf_op jit(solution)/shard_map/assemble/pallas_call | solution.py:1039
  (49 shorter events, 1.2 us)
Async XLA Ops:
  0.6 9.8 %collective-permute-start = (bf16[16,8192]{1,0:T(8,128)(2,1)}, bf16[16,8192]{1,0:T(8,128)(2,1)S(1)}, u32[]{:S(2)}, u32[]{:S(2)}) collective-permute-start(bf16[16,8192]{1,0:T(8,128)(2,1)} %bitcast.30), channel_id=1, source_target_pairs={{0,4},{1,5},{2,6},{3,7},{4,0},{5,1},{6,2},{7,3},{8,12},{9,13},{10,... | collective-permute-start | bytes 786440 | tf_op jit(solution)/shard_map/ppermute | solution.py:364
  4.5 9.7 %collective-permute-start.1 = (bf16[16,8192]{1,0:T(8,128)(2,1)}, bf16[16,8192]{1,0:T(8,128)(2,1)S(1)}, u32[]{:S(2)}, u32[]{:S(2)}) collective-permute-start(bf16[16,8192]{1,0:T(8,128)(2,1)} %bitcast.31), channel_id=1, source_target_pairs={{0,1},{1,2},{2,3},{3,0},{4,5},{5,6},{6,7},{7,4},{8,9},{9,10},{10,1... | collective-permute-start | bytes 786440 | tf_op jit(solution)/shard_map/ppermute | solution.py:364
  6.1 8.2 %collective-permute-start.2 = (bf16[16,8192]{1,0:T(8,128)(2,1)}, bf16[16,8192]{1,0:T(8,128)(2,1)S(1)}, u32[]{:S(2)}, u32[]{:S(2)}) collective-permute-start(bf16[16,8192]{1,0:T(8,128)(2,1)} %bitcast.32), channel_id=1, source_target_pairs={{0,3},{1,0},{2,1},{3,2},{4,7},{5,4},{6,5},{7,6},{8,11},{9,8},{10,9... | collective-permute-start | bytes 786440 | tf_op jit(solution)/shard_map/ppermute | solution.py:364
  10.4 8.8 %collective-permute-start.3 = (bf16[16,8192]{1,0:T(8,128)(2,1)S(1)}, bf16[16,8192]{1,0:T(8,128)(2,1)S(1)}, u32[]{:S(2)}, u32[]{:S(2)}) collective-permute-start(bf16[16,8192]{1,0:T(8,128)(2,1)S(1)} %collective-permute-done.shard_1), channel_id=1, source_target_pairs={{0,1},{1,2},{2,3},{3,0},{4,5},{5,6},{6,7},{7,4},{8,9},{9,10},{10,1... | collective-permute-start | bytes 786440 | tf_op jit(solution)/shard_map/ppermute | solution.py:364
  12.1 7.3 %collective-permute-start.4 = (bf16[16,8192]{1,0:T(8,128)(2,1)S(1)}, bf16[16,8192]{1,0:T(8,128)(2,1)S(1)}, u32[]{:S(2)}, u32[]{:S(2)}) collective-permute-start(bf16[16,8192]{1,0:T(8,128)(2,1)S(1)} %collective-permute-done.shard_1), channel_id=1, source_target_pairs={{0,3},{1,0},{2,1},{3,2},{4,7},{5,4},{6,5},{7,6},{8,11},{9,8},{10,9... | collective-permute-start | bytes 786440 | tf_op jit(solution)/shard_map/ppermute | solution.py:364
  14.2 7.9 %collective-permute-start.5 = (bf16[16,4096]{1,0:T(8,128)(2,1)S(1)}, bf16[16,4096]{1,0:T(8,128)(2,1)S(1)}, u32[]{:S(2)}, u32[]{:S(2)}) collective-permute-start(bf16[16,4096]{1,0:T(8,128)(2,1)S(1)} %slice.42), channel_id=1, source_target_pairs={{0,1},{1,2},{2,3},{3,0},{4,5},{5,6},{6,7},{7,4},{8,9},{9,10},{10,1... | collective-permute-start | bytes 393224 | tf_op jit(solution)/shard_map/ppermute | solution.py:364
  14.3 7.8 %collective-permute-start.6 = (bf16[16,4096]{1,0:T(8,128)(2,1)S(1)}, bf16[16,4096]{1,0:T(8,128)(2,1)S(1)}, u32[]{:S(2)}, u32[]{:S(2)}) collective-permute-start(bf16[16,4096]{1,0:T(8,128)(2,1)S(1)} %slice.43), channel_id=1, source_target_pairs={{0,3},{1,0},{2,1},{3,2},{4,7},{5,4},{6,5},{7,6},{8,11},{9,8},{10,9... | collective-permute-start | bytes 393224 | tf_op jit(solution)/shard_map/ppermute | solution.py:364
  19.3 5.7 %collective-permute-start.7 = (bf16[16,4096]{1,0:T(8,128)(2,1)S(1)}, bf16[16,4096]{1,0:T(8,128)(2,1)S(1)}, u32[]{:S(2)}, u32[]{:S(2)}) collective-permute-start(bf16[16,4096]{1,0:T(8,128)(2,1)S(1)} %slice.44), channel_id=1, source_target_pairs={{0,1},{1,2},{2,3},{3,0},{4,5},{5,6},{6,7},{7,4},{8,9},{9,10},{10,1... | collective-permute-start | bytes 393224 | tf_op jit(solution)/shard_map/ppermute | solution.py:364
  19.4 5.6 %collective-permute-start.8 = (bf16[16,4096]{1,0:T(8,128)(2,1)S(1)}, bf16[16,4096]{1,0:T(8,128)(2,1)S(1)}, u32[]{:S(2)}, u32[]{:S(2)}) collective-permute-start(bf16[16,4096]{1,0:T(8,128)(2,1)S(1)} %slice.45), channel_id=1, source_target_pairs={{0,3},{1,0},{2,1},{3,2},{4,7},{5,4},{6,5},{7,6},{8,11},{9,8},{10,9... | collective-permute-start | bytes 393224 | tf_op jit(solution)/shard_map/ppermute | solution.py:364
  36.2 28.2 %all-to-all-start = ((bf16[8,16,8192]{2,1,0:T(8,128)(2,1)}), bf16[8,16,8192]{2,1,0:T(8,128)(2,1)S(1)}, u32[]{:S(2)}, u32[]{:S(2)}) async-start(bf16[8,16,8192]{2,1,0:T(8,128)(2,1)} %get-tuple-element.19), calls=%async_computation | async-start | bytes 4194304 | tf_op jit(solution)/shard_map/all_to_all | solution.py:1098
  42.8 21.9 %copy-start.1 = (bf16[1,16,8192]{2,1,0:T(8,128)(2,1)S(1)}, bf16[1,16,8192]{2,1,0:T(8,128)(2,1)}, u32[]{:S(2)}) copy-start(bf16[1,16,8192]{2,1,0:T(8,128)(2,1)} %param.17) | copy-start | bytes 786436
  42.8 29.2 %copy-start = (bf16[16,8192]{1,0:T(8,128)(2,1)S(1)}, bf16[16,8192]{1,0:T(8,128)(2,1)}, u32[]{:S(2)}) copy-start(bf16[16,8192]{1,0:T(8,128)(2,1)} %up_output_hbm.1) | copy-start | bytes 786436
  42.8 29.2 %copy-start.2 = (bf16[8192,5]{0,1:T(8,128)(2,1)S(1)}, bf16[8192,5]{0,1:T(8,128)(2,1)}, u32[]{:S(2)}) copy-start(bf16[8192,5]{0,1:T(8,128)(2,1)} %param.21) | copy-start | bytes 245764
  64.7 24.7 %copy-start.3 = (s32[16]{0:T(128)S(1)}, s32[16]{0:T(128)}, u32[]{:S(2)}) copy-start(s32[16]{0:T(128)} %param.23) | copy-start | bytes 196
  64.7 12.0 %collective-permute-start.9 = (bf16[16,8192]{1,0:T(8,128)(2,1)S(1)}, bf16[16,8192]{1,0:T(8,128)(2,1)S(1)}, u32[]{:S(2)}, u32[]{:S(2)}) collective-permute-start(bf16[16,8192]{1,0:T(8,128)(2,1)S(1)} %add_convert_fusion.shard_0), channel_id=1, source_target_pairs={{0,4},{1,5},{2,6},{3,7},{4,0},{5,1},{6,2},{7,3},{8,12},{9,13},{10,... | collective-permute-start | bytes 786440 | tf_op jit(solution)/shard_map/ppermute | solution.py:364
  72.9 8.1 %collective-permute-start.10 = (bf16[16,8192]{1,0:T(8,128)(2,1)S(1)}, bf16[16,8192]{1,0:T(8,128)(2,1)S(1)}, u32[]{:S(2)}, u32[]{:S(2)}) collective-permute-start(bf16[16,8192]{1,0:T(8,128)(2,1)S(1)} %add_convert_fusion.shard_0), channel_id=1, source_target_pairs={{0,1},{1,2},{2,3},{3,0},{4,5},{5,6},{6,7},{7,4},{8,9},{9,10},{10,1... | collective-permute-start | bytes 786440 | tf_op jit(solution)/shard_map/ppermute | solution.py:364
  74.0 7.3 %collective-permute-start.11 = (bf16[16,8192]{1,0:T(8,128)(2,1)S(1)}, bf16[16,8192]{1,0:T(8,128)(2,1)S(1)}, u32[]{:S(2)}, u32[]{:S(2)}) collective-permute-start(bf16[16,8192]{1,0:T(8,128)(2,1)S(1)} %add_convert_fusion.shard_0), channel_id=1, source_target_pairs={{0,3},{1,0},{2,1},{3,2},{4,7},{5,4},{6,5},{7,6},{8,11},{9,8},{10,9... | collective-permute-start | bytes 786440 | tf_op jit(solution)/shard_map/ppermute | solution.py:364
  76.7 9.7 %collective-permute-start.12 = (bf16[16,8192]{1,0:T(8,128)(2,1)S(1)}, bf16[16,8192]{1,0:T(8,128)(2,1)S(1)}, u32[]{:S(2)}, u32[]{:S(2)}) collective-permute-start(bf16[16,8192]{1,0:T(8,128)(2,1)S(1)} %collective-permute-done.9.shard_1), channel_id=1, source_target_pairs={{0,1},{1,2},{2,3},{3,0},{4,5},{5,6},{6,7},{7,4},{8,9},{9,10},{10,1... | collective-permute-start | bytes 786440 | tf_op jit(solution)/shard_map/ppermute | solution.py:364
  78.0 8.6 %collective-permute-start.13 = (bf16[16,8192]{1,0:T(8,128)(2,1)S(1)}, bf16[16,8192]{1,0:T(8,128)(2,1)S(1)}, u32[]{:S(2)}, u32[]{:S(2)}) collective-permute-start(bf16[16,8192]{1,0:T(8,128)(2,1)S(1)} %collective-permute-done.9.shard_1), channel_id=1, source_target_pairs={{0,3},{1,0},{2,1},{3,2},{4,7},{5,4},{6,5},{7,6},{8,11},{9,8},{10,9... | collective-permute-start | bytes 786440 | tf_op jit(solution)/shard_map/ppermute | solution.py:364
  81.1 8.4 %collective-permute-start.14 = (bf16[16,4096]{1,0:T(8,128)(2,1)S(1)}, bf16[16,4096]{1,0:T(8,128)(2,1)S(1)}, u32[]{:S(2)}, u32[]{:S(2)}) collective-permute-start(bf16[16,4096]{1,0:T(8,128)(2,1)S(1)} %slice.46), channel_id=1, source_target_pairs={{0,1},{1,2},{2,3},{3,0},{4,5},{5,6},{6,7},{7,4},{8,9},{9,10},{10,1... | collective-permute-start | bytes 393224 | tf_op jit(solution)/shard_map/ppermute | solution.py:364
  81.3 8.2 %collective-permute-start.15 = (bf16[16,4096]{1,0:T(8,128)(2,1)S(1)}, bf16[16,4096]{1,0:T(8,128)(2,1)S(1)}, u32[]{:S(2)}, u32[]{:S(2)}) collective-permute-start(bf16[16,4096]{1,0:T(8,128)(2,1)S(1)} %slice.47), channel_id=1, source_target_pairs={{0,3},{1,0},{2,1},{3,2},{4,7},{5,4},{6,5},{7,6},{8,11},{9,8},{10,9... | collective-permute-start | bytes 393224 | tf_op jit(solution)/shard_map/ppermute | solution.py:364
  86.4 5.7 %collective-permute-start.16 = (bf16[16,4096]{1,0:T(8,128)(2,1)S(1)}, bf16[16,4096]{1,0:T(8,128)(2,1)S(1)}, u32[]{:S(2)}, u32[]{:S(2)}) collective-permute-start(bf16[16,4096]{1,0:T(8,128)(2,1)S(1)} %slice.48), channel_id=1, source_target_pairs={{0,1},{1,2},{2,3},{3,0},{4,5},{5,6},{6,7},{7,4},{8,9},{9,10},{10,1... | collective-permute-start | bytes 393224 | tf_op jit(solution)/shard_map/ppermute | solution.py:364
  86.7 5.4 %collective-permute-start.17 = (bf16[16,4096]{1,0:T(8,128)(2,1)S(1)}, bf16[16,4096]{1,0:T(8,128)(2,1)S(1)}, u32[]{:S(2)}, u32[]{:S(2)}) collective-permute-start(bf16[16,4096]{1,0:T(8,128)(2,1)S(1)} %slice.49), channel_id=1, source_target_pairs={{0,3},{1,0},{2,1},{3,2},{4,7},{5,4},{6,5},{7,6},{8,11},{9,8},{10,9... | collective-permute-start | bytes 393224 | tf_op jit(solution)/shard_map/ppermute | solution.py:364
  101.7 13.2 %all-to-all-start.1 = ((f32[8,40,128]{2,1,0:T(8,128)}), f32[8,40,128]{2,1,0:T(8,128)S(1)}, u32[]{:S(2)}, u32[]{:S(2)}) async-start(f32[8,40,128]{2,1,0:T(8,128)} %bitcast.39), calls=%async_computation.1 | async-start | bytes 327680 | tf_op jit(solution)/shard_map/all_to_all | solution.py:1108
  118.8 24.1 %all-to-all-start.2 = ((bf16[16,56,512]{2,1,0:T(8,128)(2,1)}), bf16[16,56,512]{2,1,0:T(8,128)(2,1)S(1)}, u32[]{:S(2)}, u32[]{:S(2)}) async-start(bf16[16,56,512]{2,1,0:T(8,128)(2,1)} %jacobian.1), calls=%async_computation.2 | async-start | bytes 1835008 | tf_op jit(solution)/shard_map/all_to_all | solution.py:1111
  183.8 5.3 %collective-permute-start.18 = (bf16[64,8,768]{2,1,0:T(8,128)(2,1)S(1)}, bf16[64,8,768]{2,1,0:T(8,128)(2,1)S(1)}, u32[]{:S(2)}, u32[]{:S(2)}) collective-permute-start(bf16[64,8,768]{2,1,0:T(8,128)(2,1)S(1)} %all_to_all.32.own_ref), channel_id=1, source_target_pairs={{0,8},{8,0},{16,24},{24,16},{32,40},{40,32},{48,56},{56,48},{64,72... | collective-permute-start | bytes 2359304 | tf_op jit(solution)/shard_map/ppermute | solution.py:1178

commit v10 on v9

--- a/solution.py
+++ b/solution.py
@@ -1096,6 +1096,7 @@
         *adapters,
     )
     out_pieces = lax.all_to_all(out_terms, "tensor", 0, 0)
+    out_pieces, side, heads = lax.optimization_barrier((out_pieces, side, heads))
     resid_own = hidden[0].astype(jnp.float32) + jnp.sum(out_pieces.astype(jnp.float32), 0)
     resid, factors, later, scalars = cotangents(
         lens,

time: 194 us -> 195 us (level)
  transfers between devices with their start and end apart: 22 -> 22, of which waited for: 10 -> 10; matrix products, arithmetic and copies ran while one was open for 2% -> 3% of each run, Pallas kernels for 1% -> 1%
where the time goes in v10:
time: 195 us; the launch traced here: 194 us
  starting transfers between devices  62.4 us (32%)
  waiting for transfers between devices  51.8 us (27%)
  blocking collectives  36.2 us (19%)
  Pallas kernels  35 us (18%)
  local copies, waits for them, and re-layouts  4.12 us (2%)
  other arithmetic  2.67 us (1%)
    ppermute x18, starting transfers between devices, permute(): return lax.ppermute(array, 'tensor', pairs)  35.3 us
    all_to_all x1, waiting for transfers between devices, local(): out_pieces = lax.all_to_all(out_terms, 'tensor', 0, 0)  19.6 us
    all_to_all x2, blocking collectives, gather_by_exchange(): return lax.all_to_all(copies, axis, 0, 0)  18.8 us
    all_to_all x1, blocking collectives, local(): lax.all_to_all(jnp.broadcast_to(own_result[None], (half,) + own_result.sh...  17.4 us
    ppermute x18, waiting for transfers between devices, permute(): return lax.ppermute(array, 'tensor', pairs)  13.5 us
    all_to_all x1, waiting for transfers between devices, local(): spread = lax.all_to_all(payload, 'dp', 0, 0)  12.7 us
    pallas_call x1, Pallas kernels, forward(): pl.pallas_call(forward_body, in_specs=[ANYWHERE] * (len(shards) + len(arr...  11.2 us
    all_to_all x1, starting transfers between devices, local(): spread = lax.all_to_all(payload, 'dp', 0, 0)  10.6 us
  transfers between devices with their start and end apart: 22, of which 10 were waited for; matrix products, arithmetic and copies ran while one was open for 3% of the time, Pallas kernels for 1%

profile of v10, /device:TPU:1, one launch (start us, length us, event | category | flops | bytes accessed | tf_op | source)
XLA Modules:
  0.0 194.0 jit_solution(14248889438544110947)
XLA Ops:
  0.6 3.8 %collective-permute-start = (bf16[16,8192]{1,0:T(8,128)(2,1)}, bf16[16,8192]{1,0:T(8,128)(2,1)S(1)}, u32[]{:S(2)}, u32[]{:S(2)}) collective-permute-start(bf16[16,8192]{1,0:T(8,128)(2,1)} %bitcast.30), channel_id=1, source_target_pairs={{0,4},{1,5},{2,6},{3,7},{4,0},{5,1},{6,2},{7,3},{8,12},{9,13},{10,... | collective-permute-start | bytes 786440 | tf_op jit(solution)/shard_map/ppermute | solution.py:364
  4.5 1.6 collective-permute-start.1
  6.1 2.1 %collective-permute-start.2 = (bf16[16,8192]{1,0:T(8,128)(2,1)}, bf16[16,8192]{1,0:T(8,128)(2,1)S(1)}, u32[]{:S(2)}, u32[]{:S(2)}) collective-permute-start(bf16[16,8192]{1,0:T(8,128)(2,1)} %bitcast.32), channel_id=1, source_target_pairs={{0,3},{1,0},{2,1},{3,2},{4,7},{5,4},{6,5},{7,6},{8,11},{9,8},{10,9... | collective-permute-start | bytes 786440 | tf_op jit(solution)/shard_map/ppermute | solution.py:364
  8.2 2.2 %collective-permute-done.shard_1 = bf16[16,8192]{1,0:T(8,128)(2,1)S(1)} collective-permute-done((bf16[16,8192]{1,0:T(8,128)(2,1)}, bf16[16,8192]{1,0:T(8,128)(2,1)S(1)}, u32[]{:S(2)}, u32[]{:S(2)}) %collective-permute-start) | collective-permute-done | bytes 262176 | tf_op jit(solution)/shard_map/ppermute | solution.py:364
  10.4 1.6 collective-permute-start.3
  12.1 2.1 %collective-permute-start.4 = (bf16[16,8192]{1,0:T(8,128)(2,1)S(1)}, bf16[16,8192]{1,0:T(8,128)(2,1)S(1)}, u32[]{:S(2)}, u32[]{:S(2)}) collective-permute-start(bf16[16,8192]{1,0:T(8,128)(2,1)S(1)} %collective-permute-done.shard_1), channel_id=1, source_target_pairs={{0,3},{1,0},{2,1},{3,2},{4,7},{5,4},{6,5},{7,6},{8,11},{9,8},{10,9... | collective-permute-start | bytes 786440 | tf_op jit(solution)/shard_map/ppermute | solution.py:364
  14.3 2.7 %collective-permute-start.6 = (bf16[16,4096]{1,0:T(8,128)(2,1)S(1)}, bf16[16,4096]{1,0:T(8,128)(2,1)S(1)}, u32[]{:S(2)}, u32[]{:S(2)}) collective-permute-start(bf16[16,4096]{1,0:T(8,128)(2,1)S(1)} %slice.43), channel_id=1, source_target_pairs={{0,3},{1,0},{2,1},{3,2},{4,7},{5,4},{6,5},{7,6},{8,11},{9,8},{10,9... | collective-permute-start | bytes 393224 | tf_op jit(solution)/shard_map/ppermute | solution.py:364
  17.0 2.2 %collective-permute-done.3.shard_4 = bf16[16,8192]{1,0:T(8,128)(2,1)S(1)} collective-permute-done((bf16[16,8192]{1,0:T(8,128)(2,1)S(1)}, bf16[16,8192]{1,0:T(8,128)(2,1)S(1)}, u32[]{:S(2)}, u32[]{:S(2)}) %collective-permute-start.3) | collective-permute-done | bytes 262176 | tf_op jit(solution)/shard_map/ppermute | solution.py:364
  19.4 2.7 %collective-permute-start.8 = (bf16[16,4096]{1,0:T(8,128)(2,1)S(1)}, bf16[16,4096]{1,0:T(8,128)(2,1)S(1)}, u32[]{:S(2)}, u32[]{:S(2)}) collective-permute-start(bf16[16,4096]{1,0:T(8,128)(2,1)S(1)} %slice.45), channel_id=1, source_target_pairs={{0,3},{1,0},{2,1},{3,2},{4,7},{5,4},{6,5},{7,6},{8,11},{9,8},{10,9... | collective-permute-start | bytes 393224 | tf_op jit(solution)/shard_map/ppermute | solution.py:364
  22.1 1.0 pad.12
  23.1 1.9 collective-permute-done.7.shard_8
  25.0 11.2 %forward.1 = (bf16[128,8192]{1,0:T(8,128)(2,1)}, bf16[8,16,8192]{2,1,0:T(8,128)(2,1)}, f32[2368,128]{1,0:T(8,128)}) custom-call(bf16[16,8192]{1,0:T(8,128)(2,1)} %bitcast.33, bf16[16,8192]{1,0:T(8,128)(2,1)S(1)} %collective-permute-done.shard_1, bf16[16,8192]{1,0:T(8,128)(2,1)S(1)} %collective-permute-done.1.shard_2, ...), custom_call_target="tpu_custom_call" | custom-call | tf_op jit(solution)/shard_map/forward/pallas_call | solution.py:569
  36.2 6.7 %all-to-all-start = ((bf16[8,16,8192]{2,1,0:T(8,128)(2,1)}), bf16[8,16,8192]{2,1,0:T(8,128)(2,1)S(1)}, u32[]{:S(2)}, u32[]{:S(2)}) async-start(bf16[8,16,8192]{2,1,0:T(8,128)(2,1)} %get-tuple-element.22), calls=%async_computation | async-start | bytes 4194304 | tf_op jit(solution)/shard_map/all_to_all | solution.py:1098
  42.9 1.0 fusion.2.heads_hbm
  44.0 0.9 maximum_maximum_fusion.side_hbm
  44.9 19.6 %all-to-all-done = bf16[8,16,8192]{2,1,0:T(8,128)(2,1)S(1)} async-done(((bf16[8,16,8192]{2,1,0:T(8,128)(2,1)}), bf16[8,16,8192]{2,1,0:T(8,128)(2,1)S(1)}, u32[]{:S(2)}, u32[]{:S(2)}) %all-to-all-start) | async-done | bytes 2097184 | tf_op jit(solution)/shard_map/all_to_all | solution.py:1098
  64.5 0.3 convert_reduce_fusion
  64.9 7.2 %collective-permute-start.9 = (bf16[16,8192]{1,0:T(8,128)(2,1)S(1)}, bf16[16,8192]{1,0:T(8,128)(2,1)S(1)}, u32[]{:S(2)}, u32[]{:S(2)}) collective-permute-start(bf16[16,8192]{1,0:T(8,128)(2,1)S(1)} %add_convert_fusion.shard_0), channel_id=1, source_target_pairs={{0,4},{1,5},{2,6},{3,7},{4,0},{5,1},{6,2},{7,3},{8,12},{9,13},{10,... | collective-permute-start | bytes 786440 | tf_op jit(solution)/shard_map/ppermute | solution.py:364
  72.1 1.0 collective-permute-start.10
  73.1 1.7 collective-permute-start.11
  74.8 2.1 %collective-permute-done.9.shard_1 = bf16[16,8192]{1,0:T(8,128)(2,1)S(1)} collective-permute-done((bf16[16,8192]{1,0:T(8,128)(2,1)S(1)}, bf16[16,8192]{1,0:T(8,128)(2,1)S(1)}, u32[]{:S(2)}, u32[]{:S(2)}) %collective-permute-start.9) | collective-permute-done | bytes 262176 | tf_op jit(solution)/shard_map/ppermute | solution.py:364
  76.8 1.4 collective-permute-start.12
  78.2 1.3 collective-permute-start.13
  80.2 0.2 collective-permute-start.14
  80.4 2.6 %collective-permute-start.15 = (bf16[16,4096]{1,0:T(8,128)(2,1)S(1)}, bf16[16,4096]{1,0:T(8,128)(2,1)S(1)}, u32[]{:S(2)}, u32[]{:S(2)}) collective-permute-start(bf16[16,4096]{1,0:T(8,128)(2,1)S(1)} %slice.47), channel_id=1, source_target_pairs={{0,3},{1,0},{2,1},{3,2},{4,7},{5,4},{6,5},{7,6},{8,11},{9,8},{10,9... | collective-permute-start | bytes 393224 | tf_op jit(solution)/shard_map/ppermute | solution.py:364
  83.0 2.0 %collective-permute-done.12.shard_4 = bf16[16,8192]{1,0:T(8,128)(2,1)S(1)} collective-permute-done((bf16[16,8192]{1,0:T(8,128)(2,1)S(1)}, bf16[16,8192]{1,0:T(8,128)(2,1)S(1)}, u32[]{:S(2)}, u32[]{:S(2)}) %collective-permute-start.12) | collective-permute-done | bytes 262176 | tf_op jit(solution)/shard_map/ppermute | solution.py:364
  85.2 2.9 %collective-permute-start.17 = (bf16[16,4096]{1,0:T(8,128)(2,1)S(1)}, bf16[16,4096]{1,0:T(8,128)(2,1)S(1)}, u32[]{:S(2)}, u32[]{:S(2)}) collective-permute-start(bf16[16,4096]{1,0:T(8,128)(2,1)S(1)} %slice.49), channel_id=1, source_target_pairs={{0,3},{1,0},{2,1},{3,2},{4,7},{5,4},{6,5},{7,6},{8,11},{9,8},{10,9... | collective-permute-start | bytes 393224 | tf_op jit(solution)/shard_map/ppermute | solution.py:364
  88.1 3.0 %collective-permute-done.16.shard_8 = bf16[16,4096]{1,0:T(8,128)(2,1)S(1)} collective-permute-done((bf16[16,4096]{1,0:T(8,128)(2,1)S(1)}, bf16[16,4096]{1,0:T(8,128)(2,1)S(1)}, u32[]{:S(2)}, u32[]{:S(2)}) %collective-permute-start.16) | collective-permute-done | bytes 131104 | tf_op jit(solution)/shard_map/ppermute | solution.py:364
  91.2 9.6 %cotangents.1 = (bf16[128,8192]{1,0:T(8,128)(2,1)}, f32[320,128]{1,0:T(8,128)}, f32[1328,128]{1,0:T(8,128)}, f32[88,128]{1,0:T(8,128)}) custom-call(s32[1]{0:T(128)S(6)} %copy.31.lens_ref, bf16[16,8192]{1,0:T(8,128)(2,1)S(1)} %add_convert_fusion.shard_0, bf16[16,8192]{1,0:T(8,128)(2,1)S(1)} %collective-permute-done.9.shard_1, ...), custom_call_target="tpu_custom_call" | custom-call | tf_op jit(solution)/shard_map/cotangents/pallas_call | solution.py:857
  100.8 6.4 %all-to-all-start.1 = ((f32[8,40,128]{2,1,0:T(8,128)}), f32[8,40,128]{2,1,0:T(8,128)S(1)}, u32[]{:S(2)}, u32[]{:S(2)}) async-start(f32[8,40,128]{2,1,0:T(8,128)} %bitcast.39), calls=%async_computation.1 | async-start | bytes 327680 | tf_op jit(solution)/shard_map/all_to_all | solution.py:1109
  107.3 2.8 %narrow_rows.1.narrow_hbm = f32[4,256,128]{2,1,0:T(8,128)} custom-call(f32[1328,128]{1,0:T(8,128)} %get-tuple-element.31.later_hbm, f32[2368,128]{1,0:T(8,128)} %get-tuple-element.25.state_hbm, f32[88,128]{1,0:T(8,128)} %get-tuple-element.30.scalars_hbm), custom_call_target="tpu_custom_call" | custom-call | bytes 8000000 | tf_op jit(solution)/shard_map/narrow_rows/pallas_call | solution.py:924
  110.1 4.2 %all-to-all-done.1.factors_hbm = f32[8,40,128]{2,1,0:T(8,128)S(1)} async-done(((f32[8,40,128]{2,1,0:T(8,128)}), f32[8,40,128]{2,1,0:T(8,128)S(1)}, u32[]{:S(2)}, u32[]{:S(2)}) %all-to-all-start.1) | async-done | bytes 163872 | tf_op jit(solution)/shard_map/all_to_all | solution.py:1109
  114.3 3.9 %jacobian.1 = bf16[16,56,512]{2,1,0:T(8,128)(2,1)} custom-call(f32[8,40,128]{2,1,0:T(8,128)S(1)} %all-to-all-done.1.factors_hbm, bf16[128,8192]{1,0:T(8,128)(2,1)} %get-tuple-element.27.tokens_hbm, bf16[128,8192]{1,0:T(8,128)(2,1)} %get-tuple-element.28.resid_hbm, bf16[48,8192]{1,0:T(8,128)(2,1)} %fusion.2.heads_hbm, ...), custom_call_target="tpu_custom_call" | custom-call | tf_op jit(solution)/shard_map/jacobian/pallas_call | solution.py:1018
  118.2 10.6 %all-to-all-start.2 = ((bf16[16,56,512]{2,1,0:T(8,128)(2,1)}), bf16[16,56,512]{2,1,0:T(8,128)(2,1)S(1)}, u32[]{:S(2)}, u32[]{:S(2)}) async-start(bf16[16,56,512]{2,1,0:T(8,128)(2,1)} %jacobian.1), calls=%async_computation.2 | async-start | bytes 1835008 | tf_op jit(solution)/shard_map/all_to_all | solution.py:1112
  128.9 0.6 gather_fusion
  129.9 0.7 slice.39.rewards_ref
  130.6 12.7 %all-to-all-done.2 = bf16[16,56,512]{2,1,0:T(8,128)(2,1)S(1)} async-done(((bf16[16,56,512]{2,1,0:T(8,128)(2,1)}), bf16[16,56,512]{2,1,0:T(8,128)(2,1)S(1)}, u32[]{:S(2)}, u32[]{:S(2)}) %all-to-all-start.2) | async-done | bytes 917536 | tf_op jit(solution)/shard_map/all_to_all | solution.py:1112
  143.3 0.3 copy.27
  143.6 0.5 copy.28
  144.1 0.6 copy.30
  144.7 2.3 %gram.1 = f32[16,128]{1,0:T(8,128)S(1)} custom-call(bf16[80,5632]{1,0:T(8,128)(2,1)S(1)} %bitcast.23, f32[48,128]{1,0:T(8,128)S(1)} %pad.14.pairs_ref, f32[8,128]{1,0:T(8,128)S(1)} %slice.39.rewards_ref, f32[3,16,8192]{2,1,0:T(8,128)} %bitcast.25, f32[16,4096]{1,0:T(8,128)} %bq_ref.1, f32[2,16,1024]{2,1,0:T(8,128)} %bkv_ref.1, f32[16,4096]{1,0:T(8,128)} %bitcast.34, ...), custom_call_target="tpu_custom_call" | custom-call | tf_op jit(solution)/shard_map/gram/pallas_call | solution.py:1139
  147.0 9.3 %all_to_all.30 = f32[16,16,128]{2,1,0:T(8,128)S(1)} all-to-all(f32[16,16,128]{2,1,0:T(8,128)S(1)} %broadcast_in_dim.24), channel_id=1, replica_groups=mesh['dp'=16,'tensor'=8] {'dp'}, dimensions={0} | all-to-all | bytes 262144 | tf_op jit(solution)/shard_map/all_to_all | solution.py:45
  156.4 9.6 %all_to_all.31.packed_ref = f32[8,16,128]{2,1,0:T(8,128)S(1)} all-to-all(f32[8,16,128]{2,1,0:T(8,128)S(1)} %broadcast_in_dim.25), channel_id=1, replica_groups=mesh['dp'=16,'tensor'=8] {'tensor'}, dimensions={0} | all-to-all | bytes 131072 | tf_op jit(solution)/shard_map/all_to_all | solution.py:45
  165.9 0.9 lanczos.1
  166.9 17.4 %all_to_all.32.own_ref = bf16[64,8,768]{2,1,0:T(8,128)(2,1)S(1)} all-to-all(bf16[64,8,768]{2,1,0:T(8,128)(2,1)S(1)} %broadcast_in_dim.26), channel_id=1, replica_groups={{0,1,2,3,4,5,6,7,16,17,18,19,20,21,22,23,32,33,34,35,36,37,38,39,48,49,..., dimensions={0} | all-to-all | bytes 1572864 | tf_op jit(solution)/shard_map/all_to_all | solution.py:1172
  184.3 3.4 %collective-permute-start.18 = (bf16[64,8,768]{2,1,0:T(8,128)(2,1)S(1)}, bf16[64,8,768]{2,1,0:T(8,128)(2,1)S(1)}, u32[]{:S(2)}, u32[]{:S(2)}) collective-permute-start(bf16[64,8,768]{2,1,0:T(8,128)(2,1)S(1)} %all_to_all.32.own_ref), channel_id=1, source_target_pairs={{0,8},{8,0},{16,24},{24,16},{32,40},{40,32},{48,56},{56,48},{64,72... | collective-permute-start | bytes 2359304 | tf_op jit(solution)/shard_map/ppermute | solution.py:1179
  187.6 1.9 collective-permute-done.18.other_ref
  189.5 4.4 %assemble.1 = (f32[3,16,8192]{2,1,0:T(8,128)}, f32[16,4096]{1,0:T(8,128)}, f32[2,16,1024]{2,1,0:T(8,128)}, f32[16,4096]{1,0:T(8,128)}, f32[16,8192]{1,0:T(8,128)}) custom-call(f32[1,128]{1,0:T(1,128)S(1)} %get-tuple-element.32.part_ref, bf16[64,8,768]{2,1,0:T(8,128)(2,1)S(1)} %all_to_all.32.own_ref, ...), custom_call_target="tpu_custom_call" | custom-call | tf_op jit(solution)/shard_map/assemble/pallas_call | solution.py:1039
  (49 shorter events, 1.2 us)
Async XLA Ops:
  0.6 9.8 %collective-permute-start = (bf16[16,8192]{1,0:T(8,128)(2,1)}, bf16[16,8192]{1,0:T(8,128)(2,1)S(1)}, u32[]{:S(2)}, u32[]{:S(2)}) collective-permute-start(bf16[16,8192]{1,0:T(8,128)(2,1)} %bitcast.30), channel_id=1, source_target_pairs={{0,4},{1,5},{2,6},{3,7},{4,0},{5,1},{6,2},{7,3},{8,12},{9,13},{10,... | collective-permute-start | bytes 786440 | tf_op jit(solution)/shard_map/ppermute | solution.py:364
  4.5 9.7 %collective-permute-start.1 = (bf16[16,8192]{1,0:T(8,128)(2,1)}, bf16[16,8192]{1,0:T(8,128)(2,1)S(1)}, u32[]{:S(2)}, u32[]{:S(2)}) collective-permute-start(bf16[16,8192]{1,0:T(8,128)(2,1)} %bitcast.31), channel_id=1, source_target_pairs={{0,1},{1,2},{2,3},{3,0},{4,5},{5,6},{6,7},{7,4},{8,9},{9,10},{10,1... | collective-permute-start | bytes 786440 | tf_op jit(solution)/shard_map/ppermute | solution.py:364
  6.1 8.2 %collective-permute-start.2 = (bf16[16,8192]{1,0:T(8,128)(2,1)}, bf16[16,8192]{1,0:T(8,128)(2,1)S(1)}, u32[]{:S(2)}, u32[]{:S(2)}) collective-permute-start(bf16[16,8192]{1,0:T(8,128)(2,1)} %bitcast.32), channel_id=1, source_target_pairs={{0,3},{1,0},{2,1},{3,2},{4,7},{5,4},{6,5},{7,6},{8,11},{9,8},{10,9... | collective-permute-start | bytes 786440 | tf_op jit(solution)/shard_map/ppermute | solution.py:364
  10.4 8.8 %collective-permute-start.3 = (bf16[16,8192]{1,0:T(8,128)(2,1)S(1)}, bf16[16,8192]{1,0:T(8,128)(2,1)S(1)}, u32[]{:S(2)}, u32[]{:S(2)}) collective-permute-start(bf16[16,8192]{1,0:T(8,128)(2,1)S(1)} %collective-permute-done.shard_1), channel_id=1, source_target_pairs={{0,1},{1,2},{2,3},{3,0},{4,5},{5,6},{6,7},{7,4},{8,9},{9,10},{10,1... | collective-permute-start | bytes 786440 | tf_op jit(solution)/shard_map/ppermute | solution.py:364
  12.1 7.3 %collective-permute-start.4 = (bf16[16,8192]{1,0:T(8,128)(2,1)S(1)}, bf16[16,8192]{1,0:T(8,128)(2,1)S(1)}, u32[]{:S(2)}, u32[]{:S(2)}) collective-permute-start(bf16[16,8192]{1,0:T(8,128)(2,1)S(1)} %collective-permute-done.shard_1), channel_id=1, source_target_pairs={{0,3},{1,0},{2,1},{3,2},{4,7},{5,4},{6,5},{7,6},{8,11},{9,8},{10,9... | collective-permute-start | bytes 786440 | tf_op jit(solution)/shard_map/ppermute | solution.py:364
  14.2 8.9 %collective-permute-start.5 = (bf16[16,4096]{1,0:T(8,128)(2,1)S(1)}, bf16[16,4096]{1,0:T(8,128)(2,1)S(1)}, u32[]{:S(2)}, u32[]{:S(2)}) collective-permute-start(bf16[16,4096]{1,0:T(8,128)(2,1)S(1)} %slice.42), channel_id=1, source_target_pairs={{0,1},{1,2},{2,3},{3,0},{4,5},{5,6},{6,7},{7,4},{8,9},{9,10},{10,1... | collective-permute-start | bytes 393224 | tf_op jit(solution)/shard_map/ppermute | solution.py:364
  14.3 8.8 %collective-permute-start.6 = (bf16[16,4096]{1,0:T(8,128)(2,1)S(1)}, bf16[16,4096]{1,0:T(8,128)(2,1)S(1)}, u32[]{:S(2)}, u32[]{:S(2)}) collective-permute-start(bf16[16,4096]{1,0:T(8,128)(2,1)S(1)} %slice.43), channel_id=1, source_target_pairs={{0,3},{1,0},{2,1},{3,2},{4,7},{5,4},{6,5},{7,6},{8,11},{9,8},{10,9... | collective-permute-start | bytes 393224 | tf_op jit(solution)/shard_map/ppermute | solution.py:364
  19.3 5.7 %collective-permute-start.7 = (bf16[16,4096]{1,0:T(8,128)(2,1)S(1)}, bf16[16,4096]{1,0:T(8,128)(2,1)S(1)}, u32[]{:S(2)}, u32[]{:S(2)}) collective-permute-start(bf16[16,4096]{1,0:T(8,128)(2,1)S(1)} %slice.44), channel_id=1, source_target_pairs={{0,1},{1,2},{2,3},{3,0},{4,5},{5,6},{6,7},{7,4},{8,9},{9,10},{10,1... | collective-permute-start | bytes 393224 | tf_op jit(solution)/shard_map/ppermute | solution.py:364
  19.4 5.6 %collective-permute-start.8 = (bf16[16,4096]{1,0:T(8,128)(2,1)S(1)}, bf16[16,4096]{1,0:T(8,128)(2,1)S(1)}, u32[]{:S(2)}, u32[]{:S(2)}) collective-permute-start(bf16[16,4096]{1,0:T(8,128)(2,1)S(1)} %slice.45), channel_id=1, source_target_pairs={{0,3},{1,0},{2,1},{3,2},{4,7},{5,4},{6,5},{7,6},{8,11},{9,8},{10,9... | collective-permute-start | bytes 393224 | tf_op jit(solution)/shard_map/ppermute | solution.py:364
  36.2 7.8 %copy-start = (bf16[16,8192]{1,0:T(8,128)(2,1)S(1)}, bf16[16,8192]{1,0:T(8,128)(2,1)}, u32[]{:S(2)}) copy-start(bf16[16,8192]{1,0:T(8,128)(2,1)} %up_output_hbm.1) | copy-start | bytes 786436
  36.2 7.8 %copy-start.2 = (bf16[8192,5]{0,1:T(8,128)(2,1)S(1)}, bf16[8192,5]{0,1:T(8,128)(2,1)}, u32[]{:S(2)}) copy-start(bf16[8192,5]{0,1:T(8,128)(2,1)} %param.21) | copy-start | bytes 245764
  36.2 28.3 %all-to-all-start = ((bf16[8,16,8192]{2,1,0:T(8,128)(2,1)}), bf16[8,16,8192]{2,1,0:T(8,128)(2,1)S(1)}, u32[]{:S(2)}, u32[]{:S(2)}) async-start(bf16[8,16,8192]{2,1,0:T(8,128)(2,1)} %get-tuple-element.22), calls=%async_computation | async-start | bytes 4194304 | tf_op jit(solution)/shard_map/all_to_all | solution.py:1098
  42.9 21.9 %copy-start.1 = (bf16[1,16,8192]{2,1,0:T(8,128)(2,1)S(1)}, bf16[1,16,8192]{2,1,0:T(8,128)(2,1)}, u32[]{:S(2)}) copy-start(bf16[1,16,8192]{2,1,0:T(8,128)(2,1)} %param.17) | copy-start | bytes 786436
  44.9 43.2 %copy-start.3 = (s32[16]{0:T(128)S(1)}, s32[16]{0:T(128)}, u32[]{:S(2)}) copy-start(s32[16]{0:T(128)} %param.23) | copy-start | bytes 196
  64.9 12.0 %collective-permute-start.9 = (bf16[16,8192]{1,0:T(8,128)(2,1)S(1)}, bf16[16,8192]{1,0:T(8,128)(2,1)S(1)}, u32[]{:S(2)}, u32[]{:S(2)}) collective-permute-start(bf16[16,8192]{1,0:T(8,128)(2,1)S(1)} %add_convert_fusion.shard_0), channel_id=1, source_target_pairs={{0,4},{1,5},{2,6},{3,7},{4,0},{5,1},{6,2},{7,3},{8,12},{9,13},{10,... | collective-permute-start | bytes 786440 | tf_op jit(solution)/shard_map/ppermute | solution.py:364
  72.1 8.1 %collective-permute-start.10 = (bf16[16,8192]{1,0:T(8,128)(2,1)S(1)}, bf16[16,8192]{1,0:T(8,128)(2,1)S(1)}, u32[]{:S(2)}, u32[]{:S(2)}) collective-permute-start(bf16[16,8192]{1,0:T(8,128)(2,1)S(1)} %add_convert_fusion.shard_0), channel_id=1, source_target_pairs={{0,1},{1,2},{2,3},{3,0},{4,5},{5,6},{6,7},{7,4},{8,9},{9,10},{10,1... | collective-permute-start | bytes 786440 | tf_op jit(solution)/shard_map/ppermute | solution.py:364
  73.1 7.3 %collective-permute-start.11 = (bf16[16,8192]{1,0:T(8,128)(2,1)S(1)}, bf16[16,8192]{1,0:T(8,128)(2,1)S(1)}, u32[]{:S(2)}, u32[]{:S(2)}) collective-permute-start(bf16[16,8192]{1,0:T(8,128)(2,1)S(1)} %add_convert_fusion.shard_0), channel_id=1, source_target_pairs={{0,3},{1,0},{2,1},{3,2},{4,7},{5,4},{6,5},{7,6},{8,11},{9,8},{10,9... | collective-permute-start | bytes 786440 | tf_op jit(solution)/shard_map/ppermute | solution.py:364
  76.8 8.2 %collective-permute-start.12 = (bf16[16,8192]{1,0:T(8,128)(2,1)S(1)}, bf16[16,8192]{1,0:T(8,128)(2,1)S(1)}, u32[]{:S(2)}, u32[]{:S(2)}) collective-permute-start(bf16[16,8192]{1,0:T(8,128)(2,1)S(1)} %collective-permute-done.9.shard_1), channel_id=1, source_target_pairs={{0,1},{1,2},{2,3},{3,0},{4,5},{5,6},{6,7},{7,4},{8,9},{9,10},{10,1... | collective-permute-start | bytes 786440 | tf_op jit(solution)/shard_map/ppermute | solution.py:364
  78.2 7.0 %collective-permute-start.13 = (bf16[16,8192]{1,0:T(8,128)(2,1)S(1)}, bf16[16,8192]{1,0:T(8,128)(2,1)S(1)}, u32[]{:S(2)}, u32[]{:S(2)}) collective-permute-start(bf16[16,8192]{1,0:T(8,128)(2,1)S(1)} %collective-permute-done.9.shard_1), channel_id=1, source_target_pairs={{0,3},{1,0},{2,1},{3,2},{4,7},{5,4},{6,5},{7,6},{8,11},{9,8},{10,9... | collective-permute-start | bytes 786440 | tf_op jit(solution)/shard_map/ppermute | solution.py:364
  80.2 7.9 %collective-permute-start.14 = (bf16[16,4096]{1,0:T(8,128)(2,1)S(1)}, bf16[16,4096]{1,0:T(8,128)(2,1)S(1)}, u32[]{:S(2)}, u32[]{:S(2)}) collective-permute-start(bf16[16,4096]{1,0:T(8,128)(2,1)S(1)} %slice.46), channel_id=1, source_target_pairs={{0,1},{1,2},{2,3},{3,0},{4,5},{5,6},{6,7},{7,4},{8,9},{9,10},{10,1... | collective-permute-start | bytes 393224 | tf_op jit(solution)/shard_map/ppermute | solution.py:364
  80.4 7.7 %collective-permute-start.15 = (bf16[16,4096]{1,0:T(8,128)(2,1)S(1)}, bf16[16,4096]{1,0:T(8,128)(2,1)S(1)}, u32[]{:S(2)}, u32[]{:S(2)}) collective-permute-start(bf16[16,4096]{1,0:T(8,128)(2,1)S(1)} %slice.47), channel_id=1, source_target_pairs={{0,3},{1,0},{2,1},{3,2},{4,7},{5,4},{6,5},{7,6},{8,11},{9,8},{10,9... | collective-permute-start | bytes 393224 | tf_op jit(solution)/shard_map/ppermute | solution.py:364
  85.1 6.1 %collective-permute-start.16 = (bf16[16,4096]{1,0:T(8,128)(2,1)S(1)}, bf16[16,4096]{1,0:T(8,128)(2,1)S(1)}, u32[]{:S(2)}, u32[]{:S(2)}) collective-permute-start(bf16[16,4096]{1,0:T(8,128)(2,1)S(1)} %slice.48), channel_id=1, source_target_pairs={{0,1},{1,2},{2,3},{3,0},{4,5},{5,6},{6,7},{7,4},{8,9},{9,10},{10,1... | collective-permute-start | bytes 393224 | tf_op jit(solution)/shard_map/ppermute | solution.py:364
  85.2 6.0 %collective-permute-start.17 = (bf16[16,4096]{1,0:T(8,128)(2,1)S(1)}, bf16[16,4096]{1,0:T(8,128)(2,1)S(1)}, u32[]{:S(2)}, u32[]{:S(2)}) collective-permute-start(bf16[16,4096]{1,0:T(8,128)(2,1)S(1)} %slice.49), channel_id=1, source_target_pairs={{0,3},{1,0},{2,1},{3,2},{4,7},{5,4},{6,5},{7,6},{8,11},{9,8},{10,9... | collective-permute-start | bytes 393224 | tf_op jit(solution)/shard_map/ppermute | solution.py:364
  100.8 13.5 %all-to-all-start.1 = ((f32[8,40,128]{2,1,0:T(8,128)}), f32[8,40,128]{2,1,0:T(8,128)S(1)}, u32[]{:S(2)}, u32[]{:S(2)}) async-start(f32[8,40,128]{2,1,0:T(8,128)} %bitcast.39), calls=%async_computation.1 | async-start | bytes 327680 | tf_op jit(solution)/shard_map/all_to_all | solution.py:1109
  118.2 25.1 %all-to-all-start.2 = ((bf16[16,56,512]{2,1,0:T(8,128)(2,1)}), bf16[16,56,512]{2,1,0:T(8,128)(2,1)S(1)}, u32[]{:S(2)}, u32[]{:S(2)}) async-start(bf16[16,56,512]{2,1,0:T(8,128)(2,1)} %jacobian.1), calls=%async_computation.2 | async-start | bytes 1835008 | tf_op jit(solution)/shard_map/all_to_all | solution.py:1112
  184.3 5.3 %collective-permute-start.18 = (bf16[64,8,768]{2,1,0:T(8,128)(2,1)S(1)}, bf16[64,8,768]{2,1,0:T(8,128)(2,1)S(1)}, u32[]{:S(2)}, u32[]{:S(2)}) collective-permute-start(bf16[64,8,768]{2,1,0:T(8,128)(2,1)S(1)} %all_to_all.32.own_ref), channel_id=1, source_target_pairs={{0,8},{8,0},{16,24},{24,16},{32,40},{40,32},{48,56},{56,48},{64,72... | collective-permute-start | bytes 2359304 | tf_op jit(solution)/shard_map/ppermute | solution.py:1179
